TPU v7x, 256 devices: a whole 4x4x8 slice. The times are simulated.
256 devices in a mesh: section: 32 (over z_lo, x, core), rep: 8 (over z_hi, y).
Axes of the slice: x: 4, y: 4, z: 8 (z_hi: 2, z_lo: 4; z = z_hi * 4 + z_lo), core: 2. Of those that a mesh axis runs over, the one named last changes fastest.
Arguments:
- features: bfloat16 [16384, 256], P('section'), may hold values from -6 to 6
- cotangent: bfloat16 [16384, 256], P('section'), may hold values from -6 to 6
- degrees: int32 [16384], P('section'), may hold values from 4 to 64
- blocks: bfloat16 [32, 8, 48, 128, 128], P('section', 'rep'), may hold values from -4 to 4
- block_rows: int32 [32, 8, 48], P('section', 'rep'), may hold values from 0 to 3
- block_cols: int32 [32, 8, 48], P('section', 'rep'), may hold values from 0 to 15
- block_count: int32 [32, 8], P('section', 'rep'), may hold values from 1 to 48, as said below
- w_self: bfloat16 [256, 256], replicated, may hold values from -0.375 to 0.375
- w_neigh: bfloat16 [256, 256], replicated, may hold values from -0.375 to 0.375
Outputs:
- activated: bfloat16 [16384, 256], P('section')
- feature_grad: float32 [16384, 256], P('section')
- grad_self: float32 [256, 256], replicated
- grad_neigh: float32 [256, 256], replicated
Inputs may be any that keep to these rules, and one draw needn't show every extreme that they name: `block_count`: live slots come first in each device's list; some device has all 48 slots live.
All inputs are finite; a program needn't handle non-finite values.
Results may differ from a plain program's by a relative error of at most 0.025.
Values may be sent and summed in bfloat16 or wider, within the bound.
No kernel may reach another device: no remote copies, remote signals or barrier semaphores. Data moves between devices by JAX's collectives and lax.ppermute only.
A program may use at most 64 MiB of HBM per device.

v0:
```python
import jax
import jax.numpy as jnp
from jax import lax
from jax.sharding import PartitionSpec as P

BLOCK = 128


def table_sum(table, values):
    high_part = values.astype(jnp.bfloat16)
    low_part = (values - high_part.astype(jnp.float32)).astype(jnp.bfloat16)
    first = jnp.einsum("rb,bif->rif", table, high_part, preferred_element_type=jnp.float32)
    second = jnp.einsum("rb,bif->rif", table, low_part, preferred_element_type=jnp.float32)
    return first + second


def body(
    features, cotangent, degrees, blocks, block_rows, block_cols, block_count, w_self, w_neigh
):
    node_rows = features.shape[0]
    feature_width = features.shape[1]
    section_count = lax.axis_size("section")
    replica_count = lax.axis_size("rep")
    panel_count = section_count // replica_count
    replica_index = lax.axis_index("rep")
    section_position = lax.axis_index("section")
    block_tiles = blocks[0, 0]
    row_index = block_rows[0, 0]
    col_index = block_cols[0, 0]
    slot_count = block_tiles.shape[0]
    row_blocks = node_rows // BLOCK
    live_mask = (jnp.arange(slot_count, dtype=jnp.int32) < block_count[0, 0]).astype(jnp.bfloat16)
    whole_features = lax.all_gather(features, "section", axis=0, tiled=True)
    grouped = whole_features.reshape(panel_count, replica_count, node_rows, feature_width)
    columns = lax.dynamic_index_in_dim(grouped, replica_index, 1, keepdims=False)
    columns = columns.reshape(panel_count * node_rows, feature_width)
    picked = jnp.take(
        columns.reshape(panel_count * row_blocks, BLOCK, feature_width), col_index, axis=0
    )
    products = jnp.einsum("bij,bjf->bif", block_tiles, picked, preferred_element_type=jnp.float32)
    row_table = (row_index[None, :] == jnp.arange(row_blocks, dtype=jnp.int32)[:, None]).astype(
        jnp.bfloat16
    ) * live_mask[None, :]
    partial_value = table_sum(row_table, products).reshape(node_rows, feature_width)
    degree_value = degrees.astype(jnp.float32)
    summed = lax.psum(partial_value, "rep")
    mean_input = (summed / degree_value[:, None]).astype(jnp.bfloat16)
    preact = jnp.dot(features, w_self, preferred_element_type=jnp.float32) + jnp.dot(
        mean_input, w_neigh, preferred_element_type=jnp.float32
    )
    sigmoid_value = jax.nn.sigmoid(preact)
    activated = (preact * sigmoid_value).astype(jnp.bfloat16)
    slope_value = sigmoid_value * (1.0 + preact * (1.0 - sigmoid_value))
    pre_grad = (cotangent.astype(jnp.float32) * slope_value).astype(jnp.bfloat16)
    grad_pair = (
        jnp.einsum("nf,ng->fg", features, pre_grad, preferred_element_type=jnp.float32),
        jnp.einsum("nf,ng->fg", mean_input, pre_grad, preferred_element_type=jnp.float32),
    )
    grad_self, grad_neigh = lax.psum((grad_pair[0], grad_pair[1]), "section")
    down_grad = (
        jnp.einsum("nf,gf->ng", pre_grad, w_neigh, preferred_element_type=jnp.float32)
        / degree_value[:, None]
    ).astype(jnp.bfloat16)
    self_part = jnp.einsum("nf,gf->ng", pre_grad, w_self, preferred_element_type=jnp.float32)
    by_rows = jnp.take(down_grad.reshape(row_blocks, BLOCK, feature_width), row_index, axis=0)
    back_terms = jnp.einsum(
        "bji,bjf->bif", block_tiles, by_rows, preferred_element_type=jnp.float32
    )
    col_table = (
        col_index[None, :] == jnp.arange(panel_count * row_blocks, dtype=jnp.int32)[:, None]
    ).astype(jnp.bfloat16) * live_mask[None, :]
    column_sums = table_sum(col_table, back_terms).reshape(panel_count * node_rows, feature_width)
    gathered_sums = lax.psum(column_sums.astype(jnp.bfloat16), "section").astype(jnp.float32)
    owner_mask = (section_position % replica_count == replica_index).astype(jnp.float32)
    own_panel = (
        lax.dynamic_slice_in_dim(
            gathered_sums, section_position // replica_count * node_rows, node_rows, 0
        )
        * owner_mask
    )
    returned = lax.psum(own_panel.astype(jnp.bfloat16), "rep").astype(jnp.float32)
    return (activated, self_part + returned, grad_self, grad_neigh)


def solution(mesh):
    return jax.shard_map(
        body,
        mesh=mesh,
        in_specs=(
            P("section", None),
            P("section", None),
            P("section"),
            P("section", "rep", None, None, None),
            P("section", "rep", None),
            P("section", "rep", None),
            P("section", "rep"),
            P(),
            P(),
        ),
        out_specs=(P("section", None), P("section", None), P(), P()),
        check_vma=False,
    )
```

profile of v0, /device:TPU:1, one launch (start us, length us, event | category | flops | bytes accessed | tf_op | source)
XLA Modules:
  0.0 907.0 jit_solution(12605827223850187749)
XLA Ops:
  7.2 0.0 copy-start
  7.2 0.0 all-gather.2.cloned.1.call-start
  7.2 0.7 all-gather.2.cloned.1.call-update
  7.9 0.0 all-reduce.6.cloned.1.call-start
  8.6 0.7 convert_element_type.67
  9.3 0.7 fusion.26
  10.0 0.7 compare_and_fusion
  10.6 72.6 %all-gather.2.cloned.1.call-done = bf16[16384,256]{1,0:T(8,128)(2,1)} async-done(((bf16[512,256]{1,0:T(8,128)(2,1)}), bf16[16384,256]{1,0:T(8,128)(2,1)}) %all-gather.2.cloned.1.call-update) | async-done | bytes 8388624 | tf_op jit(solution)/shard_map/all_gather | solution.py:33
  83.3 1.3 constant_dynamic-slice_fusion
  84.6 2.6 gather_fusion
  87.1 0.0 copy-done
  87.1 6.0 fusion.1
  93.2 5.0 copy.21
  98.1 5.0 copy.22
  103.1 0.0 copy-done.5
  103.1 2.6 fusion.29
  105.7 0.3 copy-done.1
  106.0 0.5 convolution_add_fusion.2
  106.5 0.9 copy.23
  107.4 0.0 all-reduce.6.cloned.1.call-update
  107.4 0.0 all-reduce.8.cloned.1.call-start
  107.5 0.2 fusion.39
  107.7 101.7 %all-reduce.6.cloned.1.call-done = f32[512,256]{1,0:T(8,128)} async-done(((f32[512,256]{1,0:T(8,128)}), f32[512,256]{1,0:T(8,128)}) %all-reduce.6.cloned.1.call-update) | async-done | bytes 524304 | tf_op jit(solution)/shard_map/psum | solution.py:46
  209.4 1.2 divide_convert_fusion
  210.6 1.1 multiply_convert_fusion.1
  211.7 1.2 fusion.12
  212.9 2.6 gather_fusion.1
  215.4 6.0 fusion
  221.5 5.0 copy.25
  226.4 5.0 copy.26
  231.4 2.6 fusion.16
  234.0 0.3 copy-done.2
  234.3 0.5 add_convert_fusion
  234.8 1.4 copy.27
  236.2 0.0 all-reduce.8.cloned.1.call-update
  236.2 0.0 all-reduce.12.cloned.1.call-start
  236.2 1.0 convolution_bitcast_fusion
  237.2 1.0 fusion.40
  238.2 0.0 all-reduce.12.cloned.1.call-update
  238.2 0.0 all-reduce.10.cloned.1.call-start
  238.3 277.1 %all-reduce.8.cloned.1.call-done = bf16[2048,256]{1,0:T(8,128)(2,1)} async-done(((bf16[2048,256]{1,0:T(8,128)(2,1)}), bf16[2048,256]{1,0:T(8,128)(2,1)}) %all-reduce.8.cloned.1.call-update) | async-done | bytes 1048592 | tf_op jit(solution)/shard_map/psum | solution.py:73
  515.3 1.7 multiply_convert_fusion
  517.0 0.0 all-reduce.10.cloned.1.call-update
  517.1 276.4 %all-reduce.12.cloned.1.call-done = (f32[256,256]{0,1:T(8,128)}, f32[256,256]{1,0:T(8,128)}) async-done(((f32[256,256]{0,1:T(8,128)}, f32[256,256]{1,0:T(8,128)}), (f32[256,256]{0,1:T(8,128)}, f32[256,256]{1,0:T(8,128)})) %all-reduce.12.cloned.1.call-update) | async-done | bytes 524304 | tf_op jit(solution)/shard_map/psum | solution.py:59
  793.5 1.8 copy.28
  795.3 101.5 %all-reduce.10.cloned.1.call-done = bf16[512,256]{1,0:T(8,128)(2,1)} async-done(((bf16[512,256]{1,0:T(8,128)(2,1)}), bf16[512,256]{1,0:T(8,128)(2,1)}) %all-reduce.10.cloned.1.call-update) | async-done | bytes 262160 | tf_op jit(solution)/shard_map/psum | solution.py:81
  896.8 2.0 convolution_add_fusion
  898.8 1.7 copy.38
  (17 shorter events, 0.0 us)
Async XLA Ops:
  7.2 80.0 %copy-start = (bf16[1,1,48,128,128]{4,3,2,1,0:T(8,128)(2,1)S(1)}, bf16[1,1,48,128,128]{4,3,2,1,0:T(8,128)(2,1)}, u32[]{:S(2)}) copy-start(bf16[1,1,48,128,128]{4,3,2,1,0:T(8,128)(2,1)} %param.12) | copy-start | bytes 4718596
  7.2 76.1 %all-gather.2.cloned.1.call-start = ((), (), s32[]{:S(2)}) async-start(), calls=%async_computation | async-start | bytes 8650752 | tf_op jit(solution)/shard_map/all_gather | solution.py:33
  7.9 201.5 %all-reduce.6.cloned.1.call-start = ((), (), s32[]{:S(2)}) async-start(), calls=%async_computation.1 | async-start | bytes 1048576 | tf_op jit(solution)/shard_map/psum | solution.py:46
  98.1 5.0 copy-start.5
  103.1 2.8 copy-start.1
  106.0 1.5 copy-start.3
  106.0 1.5 copy-start.4
  106.0 104.6 %copy-start.7 = (bf16[512,256]{1,0:T(8,128)(2,1)S(1)}, bf16[512,256]{1,0:T(8,128)(2,1)}, u32[]{:S(2)}) copy-start(bf16[512,256]{1,0:T(8,128)(2,1)} %param.10) | copy-start | bytes 786436
  106.0 104.6 %copy-start.8 = (bf16[256,256]{1,0:T(8,128)(2,1)S(1)}, bf16[256,256]{1,0:T(8,128)(2,1)}, u32[]{:S(2)}) copy-start(bf16[256,256]{1,0:T(8,128)(2,1)} %param.17) | copy-start | bytes 393220
  107.4 407.9 %all-reduce.8.cloned.1.call-start = ((), (), s32[]{:S(2)}) async-start(), calls=%async_computation.2 | async-start | bytes 2097152 | tf_op jit(solution)/shard_map/psum | solution.py:73
  226.4 5.0 copy-start.6
  231.4 2.8 copy-start.2
  236.2 557.3 %all-reduce.12.cloned.1.call-start = ((), (), s32[]{:S(2)}) async-start(), calls=%async_computation.4 | async-start | bytes 1048576 | tf_op jit(solution)/shard_map/psum | solution.py:59
  238.2 658.6 %all-reduce.10.cloned.1.call-start = ((), (), s32[]{:S(2)}) async-start(), calls=%async_computation.3 | async-start | bytes 524288 | tf_op jit(solution)/shard_map/psum | solution.py:81
Sparse Core Ops, SparseCore 0:
  9.9 73.3 all-gather.1
  107.5 101.8 all-reduce.5
  236.3 278.9 all-reduce.7
  518.4 275.0 all-reduce.11
  796.7 100.0 all-reduce.9
where the time goes:
time: 912 us; the launch traced here: 907 us
  waiting for transfers between devices  830 us (91%)
  local copies, waits for them, and re-layouts  32.6 us (4%)
  matrix products  24.7 us (3%)
  between operations  14.6 us (2%)
    psum x1, waiting for transfers between devices, body(): lax.psum(column_sums.astype(jnp.bfloat16), 'section').astype(jnp.float32)  277 us
    psum x1, waiting for transfers between devices, body(): grad_self, grad_neigh = lax.psum((grad_pair[0], grad_pair[1]), 'section')  276 us
    psum x1, waiting for transfers between devices, body(): summed = lax.psum(partial_value, 'rep')  102 us
    psum x1, waiting for transfers between devices, body(): lax.psum(own_panel.astype(jnp.bfloat16), 'rep').astype(jnp.float32)  102 us
    all_gather x1, waiting for transfers between devices, body(): whole_features = lax.all_gather(features, 'section', axis=0, tiled=True)  72.6 us
  transfers between devices with their start and end apart: 5, of which 5 were waited for; matrix products, arithmetic and copies ran while one was open for 1% of the time, Pallas kernels for 0%

commit v1 on v0

v1 whole, which is shorter than its diff:
```python
import jax
import jax.numpy as jnp
from jax import lax
from jax.experimental import pallas as pl
from jax.experimental.pallas import tpu as pltpu
from jax.sharding import PartitionSpec as P

BLOCK = 128
F32 = jnp.float32
BF16 = jnp.bfloat16


def densify_kernel(rows_ref, cols_ref, scalars_ref, blocks_ref, dense_ref, flipped_ref, total):
    total[...] = jnp.zeros_like(total)
    live = scalars_ref[0]
    core = scalars_ref[1]

    def add_slot(slot, carry):
        row = rows_ref[slot]
        col = cols_ref[slot]
        panel = col // 4
        within = col % 4
        half = (within // 2 + core) % 2
        place = half * 8 + panel * 2 + within % 2
        total[row, place] += blocks_ref[slot].astype(F32)
        return carry

    lax.fori_loop(0, live, add_slot, 0)
    for i in range(4):
        for j in range(16):
            tile = total[i, j]
            dense_ref[i * BLOCK : (i + 1) * BLOCK, j * BLOCK : (j + 1) * BLOCK] = tile.astype(BF16)
            flipped_ref[j * BLOCK : (j + 1) * BLOCK, i * BLOCK : (i + 1) * BLOCK] = tile.T.astype(
                BF16
            )


def densify(tiles, rows, cols, scalars):
    smem = pl.BlockSpec(memory_space=pltpu.SMEM)
    vmem = pl.BlockSpec(memory_space=pltpu.VMEM)
    return pl.pallas_call(
        densify_kernel,
        out_shape=(
            jax.ShapeDtypeStruct((512, 2048), BF16),
            jax.ShapeDtypeStruct((2048, 512), BF16),
        ),
        in_specs=[smem, smem, smem, vmem],
        out_specs=(vmem, vmem),
        scratch_shapes=[pltpu.VMEM((4, 16, BLOCK, BLOCK), F32)],
        compiler_params=pltpu.CompilerParams(vmem_limit_bytes=24 * 1024 * 1024),
        cost_estimate=pl.CostEstimate(flops=2**21, bytes_accessed=6 * 2**20, transcendentals=0),
    )(rows, cols, scalars, tiles)


def spot(chunk):
    return 2 * (chunk % 4) + chunk // 4


OUT_PAIRS = [
    ((8 * k + a) * 8 + b, (8 * k + spot(b)) * 8 + a)
    for k in range(4)
    for a in range(8)
    for b in range(8)
]
BACK_PAIRS = [(dst, src) for src, dst in OUT_PAIRS]
CORE_PAIRS = [(s, s ^ 1) for s in range(32)]
SAME_CORE = [[2 * i + c for i in range(16)] for c in range(2)]


def swap_core(x):
    return lax.ppermute(x, "section", CORE_PAIRS)


def exchange(x, axis, groups=None):
    return lax.all_to_all(x, axis, 0, 0, tiled=False, axis_index_groups=groups)


def body(
    features, cotangent, degrees, blocks, block_rows, block_cols, block_count, w_self, w_neigh
):
    rep = lax.axis_index("rep")
    core = lax.axis_index("section") % 2
    chunk = lax.dynamic_index_in_dim(features.reshape(8, 64, 256), rep, 0, keepdims=False)
    with jax.named_scope("spread_features"):
        turned = lax.ppermute(chunk, ("section", "rep"), OUT_PAIRS)
    scalars = jnp.stack([block_count[0, 0], core.astype(jnp.int32)])
    dense, flipped = densify(blocks[0, 0], block_rows[0, 0], block_cols[0, 0], scalars)
    with jax.named_scope("gather_features"):
        own_columns = exchange(
            jnp.broadcast_to(turned[None], (16, 64, 256)), "section", SAME_CORE
        ).reshape(1024, 256)
        other_columns = swap_core(own_columns)
    partial = jnp.dot(dense[:, :1024], own_columns, preferred_element_type=F32) + jnp.dot(
        dense[:, 1024:], other_columns, preferred_element_type=F32
    )
    with jax.named_scope("sum_over_rep"):
        pieces = exchange(partial.astype(BF16).reshape(8, 64, 256), "rep")
    degree_value = degrees.astype(F32)
    degree_chunk = lax.dynamic_index_in_dim(degree_value.reshape(8, 64), rep, 0, keepdims=False)
    mean_chunk = (pieces.astype(F32).sum(axis=0) / degree_chunk[:, None]).astype(BF16)
    with jax.named_scope("gather_mean"):
        mean_input = exchange(jnp.broadcast_to(mean_chunk[None], (8, 64, 256)), "rep").reshape(
            512, 256
        )
    preact = jnp.dot(features, w_self, preferred_element_type=F32) + jnp.dot(
        mean_input, w_neigh, preferred_element_type=F32
    )
    sigmoid_value = jax.nn.sigmoid(preact)
    activated = (preact * sigmoid_value).astype(BF16)
    slope_value = sigmoid_value * (1.0 + preact * (1.0 - sigmoid_value))
    pre_grad = (cotangent.astype(F32) * slope_value).astype(BF16)
    down_grad = (
        lax.dot_general(pre_grad, w_neigh, (((1,), (1,)), ((), ())), preferred_element_type=F32)
        / degree_value[:, None]
    ).astype(BF16)
    self_part = lax.dot_general(
        pre_grad, w_self, (((1,), (1,)), ((), ())), preferred_element_type=F32
    )
    both = jnp.concatenate([features, mean_input], axis=1)
    grads = lax.dot_general(both, pre_grad, (((0,), (0,)), ((), ())), preferred_element_type=F32)
    grad_slice = lax.dynamic_slice_in_dim(grads, rep * 64, 64, 0).reshape(2, 32, 256)
    grad_own = lax.dynamic_index_in_dim(grad_slice, core, 0, keepdims=False)
    grad_other = lax.dynamic_index_in_dim(grad_slice, 1 - core, 0, keepdims=False)
    back_other = jnp.dot(flipped[1024:], down_grad, preferred_element_type=F32).astype(BF16)
    with jax.named_scope("pair_sum"):
        back_arrived = swap_core(back_other)
        grad_arrived = swap_core(grad_other)
    back_own = jnp.dot(flipped[:1024], down_grad, preferred_element_type=F32)
    back_own = (back_own + back_arrived.astype(F32)).astype(BF16).reshape(16, 64, 256)
    grad_own = (grad_own + grad_arrived).astype(BF16).reshape(16, 2, 256)
    with jax.named_scope("sum_over_section"):
        terms = exchange(jnp.concatenate([back_own, grad_own], axis=1), "section", SAME_CORE)
    term_sum = terms.astype(F32).sum(axis=0).astype(BF16)
    with jax.named_scope("return_panels"):
        returned = lax.ppermute(term_sum[:64], ("section", "rep"), BACK_PAIRS)
    with jax.named_scope("gather_grads"):
        grad_rows = exchange(jnp.broadcast_to(term_sum[None, 64:], (32, 2, 256)), "section")
    grad_rows = grad_rows.reshape(16, 2, 2, 256).transpose(1, 0, 2, 3).reshape(64, 256)
    with jax.named_scope("gather_results"):
        last = jnp.concatenate([returned, grad_rows], axis=0)
        results = exchange(jnp.broadcast_to(last[None], (8, 128, 256)), "rep").astype(F32)
    feature_grad = self_part + results[:, :64].reshape(512, 256)
    grad_self = results[:4, 64:].reshape(256, 256)
    grad_neigh = results[4:, 64:].reshape(256, 256)
    return (activated, feature_grad, grad_self, grad_neigh)


def solution(mesh):
    return jax.shard_map(
        body,
        mesh=mesh,
        in_specs=(
            P("section", None),
            P("section", None),
            P("section"),
            P("section", "rep", None, None, None),
            P("section", "rep", None),
            P("section", "rep", None),
            P("section", "rep"),
            P(),
            P(),
        ),
        out_specs=(P("section", None), P("section", None), P(), P()),
        check_vma=False,
    )
```

time: 912 us -> 151 us (0.17)
  the two profiles are of different devices: /device:TPU:1 before, /device:TPU:38 now
where the time goes in v1:
time: 151 us; the launch traced here: 150 us
  blocking collectives  62.9 us (42%)
  waiting for transfers between devices  40.6 us (27%)
  starting transfers between devices  30.2 us (20%)
  matrix products  8.38 us (6%)
  local copies, waits for them, and re-layouts  4.73 us (3%)
  Pallas kernels  1.82 us (1%)
  between operations  1.56 us (1%)
    all_to_all x3, blocking collectives, exchange(): return lax.all_to_all(x, axis, 0, 0, tiled=False, axis_index_groups=groups)  62.9 us
    all_to_all x3, waiting for transfers between devices, exchange(): return lax.all_to_all(x, axis, 0, 0, tiled=False, axis_index_groups=groups)  28.7 us
    all_to_all x3, starting transfers between devices, exchange(): return lax.all_to_all(x, axis, 0, 0, tiled=False, axis_index_groups=groups)  14.9 us
    ppermute x1, starting transfers between devices, body(): turned = lax.ppermute(chunk, ('section', 'rep'), OUT_PAIRS)  10.7 us
    ppermute x1, waiting for transfers between devices, body(): returned = lax.ppermute(term_sum[:64], ('section', 'rep'), BACK_PAIRS)  9.09 us
  transfers between devices with their start and end apart: 8, of which 7 were waited for; matrix products, arithmetic and copies ran while one was open for 1% of the time, Pallas kernels for 1%

profile of v1, /device:TPU:38, one launch (start us, length us, event | category | flops | bytes accessed | tf_op | source)
XLA Modules:
  0.0 150.4 jit_solution(5405479978091195909)
XLA Ops:
  0.6 0.0 copy-start
  0.6 0.0 copy-start.1
  0.7 0.9 dynamic-slice_bitcast_fusion.1
  1.6 10.7 %collective-permute-start = (bf16[64,256]{1,0:T(8,128)(2,1)S(1)}, bf16[64,256]{1,0:T(8,128)(2,1)S(1)}, u32[]{:S(2)}, u32[]{:S(2)}) collective-permute-start(bf16[64,256]{1,0:T(8,128)(2,1)S(1)} %dynamic-slice_bitcast_fusion.1), channel_id=1, source_target_pairs={{0,0},{1,16},{2,32},{3,48},{4,8},{5,24},{6,40},{7,56},{8,1},{9,17}... | collective-permute-start | bytes 98312 | tf_op jit(solution)/shard_map/spread_features/ppermute | solution.py:85
  12.3 1.6 %collective-permute-done = bf16[64,256]{1,0:T(8,128)(2,1)S(1)} collective-permute-done((bf16[64,256]{1,0:T(8,128)(2,1)S(1)}, bf16[64,256]{1,0:T(8,128)(2,1)S(1)}, u32[]{:S(2)}, u32[]{:S(2)}) %collective-permute-start) | collective-permute-done | bytes 32800 | tf_op jit(solution)/shard_map/spread_features/ppermute | solution.py:85
  13.9 19.6 %all_to_all.30 = bf16[16,64,256]{2,1,0:T(8,128)(2,1)S(1)} all-to-all(bf16[16,64,256]{2,1,0:T(8,128)(2,1)S(1)} %broadcast_in_dim.8), channel_id=1, replica_groups={{0,16,32,48,64,80,96,112,128,144,160,176,192,208,224,240},{8,24,40,56,7..., dimensions={0} | all-to-all | bytes 1048576 | tf_op jit(solution)/shard_map/gather_features/all_to_all | solution.py:75
  33.5 1.1 collective-permute-start.1
  35.3 0.1 pad_add_fusion.scalars_ref
  35.4 0.0 copy-done.1
  35.4 0.7 copy-done.2
  36.0 0.7 copy-done.3
  36.7 1.8 %shard_map.120 = (bf16[512,2048]{1,0:T(8,128)(2,1)S(1)}, bf16[2048,512]{1,0:T(8,128)(2,1)S(1)}) custom-call(s32[48]{0:T(128)S(1)} %bitcast.42, s32[48]{0:T(128)S(1)} %bitcast.43, s32[2]{0:T(128)S(1)} %pad_add_fusion.scalars_ref, bf16[48,128,128]{2,1,0:T(8,128)(2,1)S(1)} %bitcast.41), custom_call_target="tpu_custom_call" | custom-call | flops 2097152 | bytes 6291456 | tf_op jit(solution)/shard_map/pallas_call | solution.py:41
  38.5 0.0 copy-start.4
  38.5 0.0 collective-permute-done.1
  38.5 0.4 fusion.7
  39.0 0.0 copy-start.10
  39.0 0.0 copy-start.6
  39.0 0.0 copy-start.7
  39.0 1.1 fusion
  40.2 4.8 %all-to-all-start.1 = ((bf16[8,64,256]{2,1,0:T(8,128)(2,1)}), bf16[8,64,256]{2,1,0:T(8,128)(2,1)S(1)}, u32[]{:S(2)}, u32[]{:S(2)}) async-start(bf16[8,64,256]{2,1,0:T(8,128)(2,1)} %bitcast.8), calls=%async_computation.1 | async-start | bytes 524288 | tf_op jit(solution)/shard_map/sum_over_rep/all_to_all | solution.py:75
  45.0 0.0 copy-done.10
  45.0 0.1 reshape.72
  45.1 14.4 %all-to-all-done.1 = bf16[8,64,256]{2,1,0:T(8,128)(2,1)S(1)} async-done(((bf16[8,64,256]{2,1,0:T(8,128)(2,1)}), bf16[8,64,256]{2,1,0:T(8,128)(2,1)S(1)}, u32[]{:S(2)}, u32[]{:S(2)}) %all-to-all-start.1) | async-done | bytes 262176 | tf_op jit(solution)/shard_map/sum_over_rep/all_to_all | solution.py:75
  59.5 0.1 divide_convert_fusion
  59.6 0.7 broadcast_in_dim.9
  60.3 3.4 %all-to-all-start.2 = ((bf16[8,64,256]{2,1,0:T(8,128)(2,1)}), bf16[8,64,256]{2,1,0:T(8,128)(2,1)S(1)}, u32[]{:S(2)}, u32[]{:S(2)}) async-start(bf16[8,64,256]{2,1,0:T(8,128)(2,1)} %broadcast_in_dim.9), calls=%async_computation.2 | async-start | bytes 524288 | tf_op jit(solution)/shard_map/gather_mean/all_to_all | solution.py:75
  63.8 0.2 fusion.18
  64.0 12.1 %all-to-all-done.2 = bf16[8,64,256]{2,1,0:T(8,128)(2,1)S(1)} async-done(((bf16[8,64,256]{2,1,0:T(8,128)(2,1)}), bf16[8,64,256]{2,1,0:T(8,128)(2,1)S(1)}, u32[]{:S(2)}, u32[]{:S(2)}) %all-to-all-start.2) | async-done | bytes 262176 | tf_op jit(solution)/shard_map/gather_mean/all_to_all | solution.py:75
  76.1 0.0 copy-done
  76.1 2.2 %multiply_convert_fusion = (bf16[512,256]{1,0:T(8,128)(2,1)S(1)}, bf16[512,256]{1,0:T(8,128)(2,1)}) fusion(bf16[512,256]{1,0:T(8,128)(2,1)} %param.10, f32[512,256]{1,0:T(8,128)S(1)} %fusion.18, bf16[512,256]{1,0:T(8,128)(2,1)S(1)} %bitcast.49, bf16[256,256]{1,0:T(8,128)(2,1)S(1)} %copy-done), kind=kOutput, calls=%fused_computation.19 | convolution fusion | flops 68812800 | bytes 1703936 | tf_op jit(solution)/shard_map/dot_general | solution.py:105
  78.3 0.3 fusion.1
  78.6 1.2 convolution_convert_fusion
  79.8 0.0 collective-permute-start.2
  79.9 0.3 fusion.10
  80.2 0.6 collective-permute-start.3
  80.8 1.0 collective-permute-done.3
  81.8 0.3 collective-permute-done.2
  82.1 1.5 add_convert_fusion
  83.6 21.5 %all_to_all.31 = bf16[16,66,256]{2,1,0:T(8,128)(2,1)S(1)} all-to-all(bf16[16,66,256]{2,1,0:T(8,128)(2,1)S(1)} %pad_maximum_fusion), channel_id=1, replica_groups={{0,16,32,48,64,80,96,112,128,144,160,176,192,208,224,240},{8,24,40,56,7..., dimensions={0} | all-to-all | bytes 1081344 | tf_op jit(solution)/shard_map/sum_over_section/all_to_all | solution.py:75
  105.1 0.1 reduce_sum.22
  105.2 0.6 broadcast_in_dim.10
  105.9 6.6 %all-to-all-start.4 = ((bf16[32,2,256]{2,1,0:T(2,128)(2,1)}), bf16[32,2,256]{2,1,0:T(2,128)(2,1)S(1)}, u32[]{:S(2)}, u32[]{:S(2)}) async-start(bf16[32,2,256]{2,1,0:T(2,128)(2,1)} %broadcast_in_dim.10), calls=%async_computation.4 | async-start | bytes 65536 | tf_op jit(solution)/shard_map/gather_grads/all_to_all | solution.py:75
  112.5 2.9 %collective-permute-start.4 = (bf16[64,256]{1,0:T(8,128)(2,1)S(1)}, bf16[64,256]{1,0:T(8,128)(2,1)S(1)}, u32[]{:S(2)}, u32[]{:S(2)}) collective-permute-start(bf16[64,256]{1,0:T(8,128)(2,1)S(1)} %slice.36), channel_id=1, source_target_pairs={{0,0},{16,1},{32,2},{48,3},{8,4},{24,5},{40,6},{56,7},{1,8},{17,9}... | collective-permute-start | bytes 98312 | tf_op jit(solution)/shard_map/return_panels/ppermute | solution.py:135
  115.4 2.2 %all-to-all-done.4 = bf16[32,2,256]{2,1,0:T(2,128)(2,1)S(1)} async-done(((bf16[32,2,256]{2,1,0:T(2,128)(2,1)}), bf16[32,2,256]{2,1,0:T(2,128)(2,1)S(1)}, u32[]{:S(2)}, u32[]{:S(2)}) %all-to-all-start.4) | async-done | bytes 32800 | tf_op jit(solution)/shard_map/gather_grads/all_to_all | solution.py:75
  117.6 9.1 %collective-permute-done.4 = bf16[64,256]{1,0:T(8,128)(2,1)S(1)} collective-permute-done((bf16[64,256]{1,0:T(8,128)(2,1)S(1)}, bf16[64,256]{1,0:T(8,128)(2,1)S(1)}, u32[]{:S(2)}, u32[]{:S(2)}) %collective-permute-start.4) | collective-permute-done | bytes 32800 | tf_op jit(solution)/shard_map/return_panels/ppermute | solution.py:135
  126.8 21.7 %all_to_all.32 = bf16[8,128,256]{2,1,0:T(8,128)(2,1)S(1)} all-to-all(bf16[8,128,256]{2,1,0:T(8,128)(2,1)S(1)} %broadcast_in_dim.11), channel_id=1, replica_groups=mesh['section'=32,'rep'=8] {'rep'}, dimensions={0} | all-to-all | bytes 1048576 | tf_op jit(solution)/shard_map/gather_results/all_to_all | solution.py:75
  148.6 1.1 convolution_add_fusion.1
  149.6 0.8 fusion.17
  (27 shorter events, 0.3 us)
Async XLA Ops:
  0.6 75.5 %copy-start = (bf16[256,256]{1,0:T(8,128)(2,1)S(1)}, bf16[256,256]{1,0:T(8,128)(2,1)}, u32[]{:S(2)}) copy-start(bf16[256,256]{1,0:T(8,128)(2,1)} %param.17) | copy-start | bytes 393220
  0.6 34.7 %copy-start.1 = (bf16[1,1,48,128,128]{4,3,2,1,0:T(8,128)(2,1)S(1)}, bf16[1,1,48,128,128]{4,3,2,1,0:T(8,128)(2,1)}, u32[]{:S(2)}) copy-start(bf16[1,1,48,128,128]{4,3,2,1,0:T(8,128)(2,1)} %param.12) | copy-start | bytes 4718596
  1.6 12.3 %collective-permute-start = (bf16[64,256]{1,0:T(8,128)(2,1)S(1)}, bf16[64,256]{1,0:T(8,128)(2,1)S(1)}, u32[]{:S(2)}, u32[]{:S(2)}) collective-permute-start(bf16[64,256]{1,0:T(8,128)(2,1)S(1)} %dynamic-slice_bitcast_fusion.1), channel_id=1, source_target_pairs={{0,0},{1,16},{2,32},{3,48},{4,8},{5,24},{6,40},{7,56},{8,1},{9,17}... | collective-permute-start | bytes 98312 | tf_op jit(solution)/shard_map/spread_features/ppermute | solution.py:85
  33.5 5.0 %collective-permute-start.1 = (bf16[1024,256]{1,0:T(8,128)(2,1)S(1)}, bf16[1024,256]{1,0:T(8,128)(2,1)S(1)}, u32[]{:S(2)}, u32[]{:S(2)}) collective-permute-start(bf16[1024,256]{1,0:T(8,128)(2,1)S(1)} %bitcast.45), channel_id=1, source_target_pairs={{0,8},{8,0},{16,24},{24,16},{32,40},{40,32},{48,56},{56,48},{64,72... | collective-permute-start | bytes 1572872 | tf_op jit(solution)/shard_map/gather_features/ppermute | solution.py:71
  35.4 0.7 copy-start.2
  36.0 0.7 copy-start.3
  38.5 1.7 %copy-start.4 = (bf16[2048,512]{1,0:T(8,128)(2,1)}, bf16[2048,512]{1,0:T(8,128)(2,1)S(1)}, u32[]{:S(2)}) copy-start(bf16[2048,512]{1,0:T(8,128)(2,1)S(1)} %get-tuple-element.7) | copy-start | bytes 6291460
  39.0 6.0 %copy-start.10 = (s32[512]{0:T(512)S(1)}, s32[512]{0:T(512)}, u32[]{:S(2)}) copy-start(s32[512]{0:T(512)} %param.11) | copy-start | bytes 6148
  39.0 24.8 %copy-start.6 = (bf16[256,256]{1,0:T(8,128)(2,1)S(1)}, bf16[256,256]{1,0:T(8,128)(2,1)}, u32[]{:S(2)}) copy-start(bf16[256,256]{1,0:T(8,128)(2,1)} %param.16) | copy-start | bytes 393220
  39.0 24.8 %copy-start.7 = (bf16[512,256]{1,0:T(8,128)(2,1)S(1)}, bf16[512,256]{1,0:T(8,128)(2,1)}, u32[]{:S(2)}) copy-start(bf16[512,256]{1,0:T(8,128)(2,1)} %param.9) | copy-start | bytes 786436
  40.2 19.3 %all-to-all-start.1 = ((bf16[8,64,256]{2,1,0:T(8,128)(2,1)}), bf16[8,64,256]{2,1,0:T(8,128)(2,1)S(1)}, u32[]{:S(2)}, u32[]{:S(2)}) async-start(bf16[8,64,256]{2,1,0:T(8,128)(2,1)} %bitcast.8), calls=%async_computation.1 | async-start | bytes 524288 | tf_op jit(solution)/shard_map/sum_over_rep/all_to_all | solution.py:75
  60.3 15.8 %all-to-all-start.2 = ((bf16[8,64,256]{2,1,0:T(8,128)(2,1)}), bf16[8,64,256]{2,1,0:T(8,128)(2,1)S(1)}, u32[]{:S(2)}, u32[]{:S(2)}) async-start(bf16[8,64,256]{2,1,0:T(8,128)(2,1)} %broadcast_in_dim.9), calls=%async_computation.2 | async-start | bytes 524288 | tf_op jit(solution)/shard_map/gather_mean/all_to_all | solution.py:75
  76.1 2.5 %copy-start.5 = (bf16[2048,512]{1,0:T(8,128)(2,1)S(1)}, bf16[2048,512]{1,0:T(8,128)(2,1)}, u32[]{:S(2)}) copy-start(bf16[2048,512]{1,0:T(8,128)(2,1)} %copy-done.4) | copy-start | bytes 6291460
  78.3 1.5 %copy-start.8 = (bf16[512,256]{1,0:T(8,128)(2,1)}, bf16[512,256]{1,0:T(8,128)(2,1)S(1)}, u32[]{:S(2)}) copy-start(bf16[512,256]{1,0:T(8,128)(2,1)S(1)} %get-tuple-element.10) | copy-start | bytes 786436
  79.8 2.3 %collective-permute-start.2 = (bf16[1024,256]{1,0:T(8,128)(2,1)}, bf16[1024,256]{1,0:T(8,128)(2,1)}, u32[]{:S(2)}, u32[]{:S(2)}) collective-permute-start(bf16[1024,256]{1,0:T(8,128)(2,1)} %convolution_convert_fusion), channel_id=1, source_target_pairs={{0,8},{8,0},{16,24},{24,16},{32,40},{40,32},{48,56},{56,48},{64,72... | collective-permute-start | bytes 1572872 | tf_op jit(solution)/shard_map/pair_sum/ppermute | solution.py:71
  80.2 1.6 %collective-permute-start.3 = (f32[32,256]{1,0:T(8,128)S(1)}, f32[32,256]{1,0:T(8,128)S(1)}, u32[]{:S(2)}, u32[]{:S(2)}) collective-permute-start(f32[32,256]{1,0:T(8,128)S(1)} %dynamic-slice_bitcast_fusion), channel_id=1, source_target_pairs={{0,8},{8,0},{16,24},{24,16},{32,40},{40,32},{48,56},{56,48},{64,72... | collective-permute-start | bytes 98312 | tf_op jit(solution)/shard_map/pair_sum/ppermute | solution.py:71
  105.1 43.4 %copy-start.9 = (bf16[512,256]{1,0:T(8,128)(2,1)S(1)}, bf16[512,256]{1,0:T(8,128)(2,1)}, u32[]{:S(2)}) copy-start(bf16[512,256]{1,0:T(8,128)(2,1)} %copy-done.8) | copy-start | bytes 786436
  105.9 11.7 %all-to-all-start.4 = ((bf16[32,2,256]{2,1,0:T(2,128)(2,1)}), bf16[32,2,256]{2,1,0:T(2,128)(2,1)S(1)}, u32[]{:S(2)}, u32[]{:S(2)}) async-start(bf16[32,2,256]{2,1,0:T(2,128)(2,1)} %broadcast_in_dim.10), calls=%async_computation.4 | async-start | bytes 65536 | tf_op jit(solution)/shard_map/gather_grads/all_to_all | solution.py:75
  112.5 14.2 %collective-permute-start.4 = (bf16[64,256]{1,0:T(8,128)(2,1)S(1)}, bf16[64,256]{1,0:T(8,128)(2,1)S(1)}, u32[]{:S(2)}, u32[]{:S(2)}) collective-permute-start(bf16[64,256]{1,0:T(8,128)(2,1)S(1)} %slice.36), channel_id=1, source_target_pairs={{0,0},{16,1},{32,2},{48,3},{8,4},{24,5},{40,6},{56,7},{1,8},{17,9}... | collective-permute-start | bytes 98312 | tf_op jit(solution)/shard_map/return_panels/ppermute | solution.py:135

commit v2 on v0

v2 whole, which is shorter than its diff:
```python
import jax
import jax.numpy as jnp
from jax import lax
from jax.experimental import pallas as pl
from jax.experimental.pallas import tpu as pltpu
from jax.sharding import PartitionSpec as P

BLOCK = 128
F32 = jnp.float32
BF16 = jnp.bfloat16
ROWS_T = (((1,), (1,)), ((), ()))
COLS_T = (((0,), (0,)), ((), ()))
SMEM = pl.BlockSpec(memory_space=pltpu.SMEM)
VMEM = pl.BlockSpec(memory_space=pltpu.VMEM)


def section_of(z, x, core):
    return z * 8 + x * 2 + core


def device_of(z, x, core, h, y):
    return section_of(z, x, core) * 8 + h * 4 + y


def column_of(x, core):
    return x // 2, (x % 2) * 2 + core


def other_end(x_home, y_column, place):
    return (x_home + y_column + 2 - place) % 4


EVERY = [
    (z, x, core, h, y)
    for z in range(4)
    for x in range(4)
    for core in range(2)
    for h in range(2)
    for y in range(4)
]


def out_pairs(core_to):
    pairs = []
    for z, x, core, h, y in EVERY:
        h_column, y_column = column_of(x, core)
        if h == h_column:
            x_to = other_end(x, y_column, y)
            pairs.append((device_of(z, x, core, h, y), device_of(z, x_to, core_to, h, y_column)))
    return pairs


def back_pairs(flip):
    pairs = []
    for z, x, core, h, y in EVERY:
        x_home, core_home = 2 * h + y // 2, y % 2
        y_to = other_end(x_home, y, x)
        pairs.append(
            (device_of(z, x, core, h, y), device_of(z, x_home, core_home, core ^ flip, y_to))
        )
    return pairs


CORE_PAIRS = [(s, s ^ 1) for s in range(32)]
SAME_CORE = [[2 * i + core for i in range(16)] for core in range(2)]
SAME_Z = [[8 * z + i for i in range(8)] for z in range(4)]
SAME_H = [[4 * h + i for i in range(4)] for h in range(2)]
BOTH = ("section", "rep")


def swap_core(x):
    return lax.ppermute(x, "section", CORE_PAIRS)


def exchange(x, axis, groups=None):
    return lax.all_to_all(x, axis, 0, 0, tiled=False, axis_index_groups=groups)


def densify_kernel(rows_ref, cols_ref, scalars_ref, blocks_ref, dense_ref, flipped_ref, total):
    total[...] = jnp.zeros_like(total)
    live = scalars_ref[0]
    turn = scalars_ref[1]

    def add_slot(slot, carry):
        total[rows_ref[slot], cols_ref[slot]] += blocks_ref[slot].astype(F32)
        return carry

    lax.fori_loop(0, live, add_slot, 0)
    for j in range(16):
        place = (j // 4) * 4 + (turn + 4 - j % 4) % 4
        start = pl.multiple_of(place * BLOCK, BLOCK)
        for i in range(4):
            tile = total[i, j]
            dense_ref[i * BLOCK : (i + 1) * BLOCK, j * BLOCK : (j + 1) * BLOCK] = tile.astype(BF16)
            flipped_ref[pl.ds(start, BLOCK), i * BLOCK : (i + 1) * BLOCK] = tile.T.astype(BF16)


def densify(tiles, rows, cols, scalars):
    return pl.pallas_call(
        densify_kernel,
        out_shape=(
            jax.ShapeDtypeStruct((512, 2048), BF16),
            jax.ShapeDtypeStruct((2048, 512), BF16),
        ),
        in_specs=[SMEM, SMEM, SMEM, VMEM],
        out_specs=(VMEM, VMEM),
        scratch_shapes=[pltpu.VMEM((4, 16, BLOCK, BLOCK), F32)],
        compiler_params=pltpu.CompilerParams(vmem_limit_bytes=20 * 1024 * 1024),
        cost_estimate=pl.CostEstimate(flops=2**22, bytes_accessed=12 * 2**20, transcendentals=0),
    )(rows, cols, scalars, tiles)


def forward_kernel(scalars_ref, dense_ref, own_ref, other_ref, out_ref, columns):
    core = scalars_ref[2]
    own_start = pl.multiple_of(core * BLOCK, BLOCK)
    other_start = pl.multiple_of((1 - core) * BLOCK, BLOCK)
    columns[:, pl.ds(own_start, BLOCK)] = own_ref[...]
    columns[:, pl.ds(other_start, BLOCK)] = other_ref[...]
    out_ref[...] = jnp.dot(dense_ref[...], columns[...], preferred_element_type=F32).astype(BF16)


def forward_product(scalars, dense, own, other):
    return pl.pallas_call(
        forward_kernel,
        out_shape=jax.ShapeDtypeStruct((512, 256), BF16),
        in_specs=[SMEM, VMEM, VMEM, VMEM],
        out_specs=VMEM,
        scratch_shapes=[pltpu.VMEM((2048, 256), BF16)],
        compiler_params=pltpu.CompilerParams(vmem_limit_bytes=16 * 1024 * 1024),
    )(scalars, dense, own, other)


def middle_kernel(
    scalars_ref,
    pieces_ref,
    degrees_ref,
    features_ref,
    cotangent_ref,
    w_self_ref,
    w_neigh_ref,
    flipped_ref,
    activated_ref,
    pre_grad_ref,
    own_ref,
    other_ref,
    inputs,
    down,
):
    core = scalars_ref[2]
    y = scalars_ref[3]
    own_start = pl.multiple_of(core * BLOCK, BLOCK)
    other_start = pl.multiple_of((1 - core) * BLOCK, BLOCK)
    degree_value = degrees_ref[...].astype(F32)
    summed = pieces_ref[:512].astype(F32) + pieces_ref[512:].astype(F32)
    mean_input = (summed / degree_value).astype(BF16)
    features = features_ref[...]
    inputs[:, :256] = features
    inputs[:, 256:] = mean_input
    preact = jnp.dot(features, w_self_ref[...], preferred_element_type=F32) + jnp.dot(
        mean_input, w_neigh_ref[...], preferred_element_type=F32
    )
    sigmoid_value = jax.nn.sigmoid(preact)
    activated_ref[...] = (preact * sigmoid_value).astype(BF16)
    slope_value = sigmoid_value * (1.0 + preact * (1.0 - sigmoid_value))
    pre_grad = (cotangent_ref[...].astype(F32) * slope_value).astype(BF16)
    pre_grad_ref[...] = pre_grad
    down[...] = (
        lax.dot_general(pre_grad, w_neigh_ref[...], ROWS_T, preferred_element_type=F32)
        / degree_value
    ).astype(BF16)
    flipped = flipped_ref[...]
    other_ref[:2048] = jnp.dot(
        flipped, down[:, pl.ds(other_start, BLOCK)], preferred_element_type=F32
    ).astype(BF16)
    own_ref[:2048] = jnp.dot(
        flipped, down[:, pl.ds(own_start, BLOCK)], preferred_element_type=F32
    )
    mine = inputs[:, pl.ds(pl.multiple_of(y * BLOCK, BLOCK), BLOCK)]
    other_ref[2048:] = lax.dot_general(
        mine,
        pre_grad_ref[:, pl.ds(other_start, BLOCK)],
        COLS_T,
        preferred_element_type=F32,
    ).astype(BF16)
    own_ref[2048:] = lax.dot_general(
        mine,
        pre_grad_ref[:, pl.ds(own_start, BLOCK)],
        COLS_T,
        preferred_element_type=F32,
    )


def middle(scalars, pieces, degrees, features, cotangent, w_self, w_neigh, flipped):
    return pl.pallas_call(
        middle_kernel,
        out_shape=(
            jax.ShapeDtypeStruct((512, 256), BF16),
            jax.ShapeDtypeStruct((512, 256), BF16),
            jax.ShapeDtypeStruct((2176, 128), F32),
            jax.ShapeDtypeStruct((2176, 128), BF16),
        ),
        in_specs=[SMEM] + [VMEM] * 7,
        out_specs=(VMEM,) * 4,
        scratch_shapes=[pltpu.VMEM((512, 512), BF16), pltpu.VMEM((512, 256), BF16)],
        compiler_params=pltpu.CompilerParams(vmem_limit_bytes=24 * 1024 * 1024),
    )(scalars, pieces, degrees, features, cotangent, w_self, w_neigh, flipped)


def body(
    features, cotangent, degrees, blocks, block_rows, block_cols, block_count, w_self, w_neigh
):
    section = lax.axis_index("section")
    rep = lax.axis_index("rep")
    x, core = (section // 2) % 4, section % 2
    h, y = rep // 4, rep % 4
    with jax.named_scope("spread_features"):
        y_column = (x % 2) * 2 + core
        block = lax.dynamic_index_in_dim(
            features.reshape(4, BLOCK, 256), other_end(x, y_column, y), 0, keepdims=False
        )
        arrived = [
            lax.ppermute(block[:, c * BLOCK : (c + 1) * BLOCK], BOTH, out_pairs(c))
            for c in range(2)
        ]
        chunk = jnp.where(core == 0, arrived[0], arrived[1])
    scalars = jnp.stack([block_count[0, 0], (2 * h + y // 2 + y + 2) % 4, core, y])
    scalars = scalars.astype(jnp.int32)
    dense, flipped = densify(blocks[0, 0], block_rows[0, 0], block_cols[0, 0], scalars)
    chunk, dense, flipped = lax.optimization_barrier((chunk, dense, flipped))
    with jax.named_scope("gather_features"):
        own_columns = exchange(
            jnp.broadcast_to(chunk[None], (16, BLOCK, BLOCK)), "section", SAME_CORE
        ).reshape(2048, BLOCK)
        other_columns = swap_core(own_columns)
    partial = forward_product(scalars, dense, own_columns, other_columns)
    with jax.named_scope("sum_over_y"):
        terms = exchange(partial.reshape(4, BLOCK, 256), "rep", SAME_H)
        partial = terms.astype(F32).sum(axis=0).astype(BF16)
    with jax.named_scope("gather_over_rep"):
        pieces = exchange(jnp.broadcast_to(partial[None], (8, BLOCK, 256)), "rep")
    activated, pre_grad, own, other = middle(
        scalars,
        pieces.reshape(1024, 256),
        degrees[:, None],
        features,
        cotangent,
        w_self,
        w_neigh,
        flipped,
    )
    with jax.named_scope("pair_sum"):
        both = (own + swap_core(other).astype(F32)).astype(BF16)
        grad_part = jnp.broadcast_to(both[2048:].reshape(1, 4, 32, 128), (4, 4, 32, 128))
        send = jnp.concatenate(
            [both[:2048].reshape(16, BLOCK, BLOCK), grad_part.reshape(16, 32, BLOCK)], axis=1
        )
    with jax.named_scope("sum_over_section"):
        total = exchange(send, "section", SAME_CORE).astype(F32).sum(axis=0).astype(BF16)
    with jax.named_scope("return_panels"):
        halves = [lax.ppermute(total[:BLOCK], BOTH, back_pairs(flip)) for flip in range(2)]
    with jax.named_scope("gather_grads"):
        grad_rows = exchange(
            jnp.broadcast_to(total[None, BLOCK:], (8, 32, BLOCK)), "section", SAME_Z
        )
        grad_rows = grad_rows.reshape(4, 2, 32, BLOCK).transpose(0, 2, 1, 3).reshape(BLOCK, 256)
    with jax.named_scope("gather_results"):
        returned = jnp.where(
            h == 0,
            jnp.concatenate(halves, axis=1),
            jnp.concatenate(halves[::-1], axis=1),
        )
        last = jnp.concatenate([returned, grad_rows], axis=0)
        results = exchange(jnp.broadcast_to(last[None], (4, 256, 256)), "rep", SAME_H).astype(F32)
    self_part = lax.dot_general(pre_grad, w_self, ROWS_T, preferred_element_type=F32)
    feature_grad = self_part + results[:, :BLOCK].reshape(512, 256)
    grad_self = results[:2, BLOCK:].reshape(256, 256)
    grad_neigh = results[2:, BLOCK:].reshape(256, 256)
    return (activated, feature_grad, grad_self, grad_neigh)


def solution(mesh):
    return jax.shard_map(
        body,
        mesh=mesh,
        in_specs=(
            P("section", None),
            P("section", None),
            P("section"),
            P("section", "rep", None, None, None),
            P("section", "rep", None),
            P("section", "rep", None),
            P("section", "rep"),
            P(),
            P(),
        ),
        out_specs=(P("section", None), P("section", None), P(), P()),
        check_vma=False,
    )
```

time: 912 us -> 139 us (0.15)
  waiting for transfers between devices: 830 us -> 18.9 us
  blocking collectives: 0 us -> 64.4 us
  starting transfers between devices: 0.2 us -> 38.4 us
  local copies, waits for them, and re-layouts: 32.6 us -> 8.18 us
  matrix products: 24.7 us -> 1.05 us
  between operations: 14.6 us -> 1.63 us
    psum x4 -> x0, waiting for transfers between devices: 757 us -> none  [the longest x1 277 us: body(): lax.psum(column_sums.astype(jnp.bfloat16), 'section').astype(jnp.float32)]
    all_gather x1 -> x0, waiting for transfers between devices: 72.6 us -> none  [body(): whole_features = lax.all_gather(features, 'section', axis=0, tiled=True)]
    all_to_all x0 -> x4, blocking collectives: none -> 64.4 us  [exchange(): return lax.all_to_all(x, axis, 0, 0, tiled=False, axis_index_groups=groups)]
    dot_general x12 -> x1, matrix products: 24.7 us -> 1.05 us  [body(): lax.dot_general(pre_grad, w_self, ROWS_T, preferred_element_type=F32)]
    ppermute x0 -> x6, starting transfers between devices: none -> 21.6 us  [the longest x2 9.17 us: swap_core(): return lax.ppermute(x, 'section', CORE_PAIRS)]
    convert_element_type x5 -> x0, local copies, waits for them, and re-layouts: 21.3 us -> none  [the longest x2 9.96 us: table_sum(): high_part = values.astype(jnp.bfloat16)]
    all_to_all x0 -> x2, starting transfers between devices: none -> 16.8 us  [exchange(): return lax.all_to_all(x, axis, 0, 0, tiled=False, axis_index_groups=groups)]
    all_to_all x0 -> x2, waiting for transfers between devices: none -> 15.8 us  [exchange(): return lax.all_to_all(x, axis, 0, 0, tiled=False, axis_index_groups=groups)]
  transfers between devices with their start and end apart: 5 -> 8, of which waited for: 5 -> 4; matrix products, arithmetic and copies ran while one was open for 1% -> 1% of each run, Pallas kernels for 0% -> 1%
where the time goes in v2:
time: 139 us
  blocking collectives  64.4 us (46%)
  starting transfers between devices  38.4 us (28%)
  waiting for transfers between devices  18.9 us (14%)
  local copies, waits for them, and re-layouts  8.18 us (6%)
  Pallas kernels  5.89 us (4%)
  between operations  1.63 us (1%)
    all_to_all x4, blocking collectives, exchange(): return lax.all_to_all(x, axis, 0, 0, tiled=False, axis_index_groups=groups)  64.4 us
    all_to_all x2, starting transfers between devices, exchange(): return lax.all_to_all(x, axis, 0, 0, tiled=False, axis_index_groups=groups)  16.8 us
    all_to_all x2, waiting for transfers between devices, exchange(): return lax.all_to_all(x, axis, 0, 0, tiled=False, axis_index_groups=groups)  15.8 us
    ppermute x2, starting transfers between devices, swap_core(): return lax.ppermute(x, 'section', CORE_PAIRS)  9.17 us
    ppermute x2, starting transfers between devices, body(): lax.ppermute(block[:, c * BLOCK:(c + 1) * BLOCK], BOTH, out_pairs(c))  8.71 us
    unnamed x17, local copies, waits for them, and re-layouts  4.6 us
    ppermute x2, starting transfers between devices, body(): lax.ppermute(total[:BLOCK], BOTH, back_pairs(flip))  3.72 us
    ppermute x2, waiting for transfers between devices, swap_core(): return lax.ppermute(x, 'section', CORE_PAIRS)  3.12 us
  transfers between devices with their start and end apart: 8, of which 4 were waited for; matrix products, arithmetic and copies ran while one was open for 1% of the time, Pallas kernels for 1%

profile of v2, /device:TPU:1, one launch (start us, length us, event | category | flops | bytes accessed | tf_op | source)
XLA Modules:
  0.0 138.9 jit_solution(10007438688753084624)
XLA Ops:
  0.7 0.8 dynamic-slice_bitcast_fusion
  1.6 6.8 %collective-permute-start = (bf16[128,128]{1,0:T(8,128)(2,1)S(1)}, bf16[128,128]{1,0:T(8,128)(2,1)S(1)}, u32[]{:S(2)}, u32[]{:S(2)}) collective-permute-start(bf16[128,128]{1,0:T(8,128)(2,1)S(1)} %get-tuple-element.25), channel_id=1, source_target_pairs={{0,32},{1,16},{2,0},{3,48},{8,49},{9,33},{10,17},{11,1},{16,18},{1... | collective-permute-start | bytes 98312 | tf_op jit(solution)/shard_map/spread_features/ppermute | solution.py:222
  8.4 1.9 %collective-permute-start.1 = (bf16[128,128]{1,0:T(8,128)(2,1)S(1)}, bf16[128,128]{1,0:T(8,128)(2,1)S(1)}, u32[]{:S(2)}, u32[]{:S(2)}) collective-permute-start(bf16[128,128]{1,0:T(8,128)(2,1)S(1)} %get-tuple-element.24), channel_id=1, source_target_pairs={{0,40},{1,24},{2,8},{3,56},{8,57},{9,41},{10,25},{11,9},{16,26},{1... | collective-permute-start | bytes 98312 | tf_op jit(solution)/shard_map/spread_features/ppermute | solution.py:222
  11.0 0.1 pad_add_fusion.scalars_ref
  11.1 0.0 copy-start
  11.1 1.4 %copy-done = bf16[1,1,48,128,128]{4,3,2,1,0:T(8,128)(2,1)S(1)} copy-done((bf16[1,1,48,128,128]{4,3,2,1,0:T(8,128)(2,1)S(1)}, bf16[1,1,48,128,128]{4,3,2,1,0:T(8,128)(2,1)}, u32[]{:S(2)}) %copy-start) | copy-done | bytes 1572888
  12.5 0.7 copy-done.5
  13.1 0.0 copy-start.6
  13.1 0.7 copy-done.6
  13.8 1.8 %shard_map.120 = (bf16[512,2048]{1,0:T(8,128)(2,1)S(1)}, bf16[2048,512]{1,0:T(8,128)(2,1)S(1)}) custom-call(s32[48]{0:T(128)S(1)} %bitcast.37, s32[48]{0:T(128)S(1)} %bitcast.38, s32[4]{0:T(128)S(1)} %pad_add_fusion.scalars_ref, bf16[48,128,128]{2,1,0:T(8,128)(2,1)S(1)} %bitcast.34), custom_call_target="tpu_custom_call" | custom-call | flops 4194304 | bytes 12582912 | tf_op jit(solution)/shard_map/pallas_call | solution.py:99
  15.6 0.0 collective-permute-done
  15.6 0.0 collective-permute-done.1
  15.6 0.1 broadcast_in_dim.14
  15.7 21.1 %all_to_all.30 = bf16[16,128,128]{2,1,0:T(8,128)(2,1)S(1)} all-to-all(bf16[16,128,128]{2,1,0:T(8,128)(2,1)S(1)} %broadcast_in_dim.14), channel_id=1, replica_groups={{0,16,32,48,64,80,96,112,128,144,160,176,192,208,224,240},{8,24,40,56,7..., dimensions={0} | all-to-all | bytes 1048576 | tf_op jit(solution)/shard_map/gather_features/all_to_all | solution.py:76
  36.9 2.2 %collective-permute-start.2 = (bf16[2048,128]{1,0:T(8,128)(2,1)S(1)}, bf16[2048,128]{1,0:T(8,128)(2,1)S(1)}, u32[]{:S(2)}, u32[]{:S(2)}) collective-permute-start(bf16[2048,128]{1,0:T(8,128)(2,1)S(1)} %bitcast.32), channel_id=1, source_target_pairs={{0,8},{8,0},{16,24},{24,16},{32,40},{40,32},{48,56},{56,48},{64,72... | collective-permute-start | bytes 1572872 | tf_op jit(solution)/shard_map/gather_features/ppermute | solution.py:72
  39.1 1.5 %collective-permute-done.2.other_ref = bf16[2048,128]{1,0:T(8,128)(2,1)S(1)} collective-permute-done((bf16[2048,128]{1,0:T(8,128)(2,1)S(1)}, bf16[2048,128]{1,0:T(8,128)(2,1)S(1)}, u32[]{:S(2)}, u32[]{:S(2)}) %collective-permute-start.2) | collective-permute-done | bytes 524320 | tf_op jit(solution)/shard_map/gather_features/ppermute | solution.py:72
  40.6 1.5 %shard_map.121 = bf16[512,256]{1,0:T(8,128)(2,1)S(1)} custom-call(s32[4]{0:T(128)S(1)} %pad_add_fusion.scalars_ref, bf16[512,2048]{1,0:T(8,128)(2,1)S(1)} %get-tuple-element.15.dense_ref, bf16[2048,128]{1,0:T(8,128)(2,1)S(1)} %bitcast.33, bf16[2048,128]{1,0:T(8,128)(2,1)S(1)} %collective-permute-done.2.other_ref), custom_call_target="tpu_custom_call" | custom-call | tf_op jit(solution)/shard_map/pallas_call | solution.py:123
  42.1 0.0 copy-start.7
  42.1 0.0 copy-start.1
  42.1 0.0 copy-start.2
  42.1 8.9 %all_to_all.31 = bf16[4,128,256]{2,1,0:T(8,128)(2,1)S(1)} all-to-all(bf16[4,128,256]{2,1,0:T(8,128)(2,1)S(1)} %bitcast.35), channel_id=1, replica_groups={{0,1,2,3},{4,5,6,7},{8,9,10,11},{12,13,14,15},{16,17,18,19},{20,21,22,2..., dimensions={0} | all-to-all | bytes 524288 | tf_op jit(solution)/shard_map/sum_over_y/all_to_all | solution.py:76
  51.1 0.8 broadcast_in_dim.15
  52.0 7.0 %all-to-all-start.2 = ((bf16[8,128,256]{2,1,0:T(8,128)(2,1)}), bf16[8,128,256]{2,1,0:T(8,128)(2,1)S(1)}, u32[]{:S(2)}, u32[]{:S(2)}) async-start(bf16[8,128,256]{2,1,0:T(8,128)(2,1)} %broadcast_in_dim.15), calls=%async_computation.2 | async-start | bytes 1048576 | tf_op jit(solution)/shard_map/gather_over_rep/all_to_all | solution.py:76
  59.0 0.0 copy-done.7
  59.0 0.1 copy.14.degrees_ref
  59.1 11.0 %all-to-all-done.2 = bf16[8,128,256]{2,1,0:T(8,128)(2,1)S(1)} async-done(((bf16[8,128,256]{2,1,0:T(8,128)(2,1)}), bf16[8,128,256]{2,1,0:T(8,128)(2,1)S(1)}, u32[]{:S(2)}, u32[]{:S(2)}) %all-to-all-start.2) | async-done | bytes 524320 | tf_op jit(solution)/shard_map/gather_over_rep/all_to_all | solution.py:76
  70.1 0.0 copy-done.1
  70.1 0.0 copy-done.2
  70.1 0.0 copy-start.3
  70.1 0.9 copy-done.3
  71.1 0.9 copy-done.4
  72.0 2.6 %shard_map.122 = (bf16[512,256]{1,0:T(8,128)(2,1)}, bf16[512,256]{1,0:T(8,128)(2,1)S(1)}, f32[2176,128]{1,0:T(8,128)S(1)}, bf16[2176,128]{1,0:T(8,128)(2,1)S(1)}) custom-call(s32[4]{0:T(128)S(1)} %pad_add_fusion.scalars_ref, bf16[1024,256]{1,0:T(8,128)(2,1)S(1)} %bitcast.31, s32[512,1]{1,0:T(8,128)S(1)} %copy.14.degrees_ref, bf16[512,256]{1,0:T(8,128)(2,1)S(1)} %copy-done.2, ...), custom_call_target="tpu_custom_call" | custom-call | tf_op jit(solution)/shard_map/pallas_call | solution.py:194
  74.6 7.0 %collective-permute-start.3 = (bf16[2176,128]{1,0:T(8,128)(2,1)S(1)}, bf16[2176,128]{1,0:T(8,128)(2,1)S(1)}, u32[]{:S(2)}, u32[]{:S(2)}) collective-permute-start(bf16[2176,128]{1,0:T(8,128)(2,1)S(1)} %get-tuple-element.21), channel_id=1, source_target_pairs={{0,8},{8,0},{16,24},{24,16},{32,40},{40,32},{48,56},{56,48},{64,72... | collective-permute-start | bytes 1671176 | tf_op jit(solution)/shard_map/pair_sum/ppermute | solution.py:72
  81.6 1.6 %collective-permute-done.3 = bf16[2176,128]{1,0:T(8,128)(2,1)S(1)} collective-permute-done((bf16[2176,128]{1,0:T(8,128)(2,1)S(1)}, bf16[2176,128]{1,0:T(8,128)(2,1)S(1)}, u32[]{:S(2)}, u32[]{:S(2)}) %collective-permute-start.3) | collective-permute-done | bytes 557088 | tf_op jit(solution)/shard_map/pair_sum/ppermute | solution.py:72
  83.1 0.1 add_convert_fusion
  83.4 23.4 %all_to_all.32 = bf16[16,160,128]{2,1,0:T(8,128)(2,1)S(1)} all-to-all(bf16[16,160,128]{2,1,0:T(8,128)(2,1)S(1)} %pad_maximum_fusion), channel_id=1, replica_groups={{0,16,32,48,64,80,96,112,128,144,160,176,192,208,224,240},{8,24,40,56,7..., dimensions={0} | all-to-all | bytes 1310720 | tf_op jit(solution)/shard_map/sum_over_section/all_to_all | solution.py:76
  106.8 0.1 reduce_sum.25
  106.9 3.3 %collective-permute-start.4 = (bf16[128,128]{1,0:T(8,128)(2,1)S(1)}, bf16[128,128]{1,0:T(8,128)(2,1)S(1)}, u32[]{:S(2)}, u32[]{:S(2)}) collective-permute-start(bf16[128,128]{1,0:T(8,128)(2,1)S(1)} %slice.41), channel_id=1, source_target_pairs={{0,2},{1,11},{2,17},{3,26},{4,32},{5,41},{6,51},{7,56},{8,6},{9,15... | collective-permute-start | bytes 98312 | tf_op jit(solution)/shard_map/return_panels/ppermute | solution.py:260
  110.2 0.4 collective-permute-start.5
  110.7 0.6 broadcast_in_dim.19
  111.3 9.8 %all-to-all-start.4 = ((bf16[8,32,128]{2,1,0:T(8,128)(2,1)}), bf16[8,32,128]{2,1,0:T(8,128)(2,1)S(1)}, u32[]{:S(2)}, u32[]{:S(2)}) async-start(bf16[8,32,128]{2,1,0:T(8,128)(2,1)} %broadcast_in_dim.19), calls=%async_computation.4 | async-start | bytes 131072 | tf_op jit(solution)/shard_map/gather_grads/all_to_all | solution.py:76
  121.1 0.0 collective-permute-done.4
  121.1 0.0 collective-permute-done.5
  121.1 4.8 %all-to-all-done.4 = bf16[8,32,128]{2,1,0:T(8,128)(2,1)S(1)} async-done(((bf16[8,32,128]{2,1,0:T(8,128)(2,1)}), bf16[8,32,128]{2,1,0:T(8,128)(2,1)S(1)}, u32[]{:S(2)}, u32[]{:S(2)}) %all-to-all-start.4) | async-done | bytes 65568 | tf_op jit(solution)/shard_map/gather_grads/all_to_all | solution.py:76
  125.9 0.1 copy.15
  126.1 10.9 %all_to_all.33 = bf16[4,256,256]{2,1,0:T(8,128)(2,1)S(1)} all-to-all(bf16[4,256,256]{2,1,0:T(8,128)(2,1)S(1)} %broadcast_in_dim.40), channel_id=1, replica_groups={{0,1,2,3},{4,5,6,7},{8,9,10,11},{12,13,14,15},{16,17,18,19},{20,21,22,2..., dimensions={0} | all-to-all | bytes 1048576 | tf_op jit(solution)/shard_map/gather_results/all_to_all | solution.py:76
  137.0 1.1 convolution_add_fusion
  138.0 0.8 fusion
  (16 shorter events, 0.3 us)
Async XLA Ops:
  1.6 14.0 %collective-permute-start = (bf16[128,128]{1,0:T(8,128)(2,1)S(1)}, bf16[128,128]{1,0:T(8,128)(2,1)S(1)}, u32[]{:S(2)}, u32[]{:S(2)}) collective-permute-start(bf16[128,128]{1,0:T(8,128)(2,1)S(1)} %get-tuple-element.25), channel_id=1, source_target_pairs={{0,32},{1,16},{2,0},{3,48},{8,49},{9,33},{10,17},{11,1},{16,18},{1... | collective-permute-start | bytes 98312 | tf_op jit(solution)/shard_map/spread_features/ppermute | solution.py:222
  8.4 7.2 %collective-permute-start.1 = (bf16[128,128]{1,0:T(8,128)(2,1)S(1)}, bf16[128,128]{1,0:T(8,128)(2,1)S(1)}, u32[]{:S(2)}, u32[]{:S(2)}) collective-permute-start(bf16[128,128]{1,0:T(8,128)(2,1)S(1)} %get-tuple-element.24), channel_id=1, source_target_pairs={{0,40},{1,24},{2,8},{3,56},{8,57},{9,41},{10,25},{11,9},{16,26},{1... | collective-permute-start | bytes 98312 | tf_op jit(solution)/shard_map/spread_features/ppermute | solution.py:222
  11.1 1.4 %copy-start = (bf16[1,1,48,128,128]{4,3,2,1,0:T(8,128)(2,1)S(1)}, bf16[1,1,48,128,128]{4,3,2,1,0:T(8,128)(2,1)}, u32[]{:S(2)}) copy-start(bf16[1,1,48,128,128]{4,3,2,1,0:T(8,128)(2,1)} %param.12) | copy-start | bytes 4718596
  12.5 0.7 copy-start.5
  13.1 0.7 copy-start.6
  36.9 3.7 %collective-permute-start.2 = (bf16[2048,128]{1,0:T(8,128)(2,1)S(1)}, bf16[2048,128]{1,0:T(8,128)(2,1)S(1)}, u32[]{:S(2)}, u32[]{:S(2)}) collective-permute-start(bf16[2048,128]{1,0:T(8,128)(2,1)S(1)} %bitcast.32), channel_id=1, source_target_pairs={{0,8},{8,0},{16,24},{24,16},{32,40},{40,32},{48,56},{56,48},{64,72... | collective-permute-start | bytes 1572872 | tf_op jit(solution)/shard_map/gather_features/ppermute | solution.py:72
  42.1 16.9 %copy-start.7 = (s32[512]{0:T(512)S(1)}, s32[512]{0:T(512)}, u32[]{:S(2)}) copy-start(s32[512]{0:T(512)} %param.11) | copy-start | bytes 6148
  42.1 28.0 %copy-start.1 = (bf16[256,256]{1,0:T(8,128)(2,1)S(1)}, bf16[256,256]{1,0:T(8,128)(2,1)}, u32[]{:S(2)}) copy-start(bf16[256,256]{1,0:T(8,128)(2,1)} %w_self_ref.1) | copy-start | bytes 393220
  42.1 28.0 %copy-start.2 = (bf16[512,256]{1,0:T(8,128)(2,1)S(1)}, bf16[512,256]{1,0:T(8,128)(2,1)}, u32[]{:S(2)}) copy-start(bf16[512,256]{1,0:T(8,128)(2,1)} %features_ref.1) | copy-start | bytes 786436
  52.0 18.2 %all-to-all-start.2 = ((bf16[8,128,256]{2,1,0:T(8,128)(2,1)}), bf16[8,128,256]{2,1,0:T(8,128)(2,1)S(1)}, u32[]{:S(2)}, u32[]{:S(2)}) async-start(bf16[8,128,256]{2,1,0:T(8,128)(2,1)} %broadcast_in_dim.15), calls=%async_computation.2 | async-start | bytes 1048576 | tf_op jit(solution)/shard_map/gather_over_rep/all_to_all | solution.py:76
  70.1 1.0 copy-start.3
  71.1 0.9 copy-start.4
  74.6 8.6 %collective-permute-start.3 = (bf16[2176,128]{1,0:T(8,128)(2,1)S(1)}, bf16[2176,128]{1,0:T(8,128)(2,1)S(1)}, u32[]{:S(2)}, u32[]{:S(2)}) collective-permute-start(bf16[2176,128]{1,0:T(8,128)(2,1)S(1)} %get-tuple-element.21), channel_id=1, source_target_pairs={{0,8},{8,0},{16,24},{24,16},{32,40},{40,32},{48,56},{56,48},{64,72... | collective-permute-start | bytes 1671176 | tf_op jit(solution)/shard_map/pair_sum/ppermute | solution.py:72
  106.9 14.1 %collective-permute-start.4 = (bf16[128,128]{1,0:T(8,128)(2,1)S(1)}, bf16[128,128]{1,0:T(8,128)(2,1)S(1)}, u32[]{:S(2)}, u32[]{:S(2)}) collective-permute-start(bf16[128,128]{1,0:T(8,128)(2,1)S(1)} %slice.41), channel_id=1, source_target_pairs={{0,2},{1,11},{2,17},{3,26},{4,32},{5,41},{6,51},{7,56},{8,6},{9,15... | collective-permute-start | bytes 98312 | tf_op jit(solution)/shard_map/return_panels/ppermute | solution.py:260
  110.2 10.8 %collective-permute-start.5 = (bf16[128,128]{1,0:T(8,128)(2,1)S(1)}, bf16[128,128]{1,0:T(8,128)(2,1)S(1)}, u32[]{:S(2)}, u32[]{:S(2)}) collective-permute-start(bf16[128,128]{1,0:T(8,128)(2,1)S(1)} %slice.41), channel_id=1, source_target_pairs={{0,6},{1,15},{2,21},{3,30},{4,36},{5,45},{6,55},{7,60},{8,2},{9,11... | collective-permute-start | bytes 98312 | tf_op jit(solution)/shard_map/return_panels/ppermute | solution.py:260
  111.3 14.6 %all-to-all-start.4 = ((bf16[8,32,128]{2,1,0:T(8,128)(2,1)}), bf16[8,32,128]{2,1,0:T(8,128)(2,1)S(1)}, u32[]{:S(2)}, u32[]{:S(2)}) async-start(bf16[8,32,128]{2,1,0:T(8,128)(2,1)} %broadcast_in_dim.19), calls=%async_computation.4 | async-start | bytes 131072 | tf_op jit(solution)/shard_map/gather_grads/all_to_all | solution.py:76

commit v3 on v2

v3 whole, which is shorter than its diff:
```python
import jax
import jax.numpy as jnp
from jax import lax
from jax.experimental import pallas as pl
from jax.experimental.pallas import tpu as pltpu
from jax.sharding import PartitionSpec as P

BLOCK = 128
SLOTS = 48
F32 = jnp.float32
BF16 = jnp.bfloat16
ROWS_T = (((1,), (1,)), ((), ()))
COLS_T = (((0,), (0,)), ((), ()))
SMEM = pl.BlockSpec(memory_space=pltpu.SMEM)
VMEM = pl.BlockSpec(memory_space=pltpu.VMEM)


def section_of(z, x, core):
    return z * 8 + x * 2 + core


def device_of(z, x, core, h, y):
    return section_of(z, x, core) * 8 + h * 4 + y


def column_of(x, core):
    return x // 2, (x % 2) * 2 + core


def other_end(x_home, y_column, place):
    return (x_home + y_column + 2 - place) % 4


EVERY = [
    (z, x, core, h, y)
    for z in range(4)
    for x in range(4)
    for core in range(2)
    for h in range(2)
    for y in range(4)
]


def out_pairs():
    pairs = []
    for z, x, core, h, y in EVERY:
        h_column, y_column = column_of(x, core)
        if h == h_column:
            x_to = other_end(x, y_column, y)
            pairs.append((device_of(z, x, core, h, y), device_of(z, x_to, core, h, y_column)))
    return pairs


SPLIT_PAIRS = [
    (device_of(z, x, y % 2, h, y), device_of(z, x, 1 - y % 2, h, y))
    for z, x, core, h, y in EVERY
    if core == 0
]
CORE_PAIRS = [(s, s ^ 1) for s in range(32)]
SAME_CORE = [[2 * i + core for i in range(16)] for core in range(2)]
SAME_Z = [[8 * z + i for i in range(8)] for z in range(4)]
SAME_H = [[4 * h + i for i in range(4)] for h in range(2)]
BOTH = ("section", "rep")


def swap_core(x):
    return lax.ppermute(x, "section", CORE_PAIRS)


def exchange(x, axis, groups=None):
    return lax.all_to_all(x, axis, 0, 0, tiled=False, axis_index_groups=groups)


def densify_kernel(slots_ref, blocks_hbm, dense_ref, flipped_ref, blocks, total, arrived):
    copy = pltpu.make_async_copy(blocks_hbm, blocks, arrived)
    copy.start()
    total[...] = jnp.zeros_like(total)
    copy.wait()

    def add_slot(slot, carry):
        total[slots_ref[slot], slots_ref[SLOTS + slot]] += blocks[slot].astype(F32)
        return carry

    lax.fori_loop(0, slots_ref[2 * SLOTS], add_slot, 0)
    for i in range(4):
        for j in range(16):
            tile = total[i, j]
            rows, cols = pl.ds(i * BLOCK, BLOCK), pl.ds(j * BLOCK, BLOCK)
            dense_ref[rows, cols] = tile.astype(BF16)
            flipped_ref[cols, rows] = tile.T.astype(BF16)


def densify(tiles, slots):
    return pl.pallas_call(
        densify_kernel,
        out_shape=(
            jax.ShapeDtypeStruct((512, 2048), BF16),
            jax.ShapeDtypeStruct((2048, 512), BF16),
        ),
        in_specs=[SMEM, pl.BlockSpec(memory_space=pltpu.HBM)],
        out_specs=(VMEM, VMEM),
        scratch_shapes=[
            pltpu.VMEM((SLOTS, BLOCK, BLOCK), BF16),
            pltpu.VMEM((4, 16, BLOCK, BLOCK), F32),
            pltpu.SemaphoreType.DMA,
        ],
        compiler_params=pltpu.CompilerParams(vmem_limit_bytes=56 * 1024 * 1024),
        cost_estimate=pl.CostEstimate(flops=2**22, bytes_accessed=12 * 2**20, transcendentals=0),
    )(slots, tiles)


def forward_kernel(scalars_ref, dense_ref, own_ref, other_ref, out_ref, columns):
    core = scalars_ref[0]
    own_start = pl.multiple_of(core * BLOCK, BLOCK)
    other_start = pl.multiple_of((1 - core) * BLOCK, BLOCK)
    columns[:, pl.ds(own_start, BLOCK)] = own_ref[...]
    columns[:, pl.ds(other_start, BLOCK)] = other_ref[...]
    out_ref[...] = jnp.dot(dense_ref[...], columns[...], preferred_element_type=F32).astype(BF16)


def forward_product(scalars, dense, own, other):
    return pl.pallas_call(
        forward_kernel,
        out_shape=jax.ShapeDtypeStruct((512, 256), BF16),
        in_specs=[SMEM, VMEM, VMEM, VMEM],
        out_specs=VMEM,
        scratch_shapes=[pltpu.VMEM((2048, 256), BF16)],
        compiler_params=pltpu.CompilerParams(vmem_limit_bytes=16 * 1024 * 1024),
    )(scalars, dense, own, other)


def middle_kernel(
    scalars_ref,
    pieces_ref,
    degrees_ref,
    features_ref,
    cotangent_ref,
    w_self_ref,
    w_neigh_ref,
    flipped_ref,
    activated_ref,
    pre_grad_ref,
    own_ref,
    other_ref,
    inputs,
    down,
    slices,
):
    core = scalars_ref[0]
    rep = scalars_ref[1]
    degree_value = degrees_ref[...]
    summed = pieces_ref[:512].astype(F32) + pieces_ref[512:].astype(F32)
    mean_input = (summed / degree_value).astype(BF16)
    features = features_ref[...]
    inputs[:, :256] = features
    inputs[:, 256:] = mean_input
    preact = jnp.dot(features, w_self_ref[...], preferred_element_type=F32) + jnp.dot(
        mean_input, w_neigh_ref[...], preferred_element_type=F32
    )
    sigmoid_value = jax.nn.sigmoid(preact)
    activated_ref[...] = (preact * sigmoid_value).astype(BF16)
    slope_value = sigmoid_value * (1.0 + preact * (1.0 - sigmoid_value))
    pre_grad = (cotangent_ref[...].astype(F32) * slope_value).astype(BF16)
    pre_grad_ref[...] = pre_grad
    down[...] = (
        lax.dot_general(pre_grad, w_neigh_ref[...], ROWS_T, preferred_element_type=F32)
        / degree_value
    ).astype(BF16)
    first = core == 0
    for i in range(8):
        rows = pl.ds(i * 256, 256)
        term = jnp.dot(flipped_ref[rows, :], down[...], preferred_element_type=F32)
        left, right = term[:, :BLOCK], term[:, BLOCK:]
        own_ref[rows, :] = jnp.where(first, left, right)
        other_ref[rows, :] = jnp.where(first, right, left).astype(BF16)
    pair_start = pl.multiple_of(rep // 2 * BLOCK, BLOCK)
    slices[...] = lax.dot_general(
        inputs[:, pl.ds(pair_start, BLOCK)], pre_grad, COLS_T, preferred_element_type=F32
    )
    mine = slices[pl.ds(pl.multiple_of(rep % 2 * 64, 64), 64), :]
    left, right = mine[:, :BLOCK], mine[:, BLOCK:]
    own_ref[2048:] = jnp.where(first, left, right)
    other_ref[2048:] = jnp.where(first, right, left).astype(BF16)


def middle(scalars, pieces, degrees, features, cotangent, w_self, w_neigh, flipped):
    return pl.pallas_call(
        middle_kernel,
        out_shape=(
            jax.ShapeDtypeStruct((512, 256), BF16),
            jax.ShapeDtypeStruct((512, 256), BF16),
            jax.ShapeDtypeStruct((2112, 128), F32),
            jax.ShapeDtypeStruct((2112, 128), BF16),
        ),
        in_specs=[SMEM] + [VMEM] * 7,
        out_specs=(VMEM,) * 4,
        scratch_shapes=[
            pltpu.VMEM((512, 512), BF16),
            pltpu.VMEM((512, 256), BF16),
            pltpu.VMEM((BLOCK, 256), F32),
        ],
        compiler_params=pltpu.CompilerParams(vmem_limit_bytes=24 * 1024 * 1024),
    )(scalars, pieces, degrees, features, cotangent, w_self, w_neigh, flipped)


def finish_kernel(results_ref, pre_grad_ref, w_self_ref, feature_ref, self_ref, neigh_ref):
    self_part = lax.dot_general(
        pre_grad_ref[...], w_self_ref[...], ROWS_T, preferred_element_type=F32
    )
    for x in range(4):
        rows = pl.ds(x * BLOCK, BLOCK)
        for core in range(2):
            cols = pl.ds(core * BLOCK, BLOCK)
            place = 2 * x + core
            feature_ref[rows, cols] = self_part[
                x * BLOCK : (x + 1) * BLOCK, core * BLOCK : (core + 1) * BLOCK
            ] + results_ref[place, :BLOCK].astype(F32)
            for part in range(8):
                target = self_ref if part < 4 else neigh_ref
                piece = results_ref[place, BLOCK + part * 16 : BLOCK + part * 16 + 16]
                target[pl.ds(part % 4 * 64 + x * 16, 16), cols] = piece.astype(F32)


def finish(results, pre_grad, w_self):
    return pl.pallas_call(
        finish_kernel,
        out_shape=(
            jax.ShapeDtypeStruct((512, 256), F32),
            jax.ShapeDtypeStruct((256, 256), F32),
            jax.ShapeDtypeStruct((256, 256), F32),
        ),
        in_specs=[VMEM] * 3,
        out_specs=(VMEM,) * 3,
        compiler_params=pltpu.CompilerParams(vmem_limit_bytes=16 * 1024 * 1024),
    )(results, pre_grad, w_self)


def body(
    features, cotangent, degrees, blocks, block_rows, block_cols, block_count, w_self, w_neigh
):
    section = lax.axis_index("section")
    rep = lax.axis_index("rep")
    x, core = (section // 2) % 4, section % 2
    y = rep % 4
    first = core == 0
    with jax.named_scope("spread_features"):
        y_column = (x % 2) * 2 + core
        block = lax.dynamic_index_in_dim(
            features.reshape(4, BLOCK, 256), other_end(x, y_column, y), 0, keepdims=False
        )
        block = lax.ppermute(block, BOTH, out_pairs())
    slots = jnp.concatenate([block_rows[0, 0], block_cols[0, 0], block_count[0]])
    dense, flipped = densify(blocks[0, 0], slots)
    degree_column = degrees.astype(F32)[:, None]
    block, dense, flipped, degree_column = lax.optimization_barrier(
        (block, dense, flipped, degree_column)
    )
    with jax.named_scope("split_features"):
        left, right = block[:, :BLOCK], block[:, BLOCK:]
        handed = lax.ppermute(jnp.where(first, right, left), BOTH, SPLIT_PAIRS)
        chunk = jnp.where(core == y % 2, jnp.where(first, left, right), handed)
    with jax.named_scope("gather_features"):
        own_columns = exchange(
            jnp.broadcast_to(chunk[None], (16, BLOCK, BLOCK)), "section", SAME_CORE
        ).reshape(2048, BLOCK)
        other_columns = swap_core(own_columns)
    scalars = jnp.stack([core, rep]).astype(jnp.int32)
    partial = forward_product(scalars, dense, own_columns, other_columns)
    with jax.named_scope("sum_over_y"):
        terms = exchange(partial.reshape(4, BLOCK, 256), "rep", SAME_H)
        partial = terms.astype(F32).sum(axis=0).astype(BF16)
    with jax.named_scope("gather_over_rep"):
        pieces = exchange(jnp.broadcast_to(partial[None], (8, BLOCK, 256)), "rep")
    activated, pre_grad, own, other = middle(
        scalars,
        pieces.reshape(1024, 256),
        degree_column,
        features,
        cotangent,
        w_self,
        w_neigh,
        flipped,
    )
    with jax.named_scope("pair_sum"):
        both = (own + swap_core(other).astype(F32)).astype(BF16)
        grad_part = jnp.broadcast_to(both[2048:].reshape(1, 4, 16, BLOCK), (4, 4, 16, BLOCK))
        send = jnp.concatenate(
            [both[:2048].reshape(16, BLOCK, BLOCK), grad_part.reshape(16, 16, BLOCK)], axis=1
        )
    with jax.named_scope("sum_over_section"):
        total = exchange(send, "section", SAME_CORE).astype(F32).sum(axis=0).astype(BF16)
    with jax.named_scope("gather_sums"):
        sums = exchange(jnp.broadcast_to(total[None], (8, BLOCK + 16, BLOCK)), "rep")
    with jax.named_scope("return_panels"):
        grad_rows = jnp.broadcast_to(
            sums[:, BLOCK:].reshape(1, BLOCK, BLOCK), (8, BLOCK, BLOCK)
        )
        results = exchange(
            jnp.concatenate([sums[:, :BLOCK], grad_rows], axis=1), "section", SAME_Z
        )
    feature_grad, grad_self, grad_neigh = finish(results, pre_grad, w_self)
    return (activated, feature_grad, grad_self, grad_neigh)


def solution(mesh):
    return jax.shard_map(
        body,
        mesh=mesh,
        in_specs=(
            P("section", None),
            P("section", None),
            P("section"),
            P("section", "rep", None, None, None),
            P("section", "rep", None),
            P("section", "rep", None),
            P("section", "rep"),
            P(),
            P(),
        ),
        out_specs=(P("section", None), P("section", None), P(), P()),
        check_vma=False,
    )
```

time: 139 us -> 139 us (level)
  blocking collectives: 64.4 us -> 80.8 us
  starting transfers between devices: 38.4 us -> 23.2 us
  Pallas kernels: 5.89 us -> 9.41 us
  waiting for transfers between devices: 18.9 us -> 15.8 us
  local copies, waits for them, and re-layouts: 8.18 us -> 5.51 us
  other arithmetic: 0.41 us -> 2.35 us
    all_to_all x4 -> x5, blocking collectives: 64.4 us -> 80.8 us  [exchange(): return lax.all_to_all(x, axis, 0, 0, tiled=False, axis_index_groups=groups)]
    all_to_all x2 -> x1, starting transfers between devices: 16.8 us -> 6.63 us  [exchange(): return lax.all_to_all(x, axis, 0, 0, tiled=False, axis_index_groups=groups)]
    ppermute x4 -> x2, starting transfers between devices: 12.4 us -> 7.51 us  [the longest x1 6.22 us: body(): block = lax.ppermute(block, BOTH, out_pairs())]
    all_to_all x2 -> x1, waiting for transfers between devices: 15.8 us -> 11 us  [exchange(): return lax.all_to_all(x, axis, 0, 0, tiled=False, axis_index_groups=groups)]
    pallas_call x1, Pallas kernels: 1.79 us -> 4.81 us  [densify(): pl.pallas_call(densify_kernel, out_shape=(jax.ShapeDtypeStruct((512, 2048...]
    ppermute x4 -> x2, waiting for transfers between devices: 0.01 us -> 1.78 us  [the longest x1 1.78 us: body(): handed = lax.ppermute(jnp.where(first, right, left), BOTH, SPLIT_PAIRS)]
    unnamed x17 -> x12, local copies, waits for them, and re-layouts: 4.6 us -> 3.45 us
  transfers between devices with their start and end apart: 8 -> 5, of which waited for: 4 -> 4; matrix products, arithmetic and copies ran while one was open for 1% -> 2% of each run, Pallas kernels for 1% -> 3%
where the time goes in v3:
time: 139 us
  blocking collectives  80.8 us (58%)
  starting transfers between devices  23.2 us (17%)
  waiting for transfers between devices  15.8 us (11%)
  Pallas kernels  9.41 us (7%)
  local copies, waits for them, and re-layouts  5.51 us (4%)
  other arithmetic  2.35 us (2%)
  between operations  1.56 us (1%)
    all_to_all x5, blocking collectives, exchange(): return lax.all_to_all(x, axis, 0, 0, tiled=False, axis_index_groups=groups)  80.8 us
    all_to_all x1, waiting for transfers between devices, exchange(): return lax.all_to_all(x, axis, 0, 0, tiled=False, axis_index_groups=groups)  11 us
    ppermute x2, starting transfers between devices, swap_core(): return lax.ppermute(x, 'section', CORE_PAIRS)  9.04 us
    all_to_all x1, starting transfers between devices, exchange(): return lax.all_to_all(x, axis, 0, 0, tiled=False, axis_index_groups=groups)  6.63 us
    ppermute x1, starting transfers between devices, body(): block = lax.ppermute(block, BOTH, out_pairs())  6.22 us
    pallas_call x1, Pallas kernels, densify(): pl.pallas_call(densify_kernel, out_shape=(jax.ShapeDtypeStruct((512, 2048...  4.81 us
    unnamed x12, local copies, waits for them, and re-layouts  3.45 us
    ppermute x2, waiting for transfers between devices, swap_core(): return lax.ppermute(x, 'section', CORE_PAIRS)  3.02 us
  transfers between devices with their start and end apart: 5, of which 4 were waited for; matrix products, arithmetic and copies ran while one was open for 2% of the time, Pallas kernels for 3%

profile of v3, /device:TPU:1, one launch (start us, length us, event | category | flops | bytes accessed | tf_op | source)
XLA Modules:
  0.0 138.6 jit_solution(57545631120459944)
XLA Ops:
  0.7 0.8 dynamic-slice_bitcast_fusion
  1.6 6.2 %collective-permute-start = (bf16[128,256]{1,0:T(8,128)(2,1)S(1)}, bf16[128,256]{1,0:T(8,128)(2,1)S(1)}, u32[]{:S(2)}, u32[]{:S(2)}) collective-permute-start(bf16[128,256]{1,0:T(8,128)(2,1)S(1)} %dynamic-slice_bitcast_fusion), channel_id=1, source_target_pairs={{0,32},{1,16},{2,0},{3,48},{8,57},{9,41},{10,25},{11,9},{16,18},{1... | collective-permute-start | bytes 196616 | tf_op jit(solution)/shard_map/spread_features/ppermute | solution.py:251
  8.4 0.7 convert_element_type.6
  9.1 1.3 pad_add_fusion.1.slots_ref
  10.4 4.8 %shard_map.120 = (bf16[512,2048]{1,0:T(8,128)(2,1)}, bf16[2048,512]{1,0:T(8,128)(2,1)}) custom-call(s32[97]{0:T(128)} %pad_add_fusion.1.slots_ref, bf16[48,128,128]{2,1,0:T(8,128)(2,1)} %bitcast.24), custom_call_target="tpu_custom_call" | custom-call | flops 4194304 | bytes 12582912 | tf_op jit(solution)/shard_map/pallas_call | solution.py:94
  15.2 0.0 collective-permute-done
  15.2 1.3 collective-permute-start.1
  16.5 1.8 %collective-permute-done.1 = bf16[128,128]{1,0:T(8,128)(2,1)S(1)} collective-permute-done((bf16[128,128]{1,0:T(8,128)(2,1)S(1)}, bf16[128,128]{1,0:T(8,128)(2,1)S(1)}, u32[]{:S(2)}, u32[]{:S(2)}) %collective-permute-start.1) | collective-permute-done | bytes 32800 | tf_op jit(solution)/shard_map/split_features/ppermute | solution.py:260
  18.3 0.1 broadcast_in_dim.17
  18.4 20.7 %all_to_all.30 = bf16[16,128,128]{2,1,0:T(8,128)(2,1)S(1)} all-to-all(bf16[16,128,128]{2,1,0:T(8,128)(2,1)S(1)} %broadcast_in_dim.17), channel_id=1, replica_groups={{0,16,32,48,64,80,96,112,128,144,160,176,192,208,224,240},{8,24,40,56,7..., dimensions={0} | all-to-all | bytes 1048576 | tf_op jit(solution)/shard_map/gather_features/all_to_all | solution.py:71
  39.2 1.9 %collective-permute-start.2 = (bf16[2048,128]{1,0:T(8,128)(2,1)S(1)}, bf16[2048,128]{1,0:T(8,128)(2,1)S(1)}, u32[]{:S(2)}, u32[]{:S(2)}) collective-permute-start(bf16[2048,128]{1,0:T(8,128)(2,1)S(1)} %bitcast.19), channel_id=1, source_target_pairs={{0,8},{8,0},{16,24},{24,16},{32,40},{40,32},{48,56},{56,48},{64,72... | collective-permute-start | bytes 1572872 | tf_op jit(solution)/shard_map/gather_features/ppermute | solution.py:67
  41.1 0.1 pad_add_fusion.scalars_ref
  41.2 1.5 %collective-permute-done.2.other_ref = bf16[2048,128]{1,0:T(8,128)(2,1)S(1)} collective-permute-done((bf16[2048,128]{1,0:T(8,128)(2,1)S(1)}, bf16[2048,128]{1,0:T(8,128)(2,1)S(1)}, u32[]{:S(2)}, u32[]{:S(2)}) %collective-permute-start.2) | collective-permute-done | bytes 524320 | tf_op jit(solution)/shard_map/gather_features/ppermute | solution.py:67
  42.7 0.0 copy-start.1
  42.7 1.6 %copy-done.1 = bf16[512,2048]{1,0:T(8,128)(2,1)S(1)} copy-done((bf16[512,2048]{1,0:T(8,128)(2,1)S(1)}, bf16[512,2048]{1,0:T(8,128)(2,1)}, u32[]{:S(2)}) %copy-start.1) | copy-done | bytes 2097176
  44.3 1.5 %shard_map.121 = bf16[512,256]{1,0:T(8,128)(2,1)S(1)} custom-call(s32[2]{0:T(128)S(1)} %pad_add_fusion.scalars_ref, bf16[512,2048]{1,0:T(8,128)(2,1)S(1)} %copy-done.1, bf16[2048,128]{1,0:T(8,128)(2,1)S(1)} %bitcast.20, bf16[2048,128]{1,0:T(8,128)(2,1)S(1)} %collective-permute-done.2.other_ref), custom_call_target="tpu_custom_call" | custom-call | tf_op jit(solution)/shard_map/pallas_call | solution.py:122
  45.8 0.0 copy-start.3
  45.8 8.7 %all_to_all.31 = bf16[4,128,256]{2,1,0:T(8,128)(2,1)S(1)} all-to-all(bf16[4,128,256]{2,1,0:T(8,128)(2,1)S(1)} %bitcast.21), channel_id=1, replica_groups={{0,1,2,3},{4,5,6,7},{8,9,10,11},{12,13,14,15},{16,17,18,19},{20,21,22,2..., dimensions={0} | all-to-all | bytes 524288 | tf_op jit(solution)/shard_map/sum_over_y/all_to_all | solution.py:71
  54.5 0.0 copy-start
  54.5 0.0 copy-start.2
  54.6 0.8 broadcast_in_dim.18
  55.4 6.6 %all-to-all-start.2 = ((bf16[8,128,256]{2,1,0:T(8,128)(2,1)}), bf16[8,128,256]{2,1,0:T(8,128)(2,1)S(1)}, u32[]{:S(2)}, u32[]{:S(2)}) async-start(bf16[8,128,256]{2,1,0:T(8,128)(2,1)} %broadcast_in_dim.18), calls=%async_computation.2 | async-start | bytes 1048576 | tf_op jit(solution)/shard_map/gather_over_rep/all_to_all | solution.py:71
  62.0 0.1 copy.13.degrees_ref
  62.2 11.0 %all-to-all-done.2 = bf16[8,128,256]{2,1,0:T(8,128)(2,1)S(1)} async-done(((bf16[8,128,256]{2,1,0:T(8,128)(2,1)}), bf16[8,128,256]{2,1,0:T(8,128)(2,1)S(1)}, u32[]{:S(2)}, u32[]{:S(2)}) %all-to-all-start.2) | async-done | bytes 524320 | tf_op jit(solution)/shard_map/gather_over_rep/all_to_all | solution.py:71
  73.2 0.0 copy-done.3
  73.2 0.0 copy-done
  73.2 0.0 copy-done.2
  73.2 0.0 copy-start.4
  73.2 0.9 copy-done.4
  74.1 0.0 copy-start.5
  74.1 0.9 copy-done.5
  75.0 1.9 %shard_map.122 = (bf16[512,256]{1,0:T(8,128)(2,1)}, bf16[512,256]{1,0:T(8,128)(2,1)S(1)}, f32[2112,128]{1,0:T(8,128)S(1)}, bf16[2112,128]{1,0:T(8,128)(2,1)S(1)}) custom-call(s32[2]{0:T(128)S(1)} %pad_add_fusion.scalars_ref, bf16[1024,256]{1,0:T(8,128)(2,1)S(1)} %bitcast.18, f32[512,1]{1,0:T(8,128)S(1)} %copy.13.degrees_ref, bf16[512,256]{1,0:T(8,128)(2,1)S(1)} %copy-done.3, ...), custom_call_target="tpu_custom_call" | custom-call | tf_op jit(solution)/shard_map/pallas_call | solution.py:187
  77.0 7.1 %collective-permute-start.3 = (bf16[2112,128]{1,0:T(8,128)(2,1)S(1)}, bf16[2112,128]{1,0:T(8,128)(2,1)S(1)}, u32[]{:S(2)}, u32[]{:S(2)}) collective-permute-start(bf16[2112,128]{1,0:T(8,128)(2,1)S(1)} %get-tuple-element.25), channel_id=1, source_target_pairs={{0,8},{8,0},{16,24},{24,16},{32,40},{40,32},{48,56},{56,48},{64,72... | collective-permute-start | bytes 1622024 | tf_op jit(solution)/shard_map/pair_sum/ppermute | solution.py:67
  84.1 1.6 %collective-permute-done.3 = bf16[2112,128]{1,0:T(8,128)(2,1)S(1)} collective-permute-done((bf16[2112,128]{1,0:T(8,128)(2,1)S(1)}, bf16[2112,128]{1,0:T(8,128)(2,1)S(1)}, u32[]{:S(2)}, u32[]{:S(2)}) %collective-permute-start.3) | collective-permute-done | bytes 540704 | tf_op jit(solution)/shard_map/pair_sum/ppermute | solution.py:67
  85.6 0.1 add_convert_fusion
  85.9 22.2 %all_to_all.32 = bf16[16,144,128]{2,1,0:T(8,128)(2,1)S(1)} all-to-all(bf16[16,144,128]{2,1,0:T(8,128)(2,1)S(1)} %pad_maximum_fusion), channel_id=1, replica_groups={{0,16,32,48,64,80,96,112,128,144,160,176,192,208,224,240},{8,24,40,56,7..., dimensions={0} | all-to-all | bytes 1179648 | tf_op jit(solution)/shard_map/sum_over_section/all_to_all | solution.py:71
  108.0 0.1 reduce_sum.25
  108.2 12.9 %all_to_all.33 = bf16[8,144,128]{2,1,0:T(8,128)(2,1)S(1)} all-to-all(bf16[8,144,128]{2,1,0:T(8,128)(2,1)S(1)} %broadcast_in_dim.40), channel_id=1, replica_groups=mesh['section'=32,'rep'=8] {'rep'}, dimensions={0} | all-to-all | bytes 589824 | tf_op jit(solution)/shard_map/gather_sums/all_to_all | solution.py:71
  121.2 16.3 %all_to_all.34.results_ref = bf16[8,256,128]{2,1,0:T(8,128)(2,1)S(1)} all-to-all(bf16[8,256,128]{2,1,0:T(8,128)(2,1)S(1)} %pad_maximum_fusion.1), channel_id=1, replica_groups={{0,8,16,24,32,40,48,56},{64,72,80,88,96,104,112,120},{128,136,144,152,1..., dimensions={0} | all-to-all | bytes 1048576 | tf_op jit(solution)/shard_map/return_panels/all_to_all | solution.py:71
  137.5 1.2 shard_map.123
  (12 shorter events, 0.3 us)
Async XLA Ops:
  1.6 13.6 %collective-permute-start = (bf16[128,256]{1,0:T(8,128)(2,1)S(1)}, bf16[128,256]{1,0:T(8,128)(2,1)S(1)}, u32[]{:S(2)}, u32[]{:S(2)}) collective-permute-start(bf16[128,256]{1,0:T(8,128)(2,1)S(1)} %dynamic-slice_bitcast_fusion), channel_id=1, source_target_pairs={{0,32},{1,16},{2,0},{3,48},{8,57},{9,41},{10,25},{11,9},{16,18},{1... | collective-permute-start | bytes 196616 | tf_op jit(solution)/shard_map/spread_features/ppermute | solution.py:251
  15.2 3.1 %collective-permute-start.1 = (bf16[128,128]{1,0:T(8,128)(2,1)S(1)}, bf16[128,128]{1,0:T(8,128)(2,1)S(1)}, u32[]{:S(2)}, u32[]{:S(2)}) collective-permute-start(bf16[128,128]{1,0:T(8,128)(2,1)S(1)} %broadcast_select_fusion), channel_id=1, source_target_pairs={{0,8},{9,1},{2,10},{11,3},{4,12},{13,5},{6,14},{15,7},{16,24},{25,... | collective-permute-start | bytes 98312 | tf_op jit(solution)/shard_map/split_features/ppermute | solution.py:260
  39.2 3.5 %collective-permute-start.2 = (bf16[2048,128]{1,0:T(8,128)(2,1)S(1)}, bf16[2048,128]{1,0:T(8,128)(2,1)S(1)}, u32[]{:S(2)}, u32[]{:S(2)}) collective-permute-start(bf16[2048,128]{1,0:T(8,128)(2,1)S(1)} %bitcast.19), channel_id=1, source_target_pairs={{0,8},{8,0},{16,24},{24,16},{32,40},{40,32},{48,56},{56,48},{64,72... | collective-permute-start | bytes 1572872 | tf_op jit(solution)/shard_map/gather_features/ppermute | solution.py:67
  42.7 1.6 %copy-start.1 = (bf16[512,2048]{1,0:T(8,128)(2,1)S(1)}, bf16[512,2048]{1,0:T(8,128)(2,1)}, u32[]{:S(2)}) copy-start(bf16[512,2048]{1,0:T(8,128)(2,1)} %get-tuple-element.19.dense_ref) | copy-start | bytes 6291460
  45.8 27.4 %copy-start.3 = (bf16[512,256]{1,0:T(8,128)(2,1)S(1)}, bf16[512,256]{1,0:T(8,128)(2,1)}, u32[]{:S(2)}) copy-start(bf16[512,256]{1,0:T(8,128)(2,1)} %features_ref.1) | copy-start | bytes 786436
  54.5 18.7 %copy-start = (bf16[2048,512]{1,0:T(8,128)(2,1)S(1)}, bf16[2048,512]{1,0:T(8,128)(2,1)}, u32[]{:S(2)}) copy-start(bf16[2048,512]{1,0:T(8,128)(2,1)} %get-tuple-element.22.flipped_ref) | copy-start | bytes 6291460
  54.5 18.7 %copy-start.2 = (bf16[256,256]{1,0:T(8,128)(2,1)S(1)}, bf16[256,256]{1,0:T(8,128)(2,1)}, u32[]{:S(2)}) copy-start(bf16[256,256]{1,0:T(8,128)(2,1)} %w_self_ref.3) | copy-start | bytes 393220
  55.4 17.8 %all-to-all-start.2 = ((bf16[8,128,256]{2,1,0:T(8,128)(2,1)}), bf16[8,128,256]{2,1,0:T(8,128)(2,1)S(1)}, u32[]{:S(2)}, u32[]{:S(2)}) async-start(bf16[8,128,256]{2,1,0:T(8,128)(2,1)} %broadcast_in_dim.18), calls=%async_computation.2 | async-start | bytes 1048576 | tf_op jit(solution)/shard_map/gather_over_rep/all_to_all | solution.py:71
  73.2 1.0 copy-start.4
  74.1 0.9 copy-start.5
  77.0 8.7 %collective-permute-start.3 = (bf16[2112,128]{1,0:T(8,128)(2,1)S(1)}, bf16[2112,128]{1,0:T(8,128)(2,1)S(1)}, u32[]{:S(2)}, u32[]{:S(2)}) collective-permute-start(bf16[2112,128]{1,0:T(8,128)(2,1)S(1)} %get-tuple-element.25), channel_id=1, source_target_pairs={{0,8},{8,0},{16,24},{24,16},{32,40},{40,32},{48,56},{56,48},{64,72... | collective-permute-start | bytes 1622024 | tf_op jit(solution)/shard_map/pair_sum/ppermute | solution.py:67

commit v4 on v3

v4 whole, which is shorter than its diff:
```python
import jax
import jax.numpy as jnp
from jax import lax
from jax.experimental import pallas as pl
from jax.experimental.pallas import tpu as pltpu
from jax.sharding import PartitionSpec as P

BLOCK = 128
HALF = 64
F32 = jnp.float32
BF16 = jnp.bfloat16
ROWS_T = (((1,), (1,)), ((), ()))
COLS_T = (((0,), (0,)), ((), ()))
SMEM = pl.BlockSpec(memory_space=pltpu.SMEM)
VMEM = pl.BlockSpec(memory_space=pltpu.VMEM)

CORE_PAIRS = [(s, s ^ 1) for s in range(32)]
HALF_PAIRS = [(r, r ^ 4) for r in range(8)]
Z_PAIRS = [(s, s ^ 16) for s in range(32)]
SAME_CORE = [[2 * i + core for i in range(16)] for core in range(2)]
SAME_XC = [[8 * z + i for z in range(4)] for i in range(8)]
SAME_ZC = [[8 * z + 2 * x + core for x in range(4)] for z in range(4) for core in range(2)]
SAME_Z = [[8 * z + i for i in range(8)] for z in range(4)]
SAME_H = [[4 * h + i for i in range(4)] for h in range(2)]


def other_end(x_home, y_column, place):
    return (x_home + y_column + 2 - place) % 4


def out_pairs(core_to):
    pairs = []
    for z in range(4):
        for x in range(4):
            for core in range(2):
                h, y_column = x // 2, (x % 2) * 2 + core
                for y in range(4):
                    source = (8 * z + 2 * x + core) * 8 + 4 * h + y
                    x_to = other_end(x, y_column, y)
                    target = (8 * (z ^ core_to) + 2 * x_to + core_to) * 8 + 4 * h + y_column
                    pairs.append((source, target))
    return pairs


def swap_core(x):
    return lax.ppermute(x, "section", CORE_PAIRS)


def exchange(x, axis, groups=None):
    return lax.all_to_all(x, axis, 0, 0, tiled=False, axis_index_groups=groups)


def spread(x, count):
    return jnp.broadcast_to(x[None], (count, *x.shape))


def add_up(terms):
    parts = [terms[i].astype(F32) for i in range(terms.shape[0])]
    while len(parts) > 1:
        parts = [parts[i] + parts[i + 1] for i in range(0, len(parts), 2)]
    return parts[0].astype(BF16)


def densify_kernel(rows_ref, cols_ref, count_ref, blocks_ref, dense_ref, flipped_ref, total):
    total[...] = jnp.zeros_like(total)

    def add_slot(slot, carry):
        total[rows_ref[slot], cols_ref[slot]] += blocks_ref[slot].astype(F32)
        return carry

    lax.fori_loop(0, count_ref[0, 0], add_slot, 0)
    for i in range(4):
        for j in range(16):
            tile = total[i, j]
            rows, cols = pl.ds(i * BLOCK, BLOCK), pl.ds(j * BLOCK, BLOCK)
            dense_ref[rows, cols] = tile.astype(BF16)
            flipped_ref[cols, rows] = tile.T.astype(BF16)


def densify(tiles, rows, cols, count):
    return pl.pallas_call(
        densify_kernel,
        out_shape=(
            jax.ShapeDtypeStruct((512, 2048), BF16),
            jax.ShapeDtypeStruct((2048, 512), BF16),
        ),
        in_specs=[SMEM, SMEM, SMEM, VMEM],
        out_specs=(VMEM, VMEM),
        scratch_shapes=[pltpu.VMEM((4, 16, BLOCK, BLOCK), F32)],
        compiler_params=pltpu.CompilerParams(vmem_limit_bytes=20 * 1024 * 1024),
        cost_estimate=pl.CostEstimate(flops=2**22, bytes_accessed=12 * 2**20, transcendentals=0),
    )(rows, cols, count, tiles)


def forward_kernel(scalars_ref, dense_ref, own_ref, other_ref, out_ref, columns):
    panel = scalars_ref[2]
    for x in range(4):
        for pair in range(2):
            place = (2 * x + pair) * BLOCK
            own_start = (panel ^ (2 * pair)) * 512 + x * BLOCK
            other_start = (panel ^ (2 * pair) ^ 1) * 512 + x * BLOCK
            columns[pl.ds(pl.multiple_of(own_start, BLOCK), BLOCK), :] = own_ref[
                place : place + BLOCK, :
            ]
            columns[pl.ds(pl.multiple_of(other_start, BLOCK), BLOCK), :] = other_ref[
                place : place + BLOCK, :
            ]
    out_ref[...] = jnp.dot(dense_ref[...], columns[...], preferred_element_type=F32).astype(BF16)


def forward_product(scalars, dense, own, other):
    return pl.pallas_call(
        forward_kernel,
        out_shape=jax.ShapeDtypeStruct((512, 256), BF16),
        in_specs=[SMEM, VMEM, VMEM, VMEM],
        out_specs=VMEM,
        scratch_shapes=[pltpu.VMEM((2048, 256), BF16)],
        compiler_params=pltpu.CompilerParams(vmem_limit_bytes=16 * 1024 * 1024),
    )(scalars, dense, own, other)


def middle_kernel(
    scalars_ref,
    pieces_ref,
    degrees_ref,
    features_ref,
    cotangent_ref,
    w_self_ref,
    w_neigh_ref,
    flipped_ref,
    activated_ref,
    pre_grad_ref,
    own_ref,
    other_ref,
    inputs,
    divisor,
    down,
    slices,
):
    first = scalars_ref[0] == 0
    rep = scalars_ref[1]
    degree_rows = degrees_ref[...].astype(F32)
    for i in range(4):
        turned = jnp.broadcast_to(degree_rows[i : i + 1, :], (BLOCK, BLOCK)).T
        divisor[i * BLOCK : (i + 1) * BLOCK, :BLOCK] = turned
        divisor[i * BLOCK : (i + 1) * BLOCK, BLOCK:] = turned
    mean_input = (pieces_ref[...].astype(F32) / divisor[...]).astype(BF16)
    features = features_ref[...]
    inputs[:, :256] = features
    inputs[:, 256:] = mean_input
    preact = jnp.dot(features, w_self_ref[...], preferred_element_type=F32) + jnp.dot(
        mean_input, w_neigh_ref[...], preferred_element_type=F32
    )
    sigmoid_value = jax.nn.sigmoid(preact)
    activated_ref[...] = (preact * sigmoid_value).astype(BF16)
    slope_value = sigmoid_value * (1.0 + preact * (1.0 - sigmoid_value))
    pre_grad = (cotangent_ref[...].astype(F32) * slope_value).astype(BF16)
    pre_grad_ref[...] = pre_grad
    down[...] = (
        lax.dot_general(pre_grad, w_neigh_ref[...], ROWS_T, preferred_element_type=F32)
        / divisor[...]
    ).astype(BF16)
    for i in range(8):
        term = jnp.dot(
            flipped_ref[i * 256 : (i + 1) * 256, :], down[...], preferred_element_type=F32
        )
        for part in range(2):
            rows = pl.ds((2 * i + part) * HALF, HALF)
            top = term[part * BLOCK : part * BLOCK + HALF]
            bottom = term[part * BLOCK + HALF : (part + 1) * BLOCK]
            own_ref[rows, :] = jnp.where(first, top, bottom)
            other_ref[rows, :] = jnp.where(first, bottom, top).astype(BF16)
    pair_start = pl.multiple_of(rep // 2 * BLOCK, BLOCK)
    slices[...] = lax.dot_general(
        inputs[:, pl.ds(pair_start, BLOCK)], pre_grad, COLS_T, preferred_element_type=F32
    )
    mine = slices[pl.ds(pl.multiple_of(rep % 2 * HALF, HALF), HALF), :].reshape(4, 2, 8, 256)
    top, bottom = mine[:, 0].reshape(32, 256), mine[:, 1].reshape(32, 256)
    own_ref[1024:, :] = jnp.where(first, top, bottom)
    other_ref[1024:, :] = jnp.where(first, bottom, top).astype(BF16)


def middle(scalars, pieces, degrees, features, cotangent, w_self, w_neigh, flipped):
    return pl.pallas_call(
        middle_kernel,
        out_shape=(
            jax.ShapeDtypeStruct((512, 256), BF16),
            jax.ShapeDtypeStruct((512, 256), BF16),
            jax.ShapeDtypeStruct((1056, 256), F32),
            jax.ShapeDtypeStruct((1056, 256), BF16),
        ),
        in_specs=[SMEM] + [VMEM] * 7,
        out_specs=(VMEM,) * 4,
        scratch_shapes=[
            pltpu.VMEM((512, 512), BF16),
            pltpu.VMEM((512, 256), F32),
            pltpu.VMEM((512, 256), BF16),
            pltpu.VMEM((BLOCK, 256), F32),
        ],
        compiler_params=pltpu.CompilerParams(vmem_limit_bytes=24 * 1024 * 1024),
    )(scalars, pieces, degrees, features, cotangent, w_self, w_neigh, flipped)


def finish_kernel(results_ref, pre_grad_ref, w_self_ref, feature_ref, self_ref, neigh_ref):
    self_part = lax.dot_general(
        pre_grad_ref[...], w_self_ref[...], ROWS_T, preferred_element_type=F32
    )
    for place in range(8):
        rows = pl.ds(place * HALF, HALF)
        arrived = results_ref[place].astype(F32)
        feature_ref[rows, :] = self_part[place * HALF : (place + 1) * HALF] + arrived[:HALF]
        for part in range(8):
            target = self_ref if part < 4 else neigh_ref
            start = HALF + part * 8
            target[pl.ds(part % 4 * HALF + place * 8, 8), :] = arrived[start : start + 8]


def finish(results, pre_grad, w_self):
    return pl.pallas_call(
        finish_kernel,
        out_shape=(
            jax.ShapeDtypeStruct((512, 256), F32),
            jax.ShapeDtypeStruct((256, 256), F32),
            jax.ShapeDtypeStruct((256, 256), F32),
        ),
        in_specs=[VMEM] * 3,
        out_specs=(VMEM,) * 3,
        compiler_params=pltpu.CompilerParams(vmem_limit_bytes=16 * 1024 * 1024),
    )(results, pre_grad, w_self)


def body(
    features, cotangent, degrees, blocks, block_rows, block_cols, block_count, w_self, w_neigh
):
    section = lax.axis_index("section")
    rep = lax.axis_index("rep")
    z, x, core = section // 8, (section // 2) % 4, section % 2
    scalars = jnp.stack([core, rep, z ^ core]).astype(jnp.int32)
    with jax.named_scope("spread_features"):
        place = other_end(x, (x % 2) * 2 + core, rep % 4)
        block = lax.dynamic_index_in_dim(
            features.reshape(4, BLOCK, 256), place, 0, keepdims=False
        )
        arrived = [lax.ppermute(block, ("section", "rep"), out_pairs(c)) for c in range(2)]
        block = jnp.where(core == 0, arrived[0], arrived[1])
    with jax.named_scope("gather_features"):
        pair = jnp.stack([block, lax.ppermute(block, "section", Z_PAIRS)])
        own_columns = exchange(spread(pair, 4), "section", SAME_ZC).reshape(1024, 256)
        own_columns, count = lax.optimization_barrier((own_columns, block_count))
        other_columns = swap_core(own_columns)
    dense, flipped = densify(blocks[0, 0], block_rows[0, 0], block_cols[0, 0], count)
    partial = forward_product(scalars, dense, own_columns, other_columns)
    with jax.named_scope("sum_over_y"):
        partial = add_up(exchange(partial.reshape(4, BLOCK, 256), "rep", SAME_H))
    with jax.named_scope("sum_over_h"):
        partial = add_up(jnp.stack([partial, lax.ppermute(partial, "rep", HALF_PAIRS)]))
    with jax.named_scope("gather_over_y"):
        pieces = exchange(spread(partial, 4), "rep", SAME_H)
    activated, pre_grad, own, other = middle(
        scalars,
        pieces.reshape(512, 256),
        degrees.reshape(4, BLOCK),
        features,
        cotangent,
        w_self,
        w_neigh,
        flipped,
    )
    with jax.named_scope("pair_sum"):
        both = (own + swap_core(other).astype(F32)).astype(BF16)
        main = both[:1024].reshape(4, 4, HALF, 256).transpose(1, 0, 2, 3).reshape(4, 256, 256)
        send = jnp.concatenate([main, both[1024:].reshape(4, 8, 256)], axis=1)
    with jax.named_scope("sum_over_section"):
        send = add_up(exchange(send, "section", SAME_ZC))
        send = jnp.concatenate([send[:256].reshape(4, HALF, 256), spread(send[256:], 4)], axis=1)
        total = add_up(exchange(send, "section", SAME_XC))
        arrived = lax.ppermute(total, "rep", HALF_PAIRS)
        first = rep < 4
        total = jnp.stack([jnp.where(first, total, arrived), jnp.where(first, arrived, total)])
    with jax.named_scope("gather_sums"):
        sums = exchange(spread(total, 4), "rep", SAME_H)
        sums = sums.transpose(1, 0, 2, 3).reshape(8, 72, 256)
    with jax.named_scope("return_panels"):
        grad_rows = spread(sums[:, HALF:].reshape(HALF, 256), 8)
        results = exchange(
            jnp.concatenate([sums[:, :HALF], grad_rows], axis=1), "section", SAME_Z
        )
    feature_grad, grad_self, grad_neigh = finish(results, pre_grad, w_self)
    return (activated, feature_grad, grad_self, grad_neigh)


def solution(mesh):
    return jax.shard_map(
        body,
        mesh=mesh,
        in_specs=(
            P("section", None),
            P("section", None),
            P("section"),
            P("section", "rep", None, None, None),
            P("section", "rep", None),
            P("section", "rep", None),
            P("section", "rep"),
            P(),
            P(),
        ),
        out_specs=(P("section", None), P("section", None), P(), P()),
        check_vma=False,
    )
```

time: 139 us -> 125 us (0.90)
  starting transfers between devices: 23.2 us -> 31.9 us
  waiting for transfers between devices: 15.8 us -> 8.55 us
  blocking collectives: 80.8 us -> 74.5 us
  local copies, waits for them, and re-layouts: 5.51 us -> 1.14 us
  Pallas kernels: 9.41 us -> 6.19 us
  other arithmetic: 2.35 us -> 0.57 us
    ppermute x2 -> x5, starting transfers between devices: 7.51 us -> 23.4 us  [the longest x2 8.86 us: body(): lax.ppermute(block, ('section', 'rep'), out_pairs(c))]
    all_to_all x1 -> x0, waiting for transfers between devices: 11 us -> none  [exchange(): return lax.all_to_all(x, axis, 0, 0, tiled=False, axis_index_groups=groups)]
    all_to_all x1 -> x0, starting transfers between devices: 6.63 us -> none  [exchange(): return lax.all_to_all(x, axis, 0, 0, tiled=False, axis_index_groups=groups)]
    all_to_all x5 -> x7, blocking collectives: 80.8 us -> 74.5 us  [exchange(): return lax.all_to_all(x, axis, 0, 0, tiled=False, axis_index_groups=groups)]
    ppermute x2 -> x5, waiting for transfers between devices: 1.78 us -> 6.99 us  [the longest x1 2.36 us: body(): pair = jnp.stack([block, lax.ppermute(block, 'section', Z_PAIRS)])]
    unnamed x12 -> x16, local copies, waits for them, and re-layouts: 3.45 us -> 0.05 us
    pallas_call x1, Pallas kernels: 4.81 us -> 1.76 us  [densify(): pl.pallas_call(densify_kernel, out_shape=(jax.ShapeDtypeStruct((512, 2048...]
    ppermute x2, waiting for transfers between devices: 3.02 us -> 1.56 us  [swap_core(): return lax.ppermute(x, 'section', CORE_PAIRS)]
  transfers between devices with their start and end apart: 5 -> 7, of which waited for: 4 -> 6; matrix products, arithmetic and copies ran while one was open for 2% -> 0% of each run, Pallas kernels for 3% -> 1%
where the time goes in v4:
time: 125 us
  blocking collectives  74.5 us (60%)
  starting transfers between devices  31.9 us (26%)
  waiting for transfers between devices  8.55 us (7%)
  Pallas kernels  6.19 us (5%)
  between operations  1.68 us (1%)
    all_to_all x7, blocking collectives, exchange(): return lax.all_to_all(x, axis, 0, 0, tiled=False, axis_index_groups=groups)  74.5 us
    ppermute x2, starting transfers between devices, body(): lax.ppermute(block, ('section', 'rep'), out_pairs(c))  8.86 us
    ppermute x2, starting transfers between devices, swap_core(): return lax.ppermute(x, 'section', CORE_PAIRS)  8.55 us
    ppermute x1, starting transfers between devices, body(): lax.ppermute(partial, 'rep', HALF_PAIRS)  6.23 us
    ppermute x1, starting transfers between devices, body(): arrived = lax.ppermute(total, 'rep', HALF_PAIRS)  5.2 us
    ppermute x1, starting transfers between devices, body(): pair = jnp.stack([block, lax.ppermute(block, 'section', Z_PAIRS)])  3.08 us
  transfers between devices with their start and end apart: 7, of which 6 were waited for; matrix products, arithmetic and copies ran while one was open for 0% of the time, Pallas kernels for 1%

profile of v4, /device:TPU:1, one launch (start us, length us, event | category | flops | bytes accessed | tf_op | source)
XLA Modules:
  0.0 124.5 jit_solution(6911917557773051495)
XLA Ops:
  0.7 0.8 dynamic-slice_bitcast_fusion
  1.6 7.6 %collective-permute-start.1 = (bf16[128,256]{1,0:T(8,128)(2,1)S(1)}, bf16[128,256]{1,0:T(8,128)(2,1)S(1)}, u32[]{:S(2)}, u32[]{:S(2)}) collective-permute-start(bf16[128,256]{1,0:T(8,128)(2,1)S(1)} %dynamic-slice_bitcast_fusion), channel_id=1, source_target_pairs={{0,104},{1,88},{2,72},{3,120},{8,121},{9,105},{10,89},{11,73},{16,... | collective-permute-start | bytes 196616 | tf_op jit(solution)/shard_map/spread_features/ppermute | solution.py:244
  9.1 1.3 %collective-permute-start = (bf16[128,256]{1,0:T(8,128)(2,1)S(1)}, bf16[128,256]{1,0:T(8,128)(2,1)S(1)}, u32[]{:S(2)}, u32[]{:S(2)}) collective-permute-start(bf16[128,256]{1,0:T(8,128)(2,1)S(1)} %dynamic-slice_bitcast_fusion), channel_id=1, source_target_pairs={{0,32},{1,16},{2,0},{3,48},{8,49},{9,33},{10,17},{11,1},{16,18},{1... | collective-permute-start | bytes 196616 | tf_op jit(solution)/shard_map/spread_features/ppermute | solution.py:244
  10.4 0.0 copy-start
  10.5 0.0 copy-start.6
  10.5 0.0 copy-start.7
  10.5 0.4 collective-permute-done.1
  10.9 0.9 collective-permute-done
  11.8 3.1 %collective-permute-start.2 = (bf16[128,256]{1,0:T(8,128)(2,1)S(1)}, bf16[128,256]{1,0:T(8,128)(2,1)S(1)}, u32[]{:S(2)}, u32[]{:S(2)}) collective-permute-start(bf16[128,256]{1,0:T(8,128)(2,1)S(1)} %broadcast_select_fusion), channel_id=1, source_target_pairs={{0,128},{8,136},{16,144},{24,152},{32,160},{40,168},{48,176},{56,1... | collective-permute-start | bytes 196616 | tf_op jit(solution)/shard_map/gather_features/ppermute | solution.py:247
  14.8 2.4 %collective-permute-done.2 = bf16[128,256]{1,0:T(8,128)(2,1)S(1)} collective-permute-done((bf16[128,256]{1,0:T(8,128)(2,1)S(1)}, bf16[128,256]{1,0:T(8,128)(2,1)S(1)}, u32[]{:S(2)}, u32[]{:S(2)}) %collective-permute-start.2) | collective-permute-done | bytes 65568 | tf_op jit(solution)/shard_map/gather_features/ppermute | solution.py:247
  17.3 10.6 %all_to_all.35 = bf16[4,2,128,256]{3,2,1,0:T(8,128)(2,1)S(1)} all-to-all(bf16[4,2,128,256]{3,2,1,0:T(8,128)(2,1)S(1)} %broadcast_in_dim.12), channel_id=1, replica_groups={{0,16,32,48},{8,24,40,56},{64,80,96,112},{72,88,104,120},{128,144,160,1..., dimensions={0} | all-to-all | bytes 1048576 | tf_op jit(solution)/shard_map/gather_features/all_to_all | solution.py:50
  27.9 5.1 %collective-permute-start.3 = (bf16[1024,256]{1,0:T(8,128)(2,1)S(1)}, bf16[1024,256]{1,0:T(8,128)(2,1)S(1)}, u32[]{:S(2)}, u32[]{:S(2)}) collective-permute-start(bf16[1024,256]{1,0:T(8,128)(2,1)S(1)} %bitcast.40), channel_id=1, source_target_pairs={{0,8},{8,0},{16,24},{24,16},{32,40},{40,32},{48,56},{56,48},{64,72... | collective-permute-start | bytes 1572872 | tf_op jit(solution)/shard_map/gather_features/ppermute | solution.py:46
  33.6 0.0 copy-done
  33.7 0.0 copy-done.6
  33.7 0.0 copy-done.7
  33.7 1.8 %shard_map.120 = (bf16[512,2048]{1,0:T(8,128)(2,1)S(1)}, bf16[2048,512]{1,0:T(8,128)(2,1)S(1)}) custom-call(s32[48]{0:T(128)S(1)} %bitcast.47, s32[48]{0:T(128)S(1)} %bitcast.48, s32[1,1]{1,0:T(1,128)S(6)} %copy.16.count_ref, bf16[48,128,128]{2,1,0:T(8,128)(2,1)S(1)} %bitcast.42), custom_call_target="tpu_custom_call" | custom-call | flops 4194304 | bytes 12582912 | tf_op jit(solution)/shard_map/pallas_call | solution.py:81
  35.4 0.1 pad_add_fusion.scalars_ref
  35.5 0.0 collective-permute-done.3.other_ref
  35.5 1.3 %shard_map.121 = bf16[512,256]{1,0:T(8,128)(2,1)S(1)} custom-call(s32[3]{0:T(128)S(1)} %pad_add_fusion.scalars_ref, bf16[512,2048]{1,0:T(8,128)(2,1)S(1)} %get-tuple-element.16.dense_ref, bf16[1024,256]{1,0:T(8,128)(2,1)S(1)} %bitcast.41, bf16[1024,256]{1,0:T(8,128)(2,1)S(1)} %collective-permute-done.3.other_ref), custom_call_target="tpu_custom_call" | custom-call | tf_op jit(solution)/shard_map/pallas_call | solution.py:112
  36.9 0.0 copy-start.1
  36.9 0.0 copy-start.2
  36.9 0.0 copy-start.3
  36.9 0.0 copy-start.4
  36.9 0.0 copy-start.5
  36.9 9.8 %all_to_all.36 = bf16[4,128,256]{2,1,0:T(8,128)(2,1)S(1)} all-to-all(bf16[4,128,256]{2,1,0:T(8,128)(2,1)S(1)} %bitcast.44), channel_id=1, replica_groups={{0,1,2,3},{4,5,6,7},{8,9,10,11},{12,13,14,15},{16,17,18,19},{20,21,22,2..., dimensions={0} | all-to-all | bytes 524288 | tf_op jit(solution)/shard_map/sum_over_y/all_to_all | solution.py:50
  46.8 6.2 %collective-permute-start.4 = (bf16[128,256]{1,0:T(8,128)(2,1)S(1)}, bf16[128,256]{1,0:T(8,128)(2,1)S(1)}, u32[]{:S(2)}, u32[]{:S(2)}) collective-permute-start(bf16[128,256]{1,0:T(8,128)(2,1)S(1)} %fusion), channel_id=1, source_target_pairs={{0,4},{1,5},{2,6},{3,7},{4,0},{5,1},{6,2},{7,3},{8,12},{9,13},{10,... | collective-permute-start | bytes 196616 | tf_op jit(solution)/shard_map/sum_over_h/ppermute | solution.py:256
  53.0 1.8 %collective-permute-done.4 = bf16[128,256]{1,0:T(8,128)(2,1)S(1)} collective-permute-done((bf16[128,256]{1,0:T(8,128)(2,1)S(1)}, bf16[128,256]{1,0:T(8,128)(2,1)S(1)}, u32[]{:S(2)}, u32[]{:S(2)}) %collective-permute-start.4) | collective-permute-done | bytes 65568 | tf_op jit(solution)/shard_map/sum_over_h/ppermute | solution.py:256
  54.9 7.9 %all_to_all.37 = bf16[4,128,256]{2,1,0:T(8,128)(2,1)S(1)} all-to-all(bf16[4,128,256]{2,1,0:T(8,128)(2,1)S(1)} %broadcast_in_dim.13), channel_id=1, replica_groups={{0,1,2,3},{4,5,6,7},{8,9,10,11},{12,13,14,15},{16,17,18,19},{20,21,22,2..., dimensions={0} | all-to-all | bytes 524288 | tf_op jit(solution)/shard_map/gather_over_y/all_to_all | solution.py:50
  62.8 0.0 copy-done.1
  62.8 0.0 copy-done.2
  62.8 0.0 copy-done.3
  62.8 0.0 copy-done.4
  62.8 0.0 copy-done.5
  62.8 1.9 %shard_map.122 = (bf16[512,256]{1,0:T(8,128)(2,1)}, bf16[512,256]{1,0:T(8,128)(2,1)S(1)}, f32[1056,256]{1,0:T(8,128)S(1)}, bf16[1056,256]{1,0:T(8,128)(2,1)S(1)}) custom-call(s32[3]{0:T(128)S(1)} %pad_add_fusion.scalars_ref, bf16[512,256]{1,0:T(8,128)(2,1)S(1)} %bitcast.43, s32[4,128]{1,0:T(4,128)S(1)} %bitcast.46, bf16[512,256]{1,0:T(8,128)(2,1)S(1)} %copy-done.2, ...), custom_call_target="tpu_custom_call" | custom-call | tf_op jit(solution)/shard_map/pallas_call | solution.py:184
  64.8 3.4 %collective-permute-start.5 = (bf16[1056,256]{1,0:T(8,128)(2,1)S(1)}, bf16[1056,256]{1,0:T(8,128)(2,1)S(1)}, u32[]{:S(2)}, u32[]{:S(2)}) collective-permute-start(bf16[1056,256]{1,0:T(8,128)(2,1)S(1)} %get-tuple-element.21), channel_id=1, source_target_pairs={{0,8},{8,0},{16,24},{24,16},{32,40},{40,32},{48,56},{56,48},{64,72... | collective-permute-start | bytes 1622024 | tf_op jit(solution)/shard_map/pair_sum/ppermute | solution.py:46
  68.2 1.6 %collective-permute-done.5 = bf16[1056,256]{1,0:T(8,128)(2,1)S(1)} collective-permute-done((bf16[1056,256]{1,0:T(8,128)(2,1)S(1)}, bf16[1056,256]{1,0:T(8,128)(2,1)S(1)}, u32[]{:S(2)}, u32[]{:S(2)}) %collective-permute-start.5) | collective-permute-done | bytes 540704 | tf_op jit(solution)/shard_map/pair_sum/ppermute | solution.py:46
  69.7 0.2 add_convert_fusion
  70.1 11.6 %all_to_all.38 = bf16[4,264,256]{2,1,0:T(8,128)(2,1)S(1)} all-to-all(bf16[4,264,256]{2,1,0:T(8,128)(2,1)S(1)} %pad_maximum_fusion), channel_id=1, replica_groups={{0,16,32,48},{8,24,40,56},{64,80,96,112},{72,88,104,120},{128,144,160,1..., dimensions={0} | all-to-all | bytes 1081344 | tf_op jit(solution)/shard_map/sum_over_section/all_to_all | solution.py:50
  81.6 0.1 add_convert_fusion.1
  81.8 9.3 %all_to_all.39 = bf16[4,72,256]{2,1,0:T(8,128)(2,1)S(1)} all-to-all(bf16[4,72,256]{2,1,0:T(8,128)(2,1)S(1)} %pad_maximum_fusion.2), channel_id=1, replica_groups={{0,64,128,192},{8,72,136,200},{16,80,144,208},{24,88,152,216},{32,96,16..., dimensions={0} | all-to-all | bytes 294912 | tf_op jit(solution)/shard_map/sum_over_section/all_to_all | solution.py:50
  91.1 5.2 %collective-permute-start.6 = (bf16[72,256]{1,0:T(8,128)(2,1)S(1)}, bf16[72,256]{1,0:T(8,128)(2,1)S(1)}, u32[]{:S(2)}, u32[]{:S(2)}) collective-permute-start(bf16[72,256]{1,0:T(8,128)(2,1)S(1)} %fusion.1), channel_id=1, source_target_pairs={{0,4},{1,5},{2,6},{3,7},{4,0},{5,1},{6,2},{7,3},{8,12},{9,13},{10,... | collective-permute-start | bytes 110600 | tf_op jit(solution)/shard_map/sum_over_section/ppermute | solution.py:277
  96.2 1.6 %collective-permute-done.6 = bf16[72,256]{1,0:T(8,128)(2,1)S(1)} collective-permute-done((bf16[72,256]{1,0:T(8,128)(2,1)S(1)}, bf16[72,256]{1,0:T(8,128)(2,1)S(1)}, u32[]{:S(2)}, u32[]{:S(2)}) %collective-permute-start.6) | collective-permute-done | bytes 36896 | tf_op jit(solution)/shard_map/sum_over_section/ppermute | solution.py:277
  97.9 8.1 %all_to_all.40 = bf16[4,2,72,256]{3,2,1,0:T(8,128)(2,1)S(1)} all-to-all(bf16[4,2,72,256]{3,2,1,0:T(8,128)(2,1)S(1)} %broadcast_in_dim.15), channel_id=1, replica_groups={{0,1,2,3},{4,5,6,7},{8,9,10,11},{12,13,14,15},{16,17,18,19},{20,21,22,2..., dimensions={0} | all-to-all | bytes 589824 | tf_op jit(solution)/shard_map/gather_sums/all_to_all | solution.py:50
  106.1 17.3 %all_to_all.41.results_ref = bf16[8,128,256]{2,1,0:T(8,128)(2,1)S(1)} all-to-all(bf16[8,128,256]{2,1,0:T(8,128)(2,1)S(1)} %pad_maximum_fusion.1), channel_id=1, replica_groups={{0,8,16,24,32,40,48,56},{64,72,80,88,96,104,112,120},{128,136,144,152,1..., dimensions={0} | all-to-all | bytes 1048576 | tf_op jit(solution)/shard_map/return_panels/all_to_all | solution.py:50
  123.4 1.2 shard_map.123
  (23 shorter events, 0.5 us)
Async XLA Ops:
  1.6 9.3 %collective-permute-start.1 = (bf16[128,256]{1,0:T(8,128)(2,1)S(1)}, bf16[128,256]{1,0:T(8,128)(2,1)S(1)}, u32[]{:S(2)}, u32[]{:S(2)}) collective-permute-start(bf16[128,256]{1,0:T(8,128)(2,1)S(1)} %dynamic-slice_bitcast_fusion), channel_id=1, source_target_pairs={{0,104},{1,88},{2,72},{3,120},{8,121},{9,105},{10,89},{11,73},{16,... | collective-permute-start | bytes 196616 | tf_op jit(solution)/shard_map/spread_features/ppermute | solution.py:244
  9.1 2.6 %collective-permute-start = (bf16[128,256]{1,0:T(8,128)(2,1)S(1)}, bf16[128,256]{1,0:T(8,128)(2,1)S(1)}, u32[]{:S(2)}, u32[]{:S(2)}) collective-permute-start(bf16[128,256]{1,0:T(8,128)(2,1)S(1)} %dynamic-slice_bitcast_fusion), channel_id=1, source_target_pairs={{0,32},{1,16},{2,0},{3,48},{8,49},{9,33},{10,17},{11,1},{16,18},{1... | collective-permute-start | bytes 196616 | tf_op jit(solution)/shard_map/spread_features/ppermute | solution.py:244
  10.4 23.2 %copy-start = (bf16[1,1,48,128,128]{4,3,2,1,0:T(8,128)(2,1)S(1)}, bf16[1,1,48,128,128]{4,3,2,1,0:T(8,128)(2,1)}, u32[]{:S(2)}) copy-start(bf16[1,1,48,128,128]{4,3,2,1,0:T(8,128)(2,1)} %param.12) | copy-start | bytes 4718596
  10.5 23.2 %copy-start.6 = (s32[1,1,48]{2,1,0:T(1,128)S(1)}, s32[1,1,48]{2,1,0:T(1,128)}, u32[]{:S(2)}) copy-start(s32[1,1,48]{2,1,0:T(1,128)} %param.13) | copy-start | bytes 580
  10.5 23.2 %copy-start.7 = (s32[1,1,48]{2,1,0:T(1,128)S(1)}, s32[1,1,48]{2,1,0:T(1,128)}, u32[]{:S(2)}) copy-start(s32[1,1,48]{2,1,0:T(1,128)} %param.14) | copy-start | bytes 580
  11.8 5.4 %collective-permute-start.2 = (bf16[128,256]{1,0:T(8,128)(2,1)S(1)}, bf16[128,256]{1,0:T(8,128)(2,1)S(1)}, u32[]{:S(2)}, u32[]{:S(2)}) collective-permute-start(bf16[128,256]{1,0:T(8,128)(2,1)S(1)} %broadcast_select_fusion), channel_id=1, source_target_pairs={{0,128},{8,136},{16,144},{24,152},{32,160},{40,168},{48,176},{56,1... | collective-permute-start | bytes 196616 | tf_op jit(solution)/shard_map/gather_features/ppermute | solution.py:247
  27.9 7.7 %collective-permute-start.3 = (bf16[1024,256]{1,0:T(8,128)(2,1)S(1)}, bf16[1024,256]{1,0:T(8,128)(2,1)S(1)}, u32[]{:S(2)}, u32[]{:S(2)}) collective-permute-start(bf16[1024,256]{1,0:T(8,128)(2,1)S(1)} %bitcast.40), channel_id=1, source_target_pairs={{0,8},{8,0},{16,24},{24,16},{32,40},{40,32},{48,56},{56,48},{64,72... | collective-permute-start | bytes 1572872 | tf_op jit(solution)/shard_map/gather_features/ppermute | solution.py:46
  36.9 25.9 %copy-start.1 = (bf16[256,256]{1,0:T(8,128)(2,1)S(1)}, bf16[256,256]{1,0:T(8,128)(2,1)}, u32[]{:S(2)}) copy-start(bf16[256,256]{1,0:T(8,128)(2,1)} %w_self_ref.3) | copy-start | bytes 393220
  36.9 25.9 %copy-start.2 = (bf16[512,256]{1,0:T(8,128)(2,1)S(1)}, bf16[512,256]{1,0:T(8,128)(2,1)}, u32[]{:S(2)}) copy-start(bf16[512,256]{1,0:T(8,128)(2,1)} %features_ref.1) | copy-start | bytes 786436
  36.9 25.9 %copy-start.3 = (bf16[512,256]{1,0:T(8,128)(2,1)S(1)}, bf16[512,256]{1,0:T(8,128)(2,1)}, u32[]{:S(2)}) copy-start(bf16[512,256]{1,0:T(8,128)(2,1)} %cotangent_ref.1) | copy-start | bytes 786436
  36.9 25.9 %copy-start.4 = (bf16[256,256]{1,0:T(8,128)(2,1)S(1)}, bf16[256,256]{1,0:T(8,128)(2,1)}, u32[]{:S(2)}) copy-start(bf16[256,256]{1,0:T(8,128)(2,1)} %w_neigh_ref.1) | copy-start | bytes 393220
  36.9 25.9 %copy-start.5 = (s32[512]{0:T(512)S(1)}, s32[512]{0:T(512)}, u32[]{:S(2)}) copy-start(s32[512]{0:T(512)} %param.11) | copy-start | bytes 6148
  46.8 8.0 %collective-permute-start.4 = (bf16[128,256]{1,0:T(8,128)(2,1)S(1)}, bf16[128,256]{1,0:T(8,128)(2,1)S(1)}, u32[]{:S(2)}, u32[]{:S(2)}) collective-permute-start(bf16[128,256]{1,0:T(8,128)(2,1)S(1)} %fusion), channel_id=1, source_target_pairs={{0,4},{1,5},{2,6},{3,7},{4,0},{5,1},{6,2},{7,3},{8,12},{9,13},{10,... | collective-permute-start | bytes 196616 | tf_op jit(solution)/shard_map/sum_over_h/ppermute | solution.py:256
  64.8 5.0 %collective-permute-start.5 = (bf16[1056,256]{1,0:T(8,128)(2,1)S(1)}, bf16[1056,256]{1,0:T(8,128)(2,1)S(1)}, u32[]{:S(2)}, u32[]{:S(2)}) collective-permute-start(bf16[1056,256]{1,0:T(8,128)(2,1)S(1)} %get-tuple-element.21), channel_id=1, source_target_pairs={{0,8},{8,0},{16,24},{24,16},{32,40},{40,32},{48,56},{56,48},{64,72... | collective-permute-start | bytes 1622024 | tf_op jit(solution)/shard_map/pair_sum/ppermute | solution.py:46
  91.1 6.8 %collective-permute-start.6 = (bf16[72,256]{1,0:T(8,128)(2,1)S(1)}, bf16[72,256]{1,0:T(8,128)(2,1)S(1)}, u32[]{:S(2)}, u32[]{:S(2)}) collective-permute-start(bf16[72,256]{1,0:T(8,128)(2,1)S(1)} %fusion.1), channel_id=1, source_target_pairs={{0,4},{1,5},{2,6},{3,7},{4,0},{5,1},{6,2},{7,3},{8,12},{9,13},{10,... | collective-permute-start | bytes 110600 | tf_op jit(solution)/shard_map/sum_over_section/ppermute | solution.py:277

commit v5 on v4

--- a/solution.py
+++ b/solution.py
@@ -16,11 +16,9 @@
 
 CORE_PAIRS = [(s, s ^ 1) for s in range(32)]
 HALF_PAIRS = [(r, r ^ 4) for r in range(8)]
+NEXT_Z = [(s, s ^ 8) for s in range(32)]
 Z_PAIRS = [(s, s ^ 16) for s in range(32)]
-SAME_CORE = [[2 * i + core for i in range(16)] for core in range(2)]
-SAME_XC = [[8 * z + i for z in range(4)] for i in range(8)]
 SAME_ZC = [[8 * z + 2 * x + core for x in range(4)] for z in range(4) for core in range(2)]
-SAME_Z = [[8 * z + i for i in range(8)] for z in range(4)]
 SAME_H = [[4 * h + i for i in range(4)] for h in range(2)]
 
 
@@ -42,6 +40,21 @@
     return pairs
 
 
+def back_pairs():
+    pairs = []
+    for z in range(4):
+        for x in range(4):
+            for core in range(2):
+                for h in range(2):
+                    for y in range(4):
+                        source = (8 * z + 2 * x + core) * 8 + 4 * h + y
+                        x_home, core_home = 2 * h + y // 2, y % 2
+                        y_to = other_end(x_home, y, x)
+                        target = (8 * z + 2 * x_home + core_home) * 8 + 4 * (core ^ h) + y_to
+                        pairs.append((source, target))
+    return pairs
+
+
 def swap_core(x):
     return lax.ppermute(x, "section", CORE_PAIRS)
 
@@ -61,14 +74,14 @@
     return parts[0].astype(BF16)
 
 
-def densify_kernel(rows_ref, cols_ref, count_ref, blocks_ref, dense_ref, flipped_ref, total):
+def densify_kernel(scalars_ref, rows_ref, cols_ref, blocks_ref, dense_ref, flipped_ref, total):
     total[...] = jnp.zeros_like(total)
 
     def add_slot(slot, carry):
         total[rows_ref[slot], cols_ref[slot]] += blocks_ref[slot].astype(F32)
         return carry
 
-    lax.fori_loop(0, count_ref[0, 0], add_slot, 0)
+    lax.fori_loop(0, scalars_ref[3], add_slot, 0)
     for i in range(4):
         for j in range(16):
             tile = total[i, j]
@@ -77,7 +90,7 @@
             flipped_ref[cols, rows] = tile.T.astype(BF16)
 
 
-def densify(tiles, rows, cols, count):
+def densify(scalars, tiles, rows, cols):
     return pl.pallas_call(
         densify_kernel,
         out_shape=(
@@ -89,7 +102,7 @@
         scratch_shapes=[pltpu.VMEM((4, 16, BLOCK, BLOCK), F32)],
         compiler_params=pltpu.CompilerParams(vmem_limit_bytes=20 * 1024 * 1024),
         cost_estimate=pl.CostEstimate(flops=2**22, bytes_accessed=12 * 2**20, transcendentals=0),
-    )(rows, cols, count, tiles)
+    )(scalars, rows, cols, tiles)
 
 
 def forward_kernel(scalars_ref, dense_ref, own_ref, other_ref, out_ref, columns):
@@ -135,7 +148,6 @@
     inputs,
     divisor,
     down,
-    slices,
 ):
     first = scalars_ref[0] == 0
     rep = scalars_ref[1]
@@ -161,8 +173,9 @@
         / divisor[...]
     ).astype(BF16)
     for i in range(8):
+        start = pl.multiple_of(((i // 2) ^ scalars_ref[5]) * 512 + i % 2 * 256, 256)
         term = jnp.dot(
-            flipped_ref[i * 256 : (i + 1) * 256, :], down[...], preferred_element_type=F32
+            flipped_ref[pl.ds(start, 256), :], down[...], preferred_element_type=F32
         )
         for part in range(2):
             rows = pl.ds((2 * i + part) * HALF, HALF)
@@ -170,14 +183,12 @@
             bottom = term[part * BLOCK + HALF : (part + 1) * BLOCK]
             own_ref[rows, :] = jnp.where(first, top, bottom)
             other_ref[rows, :] = jnp.where(first, bottom, top).astype(BF16)
-    pair_start = pl.multiple_of(rep // 2 * BLOCK, BLOCK)
-    slices[...] = lax.dot_general(
-        inputs[:, pl.ds(pair_start, BLOCK)], pre_grad, COLS_T, preferred_element_type=F32
-    )
-    mine = slices[pl.ds(pl.multiple_of(rep % 2 * HALF, HALF), HALF), :].reshape(4, 2, 8, 256)
-    top, bottom = mine[:, 0].reshape(32, 256), mine[:, 1].reshape(32, 256)
-    own_ref[1024:, :] = jnp.where(first, top, bottom)
-    other_ref[1024:, :] = jnp.where(first, bottom, top).astype(BF16)
+    slice_start = pl.multiple_of(rep % 4 * BLOCK, BLOCK)
+    term = lax.dot_general(
+        inputs[:, pl.ds(slice_start, BLOCK)], pre_grad, COLS_T, preferred_element_type=F32
+    )
+    own_ref[1024:, :] = jnp.where(first, term[:HALF], term[HALF:])
+    other_ref[1024:, :] = jnp.where(first, term[HALF:], term[:HALF]).astype(BF16)
 
 
 def middle(scalars, pieces, degrees, features, cotangent, w_self, w_neigh, flipped):
@@ -186,8 +197,8 @@
         out_shape=(
             jax.ShapeDtypeStruct((512, 256), BF16),
             jax.ShapeDtypeStruct((512, 256), BF16),
-            jax.ShapeDtypeStruct((1056, 256), F32),
-            jax.ShapeDtypeStruct((1056, 256), BF16),
+            jax.ShapeDtypeStruct((1088, 256), F32),
+            jax.ShapeDtypeStruct((1088, 256), BF16),
         ),
         in_specs=[SMEM] + [VMEM] * 7,
         out_specs=(VMEM,) * 4,
@@ -195,27 +206,27 @@
             pltpu.VMEM((512, 512), BF16),
             pltpu.VMEM((512, 256), F32),
             pltpu.VMEM((512, 256), BF16),
-            pltpu.VMEM((BLOCK, 256), F32),
         ],
         compiler_params=pltpu.CompilerParams(vmem_limit_bytes=24 * 1024 * 1024),
     )(scalars, pieces, degrees, features, cotangent, w_self, w_neigh, flipped)
 
 
-def finish_kernel(results_ref, pre_grad_ref, w_self_ref, feature_ref, self_ref, neigh_ref):
+def finish_kernel(
+    scalars_ref, results_ref, pre_grad_ref, w_self_ref, feature_ref, self_ref, neigh_ref
+):
     self_part = lax.dot_general(
         pre_grad_ref[...], w_self_ref[...], ROWS_T, preferred_element_type=F32
     )
-    for place in range(8):
-        rows = pl.ds(place * HALF, HALF)
-        arrived = results_ref[place].astype(F32)
-        feature_ref[rows, :] = self_part[place * HALF : (place + 1) * HALF] + arrived[:HALF]
-        for part in range(8):
-            target = self_ref if part < 4 else neigh_ref
-            start = HALF + part * 8
-            target[pl.ds(part % 4 * HALF + place * 8, 8), :] = arrived[start : start + 8]
-
-
-def finish(results, pre_grad, w_self):
+    for block in range(4):
+        rows = slice(block * BLOCK, (block + 1) * BLOCK)
+        y = (scalars_ref[4] + 4 - block) % 4
+        feature_ref[rows, :] = self_part[rows] + results_ref[y, :BLOCK, :].astype(F32)
+        target = self_ref if block < 2 else neigh_ref
+        place = block % 2 * BLOCK
+        target[place : place + BLOCK, :] = results_ref[block, BLOCK:].astype(F32)
+
+
+def finish(scalars, results, pre_grad, w_self):
     return pl.pallas_call(
         finish_kernel,
         out_shape=(
@@ -223,10 +234,10 @@
             jax.ShapeDtypeStruct((256, 256), F32),
             jax.ShapeDtypeStruct((256, 256), F32),
         ),
-        in_specs=[VMEM] * 3,
+        in_specs=[SMEM] + [VMEM] * 3,
         out_specs=(VMEM,) * 3,
         compiler_params=pltpu.CompilerParams(vmem_limit_bytes=16 * 1024 * 1024),
-    )(results, pre_grad, w_self)
+    )(scalars, results, pre_grad, w_self)
 
 
 def body(
@@ -235,20 +246,23 @@
     section = lax.axis_index("section")
     rep = lax.axis_index("rep")
     z, x, core = section // 8, (section // 2) % 4, section % 2
-    scalars = jnp.stack([core, rep, z ^ core]).astype(jnp.int32)
+    y_column = (x % 2) * 2 + core
+    scalars = jnp.stack([core, rep, z ^ core, block_count[0, 0], other_end(x, y_column, 0), z])
+    scalars = scalars.astype(jnp.int32)
     with jax.named_scope("spread_features"):
-        place = other_end(x, (x % 2) * 2 + core, rep % 4)
+        place = other_end(x, y_column, rep % 4)
         block = lax.dynamic_index_in_dim(
             features.reshape(4, BLOCK, 256), place, 0, keepdims=False
         )
         arrived = [lax.ppermute(block, ("section", "rep"), out_pairs(c)) for c in range(2)]
         block = jnp.where(core == 0, arrived[0], arrived[1])
+        block, scalars = lax.optimization_barrier((block, scalars))
     with jax.named_scope("gather_features"):
         pair = jnp.stack([block, lax.ppermute(block, "section", Z_PAIRS)])
         own_columns = exchange(spread(pair, 4), "section", SAME_ZC).reshape(1024, 256)
-        own_columns, count = lax.optimization_barrier((own_columns, block_count))
+        own_columns, row_slots = lax.optimization_barrier((own_columns, block_rows[0, 0]))
         other_columns = swap_core(own_columns)
-    dense, flipped = densify(blocks[0, 0], block_rows[0, 0], block_cols[0, 0], count)
+    dense, flipped = densify(scalars, blocks[0, 0], row_slots, block_cols[0, 0])
     partial = forward_product(scalars, dense, own_columns, other_columns)
     with jax.named_scope("sum_over_y"):
         partial = add_up(exchange(partial.reshape(4, BLOCK, 256), "rep", SAME_H))
@@ -269,23 +283,28 @@
     with jax.named_scope("pair_sum"):
         both = (own + swap_core(other).astype(F32)).astype(BF16)
         main = both[:1024].reshape(4, 4, HALF, 256).transpose(1, 0, 2, 3).reshape(4, 256, 256)
-        send = jnp.concatenate([main, both[1024:].reshape(4, 8, 256)], axis=1)
+        send = jnp.concatenate([main, spread(both[1024:], 4)], axis=1)
     with jax.named_scope("sum_over_section"):
         send = add_up(exchange(send, "section", SAME_ZC))
-        send = jnp.concatenate([send[:256].reshape(4, HALF, 256), spread(send[256:], 4)], axis=1)
-        total = add_up(exchange(send, "section", SAME_XC))
-        arrived = lax.ppermute(total, "rep", HALF_PAIRS)
-        first = rep < 4
-        total = jnp.stack([jnp.where(first, total, arrived), jnp.where(first, arrived, total)])
-    with jax.named_scope("gather_sums"):
-        sums = exchange(spread(total, 4), "rep", SAME_H)
-        sums = sums.transpose(1, 0, 2, 3).reshape(8, 72, 256)
+        main, grad_part = send[:256].reshape(2, 2, HALF, 256), send[256:]
+        kept, sent = main[:, 0].reshape(BLOCK, 256), main[:, 1].reshape(BLOCK, 256)
+        arrived = lax.ppermute(jnp.concatenate([sent, grad_part]), "section", NEXT_Z)
+        pair = jnp.concatenate([kept, grad_part]).astype(F32) + arrived.astype(F32)
+        pair = pair.astype(BF16)
+        arrived = lax.ppermute(pair[HALF:], "section", Z_PAIRS)
+        kept = jnp.concatenate([pair[:HALF], pair[BLOCK:]])
+        total = kept.astype(F32) + arrived.astype(F32)
+        total = total.astype(BF16)
     with jax.named_scope("return_panels"):
-        grad_rows = spread(sums[:, HALF:].reshape(HALF, 256), 8)
-        results = exchange(
-            jnp.concatenate([sums[:, :HALF], grad_rows], axis=1), "section", SAME_Z
-        )
-    feature_grad, grad_self, grad_neigh = finish(results, pre_grad, w_self)
+        swapped = swap_core(total)
+        first = core == 0
+        top, bottom = jnp.where(first, total, swapped), jnp.where(first, swapped, total)
+        block = jnp.concatenate([top[:HALF], bottom[:HALF]], axis=0)
+        block = lax.ppermute(block, ("section", "rep"), back_pairs())
+    with jax.named_scope("gather_results"):
+        last = jnp.concatenate([block, top[HALF:], bottom[HALF:]], axis=0)
+        results = exchange(spread(last, 4), "rep", SAME_H)
+    feature_grad, grad_self, grad_neigh = finish(scalars, results, pre_grad, w_self)
     return (activated, feature_grad, grad_self, grad_neigh)
 
 

time: 125 us -> 119 us (0.952); the launches traced: 125 us -> 117 us
  blocking collectives: 74.5 us -> 53.2 us
  starting transfers between devices: 31.9 us -> 38.6 us
  waiting for transfers between devices: 8.55 us -> 14.9 us
    all_to_all x7 -> x5, blocking collectives: 74.5 us -> 53.2 us  [exchange(): return lax.all_to_all(x, axis, 0, 0, tiled=False, axis_index_groups=groups)]
    ppermute x1 -> x3, waiting for transfers between devices: 1.61 us -> 7.78 us  [the longest x1 3.32 us: body(): arrived = lax.ppermute(pair[HALF:], 'section', Z_PAIRS)]
    ppermute x2 -> x3, starting transfers between devices: 8.55 us -> 11.9 us  [swap_core(): return lax.ppermute(x, 'section', CORE_PAIRS)]
    ppermute x1 -> x3, starting transfers between devices: 5.2 us -> 8.09 us  [the longest x1 6.19 us: body(): block = lax.ppermute(block, ('section', 'rep'), back_pairs())]
  transfers between devices with their start and end apart: 7 -> 10, of which waited for: 6 -> 8; matrix products, arithmetic and copies ran while one was open for 0% -> 0% of each run, Pallas kernels for 1% -> 1%
where the time goes in v5:
time: 119 us; the launch traced here: 117 us
  blocking collectives  53.2 us (45%)
  starting transfers between devices  38.6 us (32%)
  waiting for transfers between devices  14.9 us (13%)
  Pallas kernels  6.82 us (6%)
  between operations  1.68 us (1%)
  local copies, waits for them, and re-layouts  1.31 us (1%)
    all_to_all x5, blocking collectives, exchange(): return lax.all_to_all(x, axis, 0, 0, tiled=False, axis_index_groups=groups)  53.2 us
    ppermute x3, starting transfers between devices, swap_core(): return lax.ppermute(x, 'section', CORE_PAIRS)  11.9 us
    ppermute x2, starting transfers between devices, body(): lax.ppermute(block, ('section', 'rep'), out_pairs(c))  8.86 us
    ppermute x1, starting transfers between devices, body(): lax.ppermute(partial, 'rep', HALF_PAIRS)  6.62 us
    ppermute x1, starting transfers between devices, body(): block = lax.ppermute(block, ('section', 'rep'), back_pairs())  6.19 us
    ppermute x1, waiting for transfers between devices, body(): arrived = lax.ppermute(pair[HALF:], 'section', Z_PAIRS)  3.32 us
    ppermute x1, waiting for transfers between devices, body(): lax.ppermute(jnp.concatenate([sent, grad_part]), 'section', NEXT_Z)  3.13 us
    ppermute x1, starting transfers between devices, body(): pair = jnp.stack([block, lax.ppermute(block, 'section', Z_PAIRS)])  3.08 us
  transfers between devices with their start and end apart: 10, of which 8 were waited for; matrix products, arithmetic and copies ran while one was open for 0% of the time, Pallas kernels for 1%

profile of v5, /device:TPU:1, one launch (start us, length us, event | category | flops | bytes accessed | tf_op | source)
XLA Modules:
  0.0 116.9 jit_solution(7736141777842636249)
XLA Ops:
  0.6 0.0 copy-start.6
  0.6 0.0 copy-start.7
  0.7 0.0 copy-start
  0.7 1.0 dynamic-slice_bitcast_fusion
  1.7 7.6 %collective-permute-start.1 = (bf16[128,256]{1,0:T(8,128)(2,1)S(1)}, bf16[128,256]{1,0:T(8,128)(2,1)S(1)}, u32[]{:S(2)}, u32[]{:S(2)}) collective-permute-start(bf16[128,256]{1,0:T(8,128)(2,1)S(1)} %dynamic-slice_bitcast_fusion), channel_id=1, source_target_pairs={{0,104},{1,88},{2,72},{3,120},{8,121},{9,105},{10,89},{11,73},{16,... | collective-permute-start | bytes 196616 | tf_op jit(solution)/shard_map/spread_features/ppermute | solution.py:257
  9.3 1.3 %collective-permute-start = (bf16[128,256]{1,0:T(8,128)(2,1)S(1)}, bf16[128,256]{1,0:T(8,128)(2,1)S(1)}, u32[]{:S(2)}, u32[]{:S(2)}) collective-permute-start(bf16[128,256]{1,0:T(8,128)(2,1)S(1)} %dynamic-slice_bitcast_fusion), channel_id=1, source_target_pairs={{0,32},{1,16},{2,0},{3,48},{8,49},{9,33},{10,17},{11,1},{16,18},{1... | collective-permute-start | bytes 196616 | tf_op jit(solution)/shard_map/spread_features/ppermute | solution.py:257
  11.3 0.1 stack.32.scalars_ref
  11.3 0.0 collective-permute-done.1
  11.3 0.5 collective-permute-done
  11.9 3.1 %collective-permute-start.2 = (bf16[128,256]{1,0:T(8,128)(2,1)S(1)}, bf16[128,256]{1,0:T(8,128)(2,1)S(1)}, u32[]{:S(2)}, u32[]{:S(2)}) collective-permute-start(bf16[128,256]{1,0:T(8,128)(2,1)S(1)} %broadcast_select_fusion.2), channel_id=1, source_target_pairs={{0,128},{8,136},{16,144},{24,152},{32,160},{40,168},{48,176},{56,1... | collective-permute-start | bytes 196616 | tf_op jit(solution)/shard_map/gather_features/ppermute | solution.py:261
  15.0 2.4 %collective-permute-done.2 = bf16[128,256]{1,0:T(8,128)(2,1)S(1)} collective-permute-done((bf16[128,256]{1,0:T(8,128)(2,1)S(1)}, bf16[128,256]{1,0:T(8,128)(2,1)S(1)}, u32[]{:S(2)}, u32[]{:S(2)}) %collective-permute-start.2) | collective-permute-done | bytes 65568 | tf_op jit(solution)/shard_map/gather_features/ppermute | solution.py:261
  17.4 10.6 %all_to_all.25 = bf16[4,2,128,256]{3,2,1,0:T(8,128)(2,1)S(1)} all-to-all(bf16[4,2,128,256]{3,2,1,0:T(8,128)(2,1)S(1)} %broadcast_in_dim.8), channel_id=1, replica_groups={{0,16,32,48},{8,24,40,56},{64,80,96,112},{72,88,104,120},{128,144,160,1..., dimensions={0} | all-to-all | bytes 1048576 | tf_op jit(solution)/shard_map/gather_features/all_to_all | solution.py:63
  28.0 5.1 %collective-permute-start.3 = (bf16[1024,256]{1,0:T(8,128)(2,1)S(1)}, bf16[1024,256]{1,0:T(8,128)(2,1)S(1)}, u32[]{:S(2)}, u32[]{:S(2)}) collective-permute-start(bf16[1024,256]{1,0:T(8,128)(2,1)S(1)} %bitcast.32), channel_id=1, source_target_pairs={{0,8},{8,0},{16,24},{24,16},{32,40},{40,32},{48,56},{56,48},{64,72... | collective-permute-start | bytes 1572872 | tf_op jit(solution)/shard_map/gather_features/ppermute | solution.py:59
  33.1 0.0 copy-done.6
  33.1 0.0 copy-done.7
  33.1 0.0 copy-done
  33.1 1.6 %shard_map.120 = (bf16[512,2048]{1,0:T(8,128)(2,1)S(1)}, bf16[2048,512]{1,0:T(8,128)(2,1)S(1)}) custom-call(s32[6]{0:T(128)S(1)} %stack.32.scalars_ref, s32[48]{0:T(128)S(1)} %bitcast.39, s32[48]{0:T(128)S(1)} %bitcast.40, bf16[48,128,128]{2,1,0:T(8,128)(2,1)S(1)} %bitcast.34), custom_call_target="tpu_custom_call" | custom-call | flops 4194304 | bytes 12582912 | tf_op jit(solution)/shard_map/pallas_call | solution.py:94
  34.8 0.0 collective-permute-done.3.other_ref
  34.8 1.3 %shard_map.121 = bf16[512,256]{1,0:T(8,128)(2,1)S(1)} custom-call(s32[6]{0:T(128)S(1)} %stack.32.scalars_ref, bf16[512,2048]{1,0:T(8,128)(2,1)S(1)} %get-tuple-element.20.dense_ref, bf16[1024,256]{1,0:T(8,128)(2,1)S(1)} %bitcast.33, bf16[1024,256]{1,0:T(8,128)(2,1)S(1)} %collective-permute-done.3.other_ref), custom_call_target="tpu_custom_call" | custom-call | tf_op jit(solution)/shard_map/pallas_call | solution.py:125
  36.1 0.0 copy-start.1
  36.1 0.0 copy-start.2
  36.1 0.0 copy-start.3
  36.2 0.0 copy-start.4
  36.2 0.0 copy-start.5
  36.2 10.0 %all_to_all.26 = bf16[4,128,256]{2,1,0:T(8,128)(2,1)S(1)} all-to-all(bf16[4,128,256]{2,1,0:T(8,128)(2,1)S(1)} %bitcast.36), channel_id=1, replica_groups={{0,1,2,3},{4,5,6,7},{8,9,10,11},{12,13,14,15},{16,17,18,19},{20,21,22,2..., dimensions={0} | all-to-all | bytes 524288 | tf_op jit(solution)/shard_map/sum_over_y/all_to_all | solution.py:63
  46.2 6.6 %collective-permute-start.4 = (bf16[128,256]{1,0:T(8,128)(2,1)S(1)}, bf16[128,256]{1,0:T(8,128)(2,1)S(1)}, u32[]{:S(2)}, u32[]{:S(2)}) collective-permute-start(bf16[128,256]{1,0:T(8,128)(2,1)S(1)} %fusion), channel_id=1, source_target_pairs={{0,4},{1,5},{2,6},{3,7},{4,0},{5,1},{6,2},{7,3},{8,12},{9,13},{10,... | collective-permute-start | bytes 196616 | tf_op jit(solution)/shard_map/sum_over_h/ppermute | solution.py:270
  52.9 1.7 %collective-permute-done.4 = bf16[128,256]{1,0:T(8,128)(2,1)S(1)} collective-permute-done((bf16[128,256]{1,0:T(8,128)(2,1)S(1)}, bf16[128,256]{1,0:T(8,128)(2,1)S(1)}, u32[]{:S(2)}, u32[]{:S(2)}) %collective-permute-start.4) | collective-permute-done | bytes 65568 | tf_op jit(solution)/shard_map/sum_over_h/ppermute | solution.py:270
  54.6 7.9 %all_to_all.27 = bf16[4,128,256]{2,1,0:T(8,128)(2,1)S(1)} all-to-all(bf16[4,128,256]{2,1,0:T(8,128)(2,1)S(1)} %broadcast_in_dim.9), channel_id=1, replica_groups={{0,1,2,3},{4,5,6,7},{8,9,10,11},{12,13,14,15},{16,17,18,19},{20,21,22,2..., dimensions={0} | all-to-all | bytes 524288 | tf_op jit(solution)/shard_map/gather_over_y/all_to_all | solution.py:63
  62.5 0.0 copy-done.1
  62.5 0.0 copy-done.2
  62.5 0.0 copy-done.3
  62.5 0.0 copy-done.4
  62.6 2.1 %shard_map.122 = (bf16[512,256]{1,0:T(8,128)(2,1)}, bf16[512,256]{1,0:T(8,128)(2,1)S(1)}, f32[1088,256]{1,0:T(8,128)S(1)}, bf16[1088,256]{1,0:T(8,128)(2,1)S(1)}) custom-call(s32[6]{0:T(128)S(1)} %stack.32.scalars_ref, bf16[512,256]{1,0:T(8,128)(2,1)S(1)} %bitcast.35, s32[4,128]{1,0:T(4,128)S(1)} %bitcast.38, bf16[512,256]{1,0:T(8,128)(2,1)S(1)} %copy-done.2, ...), custom_call_target="tpu_custom_call" | custom-call | tf_op jit(solution)/shard_map/pallas_call | solution.py:195
  64.7 3.2 %collective-permute-start.5 = (bf16[1088,256]{1,0:T(8,128)(2,1)S(1)}, bf16[1088,256]{1,0:T(8,128)(2,1)S(1)}, u32[]{:S(2)}, u32[]{:S(2)}) collective-permute-start(bf16[1088,256]{1,0:T(8,128)(2,1)S(1)} %get-tuple-element.25), channel_id=1, source_target_pairs={{0,8},{8,0},{16,24},{24,16},{32,40},{40,32},{48,56},{56,48},{64,72... | collective-permute-start | bytes 1671176 | tf_op jit(solution)/shard_map/pair_sum/ppermute | solution.py:59
  67.9 1.6 %collective-permute-done.5 = bf16[1088,256]{1,0:T(8,128)(2,1)S(1)} collective-permute-done((bf16[1088,256]{1,0:T(8,128)(2,1)S(1)}, bf16[1088,256]{1,0:T(8,128)(2,1)S(1)}, u32[]{:S(2)}, u32[]{:S(2)}) %collective-permute-start.5) | collective-permute-done | bytes 557088 | tf_op jit(solution)/shard_map/pair_sum/ppermute | solution.py:59
  69.5 0.2 add_convert_fusion
  69.9 13.0 %all_to_all.28 = bf16[4,320,256]{2,1,0:T(8,128)(2,1)S(1)} all-to-all(bf16[4,320,256]{2,1,0:T(8,128)(2,1)S(1)} %pad_maximum_fusion), channel_id=1, replica_groups={{0,16,32,48},{8,24,40,56},{64,80,96,112},{72,88,104,120},{128,144,160,1..., dimensions={0} | all-to-all | bytes 1310720 | tf_op jit(solution)/shard_map/sum_over_section/all_to_all | solution.py:63
  82.9 0.1 add_convert_fusion.1
  83.0 0.4 collective-permute-start.6
  83.5 3.1 %collective-permute-done.6 = bf16[192,256]{1,0:T(8,128)(2,1)S(1)} collective-permute-done((bf16[192,256]{1,0:T(8,128)(2,1)S(1)}, bf16[192,256]{1,0:T(8,128)(2,1)S(1)}, u32[]{:S(2)}, u32[]{:S(2)}) %collective-permute-start.6) | collective-permute-done | bytes 98336 | tf_op jit(solution)/shard_map/sum_over_section/ppermute | solution.py:291
  86.6 1.5 %collective-permute-start.7 = (bf16[128,256]{1,0:T(8,128)(2,1)S(1)}, bf16[128,256]{1,0:T(8,128)(2,1)S(1)}, u32[]{:S(2)}, u32[]{:S(2)}) collective-permute-start(bf16[128,256]{1,0:T(8,128)(2,1)S(1)} %slice.105), channel_id=1, source_target_pairs={{0,128},{8,136},{16,144},{24,152},{32,160},{40,168},{48,176},{56,1... | collective-permute-start | bytes 196616 | tf_op jit(solution)/shard_map/sum_over_section/ppermute | solution.py:294
  88.1 3.3 %collective-permute-done.7 = bf16[128,256]{1,0:T(8,128)(2,1)S(1)} collective-permute-done((bf16[128,256]{1,0:T(8,128)(2,1)S(1)}, bf16[128,256]{1,0:T(8,128)(2,1)S(1)}, u32[]{:S(2)}, u32[]{:S(2)}) %collective-permute-start.7) | collective-permute-done | bytes 65568 | tf_op jit(solution)/shard_map/sum_over_section/ppermute | solution.py:294
  91.5 3.6 %collective-permute-start.8 = (bf16[128,256]{1,0:T(8,128)(2,1)S(1)}, bf16[128,256]{1,0:T(8,128)(2,1)S(1)}, u32[]{:S(2)}, u32[]{:S(2)}) collective-permute-start(bf16[128,256]{1,0:T(8,128)(2,1)S(1)} %add_convert_fusion.3), channel_id=1, source_target_pairs={{0,8},{8,0},{16,24},{24,16},{32,40},{40,32},{48,56},{56,48},{64,72... | collective-permute-start | bytes 196616 | tf_op jit(solution)/shard_map/return_panels/ppermute | solution.py:59
  95.1 0.9 collective-permute-done.8
  96.0 6.2 %collective-permute-start.9 = (bf16[128,256]{1,0:T(8,128)(2,1)S(1)}, bf16[128,256]{1,0:T(8,128)(2,1)S(1)}, u32[]{:S(2)}, u32[]{:S(2)}) collective-permute-start(bf16[128,256]{1,0:T(8,128)(2,1)S(1)} %pad_maximum_fusion.5), channel_id=1, source_target_pairs={{0,2},{1,11},{2,17},{3,26},{4,36},{5,45},{6,55},{7,60},{8,6},{9,15... | collective-permute-start | bytes 196616 | tf_op jit(solution)/shard_map/return_panels/ppermute | solution.py:303
  102.2 1.3 %collective-permute-done.9 = bf16[128,256]{1,0:T(8,128)(2,1)S(1)} collective-permute-done((bf16[128,256]{1,0:T(8,128)(2,1)S(1)}, bf16[128,256]{1,0:T(8,128)(2,1)S(1)}, u32[]{:S(2)}, u32[]{:S(2)}) %collective-permute-start.9) | collective-permute-done | bytes 65568 | tf_op jit(solution)/shard_map/return_panels/ppermute | solution.py:303
  103.6 11.6 %all_to_all.29.results_ref = bf16[4,256,256]{2,1,0:T(8,128)(2,1)S(1)} all-to-all(bf16[4,256,256]{2,1,0:T(8,128)(2,1)S(1)} %broadcast_in_dim.11), channel_id=1, replica_groups={{0,1,2,3},{4,5,6,7},{8,9,10,11},{12,13,14,15},{16,17,18,19},{20,21,22,2..., dimensions={0} | all-to-all | bytes 1048576 | tf_op jit(solution)/shard_map/gather_results/all_to_all | solution.py:63
  115.2 1.7 %shard_map.123 = (f32[512,256]{1,0:T(8,128)}, f32[256,256]{1,0:T(8,128)}, f32[256,256]{1,0:T(8,128)}) custom-call(s32[6]{0:T(128)S(1)} %stack.32.scalars_ref, bf16[4,256,256]{2,1,0:T(8,128)(2,1)S(1)} %all_to_all.29.results_ref, bf16[512,256]{1,0:T(8,128)(2,1)S(1)} %get-tuple-element.26.pre_grad_ref, bf16[256,256]{1,0:T(8,128)(2,1)S(1)} %copy-done.1), custom_call_target="tpu_custom_call" | custom-call | tf_op jit(solution)/shard_map/pallas_call | solution.py:230
  (25 shorter events, 0.5 us)
Async XLA Ops:
  0.6 32.5 %copy-start.6 = (s32[1,1,48]{2,1,0:T(1,128)S(1)}, s32[1,1,48]{2,1,0:T(1,128)}, u32[]{:S(2)}) copy-start(s32[1,1,48]{2,1,0:T(1,128)} %param.13) | copy-start | bytes 580
  0.6 32.5 %copy-start.7 = (s32[1,1,48]{2,1,0:T(1,128)S(1)}, s32[1,1,48]{2,1,0:T(1,128)}, u32[]{:S(2)}) copy-start(s32[1,1,48]{2,1,0:T(1,128)} %param.14) | copy-start | bytes 580
  0.7 32.5 %copy-start = (bf16[1,1,48,128,128]{4,3,2,1,0:T(8,128)(2,1)S(1)}, bf16[1,1,48,128,128]{4,3,2,1,0:T(8,128)(2,1)}, u32[]{:S(2)}) copy-start(bf16[1,1,48,128,128]{4,3,2,1,0:T(8,128)(2,1)} %param.12) | copy-start | bytes 4718596
  1.7 9.7 %collective-permute-start.1 = (bf16[128,256]{1,0:T(8,128)(2,1)S(1)}, bf16[128,256]{1,0:T(8,128)(2,1)S(1)}, u32[]{:S(2)}, u32[]{:S(2)}) collective-permute-start(bf16[128,256]{1,0:T(8,128)(2,1)S(1)} %dynamic-slice_bitcast_fusion), channel_id=1, source_target_pairs={{0,104},{1,88},{2,72},{3,120},{8,121},{9,105},{10,89},{11,73},{16,... | collective-permute-start | bytes 196616 | tf_op jit(solution)/shard_map/spread_features/ppermute | solution.py:257
  9.3 2.6 %collective-permute-start = (bf16[128,256]{1,0:T(8,128)(2,1)S(1)}, bf16[128,256]{1,0:T(8,128)(2,1)S(1)}, u32[]{:S(2)}, u32[]{:S(2)}) collective-permute-start(bf16[128,256]{1,0:T(8,128)(2,1)S(1)} %dynamic-slice_bitcast_fusion), channel_id=1, source_target_pairs={{0,32},{1,16},{2,0},{3,48},{8,49},{9,33},{10,17},{11,1},{16,18},{1... | collective-permute-start | bytes 196616 | tf_op jit(solution)/shard_map/spread_features/ppermute | solution.py:257
  11.9 5.4 %collective-permute-start.2 = (bf16[128,256]{1,0:T(8,128)(2,1)S(1)}, bf16[128,256]{1,0:T(8,128)(2,1)S(1)}, u32[]{:S(2)}, u32[]{:S(2)}) collective-permute-start(bf16[128,256]{1,0:T(8,128)(2,1)S(1)} %broadcast_select_fusion.2), channel_id=1, source_target_pairs={{0,128},{8,136},{16,144},{24,152},{32,160},{40,168},{48,176},{56,1... | collective-permute-start | bytes 196616 | tf_op jit(solution)/shard_map/gather_features/ppermute | solution.py:261
  28.0 6.8 %collective-permute-start.3 = (bf16[1024,256]{1,0:T(8,128)(2,1)S(1)}, bf16[1024,256]{1,0:T(8,128)(2,1)S(1)}, u32[]{:S(2)}, u32[]{:S(2)}) collective-permute-start(bf16[1024,256]{1,0:T(8,128)(2,1)S(1)} %bitcast.32), channel_id=1, source_target_pairs={{0,8},{8,0},{16,24},{24,16},{32,40},{40,32},{48,56},{56,48},{64,72... | collective-permute-start | bytes 1572872 | tf_op jit(solution)/shard_map/gather_features/ppermute | solution.py:59
  36.1 26.4 %copy-start.1 = (bf16[256,256]{1,0:T(8,128)(2,1)S(1)}, bf16[256,256]{1,0:T(8,128)(2,1)}, u32[]{:S(2)}) copy-start(bf16[256,256]{1,0:T(8,128)(2,1)} %w_self_ref.3) | copy-start | bytes 393220
  36.1 26.4 %copy-start.2 = (bf16[512,256]{1,0:T(8,128)(2,1)S(1)}, bf16[512,256]{1,0:T(8,128)(2,1)}, u32[]{:S(2)}) copy-start(bf16[512,256]{1,0:T(8,128)(2,1)} %features_ref.1) | copy-start | bytes 786436
  36.1 26.4 %copy-start.3 = (bf16[512,256]{1,0:T(8,128)(2,1)S(1)}, bf16[512,256]{1,0:T(8,128)(2,1)}, u32[]{:S(2)}) copy-start(bf16[512,256]{1,0:T(8,128)(2,1)} %cotangent_ref.1) | copy-start | bytes 786436
  36.2 26.4 %copy-start.4 = (bf16[256,256]{1,0:T(8,128)(2,1)S(1)}, bf16[256,256]{1,0:T(8,128)(2,1)}, u32[]{:S(2)}) copy-start(bf16[256,256]{1,0:T(8,128)(2,1)} %w_neigh_ref.1) | copy-start | bytes 393220
  36.2 26.4 %copy-start.5 = (s32[512]{0:T(512)S(1)}, s32[512]{0:T(512)}, u32[]{:S(2)}) copy-start(s32[512]{0:T(512)} %param.11) | copy-start | bytes 6148
  46.2 8.3 %collective-permute-start.4 = (bf16[128,256]{1,0:T(8,128)(2,1)S(1)}, bf16[128,256]{1,0:T(8,128)(2,1)S(1)}, u32[]{:S(2)}, u32[]{:S(2)}) collective-permute-start(bf16[128,256]{1,0:T(8,128)(2,1)S(1)} %fusion), channel_id=1, source_target_pairs={{0,4},{1,5},{2,6},{3,7},{4,0},{5,1},{6,2},{7,3},{8,12},{9,13},{10,... | collective-permute-start | bytes 196616 | tf_op jit(solution)/shard_map/sum_over_h/ppermute | solution.py:270
  64.7 4.8 %collective-permute-start.5 = (bf16[1088,256]{1,0:T(8,128)(2,1)S(1)}, bf16[1088,256]{1,0:T(8,128)(2,1)S(1)}, u32[]{:S(2)}, u32[]{:S(2)}) collective-permute-start(bf16[1088,256]{1,0:T(8,128)(2,1)S(1)} %get-tuple-element.25), channel_id=1, source_target_pairs={{0,8},{8,0},{16,24},{24,16},{32,40},{40,32},{48,56},{56,48},{64,72... | collective-permute-start | bytes 1671176 | tf_op jit(solution)/shard_map/pair_sum/ppermute | solution.py:59
  83.0 3.6 %collective-permute-start.6 = (bf16[192,256]{1,0:T(8,128)(2,1)S(1)}, bf16[192,256]{1,0:T(8,128)(2,1)S(1)}, u32[]{:S(2)}, u32[]{:S(2)}) collective-permute-start(bf16[192,256]{1,0:T(8,128)(2,1)S(1)} %pad_maximum_fusion.3), channel_id=1, source_target_pairs={{0,64},{8,72},{16,80},{24,88},{32,96},{40,104},{48,112},{56,120},{... | collective-permute-start | bytes 294920 | tf_op jit(solution)/shard_map/sum_over_section/ppermute | solution.py:291
  86.6 4.8 %collective-permute-start.7 = (bf16[128,256]{1,0:T(8,128)(2,1)S(1)}, bf16[128,256]{1,0:T(8,128)(2,1)S(1)}, u32[]{:S(2)}, u32[]{:S(2)}) collective-permute-start(bf16[128,256]{1,0:T(8,128)(2,1)S(1)} %slice.105), channel_id=1, source_target_pairs={{0,128},{8,136},{16,144},{24,152},{32,160},{40,168},{48,176},{56,1... | collective-permute-start | bytes 196616 | tf_op jit(solution)/shard_map/sum_over_section/ppermute | solution.py:294
  91.5 4.5 %collective-permute-start.8 = (bf16[128,256]{1,0:T(8,128)(2,1)S(1)}, bf16[128,256]{1,0:T(8,128)(2,1)S(1)}, u32[]{:S(2)}, u32[]{:S(2)}) collective-permute-start(bf16[128,256]{1,0:T(8,128)(2,1)S(1)} %add_convert_fusion.3), channel_id=1, source_target_pairs={{0,8},{8,0},{16,24},{24,16},{32,40},{40,32},{48,56},{56,48},{64,72... | collective-permute-start | bytes 196616 | tf_op jit(solution)/shard_map/return_panels/ppermute | solution.py:59
  96.0 7.5 %collective-permute-start.9 = (bf16[128,256]{1,0:T(8,128)(2,1)S(1)}, bf16[128,256]{1,0:T(8,128)(2,1)S(1)}, u32[]{:S(2)}, u32[]{:S(2)}) collective-permute-start(bf16[128,256]{1,0:T(8,128)(2,1)S(1)} %pad_maximum_fusion.5), channel_id=1, source_target_pairs={{0,2},{1,11},{2,17},{3,26},{4,36},{5,45},{6,55},{7,60},{8,6},{9,15... | collective-permute-start | bytes 196616 | tf_op jit(solution)/shard_map/return_panels/ppermute | solution.py:303

commit v6 on v5

--- a/solution.py
+++ b/solution.py
@@ -26,17 +26,18 @@
     return (x_home + y_column + 2 - place) % 4
 
 
-def out_pairs(core_to):
+def out_pairs():
     pairs = []
     for z in range(4):
         for x in range(4):
             for core in range(2):
                 h, y_column = x // 2, (x % 2) * 2 + core
                 for y in range(4):
-                    source = (8 * z + 2 * x + core) * 8 + 4 * h + y
-                    x_to = other_end(x, y_column, y)
-                    target = (8 * (z ^ core_to) + 2 * x_to + core_to) * 8 + 4 * h + y_column
-                    pairs.append((source, target))
+                    for core_to in range(2):
+                        source = (8 * z + 2 * x + core) * 8 + 4 * (h ^ core_to) + y
+                        x_to = other_end(x, y_column, y)
+                        section_to = 8 * (z ^ (2 * core_to)) + 2 * x_to + core_to
+                        pairs.append((source, section_to * 8 + 4 * h + y_column))
     return pairs
 
 
@@ -50,9 +51,15 @@
                         source = (8 * z + 2 * x + core) * 8 + 4 * h + y
                         x_home, core_home = 2 * h + y // 2, y % 2
                         y_to = other_end(x_home, y, x)
-                        target = (8 * z + 2 * x_home + core_home) * 8 + 4 * (core ^ h) + y_to
+                        z_to = z ^ (2 * core)
+                        target = (8 * z_to + 2 * x_home + core_home) * 8 + 4 * (core ^ h) + y_to
                         pairs.append((source, target))
     return pairs
+
+
+def position():
+    section, rep = lax.axis_index("section"), lax.axis_index("rep")
+    return section // 8, section // 2 % 4, section % 2, rep // 4, rep % 4
 
 
 def swap_core(x):
@@ -81,7 +88,7 @@
         total[rows_ref[slot], cols_ref[slot]] += blocks_ref[slot].astype(F32)
         return carry
 
-    lax.fori_loop(0, scalars_ref[3], add_slot, 0)
+    lax.fori_loop(0, scalars_ref[0], add_slot, 0)
     for i in range(4):
         for j in range(16):
             tile = total[i, j]
@@ -105,13 +112,14 @@
     )(scalars, rows, cols, tiles)
 
 
-def forward_kernel(scalars_ref, dense_ref, own_ref, other_ref, out_ref, columns):
-    panel = scalars_ref[2]
+def forward_kernel(dense_ref, own_ref, other_ref, out_ref, columns):
+    z, _, core, _, _ = position()
+    panel = z ^ (2 * core)
     for x in range(4):
         for pair in range(2):
             place = (2 * x + pair) * BLOCK
-            own_start = (panel ^ (2 * pair)) * 512 + x * BLOCK
-            other_start = (panel ^ (2 * pair) ^ 1) * 512 + x * BLOCK
+            own_start = (panel ^ pair) * 512 + x * BLOCK
+            other_start = (panel ^ 2 ^ pair) * 512 + x * BLOCK
             columns[pl.ds(pl.multiple_of(own_start, BLOCK), BLOCK), :] = own_ref[
                 place : place + BLOCK, :
             ]
@@ -121,19 +129,18 @@
     out_ref[...] = jnp.dot(dense_ref[...], columns[...], preferred_element_type=F32).astype(BF16)
 
 
-def forward_product(scalars, dense, own, other):
+def forward_product(dense, own, other):
     return pl.pallas_call(
         forward_kernel,
         out_shape=jax.ShapeDtypeStruct((512, 256), BF16),
-        in_specs=[SMEM, VMEM, VMEM, VMEM],
+        in_specs=[VMEM, VMEM, VMEM],
         out_specs=VMEM,
         scratch_shapes=[pltpu.VMEM((2048, 256), BF16)],
         compiler_params=pltpu.CompilerParams(vmem_limit_bytes=16 * 1024 * 1024),
-    )(scalars, dense, own, other)
+    )(dense, own, other)
 
 
 def middle_kernel(
-    scalars_ref,
     pieces_ref,
     degrees_ref,
     features_ref,
@@ -149,8 +156,8 @@
     divisor,
     down,
 ):
-    first = scalars_ref[0] == 0
-    rep = scalars_ref[1]
+    z, _, core, _, y = position()
+    first = core == 0
     degree_rows = degrees_ref[...].astype(F32)
     for i in range(4):
         turned = jnp.broadcast_to(degree_rows[i : i + 1, :], (BLOCK, BLOCK)).T
@@ -173,7 +180,7 @@
         / divisor[...]
     ).astype(BF16)
     for i in range(8):
-        start = pl.multiple_of(((i // 2) ^ scalars_ref[5]) * 512 + i % 2 * 256, 256)
+        start = pl.multiple_of(((i // 2) ^ z) * 512 + i % 2 * 256, 256)
         term = jnp.dot(
             flipped_ref[pl.ds(start, 256), :], down[...], preferred_element_type=F32
         )
@@ -183,7 +190,7 @@
             bottom = term[part * BLOCK + HALF : (part + 1) * BLOCK]
             own_ref[rows, :] = jnp.where(first, top, bottom)
             other_ref[rows, :] = jnp.where(first, bottom, top).astype(BF16)
-    slice_start = pl.multiple_of(rep % 4 * BLOCK, BLOCK)
+    slice_start = pl.multiple_of(y * BLOCK, BLOCK)
     term = lax.dot_general(
         inputs[:, pl.ds(slice_start, BLOCK)], pre_grad, COLS_T, preferred_element_type=F32
     )
@@ -191,7 +198,7 @@
     other_ref[1024:, :] = jnp.where(first, term[HALF:], term[:HALF]).astype(BF16)
 
 
-def middle(scalars, pieces, degrees, features, cotangent, w_self, w_neigh, flipped):
+def middle(pieces, degrees, features, cotangent, w_self, w_neigh, flipped):
     return pl.pallas_call(
         middle_kernel,
         out_shape=(
@@ -200,7 +207,7 @@
             jax.ShapeDtypeStruct((1088, 256), F32),
             jax.ShapeDtypeStruct((1088, 256), BF16),
         ),
-        in_specs=[SMEM] + [VMEM] * 7,
+        in_specs=[VMEM] * 7,
         out_specs=(VMEM,) * 4,
         scratch_shapes=[
             pltpu.VMEM((512, 512), BF16),
@@ -208,25 +215,25 @@
             pltpu.VMEM((512, 256), BF16),
         ],
         compiler_params=pltpu.CompilerParams(vmem_limit_bytes=24 * 1024 * 1024),
-    )(scalars, pieces, degrees, features, cotangent, w_self, w_neigh, flipped)
-
-
-def finish_kernel(
-    scalars_ref, results_ref, pre_grad_ref, w_self_ref, feature_ref, self_ref, neigh_ref
-):
+    )(pieces, degrees, features, cotangent, w_self, w_neigh, flipped)
+
+
+def finish_kernel(results_ref, pre_grad_ref, w_self_ref, feature_ref, self_ref, neigh_ref):
+    _, x, core, _, _ = position()
+    last = other_end(x, x % 2 * 2 + core, 0)
     self_part = lax.dot_general(
         pre_grad_ref[...], w_self_ref[...], ROWS_T, preferred_element_type=F32
     )
     for block in range(4):
         rows = slice(block * BLOCK, (block + 1) * BLOCK)
-        y = (scalars_ref[4] + 4 - block) % 4
+        y = (last + 4 - block) % 4
         feature_ref[rows, :] = self_part[rows] + results_ref[y, :BLOCK, :].astype(F32)
         target = self_ref if block < 2 else neigh_ref
         place = block % 2 * BLOCK
         target[place : place + BLOCK, :] = results_ref[block, BLOCK:].astype(F32)
 
 
-def finish(scalars, results, pre_grad, w_self):
+def finish(results, pre_grad, w_self):
     return pl.pallas_call(
         finish_kernel,
         out_shape=(
@@ -234,36 +241,32 @@
             jax.ShapeDtypeStruct((256, 256), F32),
             jax.ShapeDtypeStruct((256, 256), F32),
         ),
-        in_specs=[SMEM] + [VMEM] * 3,
+        in_specs=[VMEM] * 3,
         out_specs=(VMEM,) * 3,
         compiler_params=pltpu.CompilerParams(vmem_limit_bytes=16 * 1024 * 1024),
-    )(scalars, results, pre_grad, w_self)
+    )(results, pre_grad, w_self)
 
 
 def body(
     features, cotangent, degrees, blocks, block_rows, block_cols, block_count, w_self, w_neigh
 ):
-    section = lax.axis_index("section")
-    rep = lax.axis_index("rep")
-    z, x, core = section // 8, (section // 2) % 4, section % 2
-    y_column = (x % 2) * 2 + core
-    scalars = jnp.stack([core, rep, z ^ core, block_count[0, 0], other_end(x, y_column, 0), z])
-    scalars = scalars.astype(jnp.int32)
+    z, x, core, h, y = position()
+    y_column = x % 2 * 2 + core
+    scalars = jnp.stack([block_count[0, 0], core.astype(jnp.int32)])
     with jax.named_scope("spread_features"):
-        place = other_end(x, y_column, rep % 4)
+        place = other_end(x, y_column, y)
         block = lax.dynamic_index_in_dim(
             features.reshape(4, BLOCK, 256), place, 0, keepdims=False
         )
-        arrived = [lax.ppermute(block, ("section", "rep"), out_pairs(c)) for c in range(2)]
-        block = jnp.where(core == 0, arrived[0], arrived[1])
+        block = lax.ppermute(block, ("section", "rep"), out_pairs())
         block, scalars = lax.optimization_barrier((block, scalars))
     with jax.named_scope("gather_features"):
-        pair = jnp.stack([block, lax.ppermute(block, "section", Z_PAIRS)])
+        pair = jnp.stack([block, lax.ppermute(block, "section", NEXT_Z)])
         own_columns = exchange(spread(pair, 4), "section", SAME_ZC).reshape(1024, 256)
         own_columns, row_slots = lax.optimization_barrier((own_columns, block_rows[0, 0]))
         other_columns = swap_core(own_columns)
     dense, flipped = densify(scalars, blocks[0, 0], row_slots, block_cols[0, 0])
-    partial = forward_product(scalars, dense, own_columns, other_columns)
+    partial = forward_product(dense, own_columns, other_columns)
     with jax.named_scope("sum_over_y"):
         partial = add_up(exchange(partial.reshape(4, BLOCK, 256), "rep", SAME_H))
     with jax.named_scope("sum_over_h"):
@@ -271,7 +274,6 @@
     with jax.named_scope("gather_over_y"):
         pieces = exchange(spread(partial, 4), "rep", SAME_H)
     activated, pre_grad, own, other = middle(
-        scalars,
         pieces.reshape(512, 256),
         degrees.reshape(4, BLOCK),
         features,
@@ -291,20 +293,22 @@
         arrived = lax.ppermute(jnp.concatenate([sent, grad_part]), "section", NEXT_Z)
         pair = jnp.concatenate([kept, grad_part]).astype(F32) + arrived.astype(F32)
         pair = pair.astype(BF16)
-        arrived = lax.ppermute(pair[HALF:], "section", Z_PAIRS)
-        kept = jnp.concatenate([pair[:HALF], pair[BLOCK:]])
-        total = kept.astype(F32) + arrived.astype(F32)
-        total = total.astype(BF16)
+        turned = jnp.concatenate([pair[HALF:BLOCK], pair[:HALF], pair[BLOCK:]])
+        arrived = lax.ppermute(turned, "section", Z_PAIRS)
+        total = (pair.astype(F32) + arrived.astype(F32)).astype(BF16)
     with jax.named_scope("return_panels"):
-        swapped = swap_core(total)
         first = core == 0
-        top, bottom = jnp.where(first, total, swapped), jnp.where(first, swapped, total)
+        kept = jnp.where(first, total[:HALF], total[HALF:BLOCK])
+        given = jnp.where(first, total[HALF:BLOCK], total[:HALF])
+        swapped = swap_core(jnp.concatenate([given, total[BLOCK:]]))
+        kept = jnp.concatenate([kept, total[BLOCK:]])
+        top, bottom = jnp.where(first, kept, swapped), jnp.where(first, swapped, kept)
         block = jnp.concatenate([top[:HALF], bottom[:HALF]], axis=0)
         block = lax.ppermute(block, ("section", "rep"), back_pairs())
     with jax.named_scope("gather_results"):
         last = jnp.concatenate([block, top[HALF:], bottom[HALF:]], axis=0)
         results = exchange(spread(last, 4), "rep", SAME_H)
-    feature_grad, grad_self, grad_neigh = finish(scalars, results, pre_grad, w_self)
+    feature_grad, grad_self, grad_neigh = finish(results, pre_grad, w_self)
     return (activated, feature_grad, grad_self, grad_neigh)
 
 

time: 119 us -> 114 us (0.958)
  the two profiles are of different devices: /device:TPU:1 before, /device:TPU:7 now
where the time goes in v6:
time: 114 us
  blocking collectives  52.3 us (46%)
  starting transfers between devices  30.3 us (27%)
  waiting for transfers between devices  22.9 us (20%)
  Pallas kernels  5.2 us (5%)
  between operations  1.65 us (1%)
  local copies, waits for them, and re-layouts  1.22 us (1%)
    all_to_all x5, blocking collectives, exchange(): return lax.all_to_all(x, axis, 0, 0, tiled=False, axis_index_groups=groups)  52.3 us
    ppermute x3, starting transfers between devices, swap_core(): return lax.ppermute(x, 'section', CORE_PAIRS)  11.1 us
    ppermute x1, starting transfers between devices, body(): block = lax.ppermute(block, ('section', 'rep'), out_pairs())  8.39 us
    ppermute x1, waiting for transfers between devices, body(): block = lax.ppermute(block, ('section', 'rep'), back_pairs())  5.41 us
    ppermute x1, waiting for transfers between devices, body(): arrived = lax.ppermute(turned, 'section', Z_PAIRS)  4.41 us
    ppermute x1, starting transfers between devices, body(): block = lax.ppermute(block, ('section', 'rep'), back_pairs())  4.11 us
    ppermute x1, waiting for transfers between devices, body(): lax.ppermute(partial, 'rep', HALF_PAIRS)  3.76 us
    ppermute x1, starting transfers between devices, body(): lax.ppermute(partial, 'rep', HALF_PAIRS)  3.36 us
  transfers between devices with their start and end apart: 9, of which 8 were waited for; matrix products, arithmetic and copies ran while one was open for 0% of the time, Pallas kernels for 2%

profile of v6, /device:TPU:7, one launch (start us, length us, event | category | flops | bytes accessed | tf_op | source)
XLA Modules:
  0.0 114.0 jit_solution(12270171847579777708)
XLA Ops:
  0.6 0.0 copy-start.6
  0.6 0.0 copy-start.7
  0.7 0.0 copy-start
  0.7 1.0 dynamic-slice_bitcast_fusion
  1.7 8.4 %collective-permute-start = (bf16[128,256]{1,0:T(8,128)(2,1)S(1)}, bf16[128,256]{1,0:T(8,128)(2,1)S(1)}, u32[]{:S(2)}, u32[]{:S(2)}) collective-permute-start(bf16[128,256]{1,0:T(8,128)(2,1)S(1)} %dynamic-slice_bitcast_fusion), channel_id=1, source_target_pairs={{0,32},{4,168},{1,16},{5,152},{2,0},{6,136},{3,48},{7,184},{8,49},... | collective-permute-start | bytes 196616 | tf_op jit(solution)/shard_map/spread_features/ppermute | solution.py:261
  10.7 0.1 pad_add_fusion.scalars_ref
  10.8 2.4 %collective-permute-done = bf16[128,256]{1,0:T(8,128)(2,1)S(1)} collective-permute-done((bf16[128,256]{1,0:T(8,128)(2,1)S(1)}, bf16[128,256]{1,0:T(8,128)(2,1)S(1)}, u32[]{:S(2)}, u32[]{:S(2)}) %collective-permute-start) | collective-permute-done | bytes 65568 | tf_op jit(solution)/shard_map/spread_features/ppermute | solution.py:261
  13.2 1.5 %collective-permute-start.1 = (bf16[128,256]{1,0:T(8,128)(2,1)S(1)}, bf16[128,256]{1,0:T(8,128)(2,1)S(1)}, u32[]{:S(2)}, u32[]{:S(2)}) collective-permute-start(bf16[128,256]{1,0:T(8,128)(2,1)S(1)} %collective-permute-done), channel_id=1, source_target_pairs={{0,64},{8,72},{16,80},{24,88},{32,96},{40,104},{48,112},{56,120},{... | collective-permute-start | bytes 196616 | tf_op jit(solution)/shard_map/gather_features/ppermute | solution.py:264
  14.6 1.7 %collective-permute-done.1 = bf16[128,256]{1,0:T(8,128)(2,1)S(1)} collective-permute-done((bf16[128,256]{1,0:T(8,128)(2,1)S(1)}, bf16[128,256]{1,0:T(8,128)(2,1)S(1)}, u32[]{:S(2)}, u32[]{:S(2)}) %collective-permute-start.1) | collective-permute-done | bytes 65568 | tf_op jit(solution)/shard_map/gather_features/ppermute | solution.py:264
  16.3 9.1 %all_to_all.25 = bf16[4,2,128,256]{3,2,1,0:T(8,128)(2,1)S(1)} all-to-all(bf16[4,2,128,256]{3,2,1,0:T(8,128)(2,1)S(1)} %broadcast_in_dim.8), channel_id=1, replica_groups={{0,16,32,48},{8,24,40,56},{64,80,96,112},{72,88,104,120},{128,144,160,1..., dimensions={0} | all-to-all | bytes 1048576 | tf_op jit(solution)/shard_map/gather_features/all_to_all | solution.py:70
  25.4 3.3 %collective-permute-start.2 = (bf16[1024,256]{1,0:T(8,128)(2,1)S(1)}, bf16[1024,256]{1,0:T(8,128)(2,1)S(1)}, u32[]{:S(2)}, u32[]{:S(2)}) collective-permute-start(bf16[1024,256]{1,0:T(8,128)(2,1)S(1)} %bitcast.28), channel_id=1, source_target_pairs={{0,8},{8,0},{16,24},{24,16},{32,40},{40,32},{48,56},{56,48},{64,72... | collective-permute-start | bytes 1572872 | tf_op jit(solution)/shard_map/gather_features/ppermute | solution.py:66
  28.7 0.0 copy-done.6
  28.7 0.0 copy-done.7
  28.7 0.0 copy-done
  28.7 1.8 %shard_map.120 = (bf16[512,2048]{1,0:T(8,128)(2,1)S(1)}, bf16[2048,512]{1,0:T(8,128)(2,1)S(1)}) custom-call(s32[2]{0:T(128)S(1)} %pad_add_fusion.scalars_ref, s32[48]{0:T(128)S(1)} %bitcast.35, s32[48]{0:T(128)S(1)} %bitcast.36, bf16[48,128,128]{2,1,0:T(8,128)(2,1)S(1)} %bitcast.30), custom_call_target="tpu_custom_call" | custom-call | flops 4194304 | bytes 12582912 | tf_op jit(solution)/shard_map/pallas_call | solution.py:101
  30.5 0.0 collective-permute-done.2.other_ref
  30.5 0.8 shard_map.121
  31.3 0.0 copy-start.1
  31.4 0.0 copy-start.2
  31.4 0.0 copy-start.3
  31.4 0.0 copy-start.4
  31.4 0.0 copy-start.5
  31.4 9.9 %all_to_all.26 = bf16[4,128,256]{2,1,0:T(8,128)(2,1)S(1)} all-to-all(bf16[4,128,256]{2,1,0:T(8,128)(2,1)S(1)} %bitcast.32), channel_id=1, replica_groups={{0,1,2,3},{4,5,6,7},{8,9,10,11},{12,13,14,15},{16,17,18,19},{20,21,22,2..., dimensions={0} | all-to-all | bytes 524288 | tf_op jit(solution)/shard_map/sum_over_y/all_to_all | solution.py:70
  41.4 3.4 %collective-permute-start.3 = (bf16[128,256]{1,0:T(8,128)(2,1)S(1)}, bf16[128,256]{1,0:T(8,128)(2,1)S(1)}, u32[]{:S(2)}, u32[]{:S(2)}) collective-permute-start(bf16[128,256]{1,0:T(8,128)(2,1)S(1)} %fusion), channel_id=1, source_target_pairs={{0,4},{1,5},{2,6},{3,7},{4,0},{5,1},{6,2},{7,3},{8,12},{9,13},{10,... | collective-permute-start | bytes 196616 | tf_op jit(solution)/shard_map/sum_over_h/ppermute | solution.py:273
  44.7 3.8 %collective-permute-done.3 = bf16[128,256]{1,0:T(8,128)(2,1)S(1)} collective-permute-done((bf16[128,256]{1,0:T(8,128)(2,1)S(1)}, bf16[128,256]{1,0:T(8,128)(2,1)S(1)}, u32[]{:S(2)}, u32[]{:S(2)}) %collective-permute-start.3) | collective-permute-done | bytes 65568 | tf_op jit(solution)/shard_map/sum_over_h/ppermute | solution.py:273
  48.6 7.9 %all_to_all.27 = bf16[4,128,256]{2,1,0:T(8,128)(2,1)S(1)} all-to-all(bf16[4,128,256]{2,1,0:T(8,128)(2,1)S(1)} %broadcast_in_dim.9), channel_id=1, replica_groups={{0,1,2,3},{4,5,6,7},{8,9,10,11},{12,13,14,15},{16,17,18,19},{20,21,22,2..., dimensions={0} | all-to-all | bytes 524288 | tf_op jit(solution)/shard_map/gather_over_y/all_to_all | solution.py:70
  56.5 0.0 copy-done.1
  56.5 0.0 copy-done.2
  56.5 0.0 copy-done.3
  56.5 0.0 copy-done.4
  56.5 0.0 copy-done.5
  56.5 1.5 %shard_map.122 = (bf16[512,256]{1,0:T(8,128)(2,1)}, bf16[512,256]{1,0:T(8,128)(2,1)S(1)}, f32[1088,256]{1,0:T(8,128)S(1)}, bf16[1088,256]{1,0:T(8,128)(2,1)S(1)}) custom-call(bf16[512,256]{1,0:T(8,128)(2,1)S(1)} %bitcast.31, s32[4,128]{1,0:T(4,128)S(1)} %bitcast.34, bf16[512,256]{1,0:T(8,128)(2,1)S(1)} %copy-done.2, bf16[512,256]{1,0:T(8,128)(2,1)S(1)} %copy-done.3, ...), custom_call_target="tpu_custom_call" | custom-call | tf_op jit(solution)/shard_map/pallas_call | solution.py:202
  58.0 4.2 %collective-permute-start.4 = (bf16[1088,256]{1,0:T(8,128)(2,1)S(1)}, bf16[1088,256]{1,0:T(8,128)(2,1)S(1)}, u32[]{:S(2)}, u32[]{:S(2)}) collective-permute-start(bf16[1088,256]{1,0:T(8,128)(2,1)S(1)} %get-tuple-element.25), channel_id=1, source_target_pairs={{0,8},{8,0},{16,24},{24,16},{32,40},{40,32},{48,56},{56,48},{64,72... | collective-permute-start | bytes 1671176 | tf_op jit(solution)/shard_map/pair_sum/ppermute | solution.py:66
  62.2 1.6 %collective-permute-done.4 = bf16[1088,256]{1,0:T(8,128)(2,1)S(1)} collective-permute-done((bf16[1088,256]{1,0:T(8,128)(2,1)S(1)}, bf16[1088,256]{1,0:T(8,128)(2,1)S(1)}, u32[]{:S(2)}, u32[]{:S(2)}) %collective-permute-start.4) | collective-permute-done | bytes 557088 | tf_op jit(solution)/shard_map/pair_sum/ppermute | solution.py:66
  63.7 0.1 add_convert_fusion
  64.1 12.9 %all_to_all.28 = bf16[4,320,256]{2,1,0:T(8,128)(2,1)S(1)} all-to-all(bf16[4,320,256]{2,1,0:T(8,128)(2,1)S(1)} %pad_maximum_fusion), channel_id=1, replica_groups={{0,16,32,48},{8,24,40,56},{64,80,96,112},{72,88,104,120},{128,144,160,1..., dimensions={0} | all-to-all | bytes 1310720 | tf_op jit(solution)/shard_map/sum_over_section/all_to_all | solution.py:70
  77.0 0.1 add_convert_fusion.1
  77.1 0.8 collective-permute-start.5
  77.9 2.8 %collective-permute-done.5 = bf16[192,256]{1,0:T(8,128)(2,1)S(1)} collective-permute-done((bf16[192,256]{1,0:T(8,128)(2,1)S(1)}, bf16[192,256]{1,0:T(8,128)(2,1)S(1)}, u32[]{:S(2)}, u32[]{:S(2)}) %collective-permute-start.5) | collective-permute-done | bytes 98336 | tf_op jit(solution)/shard_map/sum_over_section/ppermute | solution.py:293
  80.8 1.1 collective-permute-start.6
  81.9 4.4 %collective-permute-done.6 = bf16[192,256]{1,0:T(8,128)(2,1)S(1)} collective-permute-done((bf16[192,256]{1,0:T(8,128)(2,1)S(1)}, bf16[192,256]{1,0:T(8,128)(2,1)S(1)}, u32[]{:S(2)}, u32[]{:S(2)}) %collective-permute-start.6) | collective-permute-done | bytes 98336 | tf_op jit(solution)/shard_map/sum_over_section/ppermute | solution.py:297
  86.3 3.6 %collective-permute-start.7 = (bf16[128,256]{1,0:T(8,128)(2,1)S(1)}, bf16[128,256]{1,0:T(8,128)(2,1)S(1)}, u32[]{:S(2)}, u32[]{:S(2)}) collective-permute-start(bf16[128,256]{1,0:T(8,128)(2,1)S(1)} %pad_maximum_fusion.6), channel_id=1, source_target_pairs={{0,8},{8,0},{16,24},{24,16},{32,40},{40,32},{48,56},{56,48},{64,72... | collective-permute-start | bytes 196616 | tf_op jit(solution)/shard_map/return_panels/ppermute | solution.py:66
  89.9 0.9 collective-permute-done.7
  90.9 4.1 %collective-permute-start.8 = (bf16[128,256]{1,0:T(8,128)(2,1)S(1)}, bf16[128,256]{1,0:T(8,128)(2,1)S(1)}, u32[]{:S(2)}, u32[]{:S(2)}) collective-permute-start(bf16[128,256]{1,0:T(8,128)(2,1)S(1)} %pad_maximum_fusion.8), channel_id=1, source_target_pairs={{0,2},{1,11},{2,17},{3,26},{4,36},{5,45},{6,55},{7,60},{8,134},{9,... | collective-permute-start | bytes 196616 | tf_op jit(solution)/shard_map/return_panels/ppermute | solution.py:307
  95.0 5.4 %collective-permute-done.8 = bf16[128,256]{1,0:T(8,128)(2,1)S(1)} collective-permute-done((bf16[128,256]{1,0:T(8,128)(2,1)S(1)}, bf16[128,256]{1,0:T(8,128)(2,1)S(1)}, u32[]{:S(2)}, u32[]{:S(2)}) %collective-permute-start.8) | collective-permute-done | bytes 65568 | tf_op jit(solution)/shard_map/return_panels/ppermute | solution.py:307
  100.5 12.4 %all_to_all.29.results_ref = bf16[4,256,256]{2,1,0:T(8,128)(2,1)S(1)} all-to-all(bf16[4,256,256]{2,1,0:T(8,128)(2,1)S(1)} %broadcast_in_dim.11), channel_id=1, replica_groups={{0,1,2,3},{4,5,6,7},{8,9,10,11},{12,13,14,15},{16,17,18,19},{20,21,22,2..., dimensions={0} | all-to-all | bytes 1048576 | tf_op jit(solution)/shard_map/gather_results/all_to_all | solution.py:70
  112.9 1.2 %shard_map.123 = (f32[512,256]{1,0:T(8,128)}, f32[256,256]{1,0:T(8,128)}, f32[256,256]{1,0:T(8,128)}) custom-call(bf16[4,256,256]{2,1,0:T(8,128)(2,1)S(1)} %all_to_all.29.results_ref, bf16[512,256]{1,0:T(8,128)(2,1)S(1)} %get-tuple-element.26.pre_grad_ref, bf16[256,256]{1,0:T(8,128)(2,1)S(1)} %copy-done.1), custom_call_target="tpu_custom_call" | custom-call | tf_op jit(solution)/shard_map/pallas_call | solution.py:237
  (25 shorter events, 0.5 us)
Async XLA Ops:
  0.6 28.1 %copy-start.6 = (s32[1,1,48]{2,1,0:T(1,128)S(1)}, s32[1,1,48]{2,1,0:T(1,128)}, u32[]{:S(2)}) copy-start(s32[1,1,48]{2,1,0:T(1,128)} %param.13) | copy-start | bytes 580
  0.6 28.1 %copy-start.7 = (s32[1,1,48]{2,1,0:T(1,128)S(1)}, s32[1,1,48]{2,1,0:T(1,128)}, u32[]{:S(2)}) copy-start(s32[1,1,48]{2,1,0:T(1,128)} %param.14) | copy-start | bytes 580
  0.7 28.1 %copy-start = (bf16[1,1,48,128,128]{4,3,2,1,0:T(8,128)(2,1)S(1)}, bf16[1,1,48,128,128]{4,3,2,1,0:T(8,128)(2,1)}, u32[]{:S(2)}) copy-start(bf16[1,1,48,128,128]{4,3,2,1,0:T(8,128)(2,1)} %param.12) | copy-start | bytes 4718596
  1.7 11.5 %collective-permute-start = (bf16[128,256]{1,0:T(8,128)(2,1)S(1)}, bf16[128,256]{1,0:T(8,128)(2,1)S(1)}, u32[]{:S(2)}, u32[]{:S(2)}) collective-permute-start(bf16[128,256]{1,0:T(8,128)(2,1)S(1)} %dynamic-slice_bitcast_fusion), channel_id=1, source_target_pairs={{0,32},{4,168},{1,16},{5,152},{2,0},{6,136},{3,48},{7,184},{8,49},... | collective-permute-start | bytes 196616 | tf_op jit(solution)/shard_map/spread_features/ppermute | solution.py:261
  13.2 3.1 %collective-permute-start.1 = (bf16[128,256]{1,0:T(8,128)(2,1)S(1)}, bf16[128,256]{1,0:T(8,128)(2,1)S(1)}, u32[]{:S(2)}, u32[]{:S(2)}) collective-permute-start(bf16[128,256]{1,0:T(8,128)(2,1)S(1)} %collective-permute-done), channel_id=1, source_target_pairs={{0,64},{8,72},{16,80},{24,88},{32,96},{40,104},{48,112},{56,120},{... | collective-permute-start | bytes 196616 | tf_op jit(solution)/shard_map/gather_features/ppermute | solution.py:264
  25.4 5.1 %collective-permute-start.2 = (bf16[1024,256]{1,0:T(8,128)(2,1)S(1)}, bf16[1024,256]{1,0:T(8,128)(2,1)S(1)}, u32[]{:S(2)}, u32[]{:S(2)}) collective-permute-start(bf16[1024,256]{1,0:T(8,128)(2,1)S(1)} %bitcast.28), channel_id=1, source_target_pairs={{0,8},{8,0},{16,24},{24,16},{32,40},{40,32},{48,56},{56,48},{64,72... | collective-permute-start | bytes 1572872 | tf_op jit(solution)/shard_map/gather_features/ppermute | solution.py:66
  31.3 25.1 %copy-start.1 = (bf16[256,256]{1,0:T(8,128)(2,1)S(1)}, bf16[256,256]{1,0:T(8,128)(2,1)}, u32[]{:S(2)}) copy-start(bf16[256,256]{1,0:T(8,128)(2,1)} %w_self_ref.3) | copy-start | bytes 393220
  31.4 25.1 %copy-start.2 = (bf16[512,256]{1,0:T(8,128)(2,1)S(1)}, bf16[512,256]{1,0:T(8,128)(2,1)}, u32[]{:S(2)}) copy-start(bf16[512,256]{1,0:T(8,128)(2,1)} %features_ref.1) | copy-start | bytes 786436
  31.4 25.1 %copy-start.3 = (bf16[512,256]{1,0:T(8,128)(2,1)S(1)}, bf16[512,256]{1,0:T(8,128)(2,1)}, u32[]{:S(2)}) copy-start(bf16[512,256]{1,0:T(8,128)(2,1)} %cotangent_ref.1) | copy-start | bytes 786436
  31.4 25.1 %copy-start.4 = (bf16[256,256]{1,0:T(8,128)(2,1)S(1)}, bf16[256,256]{1,0:T(8,128)(2,1)}, u32[]{:S(2)}) copy-start(bf16[256,256]{1,0:T(8,128)(2,1)} %w_neigh_ref.1) | copy-start | bytes 393220
  31.4 25.1 %copy-start.5 = (s32[512]{0:T(512)S(1)}, s32[512]{0:T(512)}, u32[]{:S(2)}) copy-start(s32[512]{0:T(512)} %param.11) | copy-start | bytes 6148
  41.4 7.1 %collective-permute-start.3 = (bf16[128,256]{1,0:T(8,128)(2,1)S(1)}, bf16[128,256]{1,0:T(8,128)(2,1)S(1)}, u32[]{:S(2)}, u32[]{:S(2)}) collective-permute-start(bf16[128,256]{1,0:T(8,128)(2,1)S(1)} %fusion), channel_id=1, source_target_pairs={{0,4},{1,5},{2,6},{3,7},{4,0},{5,1},{6,2},{7,3},{8,12},{9,13},{10,... | collective-permute-start | bytes 196616 | tf_op jit(solution)/shard_map/sum_over_h/ppermute | solution.py:273
  58.0 5.8 %collective-permute-start.4 = (bf16[1088,256]{1,0:T(8,128)(2,1)S(1)}, bf16[1088,256]{1,0:T(8,128)(2,1)S(1)}, u32[]{:S(2)}, u32[]{:S(2)}) collective-permute-start(bf16[1088,256]{1,0:T(8,128)(2,1)S(1)} %get-tuple-element.25), channel_id=1, source_target_pairs={{0,8},{8,0},{16,24},{24,16},{32,40},{40,32},{48,56},{56,48},{64,72... | collective-permute-start | bytes 1671176 | tf_op jit(solution)/shard_map/pair_sum/ppermute | solution.py:66
  77.1 3.6 %collective-permute-start.5 = (bf16[192,256]{1,0:T(8,128)(2,1)S(1)}, bf16[192,256]{1,0:T(8,128)(2,1)S(1)}, u32[]{:S(2)}, u32[]{:S(2)}) collective-permute-start(bf16[192,256]{1,0:T(8,128)(2,1)S(1)} %pad_maximum_fusion.3), channel_id=1, source_target_pairs={{0,64},{8,72},{16,80},{24,88},{32,96},{40,104},{48,112},{56,120},{... | collective-permute-start | bytes 294920 | tf_op jit(solution)/shard_map/sum_over_section/ppermute | solution.py:293
  80.8 5.5 %collective-permute-start.6 = (bf16[192,256]{1,0:T(8,128)(2,1)S(1)}, bf16[192,256]{1,0:T(8,128)(2,1)S(1)}, u32[]{:S(2)}, u32[]{:S(2)}) collective-permute-start(bf16[192,256]{1,0:T(8,128)(2,1)S(1)} %pad_maximum_fusion.5), channel_id=1, source_target_pairs={{0,128},{8,136},{16,144},{24,152},{32,160},{40,168},{48,176},{56,1... | collective-permute-start | bytes 294920 | tf_op jit(solution)/shard_map/sum_over_section/ppermute | solution.py:297
  86.3 4.5 %collective-permute-start.7 = (bf16[128,256]{1,0:T(8,128)(2,1)S(1)}, bf16[128,256]{1,0:T(8,128)(2,1)S(1)}, u32[]{:S(2)}, u32[]{:S(2)}) collective-permute-start(bf16[128,256]{1,0:T(8,128)(2,1)S(1)} %pad_maximum_fusion.6), channel_id=1, source_target_pairs={{0,8},{8,0},{16,24},{24,16},{32,40},{40,32},{48,56},{56,48},{64,72... | collective-permute-start | bytes 196616 | tf_op jit(solution)/shard_map/return_panels/ppermute | solution.py:66
  90.9 9.5 %collective-permute-start.8 = (bf16[128,256]{1,0:T(8,128)(2,1)S(1)}, bf16[128,256]{1,0:T(8,128)(2,1)S(1)}, u32[]{:S(2)}, u32[]{:S(2)}) collective-permute-start(bf16[128,256]{1,0:T(8,128)(2,1)S(1)} %pad_maximum_fusion.8), channel_id=1, source_target_pairs={{0,2},{1,11},{2,17},{3,26},{4,36},{5,45},{6,55},{7,60},{8,134},{9,... | collective-permute-start | bytes 196616 | tf_op jit(solution)/shard_map/return_panels/ppermute | solution.py:307

commit v7 on v6

--- a/solution.py
+++ b/solution.py
@@ -17,7 +17,7 @@
 CORE_PAIRS = [(s, s ^ 1) for s in range(32)]
 HALF_PAIRS = [(r, r ^ 4) for r in range(8)]
 NEXT_Z = [(s, s ^ 8) for s in range(32)]
-Z_PAIRS = [(s, s ^ 16) for s in range(32)]
+ACROSS = [(s, s ^ 17) for s in range(32)]
 SAME_ZC = [[8 * z + 2 * x + core for x in range(4)] for z in range(4) for core in range(2)]
 SAME_H = [[4 * h + i for i in range(4)] for h in range(2)]
 
@@ -157,7 +157,7 @@
     down,
 ):
     z, _, core, _, y = position()
-    first = core == 0
+    first = core == z // 2
     degree_rows = degrees_ref[...].astype(F32)
     for i in range(4):
         turned = jnp.broadcast_to(degree_rows[i : i + 1, :], (BLOCK, BLOCK)).T
@@ -179,17 +179,18 @@
         lax.dot_general(pre_grad, w_neigh_ref[...], ROWS_T, preferred_element_type=F32)
         / divisor[...]
     ).astype(BF16)
-    for i in range(8):
-        start = pl.multiple_of(((i // 2) ^ z) * 512 + i % 2 * 256, 256)
-        term = jnp.dot(
-            flipped_ref[pl.ds(start, 256), :], down[...], preferred_element_type=F32
-        )
+    panel = z ^ (2 * core)
+    for pair in range(2):
         for part in range(2):
-            rows = pl.ds((2 * i + part) * HALF, HALF)
-            top = term[part * BLOCK : part * BLOCK + HALF]
-            bottom = term[part * BLOCK + HALF : (part + 1) * BLOCK]
-            own_ref[rows, :] = jnp.where(first, top, bottom)
-            other_ref[rows, :] = jnp.where(first, bottom, top).astype(BF16)
+            rows = pl.ds(pair * 512 + part * 256, 256)
+            own_start = pl.multiple_of((panel ^ pair) * 512 + part * 256, 256)
+            other_start = pl.multiple_of((panel ^ 2 ^ pair) * 512 + part * 256, 256)
+            own_ref[rows, :] = jnp.dot(
+                flipped_ref[pl.ds(own_start, 256), :], down[...], preferred_element_type=F32
+            )
+            other_ref[rows, :] = jnp.dot(
+                flipped_ref[pl.ds(other_start, 256), :], down[...], preferred_element_type=F32
+            ).astype(BF16)
     slice_start = pl.multiple_of(y * BLOCK, BLOCK)
     term = lax.dot_general(
         inputs[:, pl.ds(slice_start, BLOCK)], pre_grad, COLS_T, preferred_element_type=F32
@@ -284,29 +285,22 @@
     )
     with jax.named_scope("pair_sum"):
         both = (own + swap_core(other).astype(F32)).astype(BF16)
-        main = both[:1024].reshape(4, 4, HALF, 256).transpose(1, 0, 2, 3).reshape(4, 256, 256)
+        main = both[:1024].reshape(2, 4, BLOCK, 256).transpose(1, 0, 2, 3).reshape(4, 256, 256)
         send = jnp.concatenate([main, spread(both[1024:], 4)], axis=1)
     with jax.named_scope("sum_over_section"):
-        send = add_up(exchange(send, "section", SAME_ZC))
-        main, grad_part = send[:256].reshape(2, 2, HALF, 256), send[256:]
-        kept, sent = main[:, 0].reshape(BLOCK, 256), main[:, 1].reshape(BLOCK, 256)
-        arrived = lax.ppermute(jnp.concatenate([sent, grad_part]), "section", NEXT_Z)
-        pair = jnp.concatenate([kept, grad_part]).astype(F32) + arrived.astype(F32)
-        pair = pair.astype(BF16)
-        turned = jnp.concatenate([pair[HALF:BLOCK], pair[:HALF], pair[BLOCK:]])
-        arrived = lax.ppermute(turned, "section", Z_PAIRS)
-        total = (pair.astype(F32) + arrived.astype(F32)).astype(BF16)
+        total = add_up(exchange(send, "section", SAME_ZC))
+        arrived = lax.ppermute(total[BLOCK:], "section", NEXT_Z)
+        kept = jnp.concatenate([total[:BLOCK], total[256:]])
+        total = (kept.astype(F32) + arrived.astype(F32)).astype(BF16)
+        arrived = lax.ppermute(total, "section", ACROSS)
+        total = (total.astype(F32) + arrived.astype(F32)).astype(BF16)
     with jax.named_scope("return_panels"):
-        first = core == 0
-        kept = jnp.where(first, total[:HALF], total[HALF:BLOCK])
-        given = jnp.where(first, total[HALF:BLOCK], total[:HALF])
-        swapped = swap_core(jnp.concatenate([given, total[BLOCK:]]))
-        kept = jnp.concatenate([kept, total[BLOCK:]])
-        top, bottom = jnp.where(first, kept, swapped), jnp.where(first, swapped, kept)
-        block = jnp.concatenate([top[:HALF], bottom[:HALF]], axis=0)
-        block = lax.ppermute(block, ("section", "rep"), back_pairs())
+        block = lax.ppermute(total[:BLOCK], ("section", "rep"), back_pairs())
+        own_rows, other_rows = total[BLOCK:], swap_core(total[BLOCK:])
     with jax.named_scope("gather_results"):
-        last = jnp.concatenate([block, top[HALF:], bottom[HALF:]], axis=0)
+        first = core == z // 2
+        top, bottom = jnp.where(first, own_rows, other_rows), jnp.where(first, other_rows, own_rows)
+        last = jnp.concatenate([block, top, bottom], axis=0)
         results = exchange(spread(last, 4), "rep", SAME_H)
     feature_grad, grad_self, grad_neigh = finish(results, pre_grad, w_self)
     return (activated, feature_grad, grad_self, grad_neigh)

time: 114 us -> 113 us (level)
  starting transfers between devices: 30.3 us -> 31.7 us
  waiting for transfers between devices: 22.9 us -> 21.7 us
    ppermute x3, starting transfers between devices: 6 us -> 9.43 us  [the longest x1 3.79 us: body(): arrived = lax.ppermute(total, 'section', ACROSS)]
    ppermute x3, starting transfers between devices: 11.1 us -> 8.08 us  [swap_core(): return lax.ppermute(x, 'section', CORE_PAIRS)]
  transfers between devices with their start and end apart: 9 -> 9, of which waited for: 8 -> 7; matrix products, arithmetic and copies ran while one was open for 0% -> 0% of each run, Pallas kernels for 2% -> 1%
where the time goes in v7:
time: 113 us
  blocking collectives  51.3 us (45%)
  starting transfers between devices  31.7 us (28%)
  waiting for transfers between devices  21.7 us (19%)
  Pallas kernels  5.1 us (5%)
  between operations  1.6 us (1%)
  local copies, waits for them, and re-layouts  1.2 us (1%)
    all_to_all x5, blocking collectives, exchange(): return lax.all_to_all(x, axis, 0, 0, tiled=False, axis_index_groups=groups)  51.3 us
    ppermute x1, starting transfers between devices, body(): block = lax.ppermute(block, ('section', 'rep'), out_pairs())  8.39 us
    ppermute x3, starting transfers between devices, swap_core(): return lax.ppermute(x, 'section', CORE_PAIRS)  8.08 us
    ppermute x1, waiting for transfers between devices, body(): block = lax.ppermute(total[:BLOCK], ('section', 'rep'), back_pairs())  5.94 us
    ppermute x1, waiting for transfers between devices, body(): arrived = lax.ppermute(total, 'section', ACROSS)  5.2 us
    ppermute x1, starting transfers between devices, body(): lax.ppermute(partial, 'rep', HALF_PAIRS)  4.3 us
    ppermute x1, starting transfers between devices, body(): arrived = lax.ppermute(total, 'section', ACROSS)  3.79 us
    ppermute x1, starting transfers between devices, body(): block = lax.ppermute(total[:BLOCK], ('section', 'rep'), back_pairs())  3.48 us
  transfers between devices with their start and end apart: 9, of which 7 were waited for; matrix products, arithmetic and copies ran while one was open for 0% of the time, Pallas kernels for 1%

profile of v7, /device:TPU:7, one launch (start us, length us, event | category | flops | bytes accessed | tf_op | source)
XLA Modules:
  0.0 113.0 jit_solution(18412866512890602692)
XLA Ops:
  0.6 0.0 copy-start.6
  0.6 0.0 copy-start.7
  0.7 0.0 copy-start
  0.7 1.0 dynamic-slice_bitcast_fusion
  1.7 8.4 %collective-permute-start = (bf16[128,256]{1,0:T(8,128)(2,1)S(1)}, bf16[128,256]{1,0:T(8,128)(2,1)S(1)}, u32[]{:S(2)}, u32[]{:S(2)}) collective-permute-start(bf16[128,256]{1,0:T(8,128)(2,1)S(1)} %dynamic-slice_bitcast_fusion), channel_id=1, source_target_pairs={{0,32},{4,168},{1,16},{5,152},{2,0},{6,136},{3,48},{7,184},{8,49},... | collective-permute-start | bytes 196616 | tf_op jit(solution)/shard_map/spread_features/ppermute | solution.py:262
  10.7 0.1 pad_add_fusion.scalars_ref
  10.8 2.4 %collective-permute-done = bf16[128,256]{1,0:T(8,128)(2,1)S(1)} collective-permute-done((bf16[128,256]{1,0:T(8,128)(2,1)S(1)}, bf16[128,256]{1,0:T(8,128)(2,1)S(1)}, u32[]{:S(2)}, u32[]{:S(2)}) %collective-permute-start) | collective-permute-done | bytes 65568 | tf_op jit(solution)/shard_map/spread_features/ppermute | solution.py:262
  13.2 1.5 %collective-permute-start.1 = (bf16[128,256]{1,0:T(8,128)(2,1)S(1)}, bf16[128,256]{1,0:T(8,128)(2,1)S(1)}, u32[]{:S(2)}, u32[]{:S(2)}) collective-permute-start(bf16[128,256]{1,0:T(8,128)(2,1)S(1)} %collective-permute-done), channel_id=1, source_target_pairs={{0,64},{8,72},{16,80},{24,88},{32,96},{40,104},{48,112},{56,120},{... | collective-permute-start | bytes 196616 | tf_op jit(solution)/shard_map/gather_features/ppermute | solution.py:265
  14.6 1.7 %collective-permute-done.1 = bf16[128,256]{1,0:T(8,128)(2,1)S(1)} collective-permute-done((bf16[128,256]{1,0:T(8,128)(2,1)S(1)}, bf16[128,256]{1,0:T(8,128)(2,1)S(1)}, u32[]{:S(2)}, u32[]{:S(2)}) %collective-permute-start.1) | collective-permute-done | bytes 65568 | tf_op jit(solution)/shard_map/gather_features/ppermute | solution.py:265
  16.3 9.1 %all_to_all.25 = bf16[4,2,128,256]{3,2,1,0:T(8,128)(2,1)S(1)} all-to-all(bf16[4,2,128,256]{3,2,1,0:T(8,128)(2,1)S(1)} %broadcast_in_dim.8), channel_id=1, replica_groups={{0,16,32,48},{8,24,40,56},{64,80,96,112},{72,88,104,120},{128,144,160,1..., dimensions={0} | all-to-all | bytes 1048576 | tf_op jit(solution)/shard_map/gather_features/all_to_all | solution.py:70
  25.4 3.3 %collective-permute-start.2 = (bf16[1024,256]{1,0:T(8,128)(2,1)S(1)}, bf16[1024,256]{1,0:T(8,128)(2,1)S(1)}, u32[]{:S(2)}, u32[]{:S(2)}) collective-permute-start(bf16[1024,256]{1,0:T(8,128)(2,1)S(1)} %bitcast.29), channel_id=1, source_target_pairs={{0,8},{8,0},{16,24},{24,16},{32,40},{40,32},{48,56},{56,48},{64,72... | collective-permute-start | bytes 1572872 | tf_op jit(solution)/shard_map/gather_features/ppermute | solution.py:66
  28.7 0.0 copy-done.6
  28.7 0.0 copy-done.7
  28.7 0.0 copy-done
  28.7 1.5 %shard_map.120 = (bf16[512,2048]{1,0:T(8,128)(2,1)S(1)}, bf16[2048,512]{1,0:T(8,128)(2,1)S(1)}) custom-call(s32[2]{0:T(128)S(1)} %pad_add_fusion.scalars_ref, s32[48]{0:T(128)S(1)} %bitcast.36, s32[48]{0:T(128)S(1)} %bitcast.37, bf16[48,128,128]{2,1,0:T(8,128)(2,1)S(1)} %bitcast.31), custom_call_target="tpu_custom_call" | custom-call | flops 4194304 | bytes 12582912 | tf_op jit(solution)/shard_map/pallas_call | solution.py:101
  30.3 0.0 collective-permute-done.2.other_ref
  30.3 0.8 shard_map.121
  31.1 0.0 copy-start.1
  31.1 0.0 copy-start.2
  31.1 0.0 copy-start.3
  31.1 0.0 copy-start.4
  31.2 0.0 copy-start.5
  31.2 9.6 %all_to_all.26 = bf16[4,128,256]{2,1,0:T(8,128)(2,1)S(1)} all-to-all(bf16[4,128,256]{2,1,0:T(8,128)(2,1)S(1)} %bitcast.33), channel_id=1, replica_groups={{0,1,2,3},{4,5,6,7},{8,9,10,11},{12,13,14,15},{16,17,18,19},{20,21,22,2..., dimensions={0} | all-to-all | bytes 524288 | tf_op jit(solution)/shard_map/sum_over_y/all_to_all | solution.py:70
  40.8 4.3 %collective-permute-start.3 = (bf16[128,256]{1,0:T(8,128)(2,1)S(1)}, bf16[128,256]{1,0:T(8,128)(2,1)S(1)}, u32[]{:S(2)}, u32[]{:S(2)}) collective-permute-start(bf16[128,256]{1,0:T(8,128)(2,1)S(1)} %fusion), channel_id=1, source_target_pairs={{0,4},{1,5},{2,6},{3,7},{4,0},{5,1},{6,2},{7,3},{8,12},{9,13},{10,... | collective-permute-start | bytes 196616 | tf_op jit(solution)/shard_map/sum_over_h/ppermute | solution.py:274
  45.1 2.9 %collective-permute-done.3 = bf16[128,256]{1,0:T(8,128)(2,1)S(1)} collective-permute-done((bf16[128,256]{1,0:T(8,128)(2,1)S(1)}, bf16[128,256]{1,0:T(8,128)(2,1)S(1)}, u32[]{:S(2)}, u32[]{:S(2)}) %collective-permute-start.3) | collective-permute-done | bytes 65568 | tf_op jit(solution)/shard_map/sum_over_h/ppermute | solution.py:274
  48.1 7.9 %all_to_all.27 = bf16[4,128,256]{2,1,0:T(8,128)(2,1)S(1)} all-to-all(bf16[4,128,256]{2,1,0:T(8,128)(2,1)S(1)} %broadcast_in_dim.9), channel_id=1, replica_groups={{0,1,2,3},{4,5,6,7},{8,9,10,11},{12,13,14,15},{16,17,18,19},{20,21,22,2..., dimensions={0} | all-to-all | bytes 524288 | tf_op jit(solution)/shard_map/gather_over_y/all_to_all | solution.py:70
  56.0 0.0 copy-done.1
  56.0 0.0 copy-done.2
  56.0 0.0 copy-done.3
  56.0 0.0 copy-done.4
  56.0 0.0 copy-done.5
  56.1 1.6 %shard_map.122 = (bf16[512,256]{1,0:T(8,128)(2,1)}, bf16[512,256]{1,0:T(8,128)(2,1)S(1)}, f32[1088,256]{1,0:T(8,128)S(1)}, bf16[1088,256]{1,0:T(8,128)(2,1)S(1)}) custom-call(bf16[512,256]{1,0:T(8,128)(2,1)S(1)} %bitcast.32, s32[4,128]{1,0:T(4,128)S(1)} %bitcast.35, bf16[512,256]{1,0:T(8,128)(2,1)S(1)} %copy-done.2, bf16[512,256]{1,0:T(8,128)(2,1)S(1)} %copy-done.3, ...), custom_call_target="tpu_custom_call" | custom-call | tf_op jit(solution)/shard_map/pallas_call | solution.py:203
  57.7 3.7 %collective-permute-start.4 = (bf16[1088,256]{1,0:T(8,128)(2,1)S(1)}, bf16[1088,256]{1,0:T(8,128)(2,1)S(1)}, u32[]{:S(2)}, u32[]{:S(2)}) collective-permute-start(bf16[1088,256]{1,0:T(8,128)(2,1)S(1)} %get-tuple-element.25), channel_id=1, source_target_pairs={{0,8},{8,0},{16,24},{24,16},{32,40},{40,32},{48,56},{56,48},{64,72... | collective-permute-start | bytes 1671176 | tf_op jit(solution)/shard_map/pair_sum/ppermute | solution.py:66
  61.4 1.6 %collective-permute-done.4 = bf16[1088,256]{1,0:T(8,128)(2,1)S(1)} collective-permute-done((bf16[1088,256]{1,0:T(8,128)(2,1)S(1)}, bf16[1088,256]{1,0:T(8,128)(2,1)S(1)}, u32[]{:S(2)}, u32[]{:S(2)}) %collective-permute-start.4) | collective-permute-done | bytes 557088 | tf_op jit(solution)/shard_map/pair_sum/ppermute | solution.py:66
  63.0 0.1 add_convert_fusion
  63.3 12.6 %all_to_all.28 = bf16[4,320,256]{2,1,0:T(8,128)(2,1)S(1)} all-to-all(bf16[4,320,256]{2,1,0:T(8,128)(2,1)S(1)} %pad_maximum_fusion), channel_id=1, replica_groups={{0,16,32,48},{8,24,40,56},{64,80,96,112},{72,88,104,120},{128,144,160,1..., dimensions={0} | all-to-all | bytes 1310720 | tf_op jit(solution)/shard_map/sum_over_section/all_to_all | solution.py:70
  75.9 0.1 add_convert_fusion.1
  76.0 2.2 %collective-permute-start.5 = (bf16[192,256]{1,0:T(8,128)(2,1)S(1)}, bf16[192,256]{1,0:T(8,128)(2,1)S(1)}, u32[]{:S(2)}, u32[]{:S(2)}) collective-permute-start(bf16[192,256]{1,0:T(8,128)(2,1)S(1)} %slice_bitcast_fusion), channel_id=1, source_target_pairs={{0,64},{8,72},{16,80},{24,88},{32,96},{40,104},{48,112},{56,120},{... | collective-permute-start | bytes 294920 | tf_op jit(solution)/shard_map/sum_over_section/ppermute | solution.py:292
  78.2 2.0 %collective-permute-done.5 = bf16[192,256]{1,0:T(8,128)(2,1)S(1)} collective-permute-done((bf16[192,256]{1,0:T(8,128)(2,1)S(1)}, bf16[192,256]{1,0:T(8,128)(2,1)S(1)}, u32[]{:S(2)}, u32[]{:S(2)}) %collective-permute-start.5) | collective-permute-done | bytes 98336 | tf_op jit(solution)/shard_map/sum_over_section/ppermute | solution.py:292
  80.2 3.8 %collective-permute-start.6 = (bf16[192,256]{1,0:T(8,128)(2,1)S(1)}, bf16[192,256]{1,0:T(8,128)(2,1)S(1)}, u32[]{:S(2)}, u32[]{:S(2)}) collective-permute-start(bf16[192,256]{1,0:T(8,128)(2,1)S(1)} %add_convert_fusion.3), channel_id=1, source_target_pairs={{0,136},{8,128},{16,152},{24,144},{32,168},{40,160},{48,184},{56,1... | collective-permute-start | bytes 294920 | tf_op jit(solution)/shard_map/sum_over_section/ppermute | solution.py:295
  84.0 5.2 %collective-permute-done.6 = bf16[192,256]{1,0:T(8,128)(2,1)S(1)} collective-permute-done((bf16[192,256]{1,0:T(8,128)(2,1)S(1)}, bf16[192,256]{1,0:T(8,128)(2,1)S(1)}, u32[]{:S(2)}, u32[]{:S(2)}) %collective-permute-start.6) | collective-permute-done | bytes 98336 | tf_op jit(solution)/shard_map/sum_over_section/ppermute | solution.py:295
  89.3 1.0 collective-permute-start.8
  90.3 3.5 %collective-permute-start.7 = (bf16[128,256]{1,0:T(8,128)(2,1)S(1)}, bf16[128,256]{1,0:T(8,128)(2,1)S(1)}, u32[]{:S(2)}, u32[]{:S(2)}) collective-permute-start(bf16[128,256]{1,0:T(8,128)(2,1)S(1)} %slice.86), channel_id=1, source_target_pairs={{0,2},{1,11},{2,17},{3,26},{4,36},{5,45},{6,55},{7,60},{8,134},{9,... | collective-permute-start | bytes 196616 | tf_op jit(solution)/shard_map/return_panels/ppermute | solution.py:298
  93.8 0.0 collective-permute-done.8
  93.8 5.9 %collective-permute-done.7 = bf16[128,256]{1,0:T(8,128)(2,1)S(1)} collective-permute-done((bf16[128,256]{1,0:T(8,128)(2,1)S(1)}, bf16[128,256]{1,0:T(8,128)(2,1)S(1)}, u32[]{:S(2)}, u32[]{:S(2)}) %collective-permute-start.7) | collective-permute-done | bytes 65568 | tf_op jit(solution)/shard_map/return_panels/ppermute | solution.py:298
  99.8 12.1 %all_to_all.29.results_ref = bf16[4,256,256]{2,1,0:T(8,128)(2,1)S(1)} all-to-all(bf16[4,256,256]{2,1,0:T(8,128)(2,1)S(1)} %broadcast_in_dim.11), channel_id=1, replica_groups={{0,1,2,3},{4,5,6,7},{8,9,10,11},{12,13,14,15},{16,17,18,19},{20,21,22,2..., dimensions={0} | all-to-all | bytes 1048576 | tf_op jit(solution)/shard_map/gather_results/all_to_all | solution.py:70
  111.9 1.2 %shard_map.123 = (f32[512,256]{1,0:T(8,128)}, f32[256,256]{1,0:T(8,128)}, f32[256,256]{1,0:T(8,128)}) custom-call(bf16[4,256,256]{2,1,0:T(8,128)(2,1)S(1)} %all_to_all.29.results_ref, bf16[512,256]{1,0:T(8,128)(2,1)S(1)} %get-tuple-element.26.pre_grad_ref, bf16[256,256]{1,0:T(8,128)(2,1)S(1)} %copy-done.1), custom_call_target="tpu_custom_call" | custom-call | tf_op jit(solution)/shard_map/pallas_call | solution.py:238
  (20 shorter events, 0.4 us)
Async XLA Ops:
  0.6 28.1 %copy-start.6 = (s32[1,1,48]{2,1,0:T(1,128)S(1)}, s32[1,1,48]{2,1,0:T(1,128)}, u32[]{:S(2)}) copy-start(s32[1,1,48]{2,1,0:T(1,128)} %param.13) | copy-start | bytes 580
  0.6 28.1 %copy-start.7 = (s32[1,1,48]{2,1,0:T(1,128)S(1)}, s32[1,1,48]{2,1,0:T(1,128)}, u32[]{:S(2)}) copy-start(s32[1,1,48]{2,1,0:T(1,128)} %param.14) | copy-start | bytes 580
  0.7 28.1 %copy-start = (bf16[1,1,48,128,128]{4,3,2,1,0:T(8,128)(2,1)S(1)}, bf16[1,1,48,128,128]{4,3,2,1,0:T(8,128)(2,1)}, u32[]{:S(2)}) copy-start(bf16[1,1,48,128,128]{4,3,2,1,0:T(8,128)(2,1)} %param.12) | copy-start | bytes 4718596
  1.7 11.5 %collective-permute-start = (bf16[128,256]{1,0:T(8,128)(2,1)S(1)}, bf16[128,256]{1,0:T(8,128)(2,1)S(1)}, u32[]{:S(2)}, u32[]{:S(2)}) collective-permute-start(bf16[128,256]{1,0:T(8,128)(2,1)S(1)} %dynamic-slice_bitcast_fusion), channel_id=1, source_target_pairs={{0,32},{4,168},{1,16},{5,152},{2,0},{6,136},{3,48},{7,184},{8,49},... | collective-permute-start | bytes 196616 | tf_op jit(solution)/shard_map/spread_features/ppermute | solution.py:262
  13.2 3.1 %collective-permute-start.1 = (bf16[128,256]{1,0:T(8,128)(2,1)S(1)}, bf16[128,256]{1,0:T(8,128)(2,1)S(1)}, u32[]{:S(2)}, u32[]{:S(2)}) collective-permute-start(bf16[128,256]{1,0:T(8,128)(2,1)S(1)} %collective-permute-done), channel_id=1, source_target_pairs={{0,64},{8,72},{16,80},{24,88},{32,96},{40,104},{48,112},{56,120},{... | collective-permute-start | bytes 196616 | tf_op jit(solution)/shard_map/gather_features/ppermute | solution.py:265
  25.4 4.8 %collective-permute-start.2 = (bf16[1024,256]{1,0:T(8,128)(2,1)S(1)}, bf16[1024,256]{1,0:T(8,128)(2,1)S(1)}, u32[]{:S(2)}, u32[]{:S(2)}) collective-permute-start(bf16[1024,256]{1,0:T(8,128)(2,1)S(1)} %bitcast.29), channel_id=1, source_target_pairs={{0,8},{8,0},{16,24},{24,16},{32,40},{40,32},{48,56},{56,48},{64,72... | collective-permute-start | bytes 1572872 | tf_op jit(solution)/shard_map/gather_features/ppermute | solution.py:66
  31.1 24.9 %copy-start.1 = (bf16[256,256]{1,0:T(8,128)(2,1)S(1)}, bf16[256,256]{1,0:T(8,128)(2,1)}, u32[]{:S(2)}) copy-start(bf16[256,256]{1,0:T(8,128)(2,1)} %w_self_ref.3) | copy-start | bytes 393220
  31.1 24.9 %copy-start.2 = (bf16[512,256]{1,0:T(8,128)(2,1)S(1)}, bf16[512,256]{1,0:T(8,128)(2,1)}, u32[]{:S(2)}) copy-start(bf16[512,256]{1,0:T(8,128)(2,1)} %features_ref.1) | copy-start | bytes 786436
  31.1 24.9 %copy-start.3 = (bf16[512,256]{1,0:T(8,128)(2,1)S(1)}, bf16[512,256]{1,0:T(8,128)(2,1)}, u32[]{:S(2)}) copy-start(bf16[512,256]{1,0:T(8,128)(2,1)} %cotangent_ref.1) | copy-start | bytes 786436
  31.1 24.9 %copy-start.4 = (bf16[256,256]{1,0:T(8,128)(2,1)S(1)}, bf16[256,256]{1,0:T(8,128)(2,1)}, u32[]{:S(2)}) copy-start(bf16[256,256]{1,0:T(8,128)(2,1)} %w_neigh_ref.1) | copy-start | bytes 393220
  31.2 24.9 %copy-start.5 = (s32[512]{0:T(512)S(1)}, s32[512]{0:T(512)}, u32[]{:S(2)}) copy-start(s32[512]{0:T(512)} %param.11) | copy-start | bytes 6148
  40.8 7.2 %collective-permute-start.3 = (bf16[128,256]{1,0:T(8,128)(2,1)S(1)}, bf16[128,256]{1,0:T(8,128)(2,1)S(1)}, u32[]{:S(2)}, u32[]{:S(2)}) collective-permute-start(bf16[128,256]{1,0:T(8,128)(2,1)S(1)} %fusion), channel_id=1, source_target_pairs={{0,4},{1,5},{2,6},{3,7},{4,0},{5,1},{6,2},{7,3},{8,12},{9,13},{10,... | collective-permute-start | bytes 196616 | tf_op jit(solution)/shard_map/sum_over_h/ppermute | solution.py:274
  57.7 5.3 %collective-permute-start.4 = (bf16[1088,256]{1,0:T(8,128)(2,1)S(1)}, bf16[1088,256]{1,0:T(8,128)(2,1)S(1)}, u32[]{:S(2)}, u32[]{:S(2)}) collective-permute-start(bf16[1088,256]{1,0:T(8,128)(2,1)S(1)} %get-tuple-element.25), channel_id=1, source_target_pairs={{0,8},{8,0},{16,24},{24,16},{32,40},{40,32},{48,56},{56,48},{64,72... | collective-permute-start | bytes 1671176 | tf_op jit(solution)/shard_map/pair_sum/ppermute | solution.py:66
  76.0 4.2 %collective-permute-start.5 = (bf16[192,256]{1,0:T(8,128)(2,1)S(1)}, bf16[192,256]{1,0:T(8,128)(2,1)S(1)}, u32[]{:S(2)}, u32[]{:S(2)}) collective-permute-start(bf16[192,256]{1,0:T(8,128)(2,1)S(1)} %slice_bitcast_fusion), channel_id=1, source_target_pairs={{0,64},{8,72},{16,80},{24,88},{32,96},{40,104},{48,112},{56,120},{... | collective-permute-start | bytes 294920 | tf_op jit(solution)/shard_map/sum_over_section/ppermute | solution.py:292
  80.2 9.0 %collective-permute-start.6 = (bf16[192,256]{1,0:T(8,128)(2,1)S(1)}, bf16[192,256]{1,0:T(8,128)(2,1)S(1)}, u32[]{:S(2)}, u32[]{:S(2)}) collective-permute-start(bf16[192,256]{1,0:T(8,128)(2,1)S(1)} %add_convert_fusion.3), channel_id=1, source_target_pairs={{0,136},{8,128},{16,152},{24,144},{32,168},{40,160},{48,184},{56,1... | collective-permute-start | bytes 294920 | tf_op jit(solution)/shard_map/sum_over_section/ppermute | solution.py:295
  89.3 4.5 %collective-permute-start.8 = (bf16[64,256]{1,0:T(8,128)(2,1)S(1)}, bf16[64,256]{1,0:T(8,128)(2,1)S(1)}, u32[]{:S(2)}, u32[]{:S(2)}) collective-permute-start(bf16[64,256]{1,0:T(8,128)(2,1)S(1)} %slice.87), channel_id=1, source_target_pairs={{0,8},{8,0},{16,24},{24,16},{32,40},{40,32},{48,56},{56,48},{64,72... | collective-permute-start | bytes 98312 | tf_op jit(solution)/shard_map/return_panels/ppermute | solution.py:66
  90.3 9.4 %collective-permute-start.7 = (bf16[128,256]{1,0:T(8,128)(2,1)S(1)}, bf16[128,256]{1,0:T(8,128)(2,1)S(1)}, u32[]{:S(2)}, u32[]{:S(2)}) collective-permute-start(bf16[128,256]{1,0:T(8,128)(2,1)S(1)} %slice.86), channel_id=1, source_target_pairs={{0,2},{1,11},{2,17},{3,26},{4,36},{5,45},{6,55},{7,60},{8,134},{9,... | collective-permute-start | bytes 196616 | tf_op jit(solution)/shard_map/return_panels/ppermute | solution.py:298

commit v8 on v7

--- a/solution.py
+++ b/solution.py
@@ -81,7 +81,7 @@
     return parts[0].astype(BF16)
 
 
-def densify_kernel(scalars_ref, rows_ref, cols_ref, blocks_ref, dense_ref, flipped_ref, total):
+def densify_kernel(scalars_ref, rows_ref, cols_ref, blocks_ref, dense_ref, total):
     total[...] = jnp.zeros_like(total)
 
     def add_slot(slot, carry):
@@ -94,18 +94,14 @@
             tile = total[i, j]
             rows, cols = pl.ds(i * BLOCK, BLOCK), pl.ds(j * BLOCK, BLOCK)
             dense_ref[rows, cols] = tile.astype(BF16)
-            flipped_ref[cols, rows] = tile.T.astype(BF16)
 
 
 def densify(scalars, tiles, rows, cols):
     return pl.pallas_call(
         densify_kernel,
-        out_shape=(
-            jax.ShapeDtypeStruct((512, 2048), BF16),
-            jax.ShapeDtypeStruct((2048, 512), BF16),
-        ),
+        out_shape=jax.ShapeDtypeStruct((512, 2048), BF16),
         in_specs=[SMEM, SMEM, SMEM, VMEM],
-        out_specs=(VMEM, VMEM),
+        out_specs=VMEM,
         scratch_shapes=[pltpu.VMEM((4, 16, BLOCK, BLOCK), F32)],
         compiler_params=pltpu.CompilerParams(vmem_limit_bytes=20 * 1024 * 1024),
         cost_estimate=pl.CostEstimate(flops=2**22, bytes_accessed=12 * 2**20, transcendentals=0),
@@ -140,44 +136,65 @@
     )(dense, own, other)
 
 
+def prepare_kernel(
+    dense_ref, degrees_ref, features_ref, w_self_ref, flipped_ref, scale_ref, base_ref
+):
+    for i in range(4):
+        for j in range(16):
+            rows, cols = pl.ds(i * BLOCK, BLOCK), pl.ds(j * BLOCK, BLOCK)
+            flipped_ref[cols, rows] = dense_ref[rows, cols].astype(F32).T.astype(BF16)
+    inverse = 1.0 / degrees_ref[...].astype(F32)
+    for i in range(4):
+        turned = jnp.broadcast_to(inverse[i : i + 1, :], (BLOCK, BLOCK)).T
+        scale_ref[i * BLOCK : (i + 1) * BLOCK, :] = turned
+    base_ref[...] = jnp.dot(features_ref[...], w_self_ref[...], preferred_element_type=F32)
+
+
+def prepare(dense, degrees, features, w_self):
+    return pl.pallas_call(
+        prepare_kernel,
+        out_shape=(
+            jax.ShapeDtypeStruct((2048, 512), BF16),
+            jax.ShapeDtypeStruct((512, BLOCK), F32),
+            jax.ShapeDtypeStruct((512, 256), F32),
+        ),
+        in_specs=[VMEM] * 4,
+        out_specs=(VMEM,) * 3,
+        compiler_params=pltpu.CompilerParams(vmem_limit_bytes=16 * 1024 * 1024),
+        cost_estimate=pl.CostEstimate(flops=2**27, bytes_accessed=5 * 2**20, transcendentals=0),
+    )(dense, degrees, features, w_self)
+
+
 def middle_kernel(
     pieces_ref,
-    degrees_ref,
+    scale_ref,
+    base_ref,
     features_ref,
     cotangent_ref,
-    w_self_ref,
     w_neigh_ref,
     flipped_ref,
-    activated_ref,
+    preact_ref,
     pre_grad_ref,
     own_ref,
     other_ref,
     inputs,
-    divisor,
     down,
 ):
     z, _, core, _, y = position()
     first = core == z // 2
-    degree_rows = degrees_ref[...].astype(F32)
-    for i in range(4):
-        turned = jnp.broadcast_to(degree_rows[i : i + 1, :], (BLOCK, BLOCK)).T
-        divisor[i * BLOCK : (i + 1) * BLOCK, :BLOCK] = turned
-        divisor[i * BLOCK : (i + 1) * BLOCK, BLOCK:] = turned
-    mean_input = (pieces_ref[...].astype(F32) / divisor[...]).astype(BF16)
-    features = features_ref[...]
-    inputs[:, :256] = features
+    scale = jnp.concatenate([scale_ref[...], scale_ref[...]], axis=1)
+    mean_input = (pieces_ref[...].astype(F32) * scale).astype(BF16)
+    inputs[:, :256] = features_ref[...]
     inputs[:, 256:] = mean_input
-    preact = jnp.dot(features, w_self_ref[...], preferred_element_type=F32) + jnp.dot(
-        mean_input, w_neigh_ref[...], preferred_element_type=F32
-    )
+    preact = base_ref[...] + jnp.dot(mean_input, w_neigh_ref[...], preferred_element_type=F32)
     sigmoid_value = jax.nn.sigmoid(preact)
-    activated_ref[...] = (preact * sigmoid_value).astype(BF16)
+    preact_ref[...] = preact
     slope_value = sigmoid_value * (1.0 + preact * (1.0 - sigmoid_value))
     pre_grad = (cotangent_ref[...].astype(F32) * slope_value).astype(BF16)
     pre_grad_ref[...] = pre_grad
     down[...] = (
         lax.dot_general(pre_grad, w_neigh_ref[...], ROWS_T, preferred_element_type=F32)
-        / divisor[...]
+        * scale
     ).astype(BF16)
     panel = z ^ (2 * core)
     for pair in range(2):
@@ -199,11 +216,11 @@
     other_ref[1024:, :] = jnp.where(first, term[HALF:], term[:HALF]).astype(BF16)
 
 
-def middle(pieces, degrees, features, cotangent, w_self, w_neigh, flipped):
+def middle(*operands):
     return pl.pallas_call(
         middle_kernel,
         out_shape=(
-            jax.ShapeDtypeStruct((512, 256), BF16),
+            jax.ShapeDtypeStruct((512, 256), F32),
             jax.ShapeDtypeStruct((512, 256), BF16),
             jax.ShapeDtypeStruct((1088, 256), F32),
             jax.ShapeDtypeStruct((1088, 256), BF16),
@@ -212,14 +229,29 @@
         out_specs=(VMEM,) * 4,
         scratch_shapes=[
             pltpu.VMEM((512, 512), BF16),
-            pltpu.VMEM((512, 256), F32),
             pltpu.VMEM((512, 256), BF16),
         ],
         compiler_params=pltpu.CompilerParams(vmem_limit_bytes=24 * 1024 * 1024),
-    )(pieces, degrees, features, cotangent, w_self, w_neigh, flipped)
-
-
-def finish_kernel(results_ref, pre_grad_ref, w_self_ref, feature_ref, self_ref, neigh_ref):
+    )(*operands)
+
+
+def activate_kernel(preact_ref, activated_ref):
+    preact = preact_ref[...]
+    activated_ref[...] = (preact * jax.nn.sigmoid(preact)).astype(BF16)
+
+
+def activate(preact):
+    return pl.pallas_call(
+        activate_kernel,
+        out_shape=jax.ShapeDtypeStruct((512, 256), BF16),
+        in_specs=[VMEM],
+        out_specs=VMEM,
+        compiler_params=pltpu.CompilerParams(vmem_limit_bytes=16 * 1024 * 1024),
+        cost_estimate=pl.CostEstimate(flops=2**21, bytes_accessed=2**20, transcendentals=2**17),
+    )(preact)
+
+
+def feature_kernel(results_ref, pre_grad_ref, w_self_ref, feature_ref):
     _, x, core, _, _ = position()
     last = other_end(x, x % 2 * 2 + core, 0)
     self_part = lax.dot_general(
@@ -229,23 +261,41 @@
         rows = slice(block * BLOCK, (block + 1) * BLOCK)
         y = (last + 4 - block) % 4
         feature_ref[rows, :] = self_part[rows] + results_ref[y, :BLOCK, :].astype(F32)
-        target = self_ref if block < 2 else neigh_ref
-        place = block % 2 * BLOCK
-        target[place : place + BLOCK, :] = results_ref[block, BLOCK:].astype(F32)
-
-
-def finish(results, pre_grad, w_self):
-    return pl.pallas_call(
-        finish_kernel,
+
+
+def finish_features(results, pre_grad, w_self):
+    return pl.pallas_call(
+        feature_kernel,
+        out_shape=jax.ShapeDtypeStruct((512, 256), F32),
+        in_specs=[VMEM] * 3,
+        out_specs=VMEM,
+        compiler_params=pltpu.CompilerParams(vmem_limit_bytes=16 * 1024 * 1024),
+        cost_estimate=pl.CostEstimate(flops=2**27, bytes_accessed=2**21, transcendentals=0),
+    )(results, pre_grad, w_self)
+
+
+def grad_kernel(own_ref, other_ref, self_ref, neigh_ref):
+    z, _, core, _, _ = position()
+    first = core == z // 2
+    for y in range(4):
+        own, other = own_ref[y].astype(F32), other_ref[y].astype(F32)
+        target = self_ref if y < 2 else neigh_ref
+        start = y % 2 * BLOCK
+        target[start : start + HALF, :] = jnp.where(first, own, other)
+        target[start + HALF : start + BLOCK, :] = jnp.where(first, other, own)
+
+
+def finish_grads(own, other):
+    return pl.pallas_call(
+        grad_kernel,
         out_shape=(
-            jax.ShapeDtypeStruct((512, 256), F32),
             jax.ShapeDtypeStruct((256, 256), F32),
             jax.ShapeDtypeStruct((256, 256), F32),
         ),
-        in_specs=[VMEM] * 3,
-        out_specs=(VMEM,) * 3,
-        compiler_params=pltpu.CompilerParams(vmem_limit_bytes=16 * 1024 * 1024),
-    )(results, pre_grad, w_self)
+        in_specs=[VMEM] * 2,
+        out_specs=(VMEM,) * 2,
+        compiler_params=pltpu.CompilerParams(vmem_limit_bytes=16 * 1024 * 1024),
+    )(own, other)
 
 
 def body(
@@ -266,22 +316,20 @@
         own_columns = exchange(spread(pair, 4), "section", SAME_ZC).reshape(1024, 256)
         own_columns, row_slots = lax.optimization_barrier((own_columns, block_rows[0, 0]))
         other_columns = swap_core(own_columns)
-    dense, flipped = densify(scalars, blocks[0, 0], row_slots, block_cols[0, 0])
+    dense = densify(scalars, blocks[0, 0], row_slots, block_cols[0, 0])
     partial = forward_product(dense, own_columns, other_columns)
     with jax.named_scope("sum_over_y"):
         partial = add_up(exchange(partial.reshape(4, BLOCK, 256), "rep", SAME_H))
     with jax.named_scope("sum_over_h"):
-        partial = add_up(jnp.stack([partial, lax.ppermute(partial, "rep", HALF_PAIRS)]))
+        partial, degree_rows = lax.optimization_barrier((partial, degrees.reshape(4, BLOCK)))
+        arrived = lax.ppermute(partial, "rep", HALF_PAIRS)
+        flipped, scale, base = prepare(dense, degree_rows, features, w_self)
+        partial = add_up(jnp.stack([partial, arrived]))
     with jax.named_scope("gather_over_y"):
+        partial, flipped = lax.optimization_barrier((partial, flipped))
         pieces = exchange(spread(partial, 4), "rep", SAME_H)
-    activated, pre_grad, own, other = middle(
-        pieces.reshape(512, 256),
-        degrees.reshape(4, BLOCK),
-        features,
-        cotangent,
-        w_self,
-        w_neigh,
-        flipped,
+    preact, pre_grad, own, other = middle(
+        pieces.reshape(512, 256), scale, base, features, cotangent, w_neigh, flipped
     )
     with jax.named_scope("pair_sum"):
         both = (own + swap_core(other).astype(F32)).astype(BF16)
@@ -296,13 +344,15 @@
         total = (total.astype(F32) + arrived.astype(F32)).astype(BF16)
     with jax.named_scope("return_panels"):
         block = lax.ppermute(total[:BLOCK], ("section", "rep"), back_pairs())
-        own_rows, other_rows = total[BLOCK:], swap_core(total[BLOCK:])
+        activated = activate(preact)
+        block, activated = lax.optimization_barrier((block, activated))
     with jax.named_scope("gather_results"):
-        first = core == z // 2
-        top, bottom = jnp.where(first, own_rows, other_rows), jnp.where(first, other_rows, own_rows)
-        last = jnp.concatenate([block, top, bottom], axis=0)
+        last = jnp.concatenate([block, total[BLOCK:]], axis=0)
         results = exchange(spread(last, 4), "rep", SAME_H)
-    feature_grad, grad_self, grad_neigh = finish(results, pre_grad, w_self)
+        own_rows = results[:, BLOCK:]
+        other_rows = swap_core(own_rows)
+    feature_grad = finish_features(results, pre_grad, w_self)
+    grad_self, grad_neigh = finish_grads(own_rows, other_rows)
     return (activated, feature_grad, grad_self, grad_neigh)
 
 

time: 113 us -> 112 us (level)
  the two profiles are of different devices: /device:TPU:7 before, /device:TPU:1 now
where the time goes in v8:
time: 112 us; the launch traced here: 111 us
  blocking collectives  48.8 us (44%)
  starting transfers between devices  29 us (26%)
  waiting for transfers between devices  23.4 us (21%)
  Pallas kernels  7.04 us (6%)
  between operations  1.59 us (1%)
  local copies, waits for them, and re-layouts  1.2 us (1%)
    all_to_all x5, blocking collectives, exchange(): return lax.all_to_all(x, axis, 0, 0, tiled=False, axis_index_groups=groups)  48.8 us
    ppermute x3, starting transfers between devices, swap_core(): return lax.ppermute(x, 'section', CORE_PAIRS)  11.2 us
    ppermute x1, waiting for transfers between devices, body(): block = lax.ppermute(block, ('section', 'rep'), out_pairs())  6.96 us
    ppermute x1, waiting for transfers between devices, body(): arrived = lax.ppermute(total, 'section', ACROSS)  5.36 us
    ppermute x1, starting transfers between devices, body(): block = lax.ppermute(block, ('section', 'rep'), out_pairs())  4.88 us
    ppermute x1, starting transfers between devices, body(): arrived = lax.ppermute(partial, 'rep', HALF_PAIRS)  4.26 us
    ppermute x1, starting transfers between devices, body(): arrived = lax.ppermute(total, 'section', ACROSS)  3.92 us
    ppermute x1, waiting for transfers between devices, body(): block = lax.ppermute(total[:BLOCK], ('section', 'rep'), back_pairs())  2.86 us
  transfers between devices with their start and end apart: 9, of which 7 were waited for; matrix products, arithmetic and copies ran while one was open for 0% of the time, Pallas kernels for 4%

profile of v8, /device:TPU:1, one launch (start us, length us, event | category | flops | bytes accessed | tf_op | source)
XLA Modules:
  0.0 111.5 jit_solution(11160267326905797859)
XLA Ops:
  0.6 0.0 copy-start.6
  0.6 0.0 copy-start.7
  0.7 0.0 copy-start
  0.7 1.0 dynamic-slice_bitcast_fusion
  1.7 4.9 %collective-permute-start = (bf16[128,256]{1,0:T(8,128)(2,1)S(1)}, bf16[128,256]{1,0:T(8,128)(2,1)S(1)}, u32[]{:S(2)}, u32[]{:S(2)}) collective-permute-start(bf16[128,256]{1,0:T(8,128)(2,1)S(1)} %dynamic-slice_bitcast_fusion), channel_id=1, source_target_pairs={{0,32},{4,168},{1,16},{5,152},{2,0},{6,136},{3,48},{7,184},{8,49},... | collective-permute-start | bytes 196616 | tf_op jit(solution)/shard_map/spread_features/ppermute | solution.py:312
  7.2 0.1 pad_add_fusion.scalars_ref
  7.3 7.0 %collective-permute-done = bf16[128,256]{1,0:T(8,128)(2,1)S(1)} collective-permute-done((bf16[128,256]{1,0:T(8,128)(2,1)S(1)}, bf16[128,256]{1,0:T(8,128)(2,1)S(1)}, u32[]{:S(2)}, u32[]{:S(2)}) %collective-permute-start) | collective-permute-done | bytes 65568 | tf_op jit(solution)/shard_map/spread_features/ppermute | solution.py:312
  14.3 1.4 %collective-permute-start.1 = (bf16[128,256]{1,0:T(8,128)(2,1)S(1)}, bf16[128,256]{1,0:T(8,128)(2,1)S(1)}, u32[]{:S(2)}, u32[]{:S(2)}) collective-permute-start(bf16[128,256]{1,0:T(8,128)(2,1)S(1)} %collective-permute-done), channel_id=1, source_target_pairs={{0,64},{8,72},{16,80},{24,88},{32,96},{40,104},{48,112},{56,120},{... | collective-permute-start | bytes 196616 | tf_op jit(solution)/shard_map/gather_features/ppermute | solution.py:315
  15.7 1.7 %collective-permute-done.1 = bf16[128,256]{1,0:T(8,128)(2,1)S(1)} collective-permute-done((bf16[128,256]{1,0:T(8,128)(2,1)S(1)}, bf16[128,256]{1,0:T(8,128)(2,1)S(1)}, u32[]{:S(2)}, u32[]{:S(2)}) %collective-permute-start.1) | collective-permute-done | bytes 65568 | tf_op jit(solution)/shard_map/gather_features/ppermute | solution.py:315
  17.4 10.4 %all_to_all.25 = bf16[4,2,128,256]{3,2,1,0:T(8,128)(2,1)S(1)} all-to-all(bf16[4,2,128,256]{3,2,1,0:T(8,128)(2,1)S(1)} %broadcast_in_dim.8), channel_id=1, replica_groups={{0,16,32,48},{8,24,40,56},{64,80,96,112},{72,88,104,120},{128,144,160,1..., dimensions={0} | all-to-all | bytes 1048576 | tf_op jit(solution)/shard_map/gather_features/all_to_all | solution.py:70
  27.8 3.3 %collective-permute-start.2 = (bf16[1024,256]{1,0:T(8,128)(2,1)S(1)}, bf16[1024,256]{1,0:T(8,128)(2,1)S(1)}, u32[]{:S(2)}, u32[]{:S(2)}) collective-permute-start(bf16[1024,256]{1,0:T(8,128)(2,1)S(1)} %bitcast.27), channel_id=1, source_target_pairs={{0,8},{8,0},{16,24},{24,16},{32,40},{40,32},{48,56},{56,48},{64,72... | collective-permute-start | bytes 1572872 | tf_op jit(solution)/shard_map/gather_features/ppermute | solution.py:66
  31.2 0.0 copy-done.6
  31.2 0.0 copy-done.7
  31.2 0.0 copy-done
  31.2 1.7 %shard_map.120.dense_ref = bf16[512,2048]{1,0:T(8,128)(2,1)S(1)} custom-call(s32[2]{0:T(128)S(1)} %pad_add_fusion.scalars_ref, s32[48]{0:T(128)S(1)} %bitcast.34, s32[48]{0:T(128)S(1)} %bitcast.35, bf16[48,128,128]{2,1,0:T(8,128)(2,1)S(1)} %bitcast.29), custom_call_target="tpu_custom_call" | custom-call | flops 4194304 | bytes 12582912 | tf_op jit(solution)/shard_map/pallas_call | solution.py:100
  32.9 0.0 copy-start.1
  32.9 0.0 copy-start.2
  32.9 0.0 copy-start.5
  32.9 0.0 collective-permute-done.2.other_ref
  32.9 0.8 shard_map.121
  33.8 8.8 %all_to_all.26 = bf16[4,128,256]{2,1,0:T(8,128)(2,1)S(1)} all-to-all(bf16[4,128,256]{2,1,0:T(8,128)(2,1)S(1)} %bitcast.31), channel_id=1, replica_groups={{0,1,2,3},{4,5,6,7},{8,9,10,11},{12,13,14,15},{16,17,18,19},{20,21,22,2..., dimensions={0} | all-to-all | bytes 524288 | tf_op jit(solution)/shard_map/sum_over_y/all_to_all | solution.py:70
  42.6 0.0 copy-start.3
  42.6 0.0 copy-start.4
  42.6 4.3 %collective-permute-start.3 = (bf16[128,256]{1,0:T(8,128)(2,1)S(1)}, bf16[128,256]{1,0:T(8,128)(2,1)S(1)}, u32[]{:S(2)}, u32[]{:S(2)}) collective-permute-start(bf16[128,256]{1,0:T(8,128)(2,1)S(1)} %fusion), channel_id=1, source_target_pairs={{0,4},{1,5},{2,6},{3,7},{4,0},{5,1},{6,2},{7,3},{8,12},{9,13},{10,... | collective-permute-start | bytes 196616 | tf_op jit(solution)/shard_map/sum_over_h/ppermute | solution.py:325
  46.9 0.0 copy-done.1
  46.9 0.0 copy-done.2
  46.9 0.7 sum_over_h.1
  47.6 2.1 %collective-permute-done.3 = bf16[128,256]{1,0:T(8,128)(2,1)S(1)} collective-permute-done((bf16[128,256]{1,0:T(8,128)(2,1)S(1)}, bf16[128,256]{1,0:T(8,128)(2,1)S(1)}, u32[]{:S(2)}, u32[]{:S(2)}) %collective-permute-start.3) | collective-permute-done | bytes 65568 | tf_op jit(solution)/shard_map/sum_over_h/ppermute | solution.py:325
  49.8 7.9 %all_to_all.27 = bf16[4,128,256]{2,1,0:T(8,128)(2,1)S(1)} all-to-all(bf16[4,128,256]{2,1,0:T(8,128)(2,1)S(1)} %broadcast_in_dim.9), channel_id=1, replica_groups={{0,1,2,3},{4,5,6,7},{8,9,10,11},{12,13,14,15},{16,17,18,19},{20,21,22,2..., dimensions={0} | all-to-all | bytes 524288 | tf_op jit(solution)/shard_map/gather_over_y/all_to_all | solution.py:70
  57.7 0.0 copy-done.3
  57.7 1.1 %shard_map.122 = (f32[512,256]{1,0:T(8,128)S(1)}, bf16[512,256]{1,0:T(8,128)(2,1)S(1)}, f32[1088,256]{1,0:T(8,128)S(1)}, bf16[1088,256]{1,0:T(8,128)(2,1)S(1)}) custom-call(bf16[512,256]{1,0:T(8,128)(2,1)S(1)} %bitcast.32, f32[512,128]{1,0:T(8,128)S(1)} %get-tuple-element.31.scale_ref, f32[512,256]{1,0:T(8,128)S(1)} %get-tuple-element.32.base_ref, ...), custom_call_target="tpu_custom_call" | custom-call | tf_op jit(solution)/shard_map/pallas_call | solution.py:220
  58.8 4.2 %collective-permute-start.4 = (bf16[1088,256]{1,0:T(8,128)(2,1)S(1)}, bf16[1088,256]{1,0:T(8,128)(2,1)S(1)}, u32[]{:S(2)}, u32[]{:S(2)}) collective-permute-start(bf16[1088,256]{1,0:T(8,128)(2,1)S(1)} %get-tuple-element.35), channel_id=1, source_target_pairs={{0,8},{8,0},{16,24},{24,16},{32,40},{40,32},{48,56},{56,48},{64,72... | collective-permute-start | bytes 1671176 | tf_op jit(solution)/shard_map/pair_sum/ppermute | solution.py:66
  63.0 1.6 %collective-permute-done.4 = bf16[1088,256]{1,0:T(8,128)(2,1)S(1)} collective-permute-done((bf16[1088,256]{1,0:T(8,128)(2,1)S(1)}, bf16[1088,256]{1,0:T(8,128)(2,1)S(1)}, u32[]{:S(2)}, u32[]{:S(2)}) %collective-permute-start.4) | collective-permute-done | bytes 557088 | tf_op jit(solution)/shard_map/pair_sum/ppermute | solution.py:66
  64.6 0.1 add_convert_fusion
  64.9 13.0 %all_to_all.28 = bf16[4,320,256]{2,1,0:T(8,128)(2,1)S(1)} all-to-all(bf16[4,320,256]{2,1,0:T(8,128)(2,1)S(1)} %pad_maximum_fusion), channel_id=1, replica_groups={{0,16,32,48},{8,24,40,56},{64,80,96,112},{72,88,104,120},{128,144,160,1..., dimensions={0} | all-to-all | bytes 1310720 | tf_op jit(solution)/shard_map/sum_over_section/all_to_all | solution.py:70
  78.0 0.1 add_convert_fusion.1
  78.1 0.7 collective-permute-start.5
  78.8 2.8 %collective-permute-done.5 = bf16[192,256]{1,0:T(8,128)(2,1)S(1)} collective-permute-done((bf16[192,256]{1,0:T(8,128)(2,1)S(1)}, bf16[192,256]{1,0:T(8,128)(2,1)S(1)}, u32[]{:S(2)}, u32[]{:S(2)}) %collective-permute-start.5) | collective-permute-done | bytes 98336 | tf_op jit(solution)/shard_map/sum_over_section/ppermute | solution.py:340
  81.7 3.9 %collective-permute-start.6 = (bf16[192,256]{1,0:T(8,128)(2,1)S(1)}, bf16[192,256]{1,0:T(8,128)(2,1)S(1)}, u32[]{:S(2)}, u32[]{:S(2)}) collective-permute-start(bf16[192,256]{1,0:T(8,128)(2,1)S(1)} %add_convert_fusion.3), channel_id=1, source_target_pairs={{0,136},{8,128},{16,152},{24,144},{32,168},{40,160},{48,184},{56,1... | collective-permute-start | bytes 294920 | tf_op jit(solution)/shard_map/sum_over_section/ppermute | solution.py:343
  85.6 5.4 %collective-permute-done.6 = bf16[192,256]{1,0:T(8,128)(2,1)S(1)} collective-permute-done((bf16[192,256]{1,0:T(8,128)(2,1)S(1)}, bf16[192,256]{1,0:T(8,128)(2,1)S(1)}, u32[]{:S(2)}, u32[]{:S(2)}) %collective-permute-start.6) | collective-permute-done | bytes 98336 | tf_op jit(solution)/shard_map/sum_over_section/ppermute | solution.py:343
  91.0 2.6 %collective-permute-start.7 = (bf16[128,256]{1,0:T(8,128)(2,1)S(1)}, bf16[128,256]{1,0:T(8,128)(2,1)S(1)}, u32[]{:S(2)}, u32[]{:S(2)}) collective-permute-start(bf16[128,256]{1,0:T(8,128)(2,1)S(1)} %slice.89), channel_id=1, source_target_pairs={{0,2},{1,11},{2,17},{3,26},{4,36},{5,45},{6,55},{7,60},{8,134},{9,... | collective-permute-start | bytes 196616 | tf_op jit(solution)/shard_map/return_panels/ppermute | solution.py:346
  93.6 0.8 return_panels.1
  94.4 2.9 %collective-permute-done.7 = bf16[128,256]{1,0:T(8,128)(2,1)S(1)} collective-permute-done((bf16[128,256]{1,0:T(8,128)(2,1)S(1)}, bf16[128,256]{1,0:T(8,128)(2,1)S(1)}, u32[]{:S(2)}, u32[]{:S(2)}) %collective-permute-start.7) | collective-permute-done | bytes 65568 | tf_op jit(solution)/shard_map/return_panels/ppermute | solution.py:346
  97.3 8.6 %all_to_all.29.results_ref = bf16[4,192,256]{2,1,0:T(8,128)(2,1)S(1)} all-to-all(bf16[4,192,256]{2,1,0:T(8,128)(2,1)S(1)} %broadcast_in_dim.11), channel_id=1, replica_groups={{0,1,2,3},{4,5,6,7},{8,9,10,11},{12,13,14,15},{16,17,18,19},{20,21,22,2..., dimensions={0} | all-to-all | bytes 786432 | tf_op jit(solution)/shard_map/gather_results/all_to_all | solution.py:70
  105.9 3.7 %collective-permute-start.8 = (bf16[4,64,256]{2,1,0:T(8,128)(2,1)S(1)}, bf16[4,64,256]{2,1,0:T(8,128)(2,1)S(1)}, u32[]{:S(2)}, u32[]{:S(2)}) collective-permute-start(bf16[4,64,256]{2,1,0:T(8,128)(2,1)S(1)} %slice.91.own_ref), channel_id=1, source_target_pairs={{0,8},{8,0},{16,24},{24,16},{32,40},{40,32},{48,56},{56,48},{64,72... | collective-permute-start | bytes 393224 | tf_op jit(solution)/shard_map/gather_results/ppermute | solution.py:66
  109.6 1.1 shard_map.123
  110.7 0.0 collective-permute-done.8.other_ref
  110.7 0.8 shard_map.124
  (22 shorter events, 0.4 us)
Async XLA Ops:
  0.6 30.5 %copy-start.6 = (s32[1,1,48]{2,1,0:T(1,128)S(1)}, s32[1,1,48]{2,1,0:T(1,128)}, u32[]{:S(2)}) copy-start(s32[1,1,48]{2,1,0:T(1,128)} %param.13) | copy-start | bytes 580
  0.6 30.5 %copy-start.7 = (s32[1,1,48]{2,1,0:T(1,128)S(1)}, s32[1,1,48]{2,1,0:T(1,128)}, u32[]{:S(2)}) copy-start(s32[1,1,48]{2,1,0:T(1,128)} %param.14) | copy-start | bytes 580
  0.7 30.5 %copy-start = (bf16[1,1,48,128,128]{4,3,2,1,0:T(8,128)(2,1)S(1)}, bf16[1,1,48,128,128]{4,3,2,1,0:T(8,128)(2,1)}, u32[]{:S(2)}) copy-start(bf16[1,1,48,128,128]{4,3,2,1,0:T(8,128)(2,1)} %param.12) | copy-start | bytes 4718596
  1.7 12.6 %collective-permute-start = (bf16[128,256]{1,0:T(8,128)(2,1)S(1)}, bf16[128,256]{1,0:T(8,128)(2,1)S(1)}, u32[]{:S(2)}, u32[]{:S(2)}) collective-permute-start(bf16[128,256]{1,0:T(8,128)(2,1)S(1)} %dynamic-slice_bitcast_fusion), channel_id=1, source_target_pairs={{0,32},{4,168},{1,16},{5,152},{2,0},{6,136},{3,48},{7,184},{8,49},... | collective-permute-start | bytes 196616 | tf_op jit(solution)/shard_map/spread_features/ppermute | solution.py:312
  14.3 3.1 %collective-permute-start.1 = (bf16[128,256]{1,0:T(8,128)(2,1)S(1)}, bf16[128,256]{1,0:T(8,128)(2,1)S(1)}, u32[]{:S(2)}, u32[]{:S(2)}) collective-permute-start(bf16[128,256]{1,0:T(8,128)(2,1)S(1)} %collective-permute-done), channel_id=1, source_target_pairs={{0,64},{8,72},{16,80},{24,88},{32,96},{40,104},{48,112},{56,120},{... | collective-permute-start | bytes 196616 | tf_op jit(solution)/shard_map/gather_features/ppermute | solution.py:315
  27.8 5.1 %collective-permute-start.2 = (bf16[1024,256]{1,0:T(8,128)(2,1)S(1)}, bf16[1024,256]{1,0:T(8,128)(2,1)S(1)}, u32[]{:S(2)}, u32[]{:S(2)}) collective-permute-start(bf16[1024,256]{1,0:T(8,128)(2,1)S(1)} %bitcast.27), channel_id=1, source_target_pairs={{0,8},{8,0},{16,24},{24,16},{32,40},{40,32},{48,56},{56,48},{64,72... | collective-permute-start | bytes 1572872 | tf_op jit(solution)/shard_map/gather_features/ppermute | solution.py:66
  32.9 14.0 %copy-start.1 = (bf16[512,256]{1,0:T(8,128)(2,1)S(1)}, bf16[512,256]{1,0:T(8,128)(2,1)}, u32[]{:S(2)}) copy-start(bf16[512,256]{1,0:T(8,128)(2,1)} %features_ref.3) | copy-start | bytes 786436
  32.9 14.0 %copy-start.2 = (bf16[256,256]{1,0:T(8,128)(2,1)S(1)}, bf16[256,256]{1,0:T(8,128)(2,1)}, u32[]{:S(2)}) copy-start(bf16[256,256]{1,0:T(8,128)(2,1)} %w_self_ref.3) | copy-start | bytes 393220
  32.9 13.9 %copy-start.5 = (s32[512]{0:T(512)S(1)}, s32[512]{0:T(512)}, u32[]{:S(2)}) copy-start(s32[512]{0:T(512)} %param.11) | copy-start | bytes 6148
  42.6 15.1 %copy-start.3 = (bf16[512,256]{1,0:T(8,128)(2,1)S(1)}, bf16[512,256]{1,0:T(8,128)(2,1)}, u32[]{:S(2)}) copy-start(bf16[512,256]{1,0:T(8,128)(2,1)} %cotangent_ref.1) | copy-start | bytes 786436
  42.6 15.1 %copy-start.4 = (bf16[256,256]{1,0:T(8,128)(2,1)S(1)}, bf16[256,256]{1,0:T(8,128)(2,1)}, u32[]{:S(2)}) copy-start(bf16[256,256]{1,0:T(8,128)(2,1)} %w_neigh_ref.1) | copy-start | bytes 393220
  42.6 7.1 %collective-permute-start.3 = (bf16[128,256]{1,0:T(8,128)(2,1)S(1)}, bf16[128,256]{1,0:T(8,128)(2,1)S(1)}, u32[]{:S(2)}, u32[]{:S(2)}) collective-permute-start(bf16[128,256]{1,0:T(8,128)(2,1)S(1)} %fusion), channel_id=1, source_target_pairs={{0,4},{1,5},{2,6},{3,7},{4,0},{5,1},{6,2},{7,3},{8,12},{9,13},{10,... | collective-permute-start | bytes 196616 | tf_op jit(solution)/shard_map/sum_over_h/ppermute | solution.py:325
  58.8 5.8 %collective-permute-start.4 = (bf16[1088,256]{1,0:T(8,128)(2,1)S(1)}, bf16[1088,256]{1,0:T(8,128)(2,1)S(1)}, u32[]{:S(2)}, u32[]{:S(2)}) collective-permute-start(bf16[1088,256]{1,0:T(8,128)(2,1)S(1)} %get-tuple-element.35), channel_id=1, source_target_pairs={{0,8},{8,0},{16,24},{24,16},{32,40},{40,32},{48,56},{56,48},{64,72... | collective-permute-start | bytes 1671176 | tf_op jit(solution)/shard_map/pair_sum/ppermute | solution.py:66
  78.1 3.6 %collective-permute-start.5 = (bf16[192,256]{1,0:T(8,128)(2,1)S(1)}, bf16[192,256]{1,0:T(8,128)(2,1)S(1)}, u32[]{:S(2)}, u32[]{:S(2)}) collective-permute-start(bf16[192,256]{1,0:T(8,128)(2,1)S(1)} %slice_bitcast_fusion), channel_id=1, source_target_pairs={{0,64},{8,72},{16,80},{24,88},{32,96},{40,104},{48,112},{56,120},{... | collective-permute-start | bytes 294920 | tf_op jit(solution)/shard_map/sum_over_section/ppermute | solution.py:340
  81.7 9.3 %collective-permute-start.6 = (bf16[192,256]{1,0:T(8,128)(2,1)S(1)}, bf16[192,256]{1,0:T(8,128)(2,1)S(1)}, u32[]{:S(2)}, u32[]{:S(2)}) collective-permute-start(bf16[192,256]{1,0:T(8,128)(2,1)S(1)} %add_convert_fusion.3), channel_id=1, source_target_pairs={{0,136},{8,128},{16,152},{24,144},{32,168},{40,160},{48,184},{56,1... | collective-permute-start | bytes 294920 | tf_op jit(solution)/shard_map/sum_over_section/ppermute | solution.py:343
  91.0 6.2 %collective-permute-start.7 = (bf16[128,256]{1,0:T(8,128)(2,1)S(1)}, bf16[128,256]{1,0:T(8,128)(2,1)S(1)}, u32[]{:S(2)}, u32[]{:S(2)}) collective-permute-start(bf16[128,256]{1,0:T(8,128)(2,1)S(1)} %slice.89), channel_id=1, source_target_pairs={{0,2},{1,11},{2,17},{3,26},{4,36},{5,45},{6,55},{7,60},{8,134},{9,... | collective-permute-start | bytes 196616 | tf_op jit(solution)/shard_map/return_panels/ppermute | solution.py:346
  105.9 4.7 %collective-permute-start.8 = (bf16[4,64,256]{2,1,0:T(8,128)(2,1)S(1)}, bf16[4,64,256]{2,1,0:T(8,128)(2,1)S(1)}, u32[]{:S(2)}, u32[]{:S(2)}) collective-permute-start(bf16[4,64,256]{2,1,0:T(8,128)(2,1)S(1)} %slice.91.own_ref), channel_id=1, source_target_pairs={{0,8},{8,0},{16,24},{24,16},{32,40},{40,32},{48,56},{56,48},{64,72... | collective-permute-start | bytes 393224 | tf_op jit(solution)/shard_map/gather_results/ppermute | solution.py:66

commit v9 on v8

--- a/solution.py
+++ b/solution.py
@@ -137,7 +137,14 @@
 
 
 def prepare_kernel(
-    dense_ref, degrees_ref, features_ref, w_self_ref, flipped_ref, scale_ref, base_ref
+    dense_ref,
+    degrees_ref,
+    features_ref,
+    w_self_ref,
+    flipped_ref,
+    scale_ref,
+    chunk_scale_ref,
+    base_ref,
 ):
     for i in range(4):
         for j in range(16):
@@ -147,6 +154,9 @@
     for i in range(4):
         turned = jnp.broadcast_to(inverse[i : i + 1, :], (BLOCK, BLOCK)).T
         scale_ref[i * BLOCK : (i + 1) * BLOCK, :] = turned
+    _, _, _, _, y = position()
+    chunk_scale = scale_ref[pl.ds(pl.multiple_of(y * BLOCK, BLOCK), BLOCK), :]
+    chunk_scale_ref[...] = jnp.concatenate([chunk_scale, chunk_scale], axis=1)
     base_ref[...] = jnp.dot(features_ref[...], w_self_ref[...], preferred_element_type=F32)
 
 
@@ -156,17 +166,46 @@
         out_shape=(
             jax.ShapeDtypeStruct((2048, 512), BF16),
             jax.ShapeDtypeStruct((512, BLOCK), F32),
+            jax.ShapeDtypeStruct((BLOCK, 256), F32),
             jax.ShapeDtypeStruct((512, 256), F32),
         ),
         in_specs=[VMEM] * 4,
-        out_specs=(VMEM,) * 3,
+        out_specs=(VMEM,) * 4,
         compiler_params=pltpu.CompilerParams(vmem_limit_bytes=16 * 1024 * 1024),
         cost_estimate=pl.CostEstimate(flops=2**27, bytes_accessed=5 * 2**20, transcendentals=0),
     )(dense, degrees, features, w_self)
 
 
+def transposed_product(flipped_ref, panel, down_ref, out_ref):
+    for pair in range(2):
+        for part in range(2):
+            start = pl.multiple_of((panel ^ pair) * 512 + part * 256, 256)
+            term = jnp.dot(
+                flipped_ref[pl.ds(start, 256), :], down_ref[...], preferred_element_type=F32
+            ).astype(out_ref.dtype)
+            for x in range(2):
+                place = (4 * part + 2 * x + pair) * BLOCK
+                out_ref[place : place + BLOCK, :] = term[x * BLOCK : (x + 1) * BLOCK]
+
+
+def own_kernel(flipped_ref, down_ref, own_ref):
+    z, _, core, _, _ = position()
+    transposed_product(flipped_ref, z ^ (2 * core), down_ref, own_ref)
+
+
+def own_product(flipped, down):
+    return pl.pallas_call(
+        own_kernel,
+        out_shape=jax.ShapeDtypeStruct((1024, 256), F32),
+        in_specs=[VMEM, VMEM],
+        out_specs=VMEM,
+        compiler_params=pltpu.CompilerParams(vmem_limit_bytes=16 * 1024 * 1024),
+        cost_estimate=pl.CostEstimate(flops=2**28, bytes_accessed=4 * 2**20, transcendentals=0),
+    )(flipped, down)
+
+
 def middle_kernel(
-    pieces_ref,
+    mean_ref,
     scale_ref,
     base_ref,
     features_ref,
@@ -175,15 +214,15 @@
     flipped_ref,
     preact_ref,
     pre_grad_ref,
-    own_ref,
+    down_ref,
+    grad_ref,
     other_ref,
     inputs,
-    down,
 ):
     z, _, core, _, y = position()
     first = core == z // 2
     scale = jnp.concatenate([scale_ref[...], scale_ref[...]], axis=1)
-    mean_input = (pieces_ref[...].astype(F32) * scale).astype(BF16)
+    mean_input = mean_ref[...]
     inputs[:, :256] = features_ref[...]
     inputs[:, 256:] = mean_input
     preact = base_ref[...] + jnp.dot(mean_input, w_neigh_ref[...], preferred_element_type=F32)
@@ -192,27 +231,16 @@
     slope_value = sigmoid_value * (1.0 + preact * (1.0 - sigmoid_value))
     pre_grad = (cotangent_ref[...].astype(F32) * slope_value).astype(BF16)
     pre_grad_ref[...] = pre_grad
-    down[...] = (
+    down_ref[...] = (
         lax.dot_general(pre_grad, w_neigh_ref[...], ROWS_T, preferred_element_type=F32)
         * scale
     ).astype(BF16)
-    panel = z ^ (2 * core)
-    for pair in range(2):
-        for part in range(2):
-            rows = pl.ds(pair * 512 + part * 256, 256)
-            own_start = pl.multiple_of((panel ^ pair) * 512 + part * 256, 256)
-            other_start = pl.multiple_of((panel ^ 2 ^ pair) * 512 + part * 256, 256)
-            own_ref[rows, :] = jnp.dot(
-                flipped_ref[pl.ds(own_start, 256), :], down[...], preferred_element_type=F32
-            )
-            other_ref[rows, :] = jnp.dot(
-                flipped_ref[pl.ds(other_start, 256), :], down[...], preferred_element_type=F32
-            ).astype(BF16)
+    transposed_product(flipped_ref, z ^ (2 * core) ^ 2, down_ref, other_ref)
     slice_start = pl.multiple_of(y * BLOCK, BLOCK)
     term = lax.dot_general(
         inputs[:, pl.ds(slice_start, BLOCK)], pre_grad, COLS_T, preferred_element_type=F32
     )
-    own_ref[1024:, :] = jnp.where(first, term[:HALF], term[HALF:])
+    grad_ref[...] = jnp.where(first, term[:HALF], term[HALF:])
     other_ref[1024:, :] = jnp.where(first, term[HALF:], term[:HALF]).astype(BF16)
 
 
@@ -222,14 +250,14 @@
         out_shape=(
             jax.ShapeDtypeStruct((512, 256), F32),
             jax.ShapeDtypeStruct((512, 256), BF16),
-            jax.ShapeDtypeStruct((1088, 256), F32),
+            jax.ShapeDtypeStruct((512, 256), BF16),
+            jax.ShapeDtypeStruct((HALF, 256), F32),
             jax.ShapeDtypeStruct((1088, 256), BF16),
         ),
         in_specs=[VMEM] * 7,
-        out_specs=(VMEM,) * 4,
+        out_specs=(VMEM,) * 5,
         scratch_shapes=[
             pltpu.VMEM((512, 512), BF16),
-            pltpu.VMEM((512, 256), BF16),
         ],
         compiler_params=pltpu.CompilerParams(vmem_limit_bytes=24 * 1024 * 1024),
     )(*operands)
@@ -323,18 +351,21 @@
     with jax.named_scope("sum_over_h"):
         partial, degree_rows = lax.optimization_barrier((partial, degrees.reshape(4, BLOCK)))
         arrived = lax.ppermute(partial, "rep", HALF_PAIRS)
-        flipped, scale, base = prepare(dense, degree_rows, features, w_self)
-        partial = add_up(jnp.stack([partial, arrived]))
+        flipped, scale, chunk_scale, base = prepare(dense, degree_rows, features, w_self)
+        summed = partial.astype(F32) + arrived.astype(F32)
+        mean_chunk = (summed * chunk_scale).astype(BF16)
     with jax.named_scope("gather_over_y"):
-        partial, flipped = lax.optimization_barrier((partial, flipped))
-        pieces = exchange(spread(partial, 4), "rep", SAME_H)
-    preact, pre_grad, own, other = middle(
-        pieces.reshape(512, 256), scale, base, features, cotangent, w_neigh, flipped
+        mean_chunk, flipped = lax.optimization_barrier((mean_chunk, flipped))
+        mean_input = exchange(spread(mean_chunk, 4), "rep", SAME_H)
+    preact, pre_grad, down, own_grad, other = middle(
+        mean_input.reshape(512, 256), scale, base, features, cotangent, w_neigh, flipped
     )
     with jax.named_scope("pair_sum"):
-        both = (own + swap_core(other).astype(F32)).astype(BF16)
-        main = both[:1024].reshape(2, 4, BLOCK, 256).transpose(1, 0, 2, 3).reshape(4, 256, 256)
-        send = jnp.concatenate([main, spread(both[1024:], 4)], axis=1)
+        arrived = swap_core(other)
+        own = own_product(flipped, down)
+        main = (own + arrived[:1024].astype(F32)).astype(BF16).reshape(4, 256, 256)
+        grad_part = (own_grad + arrived[1024:].astype(F32)).astype(BF16)
+        send = jnp.concatenate([main, spread(grad_part, 4)], axis=1)
     with jax.named_scope("sum_over_section"):
         total = add_up(exchange(send, "section", SAME_ZC))
         arrived = lax.ppermute(total[BLOCK:], "section", NEXT_Z)

time: 112 us -> 112 us (level)
  waiting for transfers between devices: 23.4 us -> 18.2 us
  starting transfers between devices: 29 us -> 33 us
  blocking collectives: 48.8 us -> 50 us
    ppermute x1, starting transfers between devices: 2.61 us -> 5 us  [body(): block = lax.ppermute(total[:BLOCK], ('section', 'rep'), back_pairs())]
    ppermute x1, waiting for transfers between devices: 5.36 us -> 3 us  [body(): arrived = lax.ppermute(total, 'section', ACROSS)]
    ppermute x1, waiting for transfers between devices: 2.86 us -> 0.55 us  [body(): block = lax.ppermute(total[:BLOCK], ('section', 'rep'), back_pairs())]
    ppermute x3, starting transfers between devices: 11.2 us -> 12.8 us  [swap_core(): return lax.ppermute(x, 'section', CORE_PAIRS)]
    all_to_all x5, blocking collectives: 48.8 us -> 50 us  [exchange(): return lax.all_to_all(x, axis, 0, 0, tiled=False, axis_index_groups=groups)]
  transfers between devices with their start and end apart: 9 -> 9, of which waited for: 7 -> 8; matrix products, arithmetic and copies ran while one was open for 0% -> 0% of each run, Pallas kernels for 4% -> 4%
where the time goes in v9:
time: 112 us; the launch traced here: 111 us
  blocking collectives  50 us (45%)
  starting transfers between devices  33 us (29%)
  waiting for transfers between devices  18.2 us (16%)
  Pallas kernels  6.84 us (6%)
  between operations  1.57 us (1%)
  local copies, waits for them, and re-layouts  1.13 us (1%)
    all_to_all x5, blocking collectives, exchange(): return lax.all_to_all(x, axis, 0, 0, tiled=False, axis_index_groups=groups)  50 us
    ppermute x3, starting transfers between devices, swap_core(): return lax.ppermute(x, 'section', CORE_PAIRS)  12.8 us
    ppermute x1, waiting for transfers between devices, body(): block = lax.ppermute(block, ('section', 'rep'), out_pairs())  6.96 us
    ppermute x1, starting transfers between devices, body(): block = lax.ppermute(total[:BLOCK], ('section', 'rep'), back_pairs())  5 us
    ppermute x1, starting transfers between devices, body(): block = lax.ppermute(block, ('section', 'rep'), out_pairs())  4.88 us
    ppermute x1, starting transfers between devices, body(): arrived = lax.ppermute(partial, 'rep', HALF_PAIRS)  4.1 us
    ppermute x1, starting transfers between devices, body(): arrived = lax.ppermute(total, 'section', ACROSS)  3.68 us
    ppermute x1, waiting for transfers between devices, body(): arrived = lax.ppermute(total, 'section', ACROSS)  3 us
  transfers between devices with their start and end apart: 9, of which 8 were waited for; matrix products, arithmetic and copies ran while one was open for 0% of the time, Pallas kernels for 4%

profile of v9, /device:TPU:1, one launch (start us, length us, event | category | flops | bytes accessed | tf_op | source)
XLA Modules:
  0.0 111.2 jit_solution(15044777208261810764)
XLA Ops:
  0.6 0.0 copy-start.6
  0.6 0.0 copy-start.7
  0.7 0.0 copy-start
  0.7 1.0 dynamic-slice_bitcast_fusion
  1.7 4.9 %collective-permute-start = (bf16[128,256]{1,0:T(8,128)(2,1)S(1)}, bf16[128,256]{1,0:T(8,128)(2,1)S(1)}, u32[]{:S(2)}, u32[]{:S(2)}) collective-permute-start(bf16[128,256]{1,0:T(8,128)(2,1)S(1)} %dynamic-slice_bitcast_fusion), channel_id=1, source_target_pairs={{0,32},{4,168},{1,16},{5,152},{2,0},{6,136},{3,48},{7,184},{8,49},... | collective-permute-start | bytes 196616 | tf_op jit(solution)/shard_map/spread_features/ppermute | solution.py:340
  7.2 0.1 pad_add_fusion.scalars_ref
  7.3 7.0 %collective-permute-done = bf16[128,256]{1,0:T(8,128)(2,1)S(1)} collective-permute-done((bf16[128,256]{1,0:T(8,128)(2,1)S(1)}, bf16[128,256]{1,0:T(8,128)(2,1)S(1)}, u32[]{:S(2)}, u32[]{:S(2)}) %collective-permute-start) | collective-permute-done | bytes 65568 | tf_op jit(solution)/shard_map/spread_features/ppermute | solution.py:340
  14.3 1.4 %collective-permute-start.1 = (bf16[128,256]{1,0:T(8,128)(2,1)S(1)}, bf16[128,256]{1,0:T(8,128)(2,1)S(1)}, u32[]{:S(2)}, u32[]{:S(2)}) collective-permute-start(bf16[128,256]{1,0:T(8,128)(2,1)S(1)} %collective-permute-done), channel_id=1, source_target_pairs={{0,64},{8,72},{16,80},{24,88},{32,96},{40,104},{48,112},{56,120},{... | collective-permute-start | bytes 196616 | tf_op jit(solution)/shard_map/gather_features/ppermute | solution.py:343
  15.7 1.7 %collective-permute-done.1 = bf16[128,256]{1,0:T(8,128)(2,1)S(1)} collective-permute-done((bf16[128,256]{1,0:T(8,128)(2,1)S(1)}, bf16[128,256]{1,0:T(8,128)(2,1)S(1)}, u32[]{:S(2)}, u32[]{:S(2)}) %collective-permute-start.1) | collective-permute-done | bytes 65568 | tf_op jit(solution)/shard_map/gather_features/ppermute | solution.py:343
  17.4 10.4 %all_to_all.25 = bf16[4,2,128,256]{3,2,1,0:T(8,128)(2,1)S(1)} all-to-all(bf16[4,2,128,256]{3,2,1,0:T(8,128)(2,1)S(1)} %broadcast_in_dim.8), channel_id=1, replica_groups={{0,16,32,48},{8,24,40,56},{64,80,96,112},{72,88,104,120},{128,144,160,1..., dimensions={0} | all-to-all | bytes 1048576 | tf_op jit(solution)/shard_map/gather_features/all_to_all | solution.py:70
  27.8 3.3 %collective-permute-start.2 = (bf16[1024,256]{1,0:T(8,128)(2,1)S(1)}, bf16[1024,256]{1,0:T(8,128)(2,1)S(1)}, u32[]{:S(2)}, u32[]{:S(2)}) collective-permute-start(bf16[1024,256]{1,0:T(8,128)(2,1)S(1)} %bitcast.24), channel_id=1, source_target_pairs={{0,8},{8,0},{16,24},{24,16},{32,40},{40,32},{48,56},{56,48},{64,72... | collective-permute-start | bytes 1572872 | tf_op jit(solution)/shard_map/gather_features/ppermute | solution.py:66
  31.2 0.0 copy-done.6
  31.2 0.0 copy-done.7
  31.2 0.0 copy-done
  31.2 1.4 %shard_map.120.dense_ref = bf16[512,2048]{1,0:T(8,128)(2,1)S(1)} custom-call(s32[2]{0:T(128)S(1)} %pad_add_fusion.scalars_ref, s32[48]{0:T(128)S(1)} %bitcast.31, s32[48]{0:T(128)S(1)} %bitcast.32, bf16[48,128,128]{2,1,0:T(8,128)(2,1)S(1)} %bitcast.26), custom_call_target="tpu_custom_call" | custom-call | flops 4194304 | bytes 12582912 | tf_op jit(solution)/shard_map/pallas_call | solution.py:100
  32.5 0.0 copy-start.1
  32.6 0.0 copy-start.2
  32.6 0.0 copy-start.5
  32.6 0.1 collective-permute-done.2.other_ref
  32.7 0.8 shard_map.121
  33.5 9.8 %all_to_all.26 = bf16[4,128,256]{2,1,0:T(8,128)(2,1)S(1)} all-to-all(bf16[4,128,256]{2,1,0:T(8,128)(2,1)S(1)} %bitcast.28), channel_id=1, replica_groups={{0,1,2,3},{4,5,6,7},{8,9,10,11},{12,13,14,15},{16,17,18,19},{20,21,22,2..., dimensions={0} | all-to-all | bytes 524288 | tf_op jit(solution)/shard_map/sum_over_y/all_to_all | solution.py:70
  43.3 0.0 copy-start.3
  43.3 0.0 copy-start.4
  43.3 4.1 %collective-permute-start.3 = (bf16[128,256]{1,0:T(8,128)(2,1)S(1)}, bf16[128,256]{1,0:T(8,128)(2,1)S(1)}, u32[]{:S(2)}, u32[]{:S(2)}) collective-permute-start(bf16[128,256]{1,0:T(8,128)(2,1)S(1)} %fusion), channel_id=1, source_target_pairs={{0,4},{1,5},{2,6},{3,7},{4,0},{5,1},{6,2},{7,3},{8,12},{9,13},{10,... | collective-permute-start | bytes 196616 | tf_op jit(solution)/shard_map/sum_over_h/ppermute | solution.py:353
  47.4 0.0 copy-done.1
  47.4 0.0 copy-done.2
  47.5 0.7 sum_over_h.1
  48.2 2.4 %collective-permute-done.3 = bf16[128,256]{1,0:T(8,128)(2,1)S(1)} collective-permute-done((bf16[128,256]{1,0:T(8,128)(2,1)S(1)}, bf16[128,256]{1,0:T(8,128)(2,1)S(1)}, u32[]{:S(2)}, u32[]{:S(2)}) %collective-permute-start.3) | collective-permute-done | bytes 65568 | tf_op jit(solution)/shard_map/sum_over_h/ppermute | solution.py:353
  50.6 7.9 %all_to_all.27 = bf16[4,128,256]{2,1,0:T(8,128)(2,1)S(1)} all-to-all(bf16[4,128,256]{2,1,0:T(8,128)(2,1)S(1)} %broadcast_in_dim.9), channel_id=1, replica_groups={{0,1,2,3},{4,5,6,7},{8,9,10,11},{12,13,14,15},{16,17,18,19},{20,21,22,2..., dimensions={0} | all-to-all | bytes 524288 | tf_op jit(solution)/shard_map/gather_over_y/all_to_all | solution.py:70
  58.5 0.9 shard_map.122
  59.4 3.7 %collective-permute-start.4 = (bf16[1088,256]{1,0:T(8,128)(2,1)S(1)}, bf16[1088,256]{1,0:T(8,128)(2,1)S(1)}, u32[]{:S(2)}, u32[]{:S(2)}) collective-permute-start(bf16[1088,256]{1,0:T(8,128)(2,1)S(1)} %get-tuple-element.38), channel_id=1, source_target_pairs={{0,8},{8,0},{16,24},{24,16},{32,40},{40,32},{48,56},{56,48},{64,72... | collective-permute-start | bytes 1671176 | tf_op jit(solution)/shard_map/pair_sum/ppermute | solution.py:66
  63.1 0.4 pair_sum.1
  63.5 1.1 %collective-permute-done.4 = bf16[1088,256]{1,0:T(8,128)(2,1)S(1)} collective-permute-done((bf16[1088,256]{1,0:T(8,128)(2,1)S(1)}, bf16[1088,256]{1,0:T(8,128)(2,1)S(1)}, u32[]{:S(2)}, u32[]{:S(2)}) %collective-permute-start.4) | collective-permute-done | bytes 557088 | tf_op jit(solution)/shard_map/pair_sum/ppermute | solution.py:66
  64.7 0.1 add_convert_fusion
  64.9 13.0 %all_to_all.28 = bf16[4,320,256]{2,1,0:T(8,128)(2,1)S(1)} all-to-all(bf16[4,320,256]{2,1,0:T(8,128)(2,1)S(1)} %pad_maximum_fusion), channel_id=1, replica_groups={{0,16,32,48},{8,24,40,56},{64,80,96,112},{72,88,104,120},{128,144,160,1..., dimensions={0} | all-to-all | bytes 1310720 | tf_op jit(solution)/shard_map/sum_over_section/all_to_all | solution.py:70
  77.9 0.1 add_convert_fusion.1
  78.0 1.2 %collective-permute-start.5 = (bf16[192,256]{1,0:T(8,128)(2,1)S(1)}, bf16[192,256]{1,0:T(8,128)(2,1)S(1)}, u32[]{:S(2)}, u32[]{:S(2)}) collective-permute-start(bf16[192,256]{1,0:T(8,128)(2,1)S(1)} %slice_bitcast_fusion), channel_id=1, source_target_pairs={{0,64},{8,72},{16,80},{24,88},{32,96},{40,104},{48,112},{56,120},{... | collective-permute-start | bytes 294920 | tf_op jit(solution)/shard_map/sum_over_section/ppermute | solution.py:371
  79.2 2.4 %collective-permute-done.5 = bf16[192,256]{1,0:T(8,128)(2,1)S(1)} collective-permute-done((bf16[192,256]{1,0:T(8,128)(2,1)S(1)}, bf16[192,256]{1,0:T(8,128)(2,1)S(1)}, u32[]{:S(2)}, u32[]{:S(2)}) %collective-permute-start.5) | collective-permute-done | bytes 98336 | tf_op jit(solution)/shard_map/sum_over_section/ppermute | solution.py:371
  81.6 3.7 %collective-permute-start.6 = (bf16[192,256]{1,0:T(8,128)(2,1)S(1)}, bf16[192,256]{1,0:T(8,128)(2,1)S(1)}, u32[]{:S(2)}, u32[]{:S(2)}) collective-permute-start(bf16[192,256]{1,0:T(8,128)(2,1)S(1)} %add_convert_fusion.3), channel_id=1, source_target_pairs={{0,136},{8,128},{16,152},{24,144},{32,168},{40,160},{48,184},{56,1... | collective-permute-start | bytes 294920 | tf_op jit(solution)/shard_map/sum_over_section/ppermute | solution.py:374
  85.3 3.0 %collective-permute-done.6 = bf16[192,256]{1,0:T(8,128)(2,1)S(1)} collective-permute-done((bf16[192,256]{1,0:T(8,128)(2,1)S(1)}, bf16[192,256]{1,0:T(8,128)(2,1)S(1)}, u32[]{:S(2)}, u32[]{:S(2)}) %collective-permute-start.6) | collective-permute-done | bytes 98336 | tf_op jit(solution)/shard_map/sum_over_section/ppermute | solution.py:374
  88.3 5.0 %collective-permute-start.7 = (bf16[128,256]{1,0:T(8,128)(2,1)S(1)}, bf16[128,256]{1,0:T(8,128)(2,1)S(1)}, u32[]{:S(2)}, u32[]{:S(2)}) collective-permute-start(bf16[128,256]{1,0:T(8,128)(2,1)S(1)} %slice.89), channel_id=1, source_target_pairs={{0,2},{1,11},{2,17},{3,26},{4,36},{5,45},{6,55},{7,60},{8,134},{9,... | collective-permute-start | bytes 196616 | tf_op jit(solution)/shard_map/return_panels/ppermute | solution.py:377
  93.3 0.8 return_panels.1
  94.1 0.5 collective-permute-done.7
  94.7 8.8 %all_to_all.29.results_ref = bf16[4,192,256]{2,1,0:T(8,128)(2,1)S(1)} all-to-all(bf16[4,192,256]{2,1,0:T(8,128)(2,1)S(1)} %broadcast_in_dim.11), channel_id=1, replica_groups={{0,1,2,3},{4,5,6,7},{8,9,10,11},{12,13,14,15},{16,17,18,19},{20,21,22,2..., dimensions={0} | all-to-all | bytes 786432 | tf_op jit(solution)/shard_map/gather_results/all_to_all | solution.py:70
  103.5 5.8 %collective-permute-start.8 = (bf16[4,64,256]{2,1,0:T(8,128)(2,1)S(1)}, bf16[4,64,256]{2,1,0:T(8,128)(2,1)S(1)}, u32[]{:S(2)}, u32[]{:S(2)}) collective-permute-start(bf16[4,64,256]{2,1,0:T(8,128)(2,1)S(1)} %slice.91.own_ref), channel_id=1, source_target_pairs={{0,8},{8,0},{16,24},{24,16},{32,40},{40,32},{48,56},{56,48},{64,72... | collective-permute-start | bytes 393224 | tf_op jit(solution)/shard_map/gather_results/ppermute | solution.py:66
  109.3 1.1 shard_map.123
  110.4 0.0 collective-permute-done.8.other_ref
  110.4 0.8 shard_map.124
  (21 shorter events, 0.3 us)
Async XLA Ops:
  0.6 30.5 %copy-start.6 = (s32[1,1,48]{2,1,0:T(1,128)S(1)}, s32[1,1,48]{2,1,0:T(1,128)}, u32[]{:S(2)}) copy-start(s32[1,1,48]{2,1,0:T(1,128)} %param.13) | copy-start | bytes 580
  0.6 30.5 %copy-start.7 = (s32[1,1,48]{2,1,0:T(1,128)S(1)}, s32[1,1,48]{2,1,0:T(1,128)}, u32[]{:S(2)}) copy-start(s32[1,1,48]{2,1,0:T(1,128)} %param.14) | copy-start | bytes 580
  0.7 30.5 %copy-start = (bf16[1,1,48,128,128]{4,3,2,1,0:T(8,128)(2,1)S(1)}, bf16[1,1,48,128,128]{4,3,2,1,0:T(8,128)(2,1)}, u32[]{:S(2)}) copy-start(bf16[1,1,48,128,128]{4,3,2,1,0:T(8,128)(2,1)} %param.12) | copy-start | bytes 4718596
  1.7 12.6 %collective-permute-start = (bf16[128,256]{1,0:T(8,128)(2,1)S(1)}, bf16[128,256]{1,0:T(8,128)(2,1)S(1)}, u32[]{:S(2)}, u32[]{:S(2)}) collective-permute-start(bf16[128,256]{1,0:T(8,128)(2,1)S(1)} %dynamic-slice_bitcast_fusion), channel_id=1, source_target_pairs={{0,32},{4,168},{1,16},{5,152},{2,0},{6,136},{3,48},{7,184},{8,49},... | collective-permute-start | bytes 196616 | tf_op jit(solution)/shard_map/spread_features/ppermute | solution.py:340
  14.3 3.1 %collective-permute-start.1 = (bf16[128,256]{1,0:T(8,128)(2,1)S(1)}, bf16[128,256]{1,0:T(8,128)(2,1)S(1)}, u32[]{:S(2)}, u32[]{:S(2)}) collective-permute-start(bf16[128,256]{1,0:T(8,128)(2,1)S(1)} %collective-permute-done), channel_id=1, source_target_pairs={{0,64},{8,72},{16,80},{24,88},{32,96},{40,104},{48,112},{56,120},{... | collective-permute-start | bytes 196616 | tf_op jit(solution)/shard_map/gather_features/ppermute | solution.py:343
  27.8 4.8 %collective-permute-start.2 = (bf16[1024,256]{1,0:T(8,128)(2,1)S(1)}, bf16[1024,256]{1,0:T(8,128)(2,1)S(1)}, u32[]{:S(2)}, u32[]{:S(2)}) collective-permute-start(bf16[1024,256]{1,0:T(8,128)(2,1)S(1)} %bitcast.24), channel_id=1, source_target_pairs={{0,8},{8,0},{16,24},{24,16},{32,40},{40,32},{48,56},{56,48},{64,72... | collective-permute-start | bytes 1572872 | tf_op jit(solution)/shard_map/gather_features/ppermute | solution.py:66
  32.5 14.9 %copy-start.1 = (bf16[512,256]{1,0:T(8,128)(2,1)S(1)}, bf16[512,256]{1,0:T(8,128)(2,1)}, u32[]{:S(2)}) copy-start(bf16[512,256]{1,0:T(8,128)(2,1)} %features_ref.3) | copy-start | bytes 786436
  32.6 14.9 %copy-start.2 = (bf16[256,256]{1,0:T(8,128)(2,1)S(1)}, bf16[256,256]{1,0:T(8,128)(2,1)}, u32[]{:S(2)}) copy-start(bf16[256,256]{1,0:T(8,128)(2,1)} %w_self_ref.3) | copy-start | bytes 393220
  32.6 14.9 %copy-start.5 = (s32[512]{0:T(512)S(1)}, s32[512]{0:T(512)}, u32[]{:S(2)}) copy-start(s32[512]{0:T(512)} %param.11) | copy-start | bytes 6148
  43.3 15.2 %copy-start.3 = (bf16[512,256]{1,0:T(8,128)(2,1)S(1)}, bf16[512,256]{1,0:T(8,128)(2,1)}, u32[]{:S(2)}) copy-start(bf16[512,256]{1,0:T(8,128)(2,1)} %cotangent_ref.1) | copy-start | bytes 786436
  43.3 15.2 %copy-start.4 = (bf16[256,256]{1,0:T(8,128)(2,1)S(1)}, bf16[256,256]{1,0:T(8,128)(2,1)}, u32[]{:S(2)}) copy-start(bf16[256,256]{1,0:T(8,128)(2,1)} %w_neigh_ref.1) | copy-start | bytes 393220
  43.3 7.2 %collective-permute-start.3 = (bf16[128,256]{1,0:T(8,128)(2,1)S(1)}, bf16[128,256]{1,0:T(8,128)(2,1)S(1)}, u32[]{:S(2)}, u32[]{:S(2)}) collective-permute-start(bf16[128,256]{1,0:T(8,128)(2,1)S(1)} %fusion), channel_id=1, source_target_pairs={{0,4},{1,5},{2,6},{3,7},{4,0},{5,1},{6,2},{7,3},{8,12},{9,13},{10,... | collective-permute-start | bytes 196616 | tf_op jit(solution)/shard_map/sum_over_h/ppermute | solution.py:353
  59.4 5.2 %collective-permute-start.4 = (bf16[1088,256]{1,0:T(8,128)(2,1)S(1)}, bf16[1088,256]{1,0:T(8,128)(2,1)S(1)}, u32[]{:S(2)}, u32[]{:S(2)}) collective-permute-start(bf16[1088,256]{1,0:T(8,128)(2,1)S(1)} %get-tuple-element.38), channel_id=1, source_target_pairs={{0,8},{8,0},{16,24},{24,16},{32,40},{40,32},{48,56},{56,48},{64,72... | collective-permute-start | bytes 1671176 | tf_op jit(solution)/shard_map/pair_sum/ppermute | solution.py:66
  78.0 3.6 %collective-permute-start.5 = (bf16[192,256]{1,0:T(8,128)(2,1)S(1)}, bf16[192,256]{1,0:T(8,128)(2,1)S(1)}, u32[]{:S(2)}, u32[]{:S(2)}) collective-permute-start(bf16[192,256]{1,0:T(8,128)(2,1)S(1)} %slice_bitcast_fusion), channel_id=1, source_target_pairs={{0,64},{8,72},{16,80},{24,88},{32,96},{40,104},{48,112},{56,120},{... | collective-permute-start | bytes 294920 | tf_op jit(solution)/shard_map/sum_over_section/ppermute | solution.py:371
  81.6 6.7 %collective-permute-start.6 = (bf16[192,256]{1,0:T(8,128)(2,1)S(1)}, bf16[192,256]{1,0:T(8,128)(2,1)S(1)}, u32[]{:S(2)}, u32[]{:S(2)}) collective-permute-start(bf16[192,256]{1,0:T(8,128)(2,1)S(1)} %add_convert_fusion.3), channel_id=1, source_target_pairs={{0,136},{8,128},{16,152},{24,144},{32,168},{40,160},{48,184},{56,1... | collective-permute-start | bytes 294920 | tf_op jit(solution)/shard_map/sum_over_section/ppermute | solution.py:374
  88.3 6.3 %collective-permute-start.7 = (bf16[128,256]{1,0:T(8,128)(2,1)S(1)}, bf16[128,256]{1,0:T(8,128)(2,1)S(1)}, u32[]{:S(2)}, u32[]{:S(2)}) collective-permute-start(bf16[128,256]{1,0:T(8,128)(2,1)S(1)} %slice.89), channel_id=1, source_target_pairs={{0,2},{1,11},{2,17},{3,26},{4,36},{5,45},{6,55},{7,60},{8,134},{9,... | collective-permute-start | bytes 196616 | tf_op jit(solution)/shard_map/return_panels/ppermute | solution.py:377
  103.5 6.8 %collective-permute-start.8 = (bf16[4,64,256]{2,1,0:T(8,128)(2,1)S(1)}, bf16[4,64,256]{2,1,0:T(8,128)(2,1)S(1)}, u32[]{:S(2)}, u32[]{:S(2)}) collective-permute-start(bf16[4,64,256]{2,1,0:T(8,128)(2,1)S(1)} %slice.91.own_ref), channel_id=1, source_target_pairs={{0,8},{8,0},{16,24},{24,16},{32,40},{40,32},{48,56},{56,48},{64,72... | collective-permute-start | bytes 393224 | tf_op jit(solution)/shard_map/gather_results/ppermute | solution.py:66

commit v10 on v9

--- a/solution.py
+++ b/solution.py
@@ -17,7 +17,7 @@
 CORE_PAIRS = [(s, s ^ 1) for s in range(32)]
 HALF_PAIRS = [(r, r ^ 4) for r in range(8)]
 NEXT_Z = [(s, s ^ 8) for s in range(32)]
-ACROSS = [(s, s ^ 17) for s in range(32)]
+Z_PAIRS = [(s, s ^ 16) for s in range(32)]
 SAME_ZC = [[8 * z + 2 * x + core for x in range(4)] for z in range(4) for core in range(2)]
 SAME_H = [[4 * h + i for i in range(4)] for h in range(2)]
 
@@ -51,9 +51,9 @@
                         source = (8 * z + 2 * x + core) * 8 + 4 * h + y
                         x_home, core_home = 2 * h + y // 2, y % 2
                         y_to = other_end(x_home, y, x)
-                        z_to = z ^ (2 * core)
-                        target = (8 * z_to + 2 * x_home + core_home) * 8 + 4 * (core ^ h) + y_to
-                        pairs.append((source, target))
+                        away = core ^ (z // 2)
+                        section_to = 8 * (z ^ (2 * away)) + 2 * x_home + core_home
+                        pairs.append((source, section_to * 8 + 4 * (h ^ away) + y_to))
     return pairs
 
 
@@ -190,7 +190,7 @@
 
 def own_kernel(flipped_ref, down_ref, own_ref):
     z, _, core, _, _ = position()
-    transposed_product(flipped_ref, z ^ (2 * core), down_ref, own_ref)
+    transposed_product(flipped_ref, 2 * core + z % 2, down_ref, own_ref)
 
 
 def own_product(flipped, down):
@@ -220,7 +220,7 @@
     inputs,
 ):
     z, _, core, _, y = position()
-    first = core == z // 2
+    first = core == 0
     scale = jnp.concatenate([scale_ref[...], scale_ref[...]], axis=1)
     mean_input = mean_ref[...]
     inputs[:, :256] = features_ref[...]
@@ -235,7 +235,7 @@
         lax.dot_general(pre_grad, w_neigh_ref[...], ROWS_T, preferred_element_type=F32)
         * scale
     ).astype(BF16)
-    transposed_product(flipped_ref, z ^ (2 * core) ^ 2, down_ref, other_ref)
+    transposed_product(flipped_ref, (2 * core + z % 2) ^ 2, down_ref, other_ref)
     slice_start = pl.multiple_of(y * BLOCK, BLOCK)
     term = lax.dot_general(
         inputs[:, pl.ds(slice_start, BLOCK)], pre_grad, COLS_T, preferred_element_type=F32
@@ -303,8 +303,7 @@
 
 
 def grad_kernel(own_ref, other_ref, self_ref, neigh_ref):
-    z, _, core, _, _ = position()
-    first = core == z // 2
+    first = position()[2] == 0
     for y in range(4):
         own, other = own_ref[y].astype(F32), other_ref[y].astype(F32)
         target = self_ref if y < 2 else neigh_ref
@@ -371,7 +370,7 @@
         arrived = lax.ppermute(total[BLOCK:], "section", NEXT_Z)
         kept = jnp.concatenate([total[:BLOCK], total[256:]])
         total = (kept.astype(F32) + arrived.astype(F32)).astype(BF16)
-        arrived = lax.ppermute(total, "section", ACROSS)
+        arrived = lax.ppermute(total, "section", Z_PAIRS)
         total = (total.astype(F32) + arrived.astype(F32)).astype(BF16)
     with jax.named_scope("return_panels"):
         block = lax.ppermute(total[:BLOCK], ("section", "rep"), back_pairs())

time: 112 us -> 111 us (level); the launches traced: 111 us -> 109 us
  waiting for transfers between devices: 18.2 us -> 16.6 us
  blocking collectives: 50 us -> 48.6 us
    ppermute x1, starting transfers between devices: 5 us -> 7.06 us  [body(): block = lax.ppermute(total[:BLOCK], ('section', 'rep'), back_pairs())]
    ppermute x1, starting transfers between devices: 3.68 us -> 2.27 us  [body(): arrived = lax.ppermute(total, 'section', Z_PAIRS)]
    all_to_all x5, blocking collectives: 50 us -> 48.6 us  [exchange(): return lax.all_to_all(x, axis, 0, 0, tiled=False, axis_index_groups=groups)]
    ppermute x3, starting transfers between devices: 12.8 us -> 11.5 us  [swap_core(): return lax.ppermute(x, 'section', CORE_PAIRS)]
    ppermute x1, starting transfers between devices: 1.15 us -> 2.28 us  [body(): arrived = lax.ppermute(total[BLOCK:], 'section', NEXT_Z)]
  transfers between devices with their start and end apart: 9 -> 9, of which waited for: 8 -> 7; matrix products, arithmetic and copies ran while one was open for 0% -> 0% of each run, Pallas kernels for 4% -> 4%
where the time goes in v10:
time: 111 us; the launch traced here: 109 us
  blocking collectives  48.6 us (44%)
  starting transfers between devices  33.7 us (30%)
  waiting for transfers between devices  16.6 us (15%)
  Pallas kernels  6.91 us (6%)
  between operations  1.57 us (1%)
  local copies, waits for them, and re-layouts  1.13 us (1%)
    all_to_all x5, blocking collectives, exchange(): return lax.all_to_all(x, axis, 0, 0, tiled=False, axis_index_groups=groups)  48.6 us
    ppermute x3, starting transfers between devices, swap_core(): return lax.ppermute(x, 'section', CORE_PAIRS)  11.5 us
    ppermute x1, starting transfers between devices, body(): block = lax.ppermute(total[:BLOCK], ('section', 'rep'), back_pairs())  7.06 us
    ppermute x1, waiting for transfers between devices, body(): block = lax.ppermute(block, ('section', 'rep'), out_pairs())  6.96 us
    ppermute x1, starting transfers between devices, body(): block = lax.ppermute(block, ('section', 'rep'), out_pairs())  4.88 us
    ppermute x1, starting transfers between devices, body(): arrived = lax.ppermute(partial, 'rep', HALF_PAIRS)  4.33 us
    ppermute x1, starting transfers between devices, body(): arrived = lax.ppermute(total[BLOCK:], 'section', NEXT_Z)  2.28 us
    ppermute x1, starting transfers between devices, body(): arrived = lax.ppermute(total, 'section', Z_PAIRS)  2.27 us
  transfers between devices with their start and end apart: 9, of which 7 were waited for; matrix products, arithmetic and copies ran while one was open for 0% of the time, Pallas kernels for 4%

profile of v10, /device:TPU:1, one launch (start us, length us, event | category | flops | bytes accessed | tf_op | source)
XLA Modules:
  0.0 109.1 jit_solution(9696504258308316034)
XLA Ops:
  0.6 0.0 copy-start.6
  0.6 0.0 copy-start.7
  0.7 0.0 copy-start
  0.7 1.0 dynamic-slice_bitcast_fusion
  1.7 4.9 %collective-permute-start = (bf16[128,256]{1,0:T(8,128)(2,1)S(1)}, bf16[128,256]{1,0:T(8,128)(2,1)S(1)}, u32[]{:S(2)}, u32[]{:S(2)}) collective-permute-start(bf16[128,256]{1,0:T(8,128)(2,1)S(1)} %dynamic-slice_bitcast_fusion), channel_id=1, source_target_pairs={{0,32},{4,168},{1,16},{5,152},{2,0},{6,136},{3,48},{7,184},{8,49},... | collective-permute-start | bytes 196616 | tf_op jit(solution)/shard_map/spread_features/ppermute | solution.py:339
  7.2 0.1 pad_add_fusion.scalars_ref
  7.3 7.0 %collective-permute-done = bf16[128,256]{1,0:T(8,128)(2,1)S(1)} collective-permute-done((bf16[128,256]{1,0:T(8,128)(2,1)S(1)}, bf16[128,256]{1,0:T(8,128)(2,1)S(1)}, u32[]{:S(2)}, u32[]{:S(2)}) %collective-permute-start) | collective-permute-done | bytes 65568 | tf_op jit(solution)/shard_map/spread_features/ppermute | solution.py:339
  14.3 1.4 %collective-permute-start.1 = (bf16[128,256]{1,0:T(8,128)(2,1)S(1)}, bf16[128,256]{1,0:T(8,128)(2,1)S(1)}, u32[]{:S(2)}, u32[]{:S(2)}) collective-permute-start(bf16[128,256]{1,0:T(8,128)(2,1)S(1)} %collective-permute-done), channel_id=1, source_target_pairs={{0,64},{8,72},{16,80},{24,88},{32,96},{40,104},{48,112},{56,120},{... | collective-permute-start | bytes 196616 | tf_op jit(solution)/shard_map/gather_features/ppermute | solution.py:342
  15.7 1.7 %collective-permute-done.1 = bf16[128,256]{1,0:T(8,128)(2,1)S(1)} collective-permute-done((bf16[128,256]{1,0:T(8,128)(2,1)S(1)}, bf16[128,256]{1,0:T(8,128)(2,1)S(1)}, u32[]{:S(2)}, u32[]{:S(2)}) %collective-permute-start.1) | collective-permute-done | bytes 65568 | tf_op jit(solution)/shard_map/gather_features/ppermute | solution.py:342
  17.4 10.4 %all_to_all.25 = bf16[4,2,128,256]{3,2,1,0:T(8,128)(2,1)S(1)} all-to-all(bf16[4,2,128,256]{3,2,1,0:T(8,128)(2,1)S(1)} %broadcast_in_dim.8), channel_id=1, replica_groups={{0,16,32,48},{8,24,40,56},{64,80,96,112},{72,88,104,120},{128,144,160,1..., dimensions={0} | all-to-all | bytes 1048576 | tf_op jit(solution)/shard_map/gather_features/all_to_all | solution.py:70
  27.8 3.3 %collective-permute-start.2 = (bf16[1024,256]{1,0:T(8,128)(2,1)S(1)}, bf16[1024,256]{1,0:T(8,128)(2,1)S(1)}, u32[]{:S(2)}, u32[]{:S(2)}) collective-permute-start(bf16[1024,256]{1,0:T(8,128)(2,1)S(1)} %bitcast.24), channel_id=1, source_target_pairs={{0,8},{8,0},{16,24},{24,16},{32,40},{40,32},{48,56},{56,48},{64,72... | collective-permute-start | bytes 1572872 | tf_op jit(solution)/shard_map/gather_features/ppermute | solution.py:66
  31.2 0.0 copy-done.6
  31.2 0.0 copy-done.7
  31.2 0.0 copy-done
  31.2 1.4 %shard_map.120.dense_ref = bf16[512,2048]{1,0:T(8,128)(2,1)S(1)} custom-call(s32[2]{0:T(128)S(1)} %pad_add_fusion.scalars_ref, s32[48]{0:T(128)S(1)} %bitcast.31, s32[48]{0:T(128)S(1)} %bitcast.32, bf16[48,128,128]{2,1,0:T(8,128)(2,1)S(1)} %bitcast.26), custom_call_target="tpu_custom_call" | custom-call | flops 4194304 | bytes 12582912 | tf_op jit(solution)/shard_map/pallas_call | solution.py:100
  32.6 0.0 copy-start.1
  32.6 0.0 copy-start.2
  32.6 0.0 copy-start.5
  32.6 0.0 collective-permute-done.2.other_ref
  32.7 0.8 shard_map.121
  33.5 9.0 %all_to_all.26 = bf16[4,128,256]{2,1,0:T(8,128)(2,1)S(1)} all-to-all(bf16[4,128,256]{2,1,0:T(8,128)(2,1)S(1)} %bitcast.28), channel_id=1, replica_groups={{0,1,2,3},{4,5,6,7},{8,9,10,11},{12,13,14,15},{16,17,18,19},{20,21,22,2..., dimensions={0} | all-to-all | bytes 524288 | tf_op jit(solution)/shard_map/sum_over_y/all_to_all | solution.py:70
  42.6 0.0 copy-start.3
  42.6 0.0 copy-start.4
  42.6 4.3 %collective-permute-start.3 = (bf16[128,256]{1,0:T(8,128)(2,1)S(1)}, bf16[128,256]{1,0:T(8,128)(2,1)S(1)}, u32[]{:S(2)}, u32[]{:S(2)}) collective-permute-start(bf16[128,256]{1,0:T(8,128)(2,1)S(1)} %fusion), channel_id=1, source_target_pairs={{0,4},{1,5},{2,6},{3,7},{4,0},{5,1},{6,2},{7,3},{8,12},{9,13},{10,... | collective-permute-start | bytes 196616 | tf_op jit(solution)/shard_map/sum_over_h/ppermute | solution.py:352
  46.9 0.0 copy-done.1
  46.9 0.0 copy-done.5
  46.9 0.7 sum_over_h.1
  47.7 2.1 %collective-permute-done.3 = bf16[128,256]{1,0:T(8,128)(2,1)S(1)} collective-permute-done((bf16[128,256]{1,0:T(8,128)(2,1)S(1)}, bf16[128,256]{1,0:T(8,128)(2,1)S(1)}, u32[]{:S(2)}, u32[]{:S(2)}) %collective-permute-start.3) | collective-permute-done | bytes 65568 | tf_op jit(solution)/shard_map/sum_over_h/ppermute | solution.py:352
  49.8 7.9 %all_to_all.27 = bf16[4,128,256]{2,1,0:T(8,128)(2,1)S(1)} all-to-all(bf16[4,128,256]{2,1,0:T(8,128)(2,1)S(1)} %broadcast_in_dim.9), channel_id=1, replica_groups={{0,1,2,3},{4,5,6,7},{8,9,10,11},{12,13,14,15},{16,17,18,19},{20,21,22,2..., dimensions={0} | all-to-all | bytes 524288 | tf_op jit(solution)/shard_map/gather_over_y/all_to_all | solution.py:70
  57.7 0.9 shard_map.122
  58.6 4.2 %collective-permute-start.4 = (bf16[1088,256]{1,0:T(8,128)(2,1)S(1)}, bf16[1088,256]{1,0:T(8,128)(2,1)S(1)}, u32[]{:S(2)}, u32[]{:S(2)}) collective-permute-start(bf16[1088,256]{1,0:T(8,128)(2,1)S(1)} %get-tuple-element.38), channel_id=1, source_target_pairs={{0,8},{8,0},{16,24},{24,16},{32,40},{40,32},{48,56},{56,48},{64,72... | collective-permute-start | bytes 1671176 | tf_op jit(solution)/shard_map/pair_sum/ppermute | solution.py:66
  62.8 0.4 pair_sum.1
  63.2 1.1 %collective-permute-done.4 = bf16[1088,256]{1,0:T(8,128)(2,1)S(1)} collective-permute-done((bf16[1088,256]{1,0:T(8,128)(2,1)S(1)}, bf16[1088,256]{1,0:T(8,128)(2,1)S(1)}, u32[]{:S(2)}, u32[]{:S(2)}) %collective-permute-start.4) | collective-permute-done | bytes 557088 | tf_op jit(solution)/shard_map/pair_sum/ppermute | solution.py:66
  64.4 0.1 add_convert_fusion
  64.6 12.5 %all_to_all.28 = bf16[4,320,256]{2,1,0:T(8,128)(2,1)S(1)} all-to-all(bf16[4,320,256]{2,1,0:T(8,128)(2,1)S(1)} %pad_maximum_fusion), channel_id=1, replica_groups={{0,16,32,48},{8,24,40,56},{64,80,96,112},{72,88,104,120},{128,144,160,1..., dimensions={0} | all-to-all | bytes 1310720 | tf_op jit(solution)/shard_map/sum_over_section/all_to_all | solution.py:70
  77.0 0.1 add_convert_fusion.1
  77.1 2.3 %collective-permute-start.5 = (bf16[192,256]{1,0:T(8,128)(2,1)S(1)}, bf16[192,256]{1,0:T(8,128)(2,1)S(1)}, u32[]{:S(2)}, u32[]{:S(2)}) collective-permute-start(bf16[192,256]{1,0:T(8,128)(2,1)S(1)} %slice_bitcast_fusion), channel_id=1, source_target_pairs={{0,64},{8,72},{16,80},{24,88},{32,96},{40,104},{48,112},{56,120},{... | collective-permute-start | bytes 294920 | tf_op jit(solution)/shard_map/sum_over_section/ppermute | solution.py:370
  79.4 2.0 %collective-permute-done.5 = bf16[192,256]{1,0:T(8,128)(2,1)S(1)} collective-permute-done((bf16[192,256]{1,0:T(8,128)(2,1)S(1)}, bf16[192,256]{1,0:T(8,128)(2,1)S(1)}, u32[]{:S(2)}, u32[]{:S(2)}) %collective-permute-start.5) | collective-permute-done | bytes 98336 | tf_op jit(solution)/shard_map/sum_over_section/ppermute | solution.py:370
  81.5 2.3 %collective-permute-start.6 = (bf16[192,256]{1,0:T(8,128)(2,1)S(1)}, bf16[192,256]{1,0:T(8,128)(2,1)S(1)}, u32[]{:S(2)}, u32[]{:S(2)}) collective-permute-start(bf16[192,256]{1,0:T(8,128)(2,1)S(1)} %add_convert_fusion.3), channel_id=1, source_target_pairs={{0,128},{8,136},{16,144},{24,152},{32,160},{40,168},{48,176},{56,1... | collective-permute-start | bytes 294920 | tf_op jit(solution)/shard_map/sum_over_section/ppermute | solution.py:373
  83.7 2.2 %collective-permute-done.6 = bf16[192,256]{1,0:T(8,128)(2,1)S(1)} collective-permute-done((bf16[192,256]{1,0:T(8,128)(2,1)S(1)}, bf16[192,256]{1,0:T(8,128)(2,1)S(1)}, u32[]{:S(2)}, u32[]{:S(2)}) %collective-permute-start.6) | collective-permute-done | bytes 98336 | tf_op jit(solution)/shard_map/sum_over_section/ppermute | solution.py:373
  86.0 7.1 %collective-permute-start.7 = (bf16[128,256]{1,0:T(8,128)(2,1)S(1)}, bf16[128,256]{1,0:T(8,128)(2,1)S(1)}, u32[]{:S(2)}, u32[]{:S(2)}) collective-permute-start(bf16[128,256]{1,0:T(8,128)(2,1)S(1)} %slice.89), channel_id=1, source_target_pairs={{0,2},{1,11},{2,17},{3,26},{4,36},{5,45},{6,55},{7,60},{8,134},{9,... | collective-permute-start | bytes 196616 | tf_op jit(solution)/shard_map/return_panels/ppermute | solution.py:376
  93.0 0.8 return_panels.1
  93.8 0.5 collective-permute-done.7
  94.4 8.8 %all_to_all.29.results_ref = bf16[4,192,256]{2,1,0:T(8,128)(2,1)S(1)} all-to-all(bf16[4,192,256]{2,1,0:T(8,128)(2,1)S(1)} %broadcast_in_dim.11), channel_id=1, replica_groups={{0,1,2,3},{4,5,6,7},{8,9,10,11},{12,13,14,15},{16,17,18,19},{20,21,22,2..., dimensions={0} | all-to-all | bytes 786432 | tf_op jit(solution)/shard_map/gather_results/all_to_all | solution.py:70
  103.2 3.9 %collective-permute-start.8 = (bf16[4,64,256]{2,1,0:T(8,128)(2,1)S(1)}, bf16[4,64,256]{2,1,0:T(8,128)(2,1)S(1)}, u32[]{:S(2)}, u32[]{:S(2)}) collective-permute-start(bf16[4,64,256]{2,1,0:T(8,128)(2,1)S(1)} %slice.91.own_ref), channel_id=1, source_target_pairs={{0,8},{8,0},{16,24},{24,16},{32,40},{40,32},{48,56},{56,48},{64,72... | collective-permute-start | bytes 393224 | tf_op jit(solution)/shard_map/gather_results/ppermute | solution.py:66
  107.2 1.1 shard_map.123
  108.2 0.0 collective-permute-done.8.other_ref
  108.2 0.8 shard_map.124
  (21 shorter events, 0.3 us)
Async XLA Ops:
  0.6 30.5 %copy-start.6 = (s32[1,1,48]{2,1,0:T(1,128)S(1)}, s32[1,1,48]{2,1,0:T(1,128)}, u32[]{:S(2)}) copy-start(s32[1,1,48]{2,1,0:T(1,128)} %param.13) | copy-start | bytes 580
  0.6 30.5 %copy-start.7 = (s32[1,1,48]{2,1,0:T(1,128)S(1)}, s32[1,1,48]{2,1,0:T(1,128)}, u32[]{:S(2)}) copy-start(s32[1,1,48]{2,1,0:T(1,128)} %param.14) | copy-start | bytes 580
  0.7 30.5 %copy-start = (bf16[1,1,48,128,128]{4,3,2,1,0:T(8,128)(2,1)S(1)}, bf16[1,1,48,128,128]{4,3,2,1,0:T(8,128)(2,1)}, u32[]{:S(2)}) copy-start(bf16[1,1,48,128,128]{4,3,2,1,0:T(8,128)(2,1)} %param.12) | copy-start | bytes 4718596
  1.7 12.6 %collective-permute-start = (bf16[128,256]{1,0:T(8,128)(2,1)S(1)}, bf16[128,256]{1,0:T(8,128)(2,1)S(1)}, u32[]{:S(2)}, u32[]{:S(2)}) collective-permute-start(bf16[128,256]{1,0:T(8,128)(2,1)S(1)} %dynamic-slice_bitcast_fusion), channel_id=1, source_target_pairs={{0,32},{4,168},{1,16},{5,152},{2,0},{6,136},{3,48},{7,184},{8,49},... | collective-permute-start | bytes 196616 | tf_op jit(solution)/shard_map/spread_features/ppermute | solution.py:339
  14.3 3.1 %collective-permute-start.1 = (bf16[128,256]{1,0:T(8,128)(2,1)S(1)}, bf16[128,256]{1,0:T(8,128)(2,1)S(1)}, u32[]{:S(2)}, u32[]{:S(2)}) collective-permute-start(bf16[128,256]{1,0:T(8,128)(2,1)S(1)} %collective-permute-done), channel_id=1, source_target_pairs={{0,64},{8,72},{16,80},{24,88},{32,96},{40,104},{48,112},{56,120},{... | collective-permute-start | bytes 196616 | tf_op jit(solution)/shard_map/gather_features/ppermute | solution.py:342
  27.8 4.8 %collective-permute-start.2 = (bf16[1024,256]{1,0:T(8,128)(2,1)S(1)}, bf16[1024,256]{1,0:T(8,128)(2,1)S(1)}, u32[]{:S(2)}, u32[]{:S(2)}) collective-permute-start(bf16[1024,256]{1,0:T(8,128)(2,1)S(1)} %bitcast.24), channel_id=1, source_target_pairs={{0,8},{8,0},{16,24},{24,16},{32,40},{40,32},{48,56},{56,48},{64,72... | collective-permute-start | bytes 1572872 | tf_op jit(solution)/shard_map/gather_features/ppermute | solution.py:66
  32.6 14.3 %copy-start.1 = (bf16[512,256]{1,0:T(8,128)(2,1)S(1)}, bf16[512,256]{1,0:T(8,128)(2,1)}, u32[]{:S(2)}) copy-start(bf16[512,256]{1,0:T(8,128)(2,1)} %features_ref.3) | copy-start | bytes 786436
  32.6 14.3 %copy-start.2 = (bf16[256,256]{1,0:T(8,128)(2,1)S(1)}, bf16[256,256]{1,0:T(8,128)(2,1)}, u32[]{:S(2)}) copy-start(bf16[256,256]{1,0:T(8,128)(2,1)} %w_self_ref.3) | copy-start | bytes 393220
  32.6 14.3 %copy-start.5 = (s32[512]{0:T(512)S(1)}, s32[512]{0:T(512)}, u32[]{:S(2)}) copy-start(s32[512]{0:T(512)} %param.11) | copy-start | bytes 6148
  42.6 15.1 %copy-start.3 = (bf16[512,256]{1,0:T(8,128)(2,1)S(1)}, bf16[512,256]{1,0:T(8,128)(2,1)}, u32[]{:S(2)}) copy-start(bf16[512,256]{1,0:T(8,128)(2,1)} %cotangent_ref.1) | copy-start | bytes 786436
  42.6 15.1 %copy-start.4 = (bf16[256,256]{1,0:T(8,128)(2,1)S(1)}, bf16[256,256]{1,0:T(8,128)(2,1)}, u32[]{:S(2)}) copy-start(bf16[256,256]{1,0:T(8,128)(2,1)} %w_neigh_ref.1) | copy-start | bytes 393220
  42.6 7.1 %collective-permute-start.3 = (bf16[128,256]{1,0:T(8,128)(2,1)S(1)}, bf16[128,256]{1,0:T(8,128)(2,1)S(1)}, u32[]{:S(2)}, u32[]{:S(2)}) collective-permute-start(bf16[128,256]{1,0:T(8,128)(2,1)S(1)} %fusion), channel_id=1, source_target_pairs={{0,4},{1,5},{2,6},{3,7},{4,0},{5,1},{6,2},{7,3},{8,12},{9,13},{10,... | collective-permute-start | bytes 196616 | tf_op jit(solution)/shard_map/sum_over_h/ppermute | solution.py:352
  58.6 5.8 %collective-permute-start.4 = (bf16[1088,256]{1,0:T(8,128)(2,1)S(1)}, bf16[1088,256]{1,0:T(8,128)(2,1)S(1)}, u32[]{:S(2)}, u32[]{:S(2)}) collective-permute-start(bf16[1088,256]{1,0:T(8,128)(2,1)S(1)} %get-tuple-element.38), channel_id=1, source_target_pairs={{0,8},{8,0},{16,24},{24,16},{32,40},{40,32},{48,56},{56,48},{64,72... | collective-permute-start | bytes 1671176 | tf_op jit(solution)/shard_map/pair_sum/ppermute | solution.py:66
  77.1 4.3 %collective-permute-start.5 = (bf16[192,256]{1,0:T(8,128)(2,1)S(1)}, bf16[192,256]{1,0:T(8,128)(2,1)S(1)}, u32[]{:S(2)}, u32[]{:S(2)}) collective-permute-start(bf16[192,256]{1,0:T(8,128)(2,1)S(1)} %slice_bitcast_fusion), channel_id=1, source_target_pairs={{0,64},{8,72},{16,80},{24,88},{32,96},{40,104},{48,112},{56,120},{... | collective-permute-start | bytes 294920 | tf_op jit(solution)/shard_map/sum_over_section/ppermute | solution.py:370
  81.5 4.5 %collective-permute-start.6 = (bf16[192,256]{1,0:T(8,128)(2,1)S(1)}, bf16[192,256]{1,0:T(8,128)(2,1)S(1)}, u32[]{:S(2)}, u32[]{:S(2)}) collective-permute-start(bf16[192,256]{1,0:T(8,128)(2,1)S(1)} %add_convert_fusion.3), channel_id=1, source_target_pairs={{0,128},{8,136},{16,144},{24,152},{32,160},{40,168},{48,176},{56,1... | collective-permute-start | bytes 294920 | tf_op jit(solution)/shard_map/sum_over_section/ppermute | solution.py:373
  86.0 8.4 %collective-permute-start.7 = (bf16[128,256]{1,0:T(8,128)(2,1)S(1)}, bf16[128,256]{1,0:T(8,128)(2,1)S(1)}, u32[]{:S(2)}, u32[]{:S(2)}) collective-permute-start(bf16[128,256]{1,0:T(8,128)(2,1)S(1)} %slice.89), channel_id=1, source_target_pairs={{0,2},{1,11},{2,17},{3,26},{4,36},{5,45},{6,55},{7,60},{8,134},{9,... | collective-permute-start | bytes 196616 | tf_op jit(solution)/shard_map/return_panels/ppermute | solution.py:376
  103.2 5.0 %collective-permute-start.8 = (bf16[4,64,256]{2,1,0:T(8,128)(2,1)S(1)}, bf16[4,64,256]{2,1,0:T(8,128)(2,1)S(1)}, u32[]{:S(2)}, u32[]{:S(2)}) collective-permute-start(bf16[4,64,256]{2,1,0:T(8,128)(2,1)S(1)} %slice.91.own_ref), channel_id=1, source_target_pairs={{0,8},{8,0},{16,24},{24,16},{32,40},{40,32},{48,56},{56,48},{64,72... | collective-permute-start | bytes 393224 | tf_op jit(solution)/shard_map/gather_results/ppermute | solution.py:66

commit v11 on v10

--- a/solution.py
+++ b/solution.py
@@ -263,43 +263,46 @@
     )(*operands)
 
 
-def activate_kernel(preact_ref, activated_ref):
+def activate_kernel(preact_ref, pre_grad_ref, w_self_ref, activated_ref, self_part_ref):
     preact = preact_ref[...]
     activated_ref[...] = (preact * jax.nn.sigmoid(preact)).astype(BF16)
-
-
-def activate(preact):
+    self_part_ref[...] = lax.dot_general(
+        pre_grad_ref[...], w_self_ref[...], ROWS_T, preferred_element_type=F32
+    )
+
+
+def activate(preact, pre_grad, w_self):
     return pl.pallas_call(
         activate_kernel,
-        out_shape=jax.ShapeDtypeStruct((512, 256), BF16),
-        in_specs=[VMEM],
-        out_specs=VMEM,
-        compiler_params=pltpu.CompilerParams(vmem_limit_bytes=16 * 1024 * 1024),
-        cost_estimate=pl.CostEstimate(flops=2**21, bytes_accessed=2**20, transcendentals=2**17),
-    )(preact)
-
-
-def feature_kernel(results_ref, pre_grad_ref, w_self_ref, feature_ref):
+        out_shape=(
+            jax.ShapeDtypeStruct((512, 256), BF16),
+            jax.ShapeDtypeStruct((512, 256), F32),
+        ),
+        in_specs=[VMEM] * 3,
+        out_specs=(VMEM,) * 2,
+        compiler_params=pltpu.CompilerParams(vmem_limit_bytes=16 * 1024 * 1024),
+        cost_estimate=pl.CostEstimate(flops=2**26, bytes_accessed=2**20, transcendentals=2**17),
+    )(preact, pre_grad, w_self)
+
+
+def feature_kernel(results_ref, self_part_ref, feature_ref):
     _, x, core, _, _ = position()
     last = other_end(x, x % 2 * 2 + core, 0)
-    self_part = lax.dot_general(
-        pre_grad_ref[...], w_self_ref[...], ROWS_T, preferred_element_type=F32
-    )
     for block in range(4):
         rows = slice(block * BLOCK, (block + 1) * BLOCK)
         y = (last + 4 - block) % 4
-        feature_ref[rows, :] = self_part[rows] + results_ref[y, :BLOCK, :].astype(F32)
-
-
-def finish_features(results, pre_grad, w_self):
+        feature_ref[rows, :] = self_part_ref[rows, :] + results_ref[y, :BLOCK, :].astype(F32)
+
+
+def finish_features(results, self_part):
     return pl.pallas_call(
         feature_kernel,
         out_shape=jax.ShapeDtypeStruct((512, 256), F32),
-        in_specs=[VMEM] * 3,
+        in_specs=[VMEM] * 2,
         out_specs=VMEM,
         compiler_params=pltpu.CompilerParams(vmem_limit_bytes=16 * 1024 * 1024),
         cost_estimate=pl.CostEstimate(flops=2**27, bytes_accessed=2**21, transcendentals=0),
-    )(results, pre_grad, w_self)
+    )(results, self_part)
 
 
 def grad_kernel(own_ref, other_ref, self_ref, neigh_ref):
@@ -374,14 +377,14 @@
         total = (total.astype(F32) + arrived.astype(F32)).astype(BF16)
     with jax.named_scope("return_panels"):
         block = lax.ppermute(total[:BLOCK], ("section", "rep"), back_pairs())
-        activated = activate(preact)
-        block, activated = lax.optimization_barrier((block, activated))
+        activated, self_part = activate(preact, pre_grad, w_self)
+        block, activated, self_part = lax.optimization_barrier((block, activated, self_part))
     with jax.named_scope("gather_results"):
         last = jnp.concatenate([block, total[BLOCK:]], axis=0)
         results = exchange(spread(last, 4), "rep", SAME_H)
         own_rows = results[:, BLOCK:]
         other_rows = swap_core(own_rows)
-    feature_grad = finish_features(results, pre_grad, w_self)
+    feature_grad = finish_features(results, self_part)
     grad_self, grad_neigh = finish_grads(own_rows, other_rows)
     return (activated, feature_grad, grad_self, grad_neigh)
 

time: 111 us -> 110 us (level)
  starting transfers between devices: 33.7 us -> 32.3 us
  blocking collectives: 48.6 us -> 49.8 us
    all_to_all x5, blocking collectives: 48.6 us -> 49.8 us  [exchange(): return lax.all_to_all(x, axis, 0, 0, tiled=False, axis_index_groups=groups)]
  transfers between devices with their start and end apart: 9 -> 9, of which waited for: 7 -> 8; matrix products, arithmetic and copies ran while one was open for 0% -> 0% of each run, Pallas kernels for 4% -> 4%
where the time goes in v11:
time: 110 us; the launch traced here: 109 us
  blocking collectives  49.8 us (45%)
  starting transfers between devices  32.3 us (29%)
  waiting for transfers between devices  16.8 us (15%)
  Pallas kernels  6.98 us (6%)
  between operations  1.58 us (1%)
  local copies, waits for them, and re-layouts  1.13 us (1%)
    all_to_all x5, blocking collectives, exchange(): return lax.all_to_all(x, axis, 0, 0, tiled=False, axis_index_groups=groups)  49.8 us
    ppermute x3, starting transfers between devices, swap_core(): return lax.ppermute(x, 'section', CORE_PAIRS)  10.6 us
    ppermute x1, starting transfers between devices, body(): block = lax.ppermute(total[:BLOCK], ('section', 'rep'), back_pairs())  7.5 us
    ppermute x1, waiting for transfers between devices, body(): block = lax.ppermute(block, ('section', 'rep'), out_pairs())  6.96 us
    ppermute x1, starting transfers between devices, body(): block = lax.ppermute(block, ('section', 'rep'), out_pairs())  4.88 us
    ppermute x1, starting transfers between devices, body(): arrived = lax.ppermute(partial, 'rep', HALF_PAIRS)  4.11 us
    ppermute x1, waiting for transfers between devices, body(): arrived = lax.ppermute(partial, 'rep', HALF_PAIRS)  2.31 us
    ppermute x1, starting transfers between devices, body(): arrived = lax.ppermute(total, 'section', Z_PAIRS)  2.25 us
  transfers between devices with their start and end apart: 9, of which 8 were waited for; matrix products, arithmetic and copies ran while one was open for 0% of the time, Pallas kernels for 4%

profile of v11, /device:TPU:1, one launch (start us, length us, event | category | flops | bytes accessed | tf_op | source)
XLA Modules:
  0.0 109.1 jit_solution(4986600626035363457)
XLA Ops:
  0.6 0.0 copy-start.6
  0.6 0.0 copy-start.7
  0.7 0.0 copy-start
  0.7 1.0 dynamic-slice_bitcast_fusion
  1.7 4.9 %collective-permute-start = (bf16[128,256]{1,0:T(8,128)(2,1)S(1)}, bf16[128,256]{1,0:T(8,128)(2,1)S(1)}, u32[]{:S(2)}, u32[]{:S(2)}) collective-permute-start(bf16[128,256]{1,0:T(8,128)(2,1)S(1)} %dynamic-slice_bitcast_fusion), channel_id=1, source_target_pairs={{0,32},{4,168},{1,16},{5,152},{2,0},{6,136},{3,48},{7,184},{8,49},... | collective-permute-start | bytes 196616 | tf_op jit(solution)/shard_map/spread_features/ppermute | solution.py:342
  7.2 0.1 pad_add_fusion.scalars_ref
  7.3 7.0 %collective-permute-done = bf16[128,256]{1,0:T(8,128)(2,1)S(1)} collective-permute-done((bf16[128,256]{1,0:T(8,128)(2,1)S(1)}, bf16[128,256]{1,0:T(8,128)(2,1)S(1)}, u32[]{:S(2)}, u32[]{:S(2)}) %collective-permute-start) | collective-permute-done | bytes 65568 | tf_op jit(solution)/shard_map/spread_features/ppermute | solution.py:342
  14.3 1.4 %collective-permute-start.1 = (bf16[128,256]{1,0:T(8,128)(2,1)S(1)}, bf16[128,256]{1,0:T(8,128)(2,1)S(1)}, u32[]{:S(2)}, u32[]{:S(2)}) collective-permute-start(bf16[128,256]{1,0:T(8,128)(2,1)S(1)} %collective-permute-done), channel_id=1, source_target_pairs={{0,64},{8,72},{16,80},{24,88},{32,96},{40,104},{48,112},{56,120},{... | collective-permute-start | bytes 196616 | tf_op jit(solution)/shard_map/gather_features/ppermute | solution.py:345
  15.7 1.7 %collective-permute-done.1 = bf16[128,256]{1,0:T(8,128)(2,1)S(1)} collective-permute-done((bf16[128,256]{1,0:T(8,128)(2,1)S(1)}, bf16[128,256]{1,0:T(8,128)(2,1)S(1)}, u32[]{:S(2)}, u32[]{:S(2)}) %collective-permute-start.1) | collective-permute-done | bytes 65568 | tf_op jit(solution)/shard_map/gather_features/ppermute | solution.py:345
  17.4 10.4 %all_to_all.25 = bf16[4,2,128,256]{3,2,1,0:T(8,128)(2,1)S(1)} all-to-all(bf16[4,2,128,256]{3,2,1,0:T(8,128)(2,1)S(1)} %broadcast_in_dim.8), channel_id=1, replica_groups={{0,16,32,48},{8,24,40,56},{64,80,96,112},{72,88,104,120},{128,144,160,1..., dimensions={0} | all-to-all | bytes 1048576 | tf_op jit(solution)/shard_map/gather_features/all_to_all | solution.py:70
  27.8 3.3 %collective-permute-start.2 = (bf16[1024,256]{1,0:T(8,128)(2,1)S(1)}, bf16[1024,256]{1,0:T(8,128)(2,1)S(1)}, u32[]{:S(2)}, u32[]{:S(2)}) collective-permute-start(bf16[1024,256]{1,0:T(8,128)(2,1)S(1)} %bitcast.24), channel_id=1, source_target_pairs={{0,8},{8,0},{16,24},{24,16},{32,40},{40,32},{48,56},{56,48},{64,72... | collective-permute-start | bytes 1572872 | tf_op jit(solution)/shard_map/gather_features/ppermute | solution.py:66
  31.2 0.0 copy-done.6
  31.2 0.0 copy-done
  31.2 1.5 %shard_map.120.dense_ref = bf16[512,2048]{1,0:T(8,128)(2,1)S(1)} custom-call(s32[2]{0:T(128)S(1)} %pad_add_fusion.scalars_ref, s32[48]{0:T(128)S(1)} %bitcast.31, s32[48]{0:T(128)S(1)} %bitcast.32, bf16[48,128,128]{2,1,0:T(8,128)(2,1)S(1)} %bitcast.26), custom_call_target="tpu_custom_call" | custom-call | flops 4194304 | bytes 12582912 | tf_op jit(solution)/shard_map/pallas_call | solution.py:100
  32.7 0.0 copy-start.1
  32.7 0.0 copy-start.2
  32.7 0.0 copy-start.5
  32.7 0.0 collective-permute-done.2.other_ref
  32.8 0.8 shard_map.121
  33.6 9.6 %all_to_all.26 = bf16[4,128,256]{2,1,0:T(8,128)(2,1)S(1)} all-to-all(bf16[4,128,256]{2,1,0:T(8,128)(2,1)S(1)} %bitcast.28), channel_id=1, replica_groups={{0,1,2,3},{4,5,6,7},{8,9,10,11},{12,13,14,15},{16,17,18,19},{20,21,22,2..., dimensions={0} | all-to-all | bytes 524288 | tf_op jit(solution)/shard_map/sum_over_y/all_to_all | solution.py:70
  43.2 0.0 copy-start.3
  43.2 0.0 copy-start.4
  43.2 4.1 %collective-permute-start.3 = (bf16[128,256]{1,0:T(8,128)(2,1)S(1)}, bf16[128,256]{1,0:T(8,128)(2,1)S(1)}, u32[]{:S(2)}, u32[]{:S(2)}) collective-permute-start(bf16[128,256]{1,0:T(8,128)(2,1)S(1)} %fusion), channel_id=1, source_target_pairs={{0,4},{1,5},{2,6},{3,7},{4,0},{5,1},{6,2},{7,3},{8,12},{9,13},{10,... | collective-permute-start | bytes 196616 | tf_op jit(solution)/shard_map/sum_over_h/ppermute | solution.py:355
  47.3 0.0 copy-done.1
  47.3 0.0 copy-done.5
  47.3 0.7 sum_over_h.1
  48.0 2.3 %collective-permute-done.3 = bf16[128,256]{1,0:T(8,128)(2,1)S(1)} collective-permute-done((bf16[128,256]{1,0:T(8,128)(2,1)S(1)}, bf16[128,256]{1,0:T(8,128)(2,1)S(1)}, u32[]{:S(2)}, u32[]{:S(2)}) %collective-permute-start.3) | collective-permute-done | bytes 65568 | tf_op jit(solution)/shard_map/sum_over_h/ppermute | solution.py:355
  50.4 7.9 %all_to_all.27 = bf16[4,128,256]{2,1,0:T(8,128)(2,1)S(1)} all-to-all(bf16[4,128,256]{2,1,0:T(8,128)(2,1)S(1)} %broadcast_in_dim.9), channel_id=1, replica_groups={{0,1,2,3},{4,5,6,7},{8,9,10,11},{12,13,14,15},{16,17,18,19},{20,21,22,2..., dimensions={0} | all-to-all | bytes 524288 | tf_op jit(solution)/shard_map/gather_over_y/all_to_all | solution.py:70
  58.3 0.0 copy-done.3
  58.3 0.9 shard_map.122
  59.2 3.7 %collective-permute-start.4 = (bf16[1088,256]{1,0:T(8,128)(2,1)S(1)}, bf16[1088,256]{1,0:T(8,128)(2,1)S(1)}, u32[]{:S(2)}, u32[]{:S(2)}) collective-permute-start(bf16[1088,256]{1,0:T(8,128)(2,1)S(1)} %get-tuple-element.41), channel_id=1, source_target_pairs={{0,8},{8,0},{16,24},{24,16},{32,40},{40,32},{48,56},{56,48},{64,72... | collective-permute-start | bytes 1671176 | tf_op jit(solution)/shard_map/pair_sum/ppermute | solution.py:66
  62.9 0.4 pair_sum.1
  63.4 1.1 %collective-permute-done.4 = bf16[1088,256]{1,0:T(8,128)(2,1)S(1)} collective-permute-done((bf16[1088,256]{1,0:T(8,128)(2,1)S(1)}, bf16[1088,256]{1,0:T(8,128)(2,1)S(1)}, u32[]{:S(2)}, u32[]{:S(2)}) %collective-permute-start.4) | collective-permute-done | bytes 557088 | tf_op jit(solution)/shard_map/pair_sum/ppermute | solution.py:66
  64.5 0.1 add_convert_fusion
  64.7 13.0 %all_to_all.28 = bf16[4,320,256]{2,1,0:T(8,128)(2,1)S(1)} all-to-all(bf16[4,320,256]{2,1,0:T(8,128)(2,1)S(1)} %pad_maximum_fusion), channel_id=1, replica_groups={{0,16,32,48},{8,24,40,56},{64,80,96,112},{72,88,104,120},{128,144,160,1..., dimensions={0} | all-to-all | bytes 1310720 | tf_op jit(solution)/shard_map/sum_over_section/all_to_all | solution.py:70
  77.7 0.1 add_convert_fusion.1
  77.9 1.6 %collective-permute-start.5 = (bf16[192,256]{1,0:T(8,128)(2,1)S(1)}, bf16[192,256]{1,0:T(8,128)(2,1)S(1)}, u32[]{:S(2)}, u32[]{:S(2)}) collective-permute-start(bf16[192,256]{1,0:T(8,128)(2,1)S(1)} %slice_bitcast_fusion), channel_id=1, source_target_pairs={{0,64},{8,72},{16,80},{24,88},{32,96},{40,104},{48,112},{56,120},{... | collective-permute-start | bytes 294920 | tf_op jit(solution)/shard_map/sum_over_section/ppermute | solution.py:373
  79.4 2.0 %collective-permute-done.5 = bf16[192,256]{1,0:T(8,128)(2,1)S(1)} collective-permute-done((bf16[192,256]{1,0:T(8,128)(2,1)S(1)}, bf16[192,256]{1,0:T(8,128)(2,1)S(1)}, u32[]{:S(2)}, u32[]{:S(2)}) %collective-permute-start.5) | collective-permute-done | bytes 98336 | tf_op jit(solution)/shard_map/sum_over_section/ppermute | solution.py:373
  81.5 2.3 %collective-permute-start.6 = (bf16[192,256]{1,0:T(8,128)(2,1)S(1)}, bf16[192,256]{1,0:T(8,128)(2,1)S(1)}, u32[]{:S(2)}, u32[]{:S(2)}) collective-permute-start(bf16[192,256]{1,0:T(8,128)(2,1)S(1)} %add_convert_fusion.3), channel_id=1, source_target_pairs={{0,128},{8,136},{16,144},{24,152},{32,160},{40,168},{48,176},{56,1... | collective-permute-start | bytes 294920 | tf_op jit(solution)/shard_map/sum_over_section/ppermute | solution.py:376
  83.7 2.2 %collective-permute-done.6 = bf16[192,256]{1,0:T(8,128)(2,1)S(1)} collective-permute-done((bf16[192,256]{1,0:T(8,128)(2,1)S(1)}, bf16[192,256]{1,0:T(8,128)(2,1)S(1)}, u32[]{:S(2)}, u32[]{:S(2)}) %collective-permute-start.6) | collective-permute-done | bytes 98336 | tf_op jit(solution)/shard_map/sum_over_section/ppermute | solution.py:376
  86.0 7.5 %collective-permute-start.7 = (bf16[128,256]{1,0:T(8,128)(2,1)S(1)}, bf16[128,256]{1,0:T(8,128)(2,1)S(1)}, u32[]{:S(2)}, u32[]{:S(2)}) collective-permute-start(bf16[128,256]{1,0:T(8,128)(2,1)S(1)} %slice.89), channel_id=1, source_target_pairs={{0,2},{1,11},{2,17},{3,26},{4,36},{5,45},{6,55},{7,60},{8,134},{9,... | collective-permute-start | bytes 196616 | tf_op jit(solution)/shard_map/return_panels/ppermute | solution.py:379
  93.5 1.0 return_panels.1
  94.4 0.4 collective-permute-done.7
  94.8 8.8 %all_to_all.29.results_ref = bf16[4,192,256]{2,1,0:T(8,128)(2,1)S(1)} all-to-all(bf16[4,192,256]{2,1,0:T(8,128)(2,1)S(1)} %broadcast_in_dim.11), channel_id=1, replica_groups={{0,1,2,3},{4,5,6,7},{8,9,10,11},{12,13,14,15},{16,17,18,19},{20,21,22,2..., dimensions={0} | all-to-all | bytes 786432 | tf_op jit(solution)/shard_map/gather_results/all_to_all | solution.py:70
  103.7 3.6 %collective-permute-start.8 = (bf16[4,64,256]{2,1,0:T(8,128)(2,1)S(1)}, bf16[4,64,256]{2,1,0:T(8,128)(2,1)S(1)}, u32[]{:S(2)}, u32[]{:S(2)}) collective-permute-start(bf16[4,64,256]{2,1,0:T(8,128)(2,1)S(1)} %slice.91.own_ref), channel_id=1, source_target_pairs={{0,8},{8,0},{16,24},{24,16},{32,40},{40,32},{48,56},{56,48},{64,72... | collective-permute-start | bytes 393224 | tf_op jit(solution)/shard_map/gather_results/ppermute | solution.py:66
  107.3 0.8 shard_map.123
  108.1 0.1 collective-permute-done.8.other_ref
  108.3 0.8 shard_map.124
  (21 shorter events, 0.3 us)
Async XLA Ops:
  0.6 30.5 %copy-start.6 = (s32[1,1,48]{2,1,0:T(1,128)S(1)}, s32[1,1,48]{2,1,0:T(1,128)}, u32[]{:S(2)}) copy-start(s32[1,1,48]{2,1,0:T(1,128)} %param.13) | copy-start | bytes 580
  0.6 30.5 %copy-start.7 = (s32[1,1,48]{2,1,0:T(1,128)S(1)}, s32[1,1,48]{2,1,0:T(1,128)}, u32[]{:S(2)}) copy-start(s32[1,1,48]{2,1,0:T(1,128)} %param.14) | copy-start | bytes 580
  0.7 30.5 %copy-start = (bf16[1,1,48,128,128]{4,3,2,1,0:T(8,128)(2,1)S(1)}, bf16[1,1,48,128,128]{4,3,2,1,0:T(8,128)(2,1)}, u32[]{:S(2)}) copy-start(bf16[1,1,48,128,128]{4,3,2,1,0:T(8,128)(2,1)} %param.12) | copy-start | bytes 4718596
  1.7 12.6 %collective-permute-start = (bf16[128,256]{1,0:T(8,128)(2,1)S(1)}, bf16[128,256]{1,0:T(8,128)(2,1)S(1)}, u32[]{:S(2)}, u32[]{:S(2)}) collective-permute-start(bf16[128,256]{1,0:T(8,128)(2,1)S(1)} %dynamic-slice_bitcast_fusion), channel_id=1, source_target_pairs={{0,32},{4,168},{1,16},{5,152},{2,0},{6,136},{3,48},{7,184},{8,49},... | collective-permute-start | bytes 196616 | tf_op jit(solution)/shard_map/spread_features/ppermute | solution.py:342
  14.3 3.1 %collective-permute-start.1 = (bf16[128,256]{1,0:T(8,128)(2,1)S(1)}, bf16[128,256]{1,0:T(8,128)(2,1)S(1)}, u32[]{:S(2)}, u32[]{:S(2)}) collective-permute-start(bf16[128,256]{1,0:T(8,128)(2,1)S(1)} %collective-permute-done), channel_id=1, source_target_pairs={{0,64},{8,72},{16,80},{24,88},{32,96},{40,104},{48,112},{56,120},{... | collective-permute-start | bytes 196616 | tf_op jit(solution)/shard_map/gather_features/ppermute | solution.py:345
  27.8 4.9 %collective-permute-start.2 = (bf16[1024,256]{1,0:T(8,128)(2,1)S(1)}, bf16[1024,256]{1,0:T(8,128)(2,1)S(1)}, u32[]{:S(2)}, u32[]{:S(2)}) collective-permute-start(bf16[1024,256]{1,0:T(8,128)(2,1)S(1)} %bitcast.24), channel_id=1, source_target_pairs={{0,8},{8,0},{16,24},{24,16},{32,40},{40,32},{48,56},{56,48},{64,72... | collective-permute-start | bytes 1572872 | tf_op jit(solution)/shard_map/gather_features/ppermute | solution.py:66
  32.7 14.6 %copy-start.1 = (bf16[512,256]{1,0:T(8,128)(2,1)S(1)}, bf16[512,256]{1,0:T(8,128)(2,1)}, u32[]{:S(2)}) copy-start(bf16[512,256]{1,0:T(8,128)(2,1)} %features_ref.3) | copy-start | bytes 786436
  32.7 14.6 %copy-start.2 = (bf16[256,256]{1,0:T(8,128)(2,1)S(1)}, bf16[256,256]{1,0:T(8,128)(2,1)}, u32[]{:S(2)}) copy-start(bf16[256,256]{1,0:T(8,128)(2,1)} %w_self_ref.3) | copy-start | bytes 393220
  32.7 14.6 %copy-start.5 = (s32[512]{0:T(512)S(1)}, s32[512]{0:T(512)}, u32[]{:S(2)}) copy-start(s32[512]{0:T(512)} %param.11) | copy-start | bytes 6148
  43.2 15.2 %copy-start.3 = (bf16[512,256]{1,0:T(8,128)(2,1)S(1)}, bf16[512,256]{1,0:T(8,128)(2,1)}, u32[]{:S(2)}) copy-start(bf16[512,256]{1,0:T(8,128)(2,1)} %cotangent_ref.1) | copy-start | bytes 786436
  43.2 15.1 %copy-start.4 = (bf16[256,256]{1,0:T(8,128)(2,1)S(1)}, bf16[256,256]{1,0:T(8,128)(2,1)}, u32[]{:S(2)}) copy-start(bf16[256,256]{1,0:T(8,128)(2,1)} %w_neigh_ref.1) | copy-start | bytes 393220
  43.2 7.2 %collective-permute-start.3 = (bf16[128,256]{1,0:T(8,128)(2,1)S(1)}, bf16[128,256]{1,0:T(8,128)(2,1)S(1)}, u32[]{:S(2)}, u32[]{:S(2)}) collective-permute-start(bf16[128,256]{1,0:T(8,128)(2,1)S(1)} %fusion), channel_id=1, source_target_pairs={{0,4},{1,5},{2,6},{3,7},{4,0},{5,1},{6,2},{7,3},{8,12},{9,13},{10,... | collective-permute-start | bytes 196616 | tf_op jit(solution)/shard_map/sum_over_h/ppermute | solution.py:355
  59.2 5.3 %collective-permute-start.4 = (bf16[1088,256]{1,0:T(8,128)(2,1)S(1)}, bf16[1088,256]{1,0:T(8,128)(2,1)S(1)}, u32[]{:S(2)}, u32[]{:S(2)}) collective-permute-start(bf16[1088,256]{1,0:T(8,128)(2,1)S(1)} %get-tuple-element.41), channel_id=1, source_target_pairs={{0,8},{8,0},{16,24},{24,16},{32,40},{40,32},{48,56},{56,48},{64,72... | collective-permute-start | bytes 1671176 | tf_op jit(solution)/shard_map/pair_sum/ppermute | solution.py:66
  77.9 3.6 %collective-permute-start.5 = (bf16[192,256]{1,0:T(8,128)(2,1)S(1)}, bf16[192,256]{1,0:T(8,128)(2,1)S(1)}, u32[]{:S(2)}, u32[]{:S(2)}) collective-permute-start(bf16[192,256]{1,0:T(8,128)(2,1)S(1)} %slice_bitcast_fusion), channel_id=1, source_target_pairs={{0,64},{8,72},{16,80},{24,88},{32,96},{40,104},{48,112},{56,120},{... | collective-permute-start | bytes 294920 | tf_op jit(solution)/shard_map/sum_over_section/ppermute | solution.py:373
  81.5 4.5 %collective-permute-start.6 = (bf16[192,256]{1,0:T(8,128)(2,1)S(1)}, bf16[192,256]{1,0:T(8,128)(2,1)S(1)}, u32[]{:S(2)}, u32[]{:S(2)}) collective-permute-start(bf16[192,256]{1,0:T(8,128)(2,1)S(1)} %add_convert_fusion.3), channel_id=1, source_target_pairs={{0,128},{8,136},{16,144},{24,152},{32,160},{40,168},{48,176},{56,1... | collective-permute-start | bytes 294920 | tf_op jit(solution)/shard_map/sum_over_section/ppermute | solution.py:376
  86.0 8.8 %collective-permute-start.7 = (bf16[128,256]{1,0:T(8,128)(2,1)S(1)}, bf16[128,256]{1,0:T(8,128)(2,1)S(1)}, u32[]{:S(2)}, u32[]{:S(2)}) collective-permute-start(bf16[128,256]{1,0:T(8,128)(2,1)S(1)} %slice.89), channel_id=1, source_target_pairs={{0,2},{1,11},{2,17},{3,26},{4,36},{5,45},{6,55},{7,60},{8,134},{9,... | collective-permute-start | bytes 196616 | tf_op jit(solution)/shard_map/return_panels/ppermute | solution.py:379
  103.7 4.6 %collective-permute-start.8 = (bf16[4,64,256]{2,1,0:T(8,128)(2,1)S(1)}, bf16[4,64,256]{2,1,0:T(8,128)(2,1)S(1)}, u32[]{:S(2)}, u32[]{:S(2)}) collective-permute-start(bf16[4,64,256]{2,1,0:T(8,128)(2,1)S(1)} %slice.91.own_ref), channel_id=1, source_target_pairs={{0,8},{8,0},{16,24},{24,16},{32,40},{40,32},{48,56},{56,48},{64,72... | collective-permute-start | bytes 393224 | tf_op jit(solution)/shard_map/gather_results/ppermute | solution.py:66

commit v12 on v11

--- a/solution.py
+++ b/solution.py
@@ -305,27 +305,10 @@
     )(results, self_part)
 
 
-def grad_kernel(own_ref, other_ref, self_ref, neigh_ref):
-    first = position()[2] == 0
-    for y in range(4):
-        own, other = own_ref[y].astype(F32), other_ref[y].astype(F32)
-        target = self_ref if y < 2 else neigh_ref
-        start = y % 2 * BLOCK
-        target[start : start + HALF, :] = jnp.where(first, own, other)
-        target[start + HALF : start + BLOCK, :] = jnp.where(first, other, own)
-
-
-def finish_grads(own, other):
-    return pl.pallas_call(
-        grad_kernel,
-        out_shape=(
-            jax.ShapeDtypeStruct((256, 256), F32),
-            jax.ShapeDtypeStruct((256, 256), F32),
-        ),
-        in_specs=[VMEM] * 2,
-        out_specs=(VMEM,) * 2,
-        compiler_params=pltpu.CompilerParams(vmem_limit_bytes=16 * 1024 * 1024),
-    )(own, other)
+def finish_grads(own, other, first):
+    top, bottom = jnp.where(first, own, other), jnp.where(first, other, own)
+    rows = jnp.concatenate([top, bottom], axis=1).astype(F32)
+    return rows[:2].reshape(256, 256), rows[2:].reshape(256, 256)
 
 
 def body(
@@ -385,7 +368,7 @@
         own_rows = results[:, BLOCK:]
         other_rows = swap_core(own_rows)
     feature_grad = finish_features(results, self_part)
-    grad_self, grad_neigh = finish_grads(own_rows, other_rows)
+    grad_self, grad_neigh = finish_grads(own_rows, other_rows, core == 0)
     return (activated, feature_grad, grad_self, grad_neigh)
 
 

time: 110 us -> 110 us (level)
  Pallas kernels: 6.98 us -> 5.88 us
  transfers between devices with their start and end apart: 9 -> 9, of which waited for: 8 -> 9; matrix products, arithmetic and copies ran while one was open for 0% -> 0% of each run, Pallas kernels for 4% -> 4%
where the time goes in v12:
time: 110 us; the launch traced here: 109 us
  blocking collectives  49.2 us (45%)
  starting transfers between devices  33.2 us (30%)
  waiting for transfers between devices  16.7 us (15%)
  Pallas kernels  5.88 us (5%)
  local copies, waits for them, and re-layouts  1.95 us (2%)
  between operations  1.58 us (1%)
    all_to_all x5, blocking collectives, exchange(): return lax.all_to_all(x, axis, 0, 0, tiled=False, axis_index_groups=groups)  49.2 us
    ppermute x3, starting transfers between devices, swap_core(): return lax.ppermute(x, 'section', CORE_PAIRS)  11.7 us
    ppermute x1, starting transfers between devices, body(): block = lax.ppermute(total[:BLOCK], ('section', 'rep'), back_pairs())  6.97 us
    ppermute x1, waiting for transfers between devices, body(): block = lax.ppermute(block, ('section', 'rep'), out_pairs())  6.96 us
    ppermute x1, starting transfers between devices, body(): block = lax.ppermute(block, ('section', 'rep'), out_pairs())  4.88 us
    ppermute x1, starting transfers between devices, body(): arrived = lax.ppermute(partial, 'rep', HALF_PAIRS)  4.36 us
    ppermute x1, starting transfers between devices, body(): arrived = lax.ppermute(total, 'section', Z_PAIRS)  2.29 us
  transfers between devices with their start and end apart: 9, of which 9 were waited for; matrix products, arithmetic and copies ran while one was open for 0% of the time, Pallas kernels for 4%

profile of v12, /device:TPU:1, one launch (start us, length us, event | category | flops | bytes accessed | tf_op | source)
XLA Modules:
  0.0 109.1 jit_solution(6916047566784823940)
XLA Ops:
  0.6 0.0 copy-start.6
  0.6 0.0 copy-start.7
  0.7 0.0 copy-start
  0.7 1.0 dynamic-slice_bitcast_fusion
  1.7 4.9 %collective-permute-start = (bf16[128,256]{1,0:T(8,128)(2,1)S(1)}, bf16[128,256]{1,0:T(8,128)(2,1)S(1)}, u32[]{:S(2)}, u32[]{:S(2)}) collective-permute-start(bf16[128,256]{1,0:T(8,128)(2,1)S(1)} %dynamic-slice_bitcast_fusion), channel_id=1, source_target_pairs={{0,32},{4,168},{1,16},{5,152},{2,0},{6,136},{3,48},{7,184},{8,49},... | collective-permute-start | bytes 196616 | tf_op jit(solution)/shard_map/spread_features/ppermute | solution.py:325
  7.2 0.1 pad_add_fusion.scalars_ref
  7.3 7.0 %collective-permute-done = bf16[128,256]{1,0:T(8,128)(2,1)S(1)} collective-permute-done((bf16[128,256]{1,0:T(8,128)(2,1)S(1)}, bf16[128,256]{1,0:T(8,128)(2,1)S(1)}, u32[]{:S(2)}, u32[]{:S(2)}) %collective-permute-start) | collective-permute-done | bytes 65568 | tf_op jit(solution)/shard_map/spread_features/ppermute | solution.py:325
  14.3 1.4 %collective-permute-start.1 = (bf16[128,256]{1,0:T(8,128)(2,1)S(1)}, bf16[128,256]{1,0:T(8,128)(2,1)S(1)}, u32[]{:S(2)}, u32[]{:S(2)}) collective-permute-start(bf16[128,256]{1,0:T(8,128)(2,1)S(1)} %collective-permute-done), channel_id=1, source_target_pairs={{0,64},{8,72},{16,80},{24,88},{32,96},{40,104},{48,112},{56,120},{... | collective-permute-start | bytes 196616 | tf_op jit(solution)/shard_map/gather_features/ppermute | solution.py:328
  15.7 1.7 %collective-permute-done.1 = bf16[128,256]{1,0:T(8,128)(2,1)S(1)} collective-permute-done((bf16[128,256]{1,0:T(8,128)(2,1)S(1)}, bf16[128,256]{1,0:T(8,128)(2,1)S(1)}, u32[]{:S(2)}, u32[]{:S(2)}) %collective-permute-start.1) | collective-permute-done | bytes 65568 | tf_op jit(solution)/shard_map/gather_features/ppermute | solution.py:328
  17.4 10.4 %all_to_all.25 = bf16[4,2,128,256]{3,2,1,0:T(8,128)(2,1)S(1)} all-to-all(bf16[4,2,128,256]{3,2,1,0:T(8,128)(2,1)S(1)} %broadcast_in_dim.8), channel_id=1, replica_groups={{0,16,32,48},{8,24,40,56},{64,80,96,112},{72,88,104,120},{128,144,160,1..., dimensions={0} | all-to-all | bytes 1048576 | tf_op jit(solution)/shard_map/gather_features/all_to_all | solution.py:70
  27.8 3.3 %collective-permute-start.2 = (bf16[1024,256]{1,0:T(8,128)(2,1)S(1)}, bf16[1024,256]{1,0:T(8,128)(2,1)S(1)}, u32[]{:S(2)}, u32[]{:S(2)}) collective-permute-start(bf16[1024,256]{1,0:T(8,128)(2,1)S(1)} %bitcast.26), channel_id=1, source_target_pairs={{0,8},{8,0},{16,24},{24,16},{32,40},{40,32},{48,56},{56,48},{64,72... | collective-permute-start | bytes 1572872 | tf_op jit(solution)/shard_map/gather_features/ppermute | solution.py:66
  31.2 0.0 copy-done.6
  31.2 0.0 copy-done.7
  31.2 0.0 copy-done
  31.2 1.3 %shard_map.120.dense_ref = bf16[512,2048]{1,0:T(8,128)(2,1)S(1)} custom-call(s32[2]{0:T(128)S(1)} %pad_add_fusion.scalars_ref, s32[48]{0:T(128)S(1)} %bitcast.33, s32[48]{0:T(128)S(1)} %bitcast.34, bf16[48,128,128]{2,1,0:T(8,128)(2,1)S(1)} %bitcast.28), custom_call_target="tpu_custom_call" | custom-call | flops 4194304 | bytes 12582912 | tf_op jit(solution)/shard_map/pallas_call | solution.py:100
  32.5 0.0 copy-start.1
  32.5 0.0 copy-start.2
  32.5 0.0 copy-start.5
  32.5 0.2 collective-permute-done.2.other_ref
  32.7 0.8 shard_map.121
  33.5 9.0 %all_to_all.26 = bf16[4,128,256]{2,1,0:T(8,128)(2,1)S(1)} all-to-all(bf16[4,128,256]{2,1,0:T(8,128)(2,1)S(1)} %bitcast.30), channel_id=1, replica_groups={{0,1,2,3},{4,5,6,7},{8,9,10,11},{12,13,14,15},{16,17,18,19},{20,21,22,2..., dimensions={0} | all-to-all | bytes 524288 | tf_op jit(solution)/shard_map/sum_over_y/all_to_all | solution.py:70
  42.6 0.0 copy-start.3
  42.6 0.0 copy-start.4
  42.6 4.4 %collective-permute-start.3 = (bf16[128,256]{1,0:T(8,128)(2,1)S(1)}, bf16[128,256]{1,0:T(8,128)(2,1)S(1)}, u32[]{:S(2)}, u32[]{:S(2)}) collective-permute-start(bf16[128,256]{1,0:T(8,128)(2,1)S(1)} %fusion), channel_id=1, source_target_pairs={{0,4},{1,5},{2,6},{3,7},{4,0},{5,1},{6,2},{7,3},{8,12},{9,13},{10,... | collective-permute-start | bytes 196616 | tf_op jit(solution)/shard_map/sum_over_h/ppermute | solution.py:338
  47.0 0.0 copy-done.1
  47.0 0.0 copy-done.2
  47.0 0.7 sum_over_h.1
  47.7 2.1 %collective-permute-done.3 = bf16[128,256]{1,0:T(8,128)(2,1)S(1)} collective-permute-done((bf16[128,256]{1,0:T(8,128)(2,1)S(1)}, bf16[128,256]{1,0:T(8,128)(2,1)S(1)}, u32[]{:S(2)}, u32[]{:S(2)}) %collective-permute-start.3) | collective-permute-done | bytes 65568 | tf_op jit(solution)/shard_map/sum_over_h/ppermute | solution.py:338
  49.8 7.9 %all_to_all.27 = bf16[4,128,256]{2,1,0:T(8,128)(2,1)S(1)} all-to-all(bf16[4,128,256]{2,1,0:T(8,128)(2,1)S(1)} %broadcast_in_dim.9), channel_id=1, replica_groups={{0,1,2,3},{4,5,6,7},{8,9,10,11},{12,13,14,15},{16,17,18,19},{20,21,22,2..., dimensions={0} | all-to-all | bytes 524288 | tf_op jit(solution)/shard_map/gather_over_y/all_to_all | solution.py:70
  57.7 0.9 shard_map.122
  58.6 4.3 %collective-permute-start.4 = (bf16[1088,256]{1,0:T(8,128)(2,1)S(1)}, bf16[1088,256]{1,0:T(8,128)(2,1)S(1)}, u32[]{:S(2)}, u32[]{:S(2)}) collective-permute-start(bf16[1088,256]{1,0:T(8,128)(2,1)S(1)} %get-tuple-element.39), channel_id=1, source_target_pairs={{0,8},{8,0},{16,24},{24,16},{32,40},{40,32},{48,56},{56,48},{64,72... | collective-permute-start | bytes 1671176 | tf_op jit(solution)/shard_map/pair_sum/ppermute | solution.py:66
  62.9 0.4 pair_sum.1
  63.3 1.1 %collective-permute-done.4 = bf16[1088,256]{1,0:T(8,128)(2,1)S(1)} collective-permute-done((bf16[1088,256]{1,0:T(8,128)(2,1)S(1)}, bf16[1088,256]{1,0:T(8,128)(2,1)S(1)}, u32[]{:S(2)}, u32[]{:S(2)}) %collective-permute-start.4) | collective-permute-done | bytes 557088 | tf_op jit(solution)/shard_map/pair_sum/ppermute | solution.py:66
  64.5 0.1 add_convert_fusion
  64.7 13.0 %all_to_all.28 = bf16[4,320,256]{2,1,0:T(8,128)(2,1)S(1)} all-to-all(bf16[4,320,256]{2,1,0:T(8,128)(2,1)S(1)} %pad_maximum_fusion), channel_id=1, replica_groups={{0,16,32,48},{8,24,40,56},{64,80,96,112},{72,88,104,120},{128,144,160,1..., dimensions={0} | all-to-all | bytes 1310720 | tf_op jit(solution)/shard_map/sum_over_section/all_to_all | solution.py:70
  77.7 0.1 add_convert_fusion.1
  77.8 1.6 %collective-permute-start.5 = (bf16[192,256]{1,0:T(8,128)(2,1)S(1)}, bf16[192,256]{1,0:T(8,128)(2,1)S(1)}, u32[]{:S(2)}, u32[]{:S(2)}) collective-permute-start(bf16[192,256]{1,0:T(8,128)(2,1)S(1)} %slice_bitcast_fusion), channel_id=1, source_target_pairs={{0,64},{8,72},{16,80},{24,88},{32,96},{40,104},{48,112},{56,120},{... | collective-permute-start | bytes 294920 | tf_op jit(solution)/shard_map/sum_over_section/ppermute | solution.py:356
  79.4 2.0 %collective-permute-done.5 = bf16[192,256]{1,0:T(8,128)(2,1)S(1)} collective-permute-done((bf16[192,256]{1,0:T(8,128)(2,1)S(1)}, bf16[192,256]{1,0:T(8,128)(2,1)S(1)}, u32[]{:S(2)}, u32[]{:S(2)}) %collective-permute-start.5) | collective-permute-done | bytes 98336 | tf_op jit(solution)/shard_map/sum_over_section/ppermute | solution.py:356
  81.5 2.3 %collective-permute-start.6 = (bf16[192,256]{1,0:T(8,128)(2,1)S(1)}, bf16[192,256]{1,0:T(8,128)(2,1)S(1)}, u32[]{:S(2)}, u32[]{:S(2)}) collective-permute-start(bf16[192,256]{1,0:T(8,128)(2,1)S(1)} %add_convert_fusion.3), channel_id=1, source_target_pairs={{0,128},{8,136},{16,144},{24,152},{32,160},{40,168},{48,176},{56,1... | collective-permute-start | bytes 294920 | tf_op jit(solution)/shard_map/sum_over_section/ppermute | solution.py:359
  83.8 2.2 %collective-permute-done.6 = bf16[192,256]{1,0:T(8,128)(2,1)S(1)} collective-permute-done((bf16[192,256]{1,0:T(8,128)(2,1)S(1)}, bf16[192,256]{1,0:T(8,128)(2,1)S(1)}, u32[]{:S(2)}, u32[]{:S(2)}) %collective-permute-start.6) | collective-permute-done | bytes 98336 | tf_op jit(solution)/shard_map/sum_over_section/ppermute | solution.py:359
  86.0 7.0 %collective-permute-start.7 = (bf16[128,256]{1,0:T(8,128)(2,1)S(1)}, bf16[128,256]{1,0:T(8,128)(2,1)S(1)}, u32[]{:S(2)}, u32[]{:S(2)}) collective-permute-start(bf16[128,256]{1,0:T(8,128)(2,1)S(1)} %slice.97), channel_id=1, source_target_pairs={{0,2},{1,11},{2,17},{3,26},{4,36},{5,45},{6,55},{7,60},{8,134},{9,... | collective-permute-start | bytes 196616 | tf_op jit(solution)/shard_map/return_panels/ppermute | solution.py:362
  92.9 1.0 return_panels.1
  93.9 0.4 collective-permute-done.7
  94.3 8.8 %all_to_all.29.results_ref = bf16[4,192,256]{2,1,0:T(8,128)(2,1)S(1)} all-to-all(bf16[4,192,256]{2,1,0:T(8,128)(2,1)S(1)} %broadcast_in_dim.11), channel_id=1, replica_groups={{0,1,2,3},{4,5,6,7},{8,9,10,11},{12,13,14,15},{16,17,18,19},{20,21,22,2..., dimensions={0} | all-to-all | bytes 786432 | tf_op jit(solution)/shard_map/gather_results/all_to_all | solution.py:70
  103.2 4.1 %collective-permute-start.8 = (bf16[4,64,256]{2,1,0:T(8,128)(2,1)S(1)}, bf16[4,64,256]{2,1,0:T(8,128)(2,1)S(1)}, u32[]{:S(2)}, u32[]{:S(2)}) collective-permute-start(bf16[4,64,256]{2,1,0:T(8,128)(2,1)S(1)} %slice.99), channel_id=1, source_target_pairs={{0,8},{8,0},{16,24},{24,16},{32,40},{40,32},{48,56},{56,48},{64,72... | collective-permute-start | bytes 393224 | tf_op jit(solution)/shard_map/gather_results/ppermute | solution.py:66
  107.3 0.8 shard_map.123
  108.1 0.1 collective-permute-done.8
  108.3 0.8 fusion.1
  (23 shorter events, 0.4 us)
Async XLA Ops:
  0.6 30.5 %copy-start.6 = (s32[1,1,48]{2,1,0:T(1,128)S(1)}, s32[1,1,48]{2,1,0:T(1,128)}, u32[]{:S(2)}) copy-start(s32[1,1,48]{2,1,0:T(1,128)} %param.13) | copy-start | bytes 580
  0.6 30.5 %copy-start.7 = (s32[1,1,48]{2,1,0:T(1,128)S(1)}, s32[1,1,48]{2,1,0:T(1,128)}, u32[]{:S(2)}) copy-start(s32[1,1,48]{2,1,0:T(1,128)} %param.14) | copy-start | bytes 580
  0.7 30.5 %copy-start = (bf16[1,1,48,128,128]{4,3,2,1,0:T(8,128)(2,1)S(1)}, bf16[1,1,48,128,128]{4,3,2,1,0:T(8,128)(2,1)}, u32[]{:S(2)}) copy-start(bf16[1,1,48,128,128]{4,3,2,1,0:T(8,128)(2,1)} %param.12) | copy-start | bytes 4718596
  1.7 12.6 %collective-permute-start = (bf16[128,256]{1,0:T(8,128)(2,1)S(1)}, bf16[128,256]{1,0:T(8,128)(2,1)S(1)}, u32[]{:S(2)}, u32[]{:S(2)}) collective-permute-start(bf16[128,256]{1,0:T(8,128)(2,1)S(1)} %dynamic-slice_bitcast_fusion), channel_id=1, source_target_pairs={{0,32},{4,168},{1,16},{5,152},{2,0},{6,136},{3,48},{7,184},{8,49},... | collective-permute-start | bytes 196616 | tf_op jit(solution)/shard_map/spread_features/ppermute | solution.py:325
  14.3 3.1 %collective-permute-start.1 = (bf16[128,256]{1,0:T(8,128)(2,1)S(1)}, bf16[128,256]{1,0:T(8,128)(2,1)S(1)}, u32[]{:S(2)}, u32[]{:S(2)}) collective-permute-start(bf16[128,256]{1,0:T(8,128)(2,1)S(1)} %collective-permute-done), channel_id=1, source_target_pairs={{0,64},{8,72},{16,80},{24,88},{32,96},{40,104},{48,112},{56,120},{... | collective-permute-start | bytes 196616 | tf_op jit(solution)/shard_map/gather_features/ppermute | solution.py:328
  27.8 4.8 %collective-permute-start.2 = (bf16[1024,256]{1,0:T(8,128)(2,1)S(1)}, bf16[1024,256]{1,0:T(8,128)(2,1)S(1)}, u32[]{:S(2)}, u32[]{:S(2)}) collective-permute-start(bf16[1024,256]{1,0:T(8,128)(2,1)S(1)} %bitcast.26), channel_id=1, source_target_pairs={{0,8},{8,0},{16,24},{24,16},{32,40},{40,32},{48,56},{56,48},{64,72... | collective-permute-start | bytes 1572872 | tf_op jit(solution)/shard_map/gather_features/ppermute | solution.py:66
  32.5 14.5 %copy-start.1 = (bf16[512,256]{1,0:T(8,128)(2,1)S(1)}, bf16[512,256]{1,0:T(8,128)(2,1)}, u32[]{:S(2)}) copy-start(bf16[512,256]{1,0:T(8,128)(2,1)} %features_ref.3) | copy-start | bytes 786436
  32.5 14.5 %copy-start.2 = (bf16[256,256]{1,0:T(8,128)(2,1)S(1)}, bf16[256,256]{1,0:T(8,128)(2,1)}, u32[]{:S(2)}) copy-start(bf16[256,256]{1,0:T(8,128)(2,1)} %w_self_ref.3) | copy-start | bytes 393220
  32.5 14.5 %copy-start.5 = (s32[512]{0:T(512)S(1)}, s32[512]{0:T(512)}, u32[]{:S(2)}) copy-start(s32[512]{0:T(512)} %param.11) | copy-start | bytes 6148
  42.6 15.2 %copy-start.3 = (bf16[512,256]{1,0:T(8,128)(2,1)S(1)}, bf16[512,256]{1,0:T(8,128)(2,1)}, u32[]{:S(2)}) copy-start(bf16[512,256]{1,0:T(8,128)(2,1)} %cotangent_ref.1) | copy-start | bytes 786436
  42.6 15.2 %copy-start.4 = (bf16[256,256]{1,0:T(8,128)(2,1)S(1)}, bf16[256,256]{1,0:T(8,128)(2,1)}, u32[]{:S(2)}) copy-start(bf16[256,256]{1,0:T(8,128)(2,1)} %w_neigh_ref.1) | copy-start | bytes 393220
  42.6 7.2 %collective-permute-start.3 = (bf16[128,256]{1,0:T(8,128)(2,1)S(1)}, bf16[128,256]{1,0:T(8,128)(2,1)S(1)}, u32[]{:S(2)}, u32[]{:S(2)}) collective-permute-start(bf16[128,256]{1,0:T(8,128)(2,1)S(1)} %fusion), channel_id=1, source_target_pairs={{0,4},{1,5},{2,6},{3,7},{4,0},{5,1},{6,2},{7,3},{8,12},{9,13},{10,... | collective-permute-start | bytes 196616 | tf_op jit(solution)/shard_map/sum_over_h/ppermute | solution.py:338
  58.6 5.9 %collective-permute-start.4 = (bf16[1088,256]{1,0:T(8,128)(2,1)S(1)}, bf16[1088,256]{1,0:T(8,128)(2,1)S(1)}, u32[]{:S(2)}, u32[]{:S(2)}) collective-permute-start(bf16[1088,256]{1,0:T(8,128)(2,1)S(1)} %get-tuple-element.39), channel_id=1, source_target_pairs={{0,8},{8,0},{16,24},{24,16},{32,40},{40,32},{48,56},{56,48},{64,72... | collective-permute-start | bytes 1671176 | tf_op jit(solution)/shard_map/pair_sum/ppermute | solution.py:66
  77.8 3.6 %collective-permute-start.5 = (bf16[192,256]{1,0:T(8,128)(2,1)S(1)}, bf16[192,256]{1,0:T(8,128)(2,1)S(1)}, u32[]{:S(2)}, u32[]{:S(2)}) collective-permute-start(bf16[192,256]{1,0:T(8,128)(2,1)S(1)} %slice_bitcast_fusion), channel_id=1, source_target_pairs={{0,64},{8,72},{16,80},{24,88},{32,96},{40,104},{48,112},{56,120},{... | collective-permute-start | bytes 294920 | tf_op jit(solution)/shard_map/sum_over_section/ppermute | solution.py:356
  81.5 4.5 %collective-permute-start.6 = (bf16[192,256]{1,0:T(8,128)(2,1)S(1)}, bf16[192,256]{1,0:T(8,128)(2,1)S(1)}, u32[]{:S(2)}, u32[]{:S(2)}) collective-permute-start(bf16[192,256]{1,0:T(8,128)(2,1)S(1)} %add_convert_fusion.3), channel_id=1, source_target_pairs={{0,128},{8,136},{16,144},{24,152},{32,160},{40,168},{48,176},{56,1... | collective-permute-start | bytes 294920 | tf_op jit(solution)/shard_map/sum_over_section/ppermute | solution.py:359
  86.0 8.3 %collective-permute-start.7 = (bf16[128,256]{1,0:T(8,128)(2,1)S(1)}, bf16[128,256]{1,0:T(8,128)(2,1)S(1)}, u32[]{:S(2)}, u32[]{:S(2)}) collective-permute-start(bf16[128,256]{1,0:T(8,128)(2,1)S(1)} %slice.97), channel_id=1, source_target_pairs={{0,2},{1,11},{2,17},{3,26},{4,36},{5,45},{6,55},{7,60},{8,134},{9,... | collective-permute-start | bytes 196616 | tf_op jit(solution)/shard_map/return_panels/ppermute | solution.py:362
  103.2 5.1 %collective-permute-start.8 = (bf16[4,64,256]{2,1,0:T(8,128)(2,1)S(1)}, bf16[4,64,256]{2,1,0:T(8,128)(2,1)S(1)}, u32[]{:S(2)}, u32[]{:S(2)}) collective-permute-start(bf16[4,64,256]{2,1,0:T(8,128)(2,1)S(1)} %slice.99), channel_id=1, source_target_pairs={{0,8},{8,0},{16,24},{24,16},{32,40},{40,32},{48,56},{56,48},{64,72... | collective-permute-start | bytes 393224 | tf_op jit(solution)/shard_map/gather_results/ppermute | solution.py:66
